TPU v7x, 32 devices: a whole 2x2x4 slice. The times are simulated.
32 devices in a mesh: dp: 8 (over z, y), seq: 4 (over x, core).
Axes of the slice: x: 2, y: 2, z: 4, core: 2. Of those that a mesh axis runs over, the one named last changes fastest.
Arguments:
- decoder_in: bfloat16 [32, 512, 768], P(('dp', 'seq')), may hold values from -6 to 6
- memory: bfloat16 [32, 8192, 768], P(None, ('dp', 'seq')), may hold values from -6 to 6
- memory_lengths: int32 [32], P(('dp', 'seq')), may hold values from 3072 to 8192, as said below
- cotangent: bfloat16 [32, 512, 768], P(('dp', 'seq')), may hold values from -6 to 6
- norm_self: float32 [768], replicated, may hold values from 0.5 to 1.5
- self_query: bfloat16 [768, 768], replicated, may hold values from -0.0546875 to 0.0546875
- self_key: bfloat16 [768, 768], replicated, may hold values from -0.21875 to 0.21875
- self_value: bfloat16 [768, 768], replicated, may hold values from -0.21875 to 0.21875
- self_out: bfloat16 [768, 768], replicated, may hold values from -0.625 to 0.625
- norm_cross: float32 [768], replicated, may hold values from 0.5 to 1.5
- cross_query: bfloat16 [768, 768], replicated, may hold values from -0.0546875 to 0.0546875
- cross_key: bfloat16 [768, 768], replicated, may hold values from -0.21875 to 0.21875
- cross_value: bfloat16 [768, 768], replicated, may hold values from -0.21875 to 0.21875
- cross_out: bfloat16 [768, 768], replicated, may hold values from -0.875 to 0.875
- norm_ffn: float32 [768], replicated, may hold values from 0.5 to 1.5
- ffn_gate: bfloat16 [768, 2048], replicated, may hold values from -0.21875 to 0.21875
- ffn_up: bfloat16 [768, 2048], replicated, may hold values from -0.21875 to 0.21875
- ffn_down: bfloat16 [2048, 768], replicated, may hold values from -0.125 to 0.125
Outputs:
- decoder_out: bfloat16 [32, 512, 768], P(('dp', 'seq'))
- decoder_in_grad: float32 [32, 512, 768], P(('dp', 'seq'))
- memory_grad: bfloat16 [32, 8192, 768], P(None, ('dp', 'seq'))
- norm_self_grad: float32 [768], P(('dp', 'seq'))
- self_query_grad: float32 [768, 768], P(('dp', 'seq'))
- self_key_grad: float32 [768, 768], P(('dp', 'seq'))
- self_value_grad: float32 [768, 768], P(('dp', 'seq'))
- self_out_grad: float32 [768, 768], P(('dp', 'seq'))
- norm_cross_grad: float32 [768], P(('dp', 'seq'))
- cross_query_grad: float32 [768, 768], P(('dp', 'seq'))
- cross_key_grad: float32 [768, 768], P(('dp', 'seq'))
- cross_value_grad: float32 [768, 768], P(('dp', 'seq'))
- cross_out_grad: float32 [768, 768], P(('dp', 'seq'))
- norm_ffn_grad: float32 [768], P(('dp', 'seq'))
- ffn_gate_grad: float32 [768, 2048], P(('dp', 'seq'))
- ffn_up_grad: float32 [768, 2048], P(('dp', 'seq'))
- ffn_down_grad: float32 [2048, 768], P(('dp', 'seq'))
Inputs may be any that keep to these rules, and one draw needn't show every extreme that they name: `memory_lengths`: memory positions of each sequence that are valid; in every draw at least one sequence uses all 8192 positions.
All inputs are finite; a program needn't handle non-finite values.
Results may differ from a plain program's by a relative error of at most 0.025.
The roundings to bfloat16 on the way count: a program that leaves them out, or rounds other values in their place, can miss the bound.
Values may be sent and summed in bfloat16 or wider, within the bound.
A program may use at most 384 MiB of HBM per device.

v0:
```python
import jax
import jax.numpy as jnp
from jax import lax
from jax.sharding import PartitionSpec as P

H = 12
HD = 64


EPSILON = 1e-06
MASKED_SCORE = -1e30


def matmul(left, right):
    return jnp.dot(left, right, preferred_element_type=jnp.float32)


def matmul_t(left, right):
    return lax.dot_general(
        left, right, (((1,), (1,)), ((), ())), preferred_element_type=jnp.float32
    )


def tmatmul(left, right):
    return lax.dot_general(
        left, right, (((0,), (0,)), ((), ())), preferred_element_type=jnp.float32
    )


def norm_apply(values, gain):
    return values * lax.rsqrt(jnp.mean(values * values, axis=-1, keepdims=True) + EPSILON) * gain


def norm_back(values, gain, grad):
    primal, pulled = jax.vjp(norm_apply, values, gain)
    return pulled(grad)


def glu_apply(gate_vals, up_vals):
    return jax.nn.gelu(gate_vals, approximate=True) * up_vals


def to_heads(matrix):
    seq_count, row_count, width = matrix.shape
    return (
        matrix.reshape(seq_count, row_count, H, HD)
        .transpose(0, 2, 1, 3)
        .reshape(seq_count * H, row_count, HD)
    )


def from_heads(stacked, seq_count):
    row_count = stacked.shape[1]
    return (
        stacked.reshape(seq_count, H, row_count, HD)
        .transpose(0, 2, 1, 3)
        .reshape(seq_count * row_count, H * HD)
    )


def allowed_keys(row_count, key_count, key_limit, causal):
    row_index = lax.broadcasted_iota(jnp.int32, (row_count, key_count), 0)
    key_index = lax.broadcasted_iota(jnp.int32, (row_count, key_count), 1)
    if causal:
        return key_index <= row_index
    return key_index < key_limit


def attend_forward(queries, keyset, valset, limits, causal):
    seq_count = queries.shape[0]

    def one_item(head_entry):
        query_h, keys_h, values_h, key_limit = head_entry
        allowed = allowed_keys(query_h.shape[0], keys_h.shape[0], key_limit, causal)
        scores = jnp.where(allowed, matmul_t(query_h, keys_h), MASKED_SCORE)
        row_max = jnp.max(scores, axis=-1, keepdims=True)
        numerators = jnp.exp(scores - row_max)
        row_total = jnp.sum(numerators, axis=-1, keepdims=True)
        probs = (numerators / row_total).astype(jnp.bfloat16)
        return (matmul(probs, values_h), (row_max + jnp.log(row_total))[:, 0])

    outputs, log_totals = lax.map(
        one_item, (to_heads(queries), to_heads(keyset), to_heads(valset), jnp.repeat(limits, H))
    )
    return (from_heads(outputs, seq_count), log_totals)


def attend_backward(queries, keyset, valset, limits, causal, log_totals, grad_attn):
    seq_count = queries.shape[0]

    def one_item(head_entry):
        query_h, keys_h, values_h, key_limit, row_lse, grad_h = head_entry
        allowed = allowed_keys(query_h.shape[0], keys_h.shape[0], key_limit, causal)
        scores = jnp.where(allowed, matmul_t(query_h, keys_h), MASKED_SCORE)
        probs = jnp.exp(scores - row_lse[:, None])
        probs_low = probs.astype(jnp.bfloat16)
        grad_probs = matmul_t(grad_h, values_h)
        row_delta = jnp.sum(probs * grad_probs, axis=-1, keepdims=True)
        grad_scores = (probs * (grad_probs - row_delta)).astype(jnp.bfloat16)
        return (
            matmul(grad_scores, keys_h),
            tmatmul(grad_scores, query_h),
            tmatmul(probs_low, grad_h),
        )

    grad_q, grad_k, grad_v = lax.map(
        one_item,
        (
            to_heads(queries),
            to_heads(keyset),
            to_heads(valset),
            jnp.repeat(limits, H),
            log_totals,
            to_heads(grad_attn),
        ),
    )
    return (
        from_heads(grad_q, seq_count).astype(jnp.bfloat16),
        from_heads(grad_k, seq_count).astype(jnp.bfloat16),
        from_heads(grad_v, seq_count).astype(jnp.bfloat16),
    )


def on_device(
    decoder_in,
    memory,
    memory_lengths,
    cotangent,
    norm_self,
    self_query,
    self_key,
    self_value,
    self_out,
    norm_cross,
    cross_query,
    cross_key,
    cross_value,
    cross_out,
    norm_ffn,
    ffn_gate,
    ffn_up,
    ffn_down,
):
    seq_count, tgt_len, width = decoder_in.shape

    def as_seqs(matrix):
        return matrix.reshape(seq_count, -1, matrix.shape[-1])

    inputs = decoder_in.astype(jnp.float32).reshape(-1, width)
    normed_one = norm_apply(inputs, norm_self).astype(jnp.bfloat16)
    query_one = matmul(normed_one, self_query).astype(jnp.bfloat16)
    key_one = matmul(normed_one, self_key).astype(jnp.bfloat16)
    value_one = matmul(normed_one, self_value).astype(jnp.bfloat16)
    attn_raw, lse_one = attend_forward(
        as_seqs(query_one), as_seqs(key_one), as_seqs(value_one), memory_lengths, True
    )
    attn_one = attn_raw.astype(jnp.bfloat16)
    hidden_one = inputs + matmul(attn_one, self_out)
    normed_two = norm_apply(hidden_one, norm_cross).astype(jnp.bfloat16)
    query_two = matmul(normed_two, cross_query).astype(jnp.bfloat16)
    memory_here = lax.all_to_all(memory, ("dp", "seq"), split_axis=0, concat_axis=1, tiled=True)
    here_rows = memory_here.reshape(-1, width)
    keys_two = matmul(here_rows, cross_key).astype(jnp.bfloat16).reshape(memory_here.shape)
    values_two = matmul(here_rows, cross_value).astype(jnp.bfloat16).reshape(memory_here.shape)
    attn_raw_two, lse_two = attend_forward(
        as_seqs(query_two), keys_two, values_two, memory_lengths, False
    )
    attn_two = attn_raw_two.astype(jnp.bfloat16)
    hidden_two = hidden_one + matmul(attn_two, cross_out)
    normed_three = norm_apply(hidden_two, norm_ffn).astype(jnp.bfloat16)
    gate_vals = matmul(normed_three, ffn_gate)
    up_vals = matmul(normed_three, ffn_up)
    inner = glu_apply(gate_vals, up_vals).astype(jnp.bfloat16)
    output = hidden_two + matmul(inner, ffn_down)
    decoder_out = output.astype(jnp.bfloat16).reshape(decoder_in.shape)
    grad_out = cotangent.astype(jnp.float32).reshape(-1, width)
    branch_three = grad_out.astype(jnp.bfloat16)
    grad_down = tmatmul(inner, branch_three)
    grad_inner = matmul_t(branch_three, ffn_down)
    glu_value, glu_pull = jax.vjp(glu_apply, gate_vals, up_vals)
    grad_gate_raw, grad_up_raw = glu_pull(grad_inner)
    grad_gate_low = grad_gate_raw.astype(jnp.bfloat16)
    grad_up_low = grad_up_raw.astype(jnp.bfloat16)
    grad_gate = tmatmul(normed_three, grad_gate_low)
    grad_up = tmatmul(normed_three, grad_up_low)
    grad_normed_three = matmul_t(grad_gate_low, ffn_gate) + matmul_t(grad_up_low, ffn_up)
    back_two, grad_norm_ffn = norm_back(hidden_two, norm_ffn, grad_normed_three)
    grad_two = grad_out + back_two
    branch_two = grad_two.astype(jnp.bfloat16)
    grad_cross_out = tmatmul(attn_two, branch_two)
    grad_attn_two = matmul_t(branch_two, cross_out).astype(jnp.bfloat16)
    grad_q_two, grad_k_two, grad_v_two = attend_backward(
        as_seqs(query_two),
        keys_two,
        values_two,
        memory_lengths,
        False,
        lse_two,
        as_seqs(grad_attn_two),
    )
    grad_cross_query = tmatmul(normed_two, grad_q_two)
    grad_normed_two = matmul_t(grad_q_two, cross_query)
    here_rows = memory_here.reshape(-1, width)
    grad_cross_key = tmatmul(here_rows, grad_k_two)
    grad_cross_value = tmatmul(here_rows, grad_v_two)
    grad_here = (
        (matmul_t(grad_k_two, cross_key) + matmul_t(grad_v_two, cross_value))
        .astype(jnp.bfloat16)
        .reshape(memory_here.shape)
    )
    memory_grad = lax.all_to_all(grad_here, ("dp", "seq"), split_axis=1, concat_axis=0, tiled=True)
    back_one, grad_norm_cross = norm_back(hidden_one, norm_cross, grad_normed_two)
    grad_one = grad_two + back_one
    branch_one = grad_one.astype(jnp.bfloat16)
    grad_self_out = tmatmul(attn_one, branch_one)
    grad_attn_one = matmul_t(branch_one, self_out).astype(jnp.bfloat16)
    grad_q_one, grad_k_one, grad_v_one = attend_backward(
        as_seqs(query_one),
        as_seqs(key_one),
        as_seqs(value_one),
        memory_lengths,
        True,
        lse_one,
        as_seqs(grad_attn_one),
    )
    grad_self_query = tmatmul(normed_one, grad_q_one)
    grad_self_key = tmatmul(normed_one, grad_k_one)
    grad_self_value = tmatmul(normed_one, grad_v_one)
    grad_normed_one = (
        matmul_t(grad_q_one, self_query)
        + matmul_t(grad_k_one, self_key)
        + matmul_t(grad_v_one, self_value)
    )
    back_in, grad_norm_self = norm_back(inputs, norm_self, grad_normed_one)
    decoder_in_grad = (grad_one + back_in).reshape(decoder_in.shape)
    summed = (
        lax.psum_scatter(grad_norm_self, ("dp", "seq"), scatter_dimension=0, tiled=True),
        lax.psum_scatter(grad_self_query, ("dp", "seq"), scatter_dimension=0, tiled=True),
        lax.psum_scatter(grad_self_key, ("dp", "seq"), scatter_dimension=0, tiled=True),
        lax.psum_scatter(grad_self_value, ("dp", "seq"), scatter_dimension=0, tiled=True),
        lax.psum_scatter(grad_self_out, ("dp", "seq"), scatter_dimension=0, tiled=True),
        lax.psum_scatter(grad_norm_cross, ("dp", "seq"), scatter_dimension=0, tiled=True),
        lax.psum_scatter(grad_cross_query, ("dp", "seq"), scatter_dimension=0, tiled=True),
        lax.psum_scatter(grad_cross_key, ("dp", "seq"), scatter_dimension=0, tiled=True),
        lax.psum_scatter(grad_cross_value, ("dp", "seq"), scatter_dimension=0, tiled=True),
        lax.psum_scatter(grad_cross_out, ("dp", "seq"), scatter_dimension=0, tiled=True),
        lax.psum_scatter(grad_norm_ffn, ("dp", "seq"), scatter_dimension=0, tiled=True),
        lax.psum_scatter(grad_gate, ("dp", "seq"), scatter_dimension=0, tiled=True),
        lax.psum_scatter(grad_up, ("dp", "seq"), scatter_dimension=0, tiled=True),
        lax.psum_scatter(grad_down, ("dp", "seq"), scatter_dimension=0, tiled=True),
    )
    return (decoder_out, decoder_in_grad, memory_grad) + tuple(summed)


def solution(mesh):
    placed = (
        P(("dp", "seq"), None, None),
        P(None, ("dp", "seq"), None),
        P(("dp", "seq")),
        P(("dp", "seq"), None, None),
        P(),
        P(),
        P(),
        P(),
        P(),
        P(),
        P(),
        P(),
        P(),
        P(),
        P(),
        P(),
        P(),
        P(),
    )
    return jax.shard_map(
        on_device,
        mesh=mesh,
        in_specs=placed,
        out_specs=(
            P(("dp", "seq"), None, None),
            P(("dp", "seq"), None, None),
            P(None, ("dp", "seq"), None),
            P(("dp", "seq")),
            P(("dp", "seq"), None),
            P(("dp", "seq"), None),
            P(("dp", "seq"), None),
            P(("dp", "seq"), None),
            P(("dp", "seq")),
            P(("dp", "seq"), None),
            P(("dp", "seq"), None),
            P(("dp", "seq"), None),
            P(("dp", "seq"), None),
            P(("dp", "seq")),
            P(("dp", "seq"), None),
            P(("dp", "seq"), None),
            P(("dp", "seq"), None),
        ),
        check_vma=False,
    )
```

profile of v0, /device:TPU:0, one launch (start us, length us, event | category | flops | bytes accessed | tf_op | source)
XLA Modules:
  0.0 2582.3 jit_solution(805177502423620843)
XLA Ops:
  42.1 41.0 %while.52 = (s32[]{:T(128)}, bf16[12,512,64]{1,2,0:T(8,128)(2,1)}, f32[12,512]{1,0:T(8,128)S(1)}, bf16[12,512,64]{2,1,0:T(8,128)(2,1)}, bf16[12,512,64]{2,1,0:T(...) while((s32[]{:T(128)}, bf16[12,512,64]{1,2,0:T(8,128)(2,1)}, f32[12,512]{1,0:T(8,128)S(1)}, ...), condition=%wide.region_4.5_spmd, body=%wide.region_1.4_spmd.sunk | while | flops 69205504 | bytes 3692641 | solution.py:82
  93.6 199.8 %all-to-all-done = bf16[32,256,768]{2,1,0:T(8,128)(2,1)} async-done(((bf16[32,256,768]{2,1,0:T(8,128)(2,1)}), bf16[32,256,768]{2,1,0:T(8,128)(2,1)}, u32[]{:S(2)}, u32[]{:S(2)}) %all-to-all-start) | async-done | bytes 12582944 | tf_op jit(solution)/shard_map/all_to_all | solution.py:161
  293.4 16.0 convolution_convert_fusion
  309.4 22.9 copy.94
  332.2 16.3 convolution_convert_fusion.1
  348.6 22.8 copy.93
  372.3 352.2 %while.53 = (s32[]{:T(128)}, bf16[12,512,64]{1,2,0:T(8,128)(2,1)}, f32[12,512]{1,0:T(8,128)S(1)}, s32[12]{0:T(128)S(1)}, bf16[12,512,64]{2,1,0:T(8,128)(2,1)}, /...) while((s32[]{:T(128)}, bf16[12,512,64]{1,2,0:T(8,128)(2,1)}, ...), condition=%wide.region_9.10_spmd, body=%wide.region_6.9_spmd.sunk | while | flops 1111498240 | bytes 54843512 | solution.py:82
  751.5 605.4 %while.54 = (s32[]{:T(128)}, bf16[12,512,64]{1,2,0:T(8,128)(2,1)}, bf16[12,8192,64]{1,2,0:T(8,128)(2,1)}, bf16[12,8192,64]{1,2,0:T(8,128)(2,1)}, s32[12]{0:T(128...) while((s32[]{:T(128)}, bf16[12,512,64]{1,2,0:T(8,128)(2,1)}, ...), condition=%wide.region_14.15_spmd, body=%wide.region_12.14_spmd.sunk | while | flops 2717916672 | bytes 203979952 | solution.py:106
  762.8 12.3 multiply_reduce_fusion.10
  813.9 12.2 multiply_reduce_fusion.10
  914.9 12.0 multiply_reduce_fusion.10
  965.2 12.0 multiply_reduce_fusion.10
  1015.5 12.0 multiply_reduce_fusion.10
  1065.8 12.0 multiply_reduce_fusion.10
  1116.1 12.0 multiply_reduce_fusion.10
  1267.0 12.0 multiply_reduce_fusion.10
  1317.3 12.0 multiply_reduce_fusion.10
  1373.3 106.3 %while.55 = (s32[]{:T(128)}, bf16[12,512,64]{1,2,0:T(8,128)(2,1)}, bf16[12,512,64]{1,2,0:T(8,128)(2,1)}, bf16[12,512,64]{1,2,0:T(8,128)(2,1)}, bf16[12,512,64]{2...) while((s32[]{:T(128)}, bf16[12,512,64]{1,2,0:T(8,128)(2,1)}, ...), condition=%wide.region_18.19_spmd, body=%wide.region_16.18_spmd.sunk | while | flops 170130944 | bytes 9059441 | solution.py:106
  1495.1 16.7 convolution_bitcast_fusion.6
  1514.9 16.2 convolution_bitcast_fusion.7
  1540.6 18.2 fusion.142
  1558.9 22.6 fusion.86
  1581.4 22.6 copy.115
  1604.5 127.0 %reduce = bf16[8192,768]{1,0:T(8,128)(2,1)} reduce(bf16[8192,1,768]{2,1,0:T(2,128)(2,1)} %bitcast.397, bf16[]{:T(256)} %broadcast.197), dimensions={1}, to_apply=%bitcast.318.reduce_sub_computation | reduce | bytes 25165826
  1731.5 21.8 reshape.312
  1776.4 292.3 %all-reduce.3 = (f32[768]{0:T(1024)S(1)}, f32[768]{0:T(1024)S(1)}, f32[768]{0:T(1024)S(1)}) all-reduce(f32[768]{0:T(1024)S(1)} %get-tuple-element.369, f32[768]{0:T(1024)S(1)} %copy-done.35, f32[768]{0:T(1024)S(1)} %copy-done.34), channel_id=2, replica_groups=mesh['dp'=8,'seq'=4] {'dp','seq'}, use_global_device_ids=true, to_apply=%region_21.22.clone | all-reduce | flops 2304 | bytes 18432
  2077.1 27.6 %reshape.313 = bf16[8192,1,768]{2,1,0:T(2,128)(2,1)} reshape(bf16[32,2,98304]{2,1,0:T(2,128)(2,1)} %all-to-all-done.1) | data formatting | bytes 25165824
  2104.7 15.2 copy.113
  2120.0 95.3 %reduce-scatter.34.cloned.1.call-done = f32[24,768]{1,0:T(8,128)} async-done(((f32[768,768]{1,0:T(8,128)}), f32[24,768]{1,0:T(8,128)}) %reduce-scatter.34.cloned.1.call-update) | async-done | bytes 73744
  2215.2 119.8 %reduce-scatter.30.cloned.1.call-done = f32[24,2048]{1,0:T(8,128)} async-done(((f32[768,2048]{1,0:T(8,128)}), f32[24,2048]{1,0:T(8,128)}) %reduce-scatter.30.cloned.1.call-update) | async-done | bytes 196624 | tf_op jit(solution)/shard_map/reduce_scatter | solution.py:249
  2335.1 120.6 %reduce-scatter.28.cloned.1.call-done = f32[24,2048]{1,0:T(8,128)} async-done(((f32[768,2048]{1,0:T(8,128)}), f32[24,2048]{1,0:T(8,128)}) %reduce-scatter.28.cloned.1.call-update) | async-done | bytes 196624 | tf_op jit(solution)/shard_map/reduce_scatter | solution.py:248
  2455.6 119.8 %reduce-scatter.32.cloned.1.call-done = f32[64,768]{1,0:T(8,128)} async-done(((f32[2048,768]{1,0:T(8,128)}), f32[64,768]{1,0:T(8,128)}) %reduce-scatter.32.cloned.1.call-update) | async-done | bytes 196624 | tf_op jit(solution)/shard_map/reduce_scatter | solution.py:250
  (528 shorter events, 1143.6 us)
Async XLA Ops:
  7.2 724.9 %copy-start = (bf16[2048,768]{1,0:T(8,128)(2,1)S(1)}, bf16[2048,768]{1,0:T(8,128)(2,1)}, u32[]{:S(2)}) copy-start(bf16[2048,768]{1,0:T(8,128)(2,1)} %param.43) | copy-start | bytes 9437188
  7.2 286.2 %all-to-all-start = ((bf16[32,256,768]{2,1,0:T(8,128)(2,1)}), bf16[32,256,768]{2,1,0:T(8,128)(2,1)}, u32[]{:S(2)}, u32[]{:S(2)}) async-start(bf16[32,256,768]{2,1,0:T(8,128)(2,1)} %param.27), calls=%async_computation | async-start | bytes 25165824 | tf_op jit(solution)/shard_map/all_to_all | solution.py:161
  14.6 2105.2 %reduce-scatter.26.cloned.1.call-start = ((), (), s32[]{:S(2)}) async-start(), calls=%async_computation.18 | async-start | bytes 2433024 | tf_op jit(solution)/shard_map/reduce_scatter | solution.py:246
  17.3 15.9 copy-start.22
  727.5 15.4 copy-start.5
  750.5 1369.4 %reduce-scatter.24.cloned.1.call-start = ((), (), s32[]{:S(2)}) async-start(), calls=%async_computation.17 | async-start | bytes 2433024 | tf_op jit(solution)/shard_map/reduce_scatter | solution.py:243
  751.5 605.4 %copy-start.26 = (f32[512]{0:T(512)S(1)}, f32[512]{0:T(512)}, u32[]{:S(2)}) copy-start(f32[512]{0:T(512)} %copy-done.25) | copy-start | bytes 6148
  751.5 605.4 %copy-start.30 = (f32[768]{0:T(1024)S(1)}, f32[768]{0:T(1024)}, u32[]{:S(2)}) copy-start(f32[768]{0:T(1024)} %param.35) | copy-start | bytes 9220
  775.1 15.8 copy-start.1
  826.1 15.5 copy-start.1
  876.5 15.4 copy-start.1
  926.9 15.4 copy-start.1
  977.2 15.4 copy-start.1
  1027.5 15.4 copy-start.1
  1077.8 15.4 copy-start.1
  1128.1 15.4 copy-start.1
  1178.4 15.4 copy-start.1
  1228.7 15.4 copy-start.1
  1329.3 15.4 copy-start.1
  1370.3 749.5 %reduce-scatter.16.cloned.1.call-start = ((), (), s32[]{:S(2)}) async-start(), calls=%async_computation.13 | async-start | bytes 2433024 | tf_op jit(solution)/shard_map/reduce_scatter | solution.py:238
  1373.3 106.3 %copy-start.21 = (f32[768]{0:T(1024)S(1)}, f32[768]{0:T(1024)}, u32[]{:S(2)}) copy-start(f32[768]{0:T(1024)} %param.30) | copy-start | bytes 9220
  1373.3 106.3 %copy-start.23 = (f32[512]{0:T(512)S(1)}, f32[512]{0:T(512)}, u32[]{:S(2)}) copy-start(f32[512]{0:T(512)} %copy-done.22) | copy-start | bytes 6148
  1483.4 636.5 %reduce-scatter.22.cloned.1.call-start = ((), (), s32[]{:S(2)}) async-start(), calls=%async_computation.16 | async-start | bytes 2433024 | tf_op jit(solution)/shard_map/reduce_scatter | solution.py:241
  1487.3 632.6 %reduce-scatter.20.cloned.1.call-start = ((), (), s32[]{:S(2)}) async-start(), calls=%async_computation.15 | async-start | bytes 2433024 | tf_op jit(solution)/shard_map/reduce_scatter | solution.py:240
  1491.2 628.8 %reduce-scatter.18.cloned.1.call-start = ((), (), s32[]{:S(2)}) async-start(), calls=%async_computation.14 | async-start | bytes 2433024 | tf_op jit(solution)/shard_map/reduce_scatter | solution.py:239
  1495.1 624.9 %reduce-scatter.36.cloned.1.call-start = ((), (), s32[]{:S(2)}) async-start(), calls=%async_computation.23 | async-start | bytes 2433024
  1514.9 700.4 %reduce-scatter.34.cloned.1.call-start = ((), (), s32[]{:S(2)}) async-start(), calls=%async_computation.22 | async-start | bytes 2433024
  1534.2 800.8 %reduce-scatter.30.cloned.1.call-start = ((), (), s32[]{:S(2)}) async-start(), calls=%async_computation.20 | async-start | bytes 6488064 | tf_op jit(solution)/shard_map/reduce_scatter | solution.py:249
  1753.3 323.7 %all-to-all-start.1 = ((bf16[32,2,98304]{2,1,0:T(2,128)(2,1)}), bf16[32,2,98304]{2,1,0:T(2,128)(2,1)}, u32[]{:S(2)}, u32[]{:S(2)}) async-start(bf16[32,2,98304]{2,1,0:T(2,128)(2,1)} %reshape.312), calls=%async_computation.1 | async-start | bytes 25165824 | tf_op jit(solution)/shard_map/all_to_all | solution.py:211
  1757.2 698.5 %reduce-scatter.28.cloned.1.call-start = ((), (), s32[]{:S(2)}) async-start(), calls=%async_computation.19 | async-start | bytes 6488064 | tf_op jit(solution)/shard_map/reduce_scatter | solution.py:248
  1763.5 811.9 %reduce-scatter.32.cloned.1.call-start = ((), (), s32[]{:S(2)}) async-start(), calls=%async_computation.21 | async-start | bytes 6488064 | tf_op jit(solution)/shard_map/reduce_scatter | solution.py:250
  1774.1 296.4 %copy-start.28 = (f32[512]{0:T(512)S(1)}, f32[512]{0:T(512)}, u32[]{:S(2)}) copy-start(f32[512]{0:T(512)} %copy-done.27) | copy-start | bytes 6148
  (33 other events, 96.3 us)
Sparse Core Ops, SparseCore 0:
  750.6 94.9 reduce-scatter.25
  1370.5 94.9 reduce-scatter.23
  1483.5 94.8 reduce-scatter.15
  1585.0 98.0 reduce-scatter.21
  1688.8 157.6 reduce-scatter.19
  1853.1 153.3 reduce-scatter.17
  2012.4 98.0 reduce-scatter.35
  2117.1 98.0 reduce-scatter.33
  2221.5 113.5 reduce-scatter.29
  2342.1 113.5 reduce-scatter.27
  2461.8 113.4 reduce-scatter.31
where the time goes:
time: 2600 us; the launch traced here: 2580 us
  matrix products  957 us (37%)
  waiting for transfers between devices  655 us (25%)
  other arithmetic  404 us (16%)
  blocking collectives  292 us (11%)
  local copies, waits for them, and re-layouts  245 us (9%)
    dot_general x83, matrix products, matmul_t(): lax.dot_general(left, right, (((1,), (1,)), ((), ())), preferred_element_...  489 us
    unnamed x1, blocking collectives  292 us
    dot_general x59, matrix products, matmul(): return jnp.dot(left, right, preferred_element_type=jnp.float32)  268 us
    dot_general x59, matrix products, tmatmul(): lax.dot_general(left, right, (((0,), (0,)), ((), ())), preferred_element_...  200 us
    all_to_all x1, waiting for transfers between devices, on_device(): lax.all_to_all(memory, ('dp', 'seq'), split_axis=0, concat_axis=1, tiled=...  200 us
    convert_element_type x24, other arithmetic, one_item(): grad_scores = (probs * (grad_probs - row_delta)).astype(jnp.bfloat16)  143 us
    unnamed x1, other arithmetic  127 us
    reduce_scatter x1, waiting for transfers between devices, on_device(): lax.psum_scatter(grad_gate, ('dp', 'seq'), scatter_dimension=0, tiled=True)  121 us
  transfers between devices with their start and end apart: 13, of which 5 were waited for; matrix products, arithmetic and copies ran while one was open for 43% of the time, Pallas kernels for 0%

commit v1 on v0

v1 whole, which is shorter than its diff:
```python
import functools

import jax
import jax.numpy as jnp
from jax import lax
from jax.experimental import pallas as pl
from jax.experimental.pallas import tpu as pltpu
from jax.sharding import Mesh
from jax.sharding import PartitionSpec as P

H = 12
HD = 64
PAIRS = 6
PLANES = 4
EPSILON = 1e-06
MASKED = -1e30
VMEM = 56 * 2**20
BF = jnp.bfloat16
F32 = jnp.float32
ALL = ("z", "y", "x", "c")
PLANE = ("y", "x", "c")


def dot(left, right, left_dim, right_dim):
    return lax.dot_general(
        left, right, (((left_dim,), (right_dim,)), ((), ())), preferred_element_type=F32
    )


def lane_masks():
    lane = lax.broadcasted_iota(jnp.int32, (1, 2 * HD), 1)
    low = jnp.where(lane < HD, 1.0, 0.0)
    first = jnp.where(lane == HD, 1.0, 0.0)
    second = jnp.where(lane == 0, 1.0, 0.0)
    low, high, first, second = (
        v.astype(BF) for v in (low, 1.0 - low, first, second)
    )
    return ((low, high, first), (high, low, second))


def causal_mask(scores):
    key = lax.broadcasted_iota(jnp.int32, scores.shape, 0)
    query = lax.broadcasted_iota(jnp.int32, scores.shape, 1)
    return jnp.where(key <= query, scores, MASKED)


def forward_kernel(*refs, causal):
    if causal:
        q_ref, kv_ref, o_ref, lse_ref = refs
    else:
        q_ref, kv_ref, bias_ref, o_ref, lse_ref = refs
        bias = bias_ref[...]
    masks = lane_masks()
    queries = q_ref[...]
    keys = kv_ref[:, 0:128]
    values = kv_ref[:, 128:256]
    all_scores = []
    for mine, other, one in masks:
        if causal:
            all_scores.append(causal_mask(dot(keys, queries * mine, 1, 1)))
        else:
            all_scores.append(dot(keys * mine + bias * one, queries * mine + one, 1, 1))
    parts = []
    for h in range(2):
        mine, other, _ = masks[h]
        scores = all_scores[h]
        row_max = jnp.max(scores, axis=0, keepdims=True)
        probs = jnp.exp(scores - row_max).astype(BF)
        both = dot(values * mine + other, probs, 0, 0)
        halves = (both[:HD], both[HD:])
        total = halves[1 - h]
        parts.append(halves[h] / total)
        lse_ref[0, h : h + 1, :] = row_max + jnp.log(total[0:1])
    o_ref[...] = jnp.concatenate(parts, axis=0).T.astype(BF)


def backward_kernel(*refs, causal):
    if causal:
        q_ref, da_ref, kv_ref, lse_ref, dkv_ref, dq_ref = refs
    else:
        q_ref, da_ref, kv_ref, bias_ref, lse_ref, delta_ref, dkv_ref, dq_ref = refs
        bias = bias_ref[...]
    queries = q_ref[...]
    grad = da_ref[...]
    keys = kv_ref[:, 0:128]
    values = kv_ref[:, 128:256]
    grad_k = None
    grad_v = None
    grad_q = []
    for h, (mine, other, one) in enumerate(lane_masks()):
        query_h = queries * mine
        grad_h = grad * mine
        if causal:
            scores = causal_mask(dot(keys, query_h, 1, 1))
        else:
            scores = dot(keys * mine + bias * one, query_h + one, 1, 1)
        probs = jnp.exp(scores - lse_ref[0, h : h + 1, :])
        grad_p = dot(values, grad_h, 1, 1)
        if causal:
            delta = jnp.sum(probs * grad_p, axis=0, keepdims=True)
        else:
            delta = delta_ref[0, h : h + 1, :]
        grad_s = (probs * (grad_p - delta)).astype(BF)
        term_v = dot(probs.astype(BF), grad_h, 1, 0)
        term_k = dot(grad_s, query_h, 1, 0)
        grad_v = term_v if grad_v is None else grad_v + term_v
        grad_k = term_k if grad_k is None else grad_k + term_k
        grad_q.append(dot(keys, grad_s, 0, 0)[h * HD : (h + 1) * HD])
    dkv_ref[:, 0:128] = grad_k.astype(BF)
    dkv_ref[:, 128:256] = grad_v.astype(BF)
    dq_ref[...] = jnp.concatenate(grad_q, axis=0).T.astype(BF)


def specs(tokens, keys):
    return (
        pl.BlockSpec((tokens, 128), lambda p: (0, p)),
        pl.BlockSpec((keys, 256), lambda p: (0, p)),
        pl.BlockSpec((keys, 128), lambda p: (0, 0)),
        pl.BlockSpec((1, 2, tokens), lambda p: (p, 0, 0)),
    )


def estimate(tokens, keys, count):
    work = tokens * keys * H
    return pl.CostEstimate(
        flops=2 * 4 * count * work * HD, bytes_accessed=keys * 6144, transcendentals=work
    )


def attend(queries, keyvals, bias=None):
    tokens, keys = queries.shape[0], keyvals.shape[0]
    col, pair, mask, row = specs(tokens, keys)
    causal = bias is None
    return pl.pallas_call(
        functools.partial(forward_kernel, causal=causal),
        grid=(PAIRS,),
        out_shape=[
            jax.ShapeDtypeStruct((tokens, H * HD), BF),
            jax.ShapeDtypeStruct((PAIRS, 2, tokens), F32),
        ],
        in_specs=[col, pair] + ([] if causal else [mask]),
        out_specs=[col, row],
        compiler_params=pltpu.CompilerParams(vmem_limit_bytes=VMEM),
        cost_estimate=estimate(tokens, keys, 2),
    )(queries, keyvals, *(() if causal else (bias,)))


def attend_back(queries, grad, keyvals, lse, bias=None, delta=None):
    tokens, keys = queries.shape[0], keyvals.shape[0]
    col, pair, mask, row = specs(tokens, keys)
    causal = bias is None
    if causal:
        in_specs, args = [col, col, pair, row], (queries, grad, keyvals, lse)
    else:
        in_specs = [col, col, pair, mask, row, row]
        args = (queries, grad, keyvals, bias, lse, delta)
    return pl.pallas_call(
        functools.partial(backward_kernel, causal=causal),
        grid=(PAIRS,),
        out_shape=[
            jax.ShapeDtypeStruct((keys, 2 * H * HD), BF),
            jax.ShapeDtypeStruct((tokens, H * HD), BF),
        ],
        in_specs=in_specs,
        out_specs=[pair, col],
        compiler_params=pltpu.CompilerParams(vmem_limit_bytes=VMEM),
        cost_estimate=estimate(tokens, keys, 4),
    )(*args)


def place_kernel(*refs, plane_size):
    *blocks, out_ref, sems = refs
    z = lax.axis_index("z")
    me = lax.axis_index(PLANE)
    copies = []
    for n, block in enumerate(blocks):
        r, k = divmod(n, plane_size)
        row = (z ^ r) * plane_size + (me ^ k)
        copies.append(pltpu.make_async_copy(block, out_ref.at[row], sems.at[n]))
    for copy in copies:
        copy.start()
    for copy in copies:
        copy.wait()


def place(blocks, plane_size):
    shape = blocks[0].shape
    hbm = pl.BlockSpec(memory_space=pl.ANY)
    return pl.pallas_call(
        functools.partial(place_kernel, plane_size=plane_size),
        out_shape=jax.ShapeDtypeStruct((len(blocks),) + shape, blocks[0].dtype),
        in_specs=[hbm] * len(blocks),
        out_specs=hbm,
        scratch_shapes=[pltpu.SemaphoreType.DMA((len(blocks),))],
    )(*blocks)


def interleave(keys, values):
    width = keys.shape[0]
    return jnp.stack(
        [keys.reshape(width, PAIRS, 128), values.reshape(width, PAIRS, 128)], axis=2
    ).reshape(width, 2 * H * HD)


def separate(both):
    rows = both.shape[0]
    parts = both.reshape(rows, PAIRS, 2, 128)
    return parts[:, :, 0].reshape(rows, H * HD), parts[:, :, 1].reshape(rows, H * HD)


def per_row(stat):
    tokens = stat.shape[-1]
    return jnp.repeat(stat.reshape(H, tokens).T, HD, axis=1)


def norm_apply(values, gain):
    return values * lax.rsqrt(jnp.mean(values * values, axis=-1, keepdims=True) + EPSILON) * gain


def norm_back(values, gain, grad):
    r = lax.rsqrt(jnp.mean(values * values, axis=-1, keepdims=True) + EPSILON)
    u = gain * grad
    dv = r * u - values * (r * r * r) * jnp.mean(u * values, axis=-1, keepdims=True)
    return dv, jnp.sum(grad * values * r, axis=0)


def glu_apply(gate_vals, up_vals):
    return jax.nn.gelu(gate_vals, approximate=True) * up_vals


def matmul(left, right):
    return dot(left, right, 1, 0)


def matmul_t(left, right):
    return dot(left, right, 1, 1)


def tmatmul(left, right):
    return dot(left, right, 0, 0)


def scatter_sum(arrays, devices):
    flat = [a.astype(BF).reshape(devices, -1) for a in arrays]
    sizes = [f.shape[1] for f in flat]
    extra = -sum(sizes) % 128
    if extra:
        flat.append(jnp.zeros((devices, extra), BF))
    joined = jnp.concatenate(flat, axis=1)
    mine = lax.psum_scatter(
        joined.reshape(devices, -1, 128), ALL, scatter_dimension=0, tiled=True
    ).reshape(-1).astype(F32)
    out = []
    at = 0
    for size, a in zip(sizes, arrays):
        out.append(mine[at : at + size].reshape((a.shape[0] // devices,) + a.shape[1:]))
        at += size
    return out


def on_device(
    plane_size,
    decoder_in,
    memory,
    memory_lengths,
    cotangent,
    norm_self,
    self_query,
    self_key,
    self_value,
    self_out,
    norm_cross,
    cross_query,
    cross_key,
    cross_value,
    cross_out,
    norm_ffn,
    ffn_gate,
    ffn_up,
    ffn_down,
):
    devices, positions, width = memory.shape
    z = lax.axis_index("z")
    me = lax.axis_index(PLANE)

    def along_z(value, r):
        if r == 0:
            return value
        return lax.ppermute(value, "z", [(i, i ^ r) for i in range(PLANES)])

    def in_plane(value, k):
        if k == 0:
            return value
        return lax.ppermute(value, PLANE, [(i, i ^ k) for i in range(plane_size)])

    by_plane = memory.reshape(PLANES, plane_size, positions, width)
    arrived = {}
    for r in (1, 2, 3, 0):
        group = lax.dynamic_index_in_dim(by_plane, z ^ r, 0, keepdims=False)
        blocks = []
        for k in range(plane_size):
            block = lax.dynamic_index_in_dim(group, me ^ k, 0, keepdims=False)
            blocks.append(in_plane(block, k))
        arrived[r] = blocks

    within = jnp.arange(positions, dtype=jnp.int32)
    places = jnp.concatenate([(z * plane_size + (me ^ k)) * positions + within for k in range(plane_size)])

    inputs = decoder_in[0].astype(F32)
    normed_one = norm_apply(inputs, norm_self).astype(BF)
    self_weights = jnp.concatenate([self_query, interleave(self_key, self_value)], axis=1)
    qkv_one = matmul(normed_one, self_weights).astype(BF)
    query_one, keyval_one = qkv_one[:, :width], qkv_one[:, width:]
    attn_one, lse_one = attend(query_one, keyval_one)
    hidden_one = inputs + matmul(attn_one, self_out)
    normed_two = norm_apply(hidden_one, norm_cross).astype(BF)
    query_two = matmul(normed_two, cross_query).astype(BF)

    cross_weights = interleave(cross_key, cross_value)
    queries, rows, keyvals, biases, partial = {}, {}, {}, {}, {}
    for r in (1, 2, 3, 0):
        queries[r] = along_z(query_two, r)
        limit = along_z(memory_lengths, r)
        bias = jnp.where(places < limit, 0.0, MASKED).astype(BF)
        biases[r] = jnp.broadcast_to(bias[:, None], (bias.shape[0], 128))
    for r in (1, 2, 3, 0):
        rows[r] = jnp.concatenate(arrived[r], axis=0)
        keyvals[r] = matmul(rows[r], cross_weights).astype(BF)
        out_r, lse_r = attend(queries[r], keyvals[r], biases[r])
        partial[r] = (along_z(out_r, r), along_z(lse_r, r))
    lses = jnp.stack([partial[r][1] for r in range(PLANES)])
    top = jnp.max(lses, axis=0)
    scale = jnp.exp(lses - top)
    total = jnp.sum(scale, axis=0)
    lse_two = top + jnp.log(total)
    share = scale / total
    attn_raw_two = sum(per_row(share[r]) * partial[r][0].astype(F32) for r in range(PLANES))
    attn_two = attn_raw_two.astype(BF)
    hidden_two = hidden_one + matmul(attn_two, cross_out)

    normed_three = norm_apply(hidden_two, norm_ffn).astype(BF)
    gate_vals = matmul(normed_three, ffn_gate)
    up_vals = matmul(normed_three, ffn_up)
    inner = glu_apply(gate_vals, up_vals).astype(BF)
    output = hidden_two + matmul(inner, ffn_down)
    decoder_out = output.astype(BF)[None]

    branch_three = cotangent[0]
    grad_out = branch_three.astype(F32)
    grad_inner = matmul_t(branch_three, ffn_down)
    _, glu_pull = jax.vjp(glu_apply, gate_vals, up_vals)
    grad_gate_raw, grad_up_raw = glu_pull(grad_inner)
    grad_gate_low = grad_gate_raw.astype(BF)
    grad_up_low = grad_up_raw.astype(BF)
    grad_normed_three = matmul_t(grad_gate_low, ffn_gate) + matmul_t(grad_up_low, ffn_up)
    back_two, grad_norm_ffn = norm_back(hidden_two, norm_ffn, grad_normed_three)
    grad_two = grad_out + back_two
    branch_two = grad_two.astype(BF)
    grad_attn_two = matmul_t(branch_two, cross_out).astype(BF)
    products = grad_attn_two.astype(F32) * attn_raw_two
    delta_two = jnp.sum(products.reshape(-1, H, HD), axis=-1).T.reshape(PAIRS, 2, -1)

    grad_down = tmatmul(inner, branch_three)
    grad_gate = tmatmul(normed_three, grad_gate_low)
    grad_up = tmatmul(normed_three, grad_up_low)
    grad_cross_out = tmatmul(attn_two, branch_two)
    ffn_sums = scatter_sum((grad_gate, grad_up, grad_down, grad_cross_out), devices)

    order = (0, 2, 3, 1)
    stats = jnp.stack([lse_two, delta_two])
    sent = {r: (along_z(grad_attn_two, r), along_z(stats, r)) for r in order}
    returned = {}
    grad_q = {}
    grad_weights = None
    for r in order:
        grad_r, stats_r = sent[r]
        grad_kv, grad_q_r = attend_back(
            queries[r], grad_r, keyvals[r], stats_r[0], biases[r], stats_r[1]
        )
        grad_q[r] = along_z(grad_q_r, r)
        grad_rows = matmul_t(grad_kv, cross_weights).astype(BF)
        returned[r] = [
            in_plane(grad_rows[k * positions : (k + 1) * positions], k) for k in range(plane_size)
        ]
        term = tmatmul(rows[r], grad_kv)
        grad_weights = term if grad_weights is None else grad_weights + term
    memory_grad = place(
        [block for r in range(PLANES) for block in returned[r]], plane_size
    )

    grad_q_two = sum(grad_q[r].astype(F32) for r in range(PLANES)).astype(BF)
    grad_cross_query = tmatmul(normed_two, grad_q_two)
    grad_normed_two = matmul_t(grad_q_two, cross_query)
    back_one, grad_norm_cross = norm_back(hidden_one, norm_cross, grad_normed_two)
    grad_one = grad_two + back_one
    branch_one = grad_one.astype(BF)
    cross_sums = scatter_sum((grad_weights, grad_cross_query), devices)
    grad_self_out = tmatmul(attn_one, branch_one)
    grad_attn_one = matmul_t(branch_one, self_out).astype(BF)
    grad_kv_one, grad_q_one = attend_back(query_one, grad_attn_one, keyval_one, lse_one)
    grad_qkv = jnp.concatenate([grad_q_one, grad_kv_one], axis=1)
    grad_self = tmatmul(normed_one, grad_qkv)
    grad_normed_one = matmul_t(grad_qkv, self_weights)
    back_in, grad_norm_self = norm_back(inputs, norm_self, grad_normed_one)
    decoder_in_grad = (grad_one + back_in)[None]
    self_sums = scatter_sum(
        (grad_self, grad_self_out, grad_norm_self, grad_norm_cross, grad_norm_ffn), devices
    )

    sum_cross_key, sum_cross_value = separate(cross_sums[0])
    sum_self_query = self_sums[0][:, :width]
    sum_self_key, sum_self_value = separate(self_sums[0][:, width:])
    return (
        decoder_out,
        decoder_in_grad,
        memory_grad,
        self_sums[2],
        sum_self_query,
        sum_self_key,
        sum_self_value,
        self_sums[1],
        self_sums[3],
        cross_sums[1],
        sum_cross_key,
        sum_cross_value,
        ffn_sums[3],
        self_sums[4],
        ffn_sums[0],
        ffn_sums[1],
        ffn_sums[2],
    )


def solution(mesh):
    dp, seq = mesh.devices.shape
    cores = 2
    lines = dp // PLANES
    split = Mesh(mesh.devices.reshape(PLANES, lines, seq // cores, cores), ALL)
    plane_size = lines * seq
    first = P(ALL)
    middle = P(None, ALL)
    whole = P()
    return jax.shard_map(
        functools.partial(on_device, plane_size),
        mesh=split,
        in_specs=(first, middle, first, first) + (whole,) * 14,
        out_specs=(first, first, middle) + (first,) * 14,
        check_vma=False,
    )
```

time: 2600 us -> 1370 us (0.53)
  matrix products: 957 us -> 151 us
  Pallas kernels: 0 us -> 625 us
  waiting for transfers between devices: 655 us -> 261 us
  other arithmetic: 404 us -> 41.7 us
  blocking collectives: 292 us -> 0 us
  starting transfers between devices: 11.7 us -> 115 us
  local copies, waits for them, and re-layouts: 245 us -> 145 us
    dot_general x201 -> x33, matrix products: 957 us -> 151 us  [dot(): lax.dot_general(left, right, (((left_dim,), (right_dim,)), ((), ())), pre...]
    pallas_call x0 -> x11, Pallas kernels: none -> 625 us  [the longest x1 383 us: place(): pl.pallas_call(functools.partial(place_kernel, plane_size=plane_size), ou...]
    reduce_scatter x9 -> x2, waiting for transfers between devices: 360 us -> 0.01 us  [scatter_sum(): lax.psum_scatter(joined.reshape(devices, -1, 128), ALL, scatter_dimension...]
    unnamed x1 -> x0, blocking collectives: 292 us -> none
    ppermute x0 -> x77, waiting for transfers between devices: none -> 261 us  [the longest x56 215 us: in_plane(): return lax.ppermute(value, PLANE, [(i, i ^ k) for i in range(plane_size)])]
    all_to_all x2 -> x0, waiting for transfers between devices: 200 us -> none  [the longest x1 200 us: on_device(): lax.all_to_all(memory, ('dp', 'seq'), split_axis=0, concat_axis=1, tiled=...]
    convert_element_type x25 -> x5, other arithmetic: 143 us -> 6.47 us  [the longest x1 2.38 us: on_device(): grad_q_two = sum((grad_q[r].astype(F32) for r in range(PLANES))).astype(BF)]
    ppermute x0 -> x77, starting transfers between devices: none -> 115 us  [the longest x56 71.3 us: in_plane(): return lax.ppermute(value, PLANE, [(i, i ^ k) for i in range(plane_size)])]
  transfers between devices with their start and end apart: 13 -> 80, of which waited for: 5 -> 31; matrix products, arithmetic and copies ran while one was open for 43% -> 19% of each run, Pallas kernels for 0% -> 45%
where the time goes in v1:
time: 1370 us; the launch traced here: 1360 us
  Pallas kernels  625 us (46%)
  waiting for transfers between devices  261 us (19%)
  matrix products  151 us (11%)
  local copies, waits for them, and re-layouts  145 us (11%)
  starting transfers between devices  115 us (8%)
  other arithmetic  41.7 us (3%)
  between operations  16.8 us (1%)
    pallas_call x1, Pallas kernels, place(): pl.pallas_call(functools.partial(place_kernel, plane_size=plane_size), ou...  383 us
    ppermute x56, waiting for transfers between devices, in_plane(): return lax.ppermute(value, PLANE, [(i, i ^ k) for i in range(plane_size)])  215 us
    dot_general x33, matrix products, dot(): lax.dot_general(left, right, (((left_dim,), (right_dim,)), ((), ())), pre...  151 us
    pallas_call x5, Pallas kernels, attend_back(): pl.pallas_call(functools.partial(backward_kernel, causal=causal), grid=(P...  150 us
    pallas_call x5, Pallas kernels, attend(): pl.pallas_call(functools.partial(forward_kernel, causal=causal), grid=(PA...  92.5 us
    ppermute x56, starting transfers between devices, in_plane(): return lax.ppermute(value, PLANE, [(i, i ^ k) for i in range(plane_size)])  71.3 us
    ppermute x21, waiting for transfers between devices, along_z(): return lax.ppermute(value, 'z', [(i, i ^ r) for i in range(PLANES)])  45.9 us
    unnamed x284, local copies, waits for them, and re-layouts  45.4 us
  transfers between devices with their start and end apart: 80, of which 31 were waited for; matrix products, arithmetic and copies ran while one was open for 19% of the time, Pallas kernels for 45%

profile of v1, /device:TPU:0, one launch (start us, length us, event | category | flops | bytes accessed | tf_op | source)
XLA Modules:
  0.0 1356.3 jit_solution(4578751176351406352)
XLA Ops:
  12.9 8.3 dynamic-slice_bitcast_fusion.14
  82.7 21.3 %collective-permute-done.4 = bf16[256,768]{1,0:T(8,128)(2,1)S(1)} collective-permute-done((bf16[256,768]{1,0:T(8,128)(2,1)S(1)}, bf16[256,768]{1,0:T(8,128)(2,1)S(1)}, u32[]{:S(2)}, u32[]{:S(2)}) %collective-permute-start.4) | collective-permute-done | bytes 393248 | tf_op jit(solution)/shard_map/ppermute | solution.py:294
  115.7 8.1 collective-permute-done.19
  128.8 8.1 collective-permute-done.23
  162.9 18.2 %collective-permute-done.32 = bf16[256,768]{1,0:T(8,128)(2,1)S(1)} collective-permute-done((bf16[256,768]{1,0:T(8,128)(2,1)S(1)}, bf16[256,768]{1,0:T(8,128)(2,1)S(1)}, u32[]{:S(2)}, u32[]{:S(2)}) %collective-permute-start.32) | collective-permute-done | bytes 393248 | tf_op jit(solution)/shard_map/ppermute | solution.py:294
  191.6 9.2 collective-permute-done.9
  204.8 9.0 collective-permute-done.13
  227.2 14.1 %collective-permute-done.17.refs_0_ = bf16[512,768]{1,0:T(8,128)(2,1)S(1)} collective-permute-done((bf16[512,768]{1,0:T(8,128)(2,1)S(1)}, bf16[512,768]{1,0:T(8,128)(2,1)S(1)}, u32[]{:S(2)}, u32[]{:S(2)}) %collective-permute-start.17) | collective-permute-done | bytes 786464 | tf_op jit(solution)/shard_map/ppermute | solution.py:289
  242.4 21.3 %shard_map.308 = (bf16[512,768]{1,0:T(8,128)(2,1)}, f32[6,2,512]{2,1,0:T(2,128)}) custom-call(bf16[512,768]{1,0:T(8,128)(2,1)} %copy-done.109, bf16[2048,1536]{1,0:T(8,128)(2,1)} %convolution_convert_fusion.1.refs_1_.refs_2_, bf16[2048,128]{1,0:T(8,128)(2,1)} %broadcast_in_dim.40.refs_2_.refs_3_), custom_call_target="tpu_custom_call" | custom-call | flops 12884901888 | bytes 12582912 | tf_op jit(solution)/shard_map/pallas_call | solution.py:134
  265.0 21.2 %shard_map.309 = (bf16[512,768]{1,0:T(8,128)(2,1)}, f32[6,2,512]{2,1,0:T(2,128)}) custom-call(bf16[512,768]{1,0:T(8,128)(2,1)} %copy-done.106, bf16[2048,1536]{1,0:T(8,128)(2,1)} %convolution_convert_fusion.refs_1_.refs_2_, bf16[2048,128]{1,0:T(8,128)(2,1)} %broadcast_in_dim.41.refs_2_.refs_3_), custom_call_target="tpu_custom_call" | custom-call | flops 12884901888 | bytes 12582912 | tf_op jit(solution)/shard_map/pallas_call | solution.py:134
  288.4 21.2 %shard_map.307 = (bf16[512,768]{1,0:T(8,128)(2,1)}, f32[6,2,512]{2,1,0:T(2,128)}) custom-call(bf16[512,768]{1,0:T(8,128)(2,1)} %copy-done.108, bf16[2048,1536]{1,0:T(8,128)(2,1)} %convolution_convert_fusion.2.refs_1_.refs_2_, bf16[2048,128]{1,0:T(8,128)(2,1)} %broadcast_in_dim.39.refs_2_.refs_3_), custom_call_target="tpu_custom_call" | custom-call | flops 12884901888 | bytes 12582912 | tf_op jit(solution)/shard_map/pallas_call | solution.py:134
  313.0 21.4 %shard_map.306 = (bf16[512,768]{1,0:T(8,128)(2,1)}, f32[6,2,512]{2,1,0:T(2,128)}) custom-call(bf16[512,768]{1,0:T(8,128)(2,1)} %convolution_convert_fusion.18.refs_0_, bf16[2048,1536]{1,0:T(8,128)(2,1)} %convolution_convert_fusion.3.refs_1_.refs_2_, bf16[2048,128]{1,0:T(8,128)(2,1)} %broadcast_in_dim.38.refs_2_.refs_3_), custom_call_target="tpu_custom_call" | custom-call | flops 12884901888 | bytes 12582912 | tf_op jit(solution)/shard_map/pallas_call | solution.py:134
  357.4 30.6 %collective-permute-done.38 = bf16[512,768]{1,0:T(8,128)(2,1)} collective-permute-done((bf16[512,768]{1,0:T(8,128)(2,1)}, bf16[512,768]{1,0:T(8,128)(2,1)}, u32[]{:S(2)}, u32[]{:S(2)}) %collective-permute-start.38) | collective-permute-done | bytes 786464 | tf_op jit(solution)/shard_map/ppermute | solution.py:289
  420.8 16.1 %collective-permute-start.44 = (f32[2,6,2,512]{3,2,1,0:T(2,128)S(1)}, f32[2,6,2,512]{3,2,1,0:T(2,128)S(1)}, u32[]{:S(2)}, u32[]{:S(2)}) collective-permute-start(f32[2,6,2,512]{3,2,1,0:T(2,128)S(1)} %pad_maximum_fusion.5), channel_id=1, source_target_pairs={{0,16},{8,24},{16,0},{24,8},{1,17},{9,25},{17,1},{25,9},{2,18},{10... | collective-permute-start | bytes 147464 | tf_op jit(solution)/shard_map/ppermute | solution.py:289
  438.9 33.9 %shard_map.310 = (bf16[2048,1536]{1,0:T(8,128)(2,1)}, bf16[512,768]{1,0:T(8,128)(2,1)}) custom-call(bf16[512,768]{1,0:T(8,128)(2,1)} %convolution_convert_fusion.18.refs_0_, bf16[512,768]{1,0:T(8,128)(2,1)} %get-tuple-element.168.refs_1_, bf16[2048,1536]{1,0:T(8,128)(2,1)} %convolution_convert_fusion.3.refs_1_.refs_2_, ...), custom_call_target="tpu_custom_call" | custom-call | flops 25769803776 | bytes 12582912 | tf_op jit(solution)/shard_map/pallas_call | solution.py:157
  472.8 9.7 fusion.45
  486.9 33.9 %shard_map.312 = (bf16[2048,1536]{1,0:T(8,128)(2,1)}, bf16[512,768]{1,0:T(8,128)(2,1)}) custom-call(bf16[512,768]{1,0:T(8,128)(2,1)} %copy-done.109, bf16[512,768]{1,0:T(8,128)(2,1)} %collective-permute-done.43.refs_1_, bf16[2048,1536]{1,0:T(8,128)(2,1)} %convolution_convert_fusion.1.refs_1_.refs_2_, bf16[2048,128]{1,0:T(8,128)(2,1)} %broadcast_in_dim.40.refs_2_.refs_3_, ...), custom_call_target="tpu_custom_call" | custom-call | flops 25769803776 | bytes 12582912 | tf_op jit(solution)/shard_map/pallas_call | solution.py:157
  521.9 34.2 %shard_map.311 = (bf16[2048,1536]{1,0:T(8,128)(2,1)}, bf16[512,768]{1,0:T(8,128)(2,1)}) custom-call(bf16[512,768]{1,0:T(8,128)(2,1)} %copy-done.108, bf16[512,768]{1,0:T(8,128)(2,1)} %collective-permute-done.40.refs_1_, bf16[2048,1536]{1,0:T(8,128)(2,1)} %convolution_convert_fusion.2.refs_1_.refs_2_, bf16[2048,128]{1,0:T(8,128)(2,1)} %broadcast_in_dim.39.refs_2_.refs_3_, ...), custom_call_target="tpu_custom_call" | custom-call | flops 25769803776 | bytes 12582912 | tf_op jit(solution)/shard_map/pallas_call | solution.py:157
  558.0 34.0 %shard_map.313 = (bf16[2048,1536]{1,0:T(8,128)(2,1)}, bf16[512,768]{1,0:T(8,128)(2,1)}) custom-call(bf16[512,768]{1,0:T(8,128)(2,1)} %copy-done.106, bf16[512,768]{1,0:T(8,128)(2,1)} %copy-done.110, bf16[2048,1536]{1,0:T(8,128)(2,1)} %convolution_convert_fusion.refs_1_.refs_2_, bf16[2048,128]{1,0:T(8,128)(2,1)} %broadcast_in_dim.41.refs_2_.refs_3_, ...), custom_call_target="tpu_custom_call" | custom-call | flops 25769803776 | bytes 12582912 | tf_op jit(solution)/shard_map/pallas_call | solution.py:157
  594.3 7.9 fusion.47
  633.7 14.0 %shard_map.314 = (bf16[512,1536]{1,0:T(8,128)(2,1)}, bf16[512,768]{1,0:T(8,128)(2,1)}) custom-call(bf16[512,768]{1,0:T(8,128)(2,1)} %slice.276.refs_0_, bf16[512,768]{1,0:T(8,128)(2,1)} %convolution_convert_fusion.16.refs_1_, bf16[512,1536]{1,0:T(8,128)(2,1)} %slice.277.refs_1_.refs_2_, f32[6,2,512]{2,1,0:T(2,128)} %get-tuple-element.50.refs_3_), custom_call_target="tpu_custom_call" | custom-call | flops 6442450944 | bytes 3145728 | tf_op jit(solution)/shard_map/pallas_call | solution.py:157
  733.3 11.3 maximum_bitcast_fusion
  749.6 7.9 convolution_convert_fusion.12
  762.9 8.6 convolution_convert_fusion.9
  779.9 7.8 collective-permute-done.53.refs_5_
  788.9 8.0 collective-permute-done.52.refs_4_
  801.0 9.2 collective-permute-done.76.refs_31_
  863.8 9.4 collective-permute-done.68.refs_22_
  890.2 9.3 collective-permute-done.64.refs_18_
  905.0 11.2 collective-permute-done.62.refs_15_
  917.6 9.4 collective-permute-done.61.refs_14_
  946.1 382.6 %shard_map.315 = bf16[32,256,768]{2,1,0:T(8,128)(2,1)} custom-call(bf16[256,768]{1,0:T(8,128)(2,1)} %get-tuple-element.135.refs_0_, bf16[256,768]{1,0:T(8,128)(2,1)} %copy-done.54, bf16[256,768]{1,0:T(8,128)(2,1)} %copy-done.52, bf16[256,768]{1,0:T(8,128)(2,1)} %copy-done.49, bf16[256,768]{1,0:T(8,128)(2,1)} %copy-done.48, bf16[256,768]{1,0:T(8,128)(2,1)} %copy-done.47, ...), custom_call_target="tpu_custom_call" | custom-call | tf_op jit(solution)/shard_map/pallas_call | solution.py:189
  (569 shorter events, 469.3 us)
Async XLA Ops:
  7.2 1325.1 %reduce-scatter.7.cloned.1.call-start = ((), (), s32[]{:S(2)}) async-start(), calls=%async_computation.3 | async-start | bytes 3649536 | tf_op jit(solution)/shard_map/reduce_scatter | solution.py:250
  7.2 57.5 %collective-permute-start.15 = (s32[1]{0:T(128)}, s32[1]{0:T(128)}, u32[]{:S(2)}, u32[]{:S(2)}) collective-permute-start(s32[1]{0:T(128)} %param.20), channel_id=1, source_target_pairs={{0,8},{8,0},{16,24},{24,16},{1,9},{9,1},{17,25},{25,17},{2,10},{10... | collective-permute-start | bytes 20 | tf_op jit(solution)/shard_map/ppermute | solution.py:289
  10.3 57.4 %collective-permute-start.35 = (s32[1]{0:T(128)}, s32[1]{0:T(128)}, u32[]{:S(2)}, u32[]{:S(2)}) collective-permute-start(s32[1]{0:T(128)} %param.20), channel_id=1, source_target_pairs={{0,24},{8,16},{16,8},{24,0},{1,25},{9,17},{17,9},{25,1},{2,26},{10... | collective-permute-start | bytes 20 | tf_op jit(solution)/shard_map/ppermute | solution.py:289
  12.8 56.4 %collective-permute-start.25 = (s32[1]{0:T(128)}, s32[1]{0:T(128)}, u32[]{:S(2)}, u32[]{:S(2)}) collective-permute-start(s32[1]{0:T(128)} %param.20), channel_id=1, source_target_pairs={{0,16},{8,24},{16,0},{24,8},{1,17},{9,25},{17,1},{25,9},{2,18},{10... | collective-permute-start | bytes 20 | tf_op jit(solution)/shard_map/ppermute | solution.py:289
  21.2 51.9 %collective-permute-start.1 = (bf16[256,768]{1,0:T(8,128)(2,1)}, bf16[256,768]{1,0:T(8,128)(2,1)S(1)}, u32[]{:S(2)}, u32[]{:S(2)}) collective-permute-start(bf16[256,768]{1,0:T(8,128)(2,1)} %get-tuple-element.95), channel_id=1, source_target_pairs={{0,2},{1,3},{2,0},{3,1},{4,6},{5,7},{6,4},{7,5},{8,10},{9,11},{10,... | collective-permute-start | bytes 1179656 | tf_op jit(solution)/shard_map/ppermute | solution.py:294
  22.7 48.6 %collective-permute-start = (bf16[256,768]{1,0:T(8,128)(2,1)}, bf16[256,768]{1,0:T(8,128)(2,1)}, u32[]{:S(2)}, u32[]{:S(2)}) collective-permute-start(bf16[256,768]{1,0:T(8,128)(2,1)} %get-tuple-element.96), channel_id=1, source_target_pairs={{0,1},{1,0},{2,3},{3,2},{4,5},{5,4},{6,7},{7,6},{8,9},{9,8},{10,11... | collective-permute-start | bytes 1179656 | tf_op jit(solution)/shard_map/ppermute | solution.py:294
  64.7 199.1 %collective-permute-start.27 = (bf16[512,768]{1,0:T(8,128)(2,1)}, bf16[512,768]{1,0:T(8,128)(2,1)S(1)}, u32[]{:S(2)}, u32[]{:S(2)}) collective-permute-start(bf16[512,768]{1,0:T(8,128)(2,1)} %convolution_convert_fusion.18.refs_0_), channel_id=1, source_target_pairs={{0,24},{8,16},{16,8},{24,0},{1,25},{9,17},{17,9},{25,1},{2,26},{10... | collective-permute-start | bytes 2359304 | tf_op jit(solution)/shard_map/ppermute | solution.py:289
  81.0 44.6 %collective-permute-start.21 = (bf16[256,768]{1,0:T(8,128)(2,1)S(1)}, bf16[256,768]{1,0:T(8,128)(2,1)S(1)}, u32[]{:S(2)}, u32[]{:S(2)}) collective-permute-start(bf16[256,768]{1,0:T(8,128)(2,1)S(1)} %copy-done.41), channel_id=1, source_target_pairs={{0,4},{1,5},{2,6},{3,7},{4,0},{5,1},{6,2},{7,3},{8,12},{9,13},{10,... | collective-permute-start | bytes 1179656 | tf_op jit(solution)/shard_map/ppermute | solution.py:294
  161.3 41.9 %collective-permute-start.11 = (bf16[256,768]{1,0:T(8,128)(2,1)S(1)}, bf16[256,768]{1,0:T(8,128)(2,1)S(1)}, u32[]{:S(2)}, u32[]{:S(2)}) collective-permute-start(bf16[256,768]{1,0:T(8,128)(2,1)S(1)} %copy-done.27), channel_id=1, source_target_pairs={{0,4},{1,5},{2,6},{3,7},{4,0},{5,1},{6,2},{7,3},{8,12},{9,13},{10,... | collective-permute-start | bytes 1179656 | tf_op jit(solution)/shard_map/ppermute | solution.py:294
  203.1 38.1 %collective-permute-start.17 = (bf16[512,768]{1,0:T(8,128)(2,1)S(1)}, bf16[512,768]{1,0:T(8,128)(2,1)S(1)}, u32[]{:S(2)}, u32[]{:S(2)}) collective-permute-start(bf16[512,768]{1,0:T(8,128)(2,1)S(1)} %copy-done.107), channel_id=1, source_target_pairs={{0,16},{8,24},{16,0},{24,8},{1,17},{9,25},{17,1},{25,9},{2,18},{10... | collective-permute-start | bytes 2359304 | tf_op jit(solution)/shard_map/ppermute | solution.py:289
  203.6 83.7 %collective-permute-start.7 = (bf16[512,768]{1,0:T(8,128)(2,1)S(1)}, bf16[512,768]{1,0:T(8,128)(2,1)S(1)}, u32[]{:S(2)}, u32[]{:S(2)}) collective-permute-start(bf16[512,768]{1,0:T(8,128)(2,1)S(1)} %copy-done.107), channel_id=1, source_target_pairs={{0,8},{8,0},{16,24},{24,16},{1,9},{9,1},{17,25},{25,17},{2,10},{10... | collective-permute-start | bytes 2359304 | tf_op jit(solution)/shard_map/ppermute | solution.py:289
  263.7 73.1 %collective-permute-start.26 = (f32[6,2,512]{2,1,0:T(2,128)}, f32[6,2,512]{2,1,0:T(2,128)S(1)}, u32[]{:S(2)}, u32[]{:S(2)}) collective-permute-start(f32[6,2,512]{2,1,0:T(2,128)} %get-tuple-element.40), channel_id=1, source_target_pairs={{0,16},{8,24},{16,0},{24,8},{1,17},{9,25},{17,1},{25,9},{2,18},{10... | collective-permute-start | bytes 73736 | tf_op jit(solution)/shard_map/ppermute | solution.py:289
  286.1 51.8 %collective-permute-start.36 = (f32[6,2,512]{2,1,0:T(2,128)}, f32[6,2,512]{2,1,0:T(2,128)S(1)}, u32[]{:S(2)}, u32[]{:S(2)}) collective-permute-start(f32[6,2,512]{2,1,0:T(2,128)} %get-tuple-element.41), channel_id=1, source_target_pairs={{0,24},{8,16},{16,8},{24,0},{1,25},{9,17},{17,9},{25,1},{2,26},{10... | collective-permute-start | bytes 73736 | tf_op jit(solution)/shard_map/ppermute | solution.py:289
  334.4 53.5 %collective-permute-start.38 = (bf16[512,768]{1,0:T(8,128)(2,1)}, bf16[512,768]{1,0:T(8,128)(2,1)}, u32[]{:S(2)}, u32[]{:S(2)}) collective-permute-start(bf16[512,768]{1,0:T(8,128)(2,1)} %get-tuple-element.44), channel_id=1, source_target_pairs={{0,16},{8,24},{16,0},{24,8},{1,17},{9,25},{17,1},{25,9},{2,18},{10... | collective-permute-start | bytes 2359304 | tf_op jit(solution)/shard_map/ppermute | solution.py:289
  335.4 52.6 %collective-permute-start.39 = (bf16[512,768]{1,0:T(8,128)(2,1)}, bf16[512,768]{1,0:T(8,128)(2,1)}, u32[]{:S(2)}, u32[]{:S(2)}) collective-permute-start(bf16[512,768]{1,0:T(8,128)(2,1)} %get-tuple-element.45), channel_id=1, source_target_pairs={{0,24},{8,16},{16,8},{24,0},{1,25},{9,17},{17,9},{25,1},{2,26},{10... | collective-permute-start | bytes 2359304 | tf_op jit(solution)/shard_map/ppermute | solution.py:289
  336.8 52.3 %collective-permute-start.37 = (bf16[512,768]{1,0:T(8,128)(2,1)}, bf16[512,768]{1,0:T(8,128)(2,1)}, u32[]{:S(2)}, u32[]{:S(2)}) collective-permute-start(bf16[512,768]{1,0:T(8,128)(2,1)} %get-tuple-element.43), channel_id=1, source_target_pairs={{0,8},{8,0},{16,24},{24,16},{1,9},{9,1},{17,25},{25,17},{2,10},{10... | collective-permute-start | bytes 2359304 | tf_op jit(solution)/shard_map/ppermute | solution.py:289
  419.2 63.4 %collective-permute-start.47 = (f32[2,6,2,512]{3,2,1,0:T(2,128)S(1)}, f32[2,6,2,512]{3,2,1,0:T(2,128)S(1)}, u32[]{:S(2)}, u32[]{:S(2)}) collective-permute-start(f32[2,6,2,512]{3,2,1,0:T(2,128)S(1)} %pad_maximum_fusion.5), channel_id=1, source_target_pairs={{0,24},{8,16},{16,8},{24,0},{1,25},{9,17},{17,9},{25,1},{2,26},{10... | collective-permute-start | bytes 147464 | tf_op jit(solution)/shard_map/ppermute | solution.py:289
  420.8 64.9 %collective-permute-start.44 = (f32[2,6,2,512]{3,2,1,0:T(2,128)S(1)}, f32[2,6,2,512]{3,2,1,0:T(2,128)S(1)}, u32[]{:S(2)}, u32[]{:S(2)}) collective-permute-start(f32[2,6,2,512]{3,2,1,0:T(2,128)S(1)} %pad_maximum_fusion.5), channel_id=1, source_target_pairs={{0,16},{8,24},{16,0},{24,8},{1,17},{9,25},{17,1},{25,9},{2,18},{10... | collective-permute-start | bytes 147464 | tf_op jit(solution)/shard_map/ppermute | solution.py:289
  436.8 49.4 %collective-permute-start.41 = (f32[2,6,2,512]{3,2,1,0:T(2,128)S(1)}, f32[2,6,2,512]{3,2,1,0:T(2,128)S(1)}, u32[]{:S(2)}, u32[]{:S(2)}) collective-permute-start(f32[2,6,2,512]{3,2,1,0:T(2,128)S(1)} %pad_maximum_fusion.5), channel_id=1, source_target_pairs={{0,8},{8,0},{16,24},{24,16},{1,9},{9,1},{17,25},{25,17},{2,10},{10... | collective-permute-start | bytes 147464 | tf_op jit(solution)/shard_map/ppermute | solution.py:289
  436.8 50.0 %collective-permute-start.43 = (bf16[512,768]{1,0:T(8,128)(2,1)}, bf16[512,768]{1,0:T(8,128)(2,1)}, u32[]{:S(2)}, u32[]{:S(2)}) collective-permute-start(bf16[512,768]{1,0:T(8,128)(2,1)} %get-tuple-element.168.refs_1_), channel_id=1, source_target_pairs={{0,16},{8,24},{16,0},{24,8},{1,17},{9,25},{17,1},{25,9},{2,18},{10... | collective-permute-start | bytes 2359304 | tf_op jit(solution)/shard_map/ppermute | solution.py:289
  438.9 83.0 %collective-permute-start.40 = (bf16[512,768]{1,0:T(8,128)(2,1)}, bf16[512,768]{1,0:T(8,128)(2,1)}, u32[]{:S(2)}, u32[]{:S(2)}) collective-permute-start(bf16[512,768]{1,0:T(8,128)(2,1)} %get-tuple-element.168.refs_1_), channel_id=1, source_target_pairs={{0,8},{8,0},{16,24},{24,16},{1,9},{9,1},{17,25},{25,17},{2,10},{10... | collective-permute-start | bytes 2359304 | tf_op jit(solution)/shard_map/ppermute | solution.py:289
  482.6 74.4 %collective-permute-start.46 = (bf16[512,768]{1,0:T(8,128)(2,1)}, bf16[512,768]{1,0:T(8,128)(2,1)S(1)}, u32[]{:S(2)}, u32[]{:S(2)}) collective-permute-start(bf16[512,768]{1,0:T(8,128)(2,1)} %get-tuple-element.168.refs_1_), channel_id=1, source_target_pairs={{0,24},{8,16},{16,8},{24,0},{1,25},{9,17},{17,9},{25,1},{2,26},{10... | collective-permute-start | bytes 2359304 | tf_op jit(solution)/shard_map/ppermute | solution.py:289
  520.8 98.1 %collective-permute-start.45 = (bf16[512,768]{1,0:T(8,128)(2,1)}, bf16[512,768]{1,0:T(8,128)(2,1)}, u32[]{:S(2)}, u32[]{:S(2)}) collective-permute-start(bf16[512,768]{1,0:T(8,128)(2,1)} %get-tuple-element.48), channel_id=1, source_target_pairs={{0,16},{8,24},{16,0},{24,8},{1,17},{9,25},{17,1},{25,9},{2,18},{10... | collective-permute-start | bytes 2359304 | tf_op jit(solution)/shard_map/ppermute | solution.py:289
  556.1 62.8 %collective-permute-start.42 = (bf16[512,768]{1,0:T(8,128)(2,1)}, bf16[512,768]{1,0:T(8,128)(2,1)}, u32[]{:S(2)}, u32[]{:S(2)}) collective-permute-start(bf16[512,768]{1,0:T(8,128)(2,1)} %get-tuple-element.47), channel_id=1, source_target_pairs={{0,8},{8,0},{16,24},{24,16},{1,9},{9,1},{17,25},{25,17},{2,10},{10... | collective-permute-start | bytes 2359304 | tf_op jit(solution)/shard_map/ppermute | solution.py:289
  665.8 670.0 %reduce-scatter.11.cloned.1.call-start = ((), (), s32[]{:S(2)}) async-start(), calls=%async_computation.5 | async-start | bytes 4933632
  696.2 646.9 %reduce-scatter.9.cloned.1.call-start = ((), (), s32[]{:S(2)}) async-start(), calls=%async_computation.4 | async-start | bytes 10948608 | tf_op jit(solution)/shard_map/reduce_scatter | solution.py:250
  798.3 39.2 %collective-permute-start.73 = (bf16[256,768]{1,0:T(8,128)(2,1)S(1)}, bf16[256,768]{1,0:T(8,128)(2,1)S(1)}, u32[]{:S(2)}, u32[]{:S(2)}) collective-permute-start(bf16[256,768]{1,0:T(8,128)(2,1)S(1)} %get-tuple-element.107), channel_id=1, source_target_pairs={{0,4},{1,5},{2,6},{3,7},{4,0},{5,1},{6,2},{7,3},{8,12},{9,13},{10,... | collective-permute-start | bytes 1179656 | tf_op jit(solution)/shard_map/ppermute | solution.py:294
  799.7 41.3 %collective-permute-start.72 = (bf16[256,768]{1,0:T(8,128)(2,1)S(1)}, bf16[256,768]{1,0:T(8,128)(2,1)S(1)}, u32[]{:S(2)}, u32[]{:S(2)}) collective-permute-start(bf16[256,768]{1,0:T(8,128)(2,1)S(1)} %get-tuple-element.108), channel_id=1, source_target_pairs={{0,3},{1,2},{2,1},{3,0},{4,7},{5,6},{6,5},{7,4},{8,11},{9,10},{10,... | collective-permute-start | bytes 1179656 | tf_op jit(solution)/shard_map/ppermute | solution.py:294
  846.9 38.0 %collective-permute-start.66 = (bf16[256,768]{1,0:T(8,128)(2,1)S(1)}, bf16[256,768]{1,0:T(8,128)(2,1)S(1)}, u32[]{:S(2)}, u32[]{:S(2)}) collective-permute-start(bf16[256,768]{1,0:T(8,128)(2,1)S(1)} %get-tuple-element.115), channel_id=1, source_target_pairs={{0,4},{1,5},{2,6},{3,7},{4,0},{5,1},{6,2},{7,3},{8,12},{9,13},{10,... | collective-permute-start | bytes 1179656 | tf_op jit(solution)/shard_map/ppermute | solution.py:294
  875.8 40.4 %collective-permute-start.62 = (bf16[256,768]{1,0:T(8,128)(2,1)S(1)}, bf16[256,768]{1,0:T(8,128)(2,1)S(1)}, u32[]{:S(2)}, u32[]{:S(2)}) collective-permute-start(bf16[256,768]{1,0:T(8,128)(2,1)S(1)} %get-tuple-element.120), channel_id=1, source_target_pairs={{0,7},{1,6},{2,5},{3,4},{4,3},{5,2},{6,1},{7,0},{8,15},{9,14},{10,... | collective-permute-start | bytes 1179656 | tf_op jit(solution)/shard_map/ppermute | solution.py:294
  885.0 42.0 %collective-permute-start.61 = (bf16[256,768]{1,0:T(8,128)(2,1)S(1)}, bf16[256,768]{1,0:T(8,128)(2,1)S(1)}, u32[]{:S(2)}, u32[]{:S(2)}) collective-permute-start(bf16[256,768]{1,0:T(8,128)(2,1)S(1)} %get-tuple-element.121), channel_id=1, source_target_pairs={{0,6},{1,7},{2,4},{3,5},{4,2},{5,3},{6,0},{7,1},{8,14},{9,15},{10,... | collective-permute-start | bytes 1179656 | tf_op jit(solution)/shard_map/ppermute | solution.py:294
  890.2 41.6 %collective-permute-start.60 = (bf16[256,768]{1,0:T(8,128)(2,1)S(1)}, bf16[256,768]{1,0:T(8,128)(2,1)S(1)}, u32[]{:S(2)}, u32[]{:S(2)}) collective-permute-start(bf16[256,768]{1,0:T(8,128)(2,1)S(1)} %get-tuple-element.122), channel_id=1, source_target_pairs={{0,5},{1,4},{2,7},{3,6},{4,1},{5,0},{6,3},{7,2},{8,13},{9,12},{10,... | collective-permute-start | bytes 1179656 | tf_op jit(solution)/shard_map/ppermute | solution.py:294
  (171 other events, 4135.0 us)
Sparse Core Ops, SparseCore 0:
  665.9 121.8 reduce-scatter.6
  790.1 150.7 reduce-scatter.10
  948.0 137.8 reduce-scatter.8

commit v2 on v1

v2 whole, which is shorter than its diff:
```python
import functools

import jax
import jax.numpy as jnp
from jax import lax
from jax.experimental import pallas as pl
from jax.experimental.pallas import tpu as pltpu
from jax.sharding import Mesh
from jax.sharding import PartitionSpec as P

H = 12
HD = 64
PAIRS = 6
PLANES = 4
EPSILON = 1e-06
MASKED = -1e30
VMEM = 56 * 2**20
BF = jnp.bfloat16
F32 = jnp.float32
ALL = ("z", "y", "x", "c")
PLANE = ("y", "x", "c")


def dot(left, right, left_dim, right_dim):
    return lax.dot_general(
        left, right, (((left_dim,), (right_dim,)), ((), ())), preferred_element_type=F32
    )


def lane_masks():
    lane = lax.broadcasted_iota(jnp.int32, (1, 2 * HD), 1)
    low = jnp.where(lane < HD, 1.0, 0.0)
    first = jnp.where(lane == HD, 1.0, 0.0)
    second = jnp.where(lane == 0, 1.0, 0.0)
    low, high, first, second = (
        v.astype(BF) for v in (low, 1.0 - low, first, second)
    )
    return ((low, high, first), (high, low, second))


def causal_mask(scores):
    key = lax.broadcasted_iota(jnp.int32, scores.shape, 0)
    query = lax.broadcasted_iota(jnp.int32, scores.shape, 1)
    return jnp.where(key <= query, scores, MASKED)


def rem(value, size):
    return lax.rem(value, size)


class Courier:
    def __init__(self, sizes, jobs):
        self.sizes = sizes
        self.jobs = jobs
        self.plane = sizes[1] * sizes[2] * sizes[3]
        self.in_plane = any(job[0] != "line" for job in jobs)
        self.lines = [job[1] for job in jobs if job[0] == "line"]

    def out_shape(self):
        shapes = []
        for kind, _, value in self.jobs:
            shape = value.shape
            if kind == "fetch":
                shape = (self.plane,) + shape[1:]
            shapes.append(jax.ShapeDtypeStruct(shape, value.dtype))
        return shapes

    def specs(self):
        return [pl.BlockSpec(memory_space=pl.ANY)] * len(self.jobs)

    def values(self):
        return [job[2] for job in self.jobs]

    def scratch(self):
        count = sum(1 if job[0] == "line" else self.plane - 1 for job in self.jobs)
        own = max(1, sum(job[0] != "line" for job in self.jobs))
        return [pltpu.SemaphoreType.DMA((n,)) for n in (count, count, own)]

    def params(self, ident):
        return pltpu.CompilerParams(
            vmem_limit_bytes=VMEM, collective_id=ident, has_side_effects=True
        )

    def me(self):
        _, _, x_size, c_size = self.sizes
        y, x, c = (lax.axis_index(name) for name in PLANE)
        return (y * x_size + x) * c_size + c

    def along(self, offset):
        return {"z": rem(lax.axis_index("z") + (offset + PLANES), PLANES)}

    def across(self, offset):
        _, _, x_size, c_size = self.sizes
        other = rem(self.me() + offset, self.plane)
        line = lax.div(other, c_size)
        return other, {"y": lax.div(line, x_size), "x": rem(line, x_size), "c": rem(other, c_size)}

    def greet(self):
        barrier = pltpu.get_barrier_semaphore()
        count = 0
        if self.in_plane:
            for k in range(1, self.plane):
                _, device = self.across(k)
                pl.semaphore_signal(
                    barrier, inc=1, device_id=device, device_id_type=pl.DeviceIdType.MESH
                )
                count += 1
        for offset in self.lines:
            pl.semaphore_signal(
                barrier,
                inc=1,
                device_id=self.along(-offset),
                device_id_type=pl.DeviceIdType.MESH,
            )
            count += 1
        pl.semaphore_wait(barrier, count)

    def copies(self, sources, targets, sems):
        send, receive, own = sems
        remote = []
        local = []

        def add(source, target, device):
            n = len(remote)
            remote.append(
                pltpu.make_async_remote_copy(
                    src_ref=source,
                    dst_ref=target,
                    send_sem=send.at[n],
                    recv_sem=receive.at[n],
                    device_id=device,
                    device_id_type=pl.DeviceIdType.MESH,
                )
            )

        me = self.me()
        for (kind, offset, _), source, target in zip(self.jobs, sources, targets):
            if kind == "line":
                add(source, target, self.along(offset))
                continue
            base = 0
            if kind == "fetch":
                base = rem(lax.axis_index("z") + offset, PLANES) * self.plane
            for k in range(1, self.plane):
                other, device = self.across(k)
                add(source.at[base + other], target.at[me], device)
            local.append(
                pltpu.make_async_copy(source.at[base + me], target.at[me], own.at[len(local)])
            )
        return local + remote

    def start(self, sources, targets, sems):
        self.greet()
        for copy in self.copies(sources, targets, sems):
            copy.start()

    def wait(self, sources, targets, sems):
        for copy in self.copies(sources, targets, sems):
            copy.wait()


def forward_pair(queries, keys, values, bias):
    masks = lane_masks()
    all_scores = []
    for mine, other, one in masks:
        if bias is None:
            all_scores.append(causal_mask(dot(keys, queries * mine, 1, 1)))
        else:
            all_scores.append(dot(keys * mine + bias * one, queries * mine + one, 1, 1))
    parts = []
    lse = []
    for h in range(2):
        mine, other, _ = masks[h]
        scores = all_scores[h]
        row_max = jnp.max(scores, axis=0, keepdims=True)
        probs = jnp.exp(scores - row_max).astype(BF)
        both = dot(values * mine + other, probs, 0, 0)
        halves = (both[:HD], both[HD:])
        total = halves[1 - h]
        parts.append(halves[h] / total)
        lse.append(row_max + jnp.log(total[0:1]))
    return jnp.concatenate(parts, axis=0).T.astype(BF), lse


def backward_pair(queries, grad, keys, values, bias, lse, delta):
    grad_k = None
    grad_v = None
    grad_q = []
    for h, (mine, other, one) in enumerate(lane_masks()):
        query_h = queries * mine
        grad_h = grad * mine
        if bias is None:
            scores = causal_mask(dot(keys, query_h, 1, 1))
        else:
            scores = dot(keys * mine + bias * one, query_h + one, 1, 1)
        probs = jnp.exp(scores - lse[h])
        grad_p = dot(values, grad_h, 1, 1)
        if delta is None:
            delta_h = jnp.sum(probs * grad_p, axis=0, keepdims=True)
        else:
            delta_h = delta[h]
        grad_s = (probs * (grad_p - delta_h)).astype(BF)
        term_v = dot(probs.astype(BF), grad_h, 1, 0)
        term_k = dot(grad_s, query_h, 1, 0)
        grad_v = term_v if grad_v is None else grad_v + term_v
        grad_k = term_k if grad_k is None else grad_k + term_k
        grad_q.append(dot(keys, grad_s, 0, 0)[h * HD : (h + 1) * HD])
    grad_kv = jnp.concatenate([grad_k, grad_v], axis=1).astype(BF)
    return grad_kv, jnp.concatenate(grad_q, axis=0).T.astype(BF)


def two_rows(ref):
    return [ref[0, h : h + 1, :] for h in range(2)]


def split_refs(refs, *counts):
    groups = []
    at = 0
    for count in counts:
        groups.append(refs[at : at + count])
        at += count
    return groups


def carried(courier, body):
    jobs = len(courier.jobs)

    def kernel(ins, outs, scratch, refs):
        own_in, sources, own_out, targets, own_scratch, sems = split_refs(
            refs, ins, jobs, outs, jobs, scratch, 3
        )

        @pl.when(pl.program_id(0) == 0)
        def _():
            courier.start(sources, targets, sems)

        body(own_in, own_out, own_scratch)

        @pl.when(pl.program_id(0) == PAIRS - 1)
        def _():
            courier.wait(sources, targets, sems)

    return kernel


def call(courier, ident, body, args, in_specs, out_shape, out_specs, scratch, flops):
    kernel = carried(courier, body)
    counts = (len(args), len(out_shape), len(scratch))
    outs = pl.pallas_call(
        lambda *refs: kernel(*counts, refs),
        grid=(PAIRS,),
        out_shape=out_shape + courier.out_shape(),
        in_specs=in_specs + courier.specs(),
        out_specs=out_specs + courier.specs(),
        scratch_shapes=scratch + courier.scratch(),
        compiler_params=courier.params(ident),
        cost_estimate=pl.CostEstimate(flops=flops, bytes_accessed=2**24, transcendentals=2**20),
    )(*args, *courier.values())
    return outs[: len(out_shape)], outs[len(out_shape) :]


def block_specs(tokens, keys):
    return dict(
        col=pl.BlockSpec((tokens, 128), lambda p: (0, p)),
        pair=pl.BlockSpec((keys, 256), lambda p: (0, p)),
        bias=pl.BlockSpec((keys, 128), lambda p: (0, 0)),
        rows=pl.BlockSpec((keys, H * HD), lambda p: (0, 0)),
        weight=pl.BlockSpec((H * HD, 128), lambda p: (0, p)),
        stat=pl.BlockSpec((1, 2, tokens), lambda p: (p, 0, 0)),
    )


def self_forward(courier, ident, queries, keyvals):
    tokens = queries.shape[0]
    spec = block_specs(tokens, tokens)

    def body(ins, outs, _):
        q_ref, kv_ref = ins
        o_ref, lse_ref = outs
        out, lse = forward_pair(q_ref[...], kv_ref[:, :128], kv_ref[:, 128:], None)
        o_ref[...] = out
        for h in range(2):
            lse_ref[0, h : h + 1, :] = lse[h]

    return call(
        courier,
        ident,
        body,
        [queries, keyvals],
        [spec["col"], spec["pair"]],
        [
            jax.ShapeDtypeStruct((tokens, H * HD), BF),
            jax.ShapeDtypeStruct((PAIRS, 2, tokens), F32),
        ],
        [spec["col"], spec["stat"]],
        [],
        2**32,
    )


def cross_forward(courier, ident, queries, rows, bias, key_weight, value_weight):
    tokens, keys = queries.shape[0], rows.shape[0]
    spec = block_specs(tokens, keys)

    def body(ins, outs, _):
        q_ref, rows_ref, bias_ref, wk_ref, wv_ref = ins
        o_ref, lse_ref, kv_ref = outs
        weights = jnp.concatenate([wk_ref[...], wv_ref[...]], axis=1)
        kv_ref[...] = dot(rows_ref[...], weights, 1, 0).astype(BF)
        out, lse = forward_pair(q_ref[...], kv_ref[:, :128], kv_ref[:, 128:], bias_ref[...])
        o_ref[...] = out
        for h in range(2):
            lse_ref[0, h : h + 1, :] = lse[h]

    return call(
        courier,
        ident,
        body,
        [queries, rows, bias, key_weight, value_weight],
        [spec["col"], spec["rows"], spec["bias"], spec["weight"], spec["weight"]],
        [
            jax.ShapeDtypeStruct((tokens, H * HD), BF),
            jax.ShapeDtypeStruct((PAIRS, 2, tokens), F32),
            jax.ShapeDtypeStruct((keys, 2 * H * HD), BF),
        ],
        [spec["col"], spec["stat"], spec["pair"]],
        [],
        2**34,
    )


def cross_backward(courier, ident, queries, grad, keyvals, bias, lse, delta, key_weight, value_weight):
    tokens, keys = queries.shape[0], keyvals.shape[0]
    width = H * HD
    spec = block_specs(tokens, keys)

    def body(ins, outs, scratch):
        q_ref, da_ref, kv_ref, bias_ref, lse_ref, delta_ref, wk_ref, wv_ref = ins
        dkv_ref, dq_ref, dm_ref = outs
        (total_ref,) = scratch
        step = pl.program_id(0)

        @pl.when(step == 0)
        def _():
            total_ref[...] = jnp.zeros_like(total_ref)

        weights = jnp.concatenate([wk_ref[...], wv_ref[...]], axis=1)
        grad_kv, grad_q = backward_pair(
            q_ref[...],
            da_ref[...],
            kv_ref[:, :128],
            kv_ref[:, 128:],
            bias_ref[...],
            two_rows(lse_ref),
            two_rows(delta_ref),
        )
        dkv_ref[...] = grad_kv
        dq_ref[...] = grad_q
        total_ref[...] += dot(grad_kv, weights, 1, 1)

        @pl.when(step == PAIRS - 1)
        def _():
            dm_ref[...] = total_ref[...].astype(BF)

    return call(
        courier,
        ident,
        body,
        [queries, grad, keyvals, bias, lse, delta, key_weight, value_weight],
        [spec[n] for n in ("col", "col", "pair", "bias", "stat", "stat", "weight", "weight")],
        [
            jax.ShapeDtypeStruct((keys, 2 * width), BF),
            jax.ShapeDtypeStruct((tokens, width), BF),
            jax.ShapeDtypeStruct((keys, width), BF),
        ],
        [spec["pair"], spec["col"], spec["rows"]],
        [pltpu.VMEM((keys, width), F32)],
        2**35,
    )


def weight_terms(courier, ident, rows, grads):
    keys, width = rows[0].shape
    spec = block_specs(keys, keys)
    count = len(rows)

    def body(ins, outs, _):
        total = None
        for rows_ref, grad_ref in zip(ins[:count], ins[count:]):
            term = dot(rows_ref[...], grad_ref[...], 0, 0)
            total = term if total is None else total + term
        outs[0][...] = total.astype(BF)

    return call(
        courier,
        ident,
        body,
        list(rows) + list(grads),
        [spec["rows"]] * count + [spec["pair"]] * count,
        [jax.ShapeDtypeStruct((width, 2 * width), BF)],
        [pl.BlockSpec((width, 256), lambda p: (0, p))],
        [],
        2**34,
    )


def self_backward_kernel(q_ref, da_ref, kv_ref, lse_ref, dkv_ref, dq_ref):
    dkv_ref[...], dq_ref[...] = backward_pair(
        q_ref[...], da_ref[...], kv_ref[:, :128], kv_ref[:, 128:], None, two_rows(lse_ref), None
    )


def self_backward(queries, grad, keyvals, lse):
    tokens = queries.shape[0]
    spec = block_specs(tokens, tokens)
    return pl.pallas_call(
        self_backward_kernel,
        grid=(PAIRS,),
        out_shape=[
            jax.ShapeDtypeStruct((tokens, 2 * H * HD), BF),
            jax.ShapeDtypeStruct((tokens, H * HD), BF),
        ],
        in_specs=[spec["col"], spec["col"], spec["pair"], spec["stat"]],
        out_specs=[spec["pair"], spec["col"]],
        compiler_params=pltpu.CompilerParams(vmem_limit_bytes=VMEM),
        cost_estimate=pl.CostEstimate(flops=2**33, bytes_accessed=2**23, transcendentals=2**20),
    )(queries, grad, keyvals, lse)


def place_kernel(*refs):
    *blocks, out_ref, held, arrive, leave = refs
    z = lax.axis_index("z")
    size = held.shape[1]
    inward = []
    outward = []
    for r, block in enumerate(blocks):
        at = rem(z + r, PLANES) * size
        inward.append(pltpu.make_async_copy(block, held.at[r], arrive.at[r]))
        outward.append(
            pltpu.make_async_copy(held.at[r], out_ref.at[pl.ds(at, size)], leave.at[r])
        )
        inward[r].start()
    for r in range(len(blocks)):
        inward[r].wait()
        outward[r].start()
    for copy in outward:
        copy.wait()


def place(blocks):
    shape = blocks[0].shape
    count = len(blocks)
    hbm = pl.BlockSpec(memory_space=pl.ANY)
    return pl.pallas_call(
        place_kernel,
        out_shape=jax.ShapeDtypeStruct((count * shape[0],) + shape[1:], blocks[0].dtype),
        in_specs=[hbm] * count,
        out_specs=hbm,
        scratch_shapes=[
            pltpu.VMEM((count,) + shape, blocks[0].dtype),
            pltpu.SemaphoreType.DMA((count,)),
            pltpu.SemaphoreType.DMA((count,)),
        ],
        compiler_params=pltpu.CompilerParams(vmem_limit_bytes=VMEM),
    )(*blocks)


def interleave(keys, values):
    width = keys.shape[0]
    return jnp.stack(
        [keys.reshape(width, PAIRS, 128), values.reshape(width, PAIRS, 128)], axis=2
    ).reshape(width, 2 * H * HD)


def separate(both):
    rows = both.shape[0]
    parts = both.reshape(rows, PAIRS, 2, 128)
    return parts[:, :, 0].reshape(rows, H * HD), parts[:, :, 1].reshape(rows, H * HD)


def per_row(stat):
    tokens = stat.shape[-1]
    return jnp.repeat(stat.reshape(H, tokens).T, HD, axis=1)


def norm_apply(values, gain):
    return values * lax.rsqrt(jnp.mean(values * values, axis=-1, keepdims=True) + EPSILON) * gain


def norm_back(values, gain, grad):
    r = lax.rsqrt(jnp.mean(values * values, axis=-1, keepdims=True) + EPSILON)
    u = gain * grad
    dv = r * u - values * (r * r * r) * jnp.mean(u * values, axis=-1, keepdims=True)
    return dv, jnp.sum(grad * values * r, axis=0)


def glu_apply(gate_vals, up_vals):
    return jax.nn.gelu(gate_vals, approximate=True) * up_vals


def matmul(left, right):
    return dot(left, right, 1, 0)


def matmul_t(left, right):
    return dot(left, right, 1, 1)


def tmatmul(left, right):
    return dot(left, right, 0, 0)


def scatter_sum(arrays, devices):
    flat = [a.astype(BF).reshape(devices, -1) for a in arrays]
    sizes = [f.shape[1] for f in flat]
    extra = -sum(sizes) % 128
    if extra:
        flat.append(jnp.zeros((devices, extra), BF))
    joined = jnp.concatenate(flat, axis=1)
    mine = lax.psum_scatter(
        joined.reshape(devices, -1, 128), ALL, scatter_dimension=0, tiled=True
    ).reshape(-1).astype(F32)
    out = []
    at = 0
    for size, a in zip(sizes, arrays):
        out.append(mine[at : at + size].reshape((a.shape[0] // devices,) + a.shape[1:]))
        at += size
    return out


def on_device(
    sizes,
    decoder_in,
    memory,
    memory_lengths,
    cotangent,
    norm_self,
    self_query,
    self_key,
    self_value,
    self_out,
    norm_cross,
    cross_query,
    cross_key,
    cross_value,
    cross_out,
    norm_ffn,
    ffn_gate,
    ffn_up,
    ffn_down,
):
    devices, positions, width = memory.shape
    plane_size = sizes[1] * sizes[2] * sizes[3]
    z = lax.axis_index("z")

    def along_z(value, r):
        return lax.ppermute(value, "z", [(i, (i + r) % PLANES) for i in range(PLANES)])

    def flat(blocks):
        return blocks.reshape(plane_size * positions, width)

    def cut(rows):
        return rows.reshape(plane_size, positions, width)

    span = plane_size * positions
    places = z * span + jnp.arange(span, dtype=jnp.int32)

    inputs = decoder_in[0].astype(F32)
    normed_one = norm_apply(inputs, norm_self).astype(BF)
    self_weights = jnp.concatenate([self_query, interleave(self_key, self_value)], axis=1)
    qkv_one = matmul(normed_one, self_weights).astype(BF)
    query_one, keyval_one = qkv_one[:, :width], qkv_one[:, width:]
    (attn_one, lse_one), (fetched,) = self_forward(
        Courier(sizes, [("fetch", 1, memory)]), 0, query_one, keyval_one
    )
    hidden_one = inputs + matmul(attn_one, self_out)
    normed_two = norm_apply(hidden_one, norm_cross).astype(BF)
    query_two = matmul(normed_two, cross_query).astype(BF)

    queries, rows, keyvals, biases, partial, stats_out = {}, {}, {}, {}, {}, {}
    for r in range(PLANES):
        limit = memory_lengths if r == 0 else along_z(memory_lengths, -r)
        bias = jnp.where(places < limit, 0.0, MASKED).astype(BF)
        biases[r] = jnp.broadcast_to(bias[:, None], (bias.shape[0], 128))
    queries[0] = query_two
    queries[1] = along_z(query_two, -1)
    order = (1, 2, 3, 0)
    for at, r in enumerate(order):
        rows[r] = flat(fetched)
        jobs = []
        if at + 1 < PLANES:
            jobs.append(("fetch", order[at + 1], memory))
        if at + 2 < PLANES:
            jobs.append(("line", -order[at + 1], query_two))
        if at >= 1:
            before = order[at - 1]
            jobs.append(("line", before, partial[before]))
            jobs.append(("line", before, stats_out[before]))
        (partial[r], stats_out[r], keyvals[r]), moved = cross_forward(
            Courier(sizes, jobs), 1 + at, queries[r], rows[r], biases[r], cross_key, cross_value
        )
        moved = list(moved)
        if at + 1 < PLANES:
            fetched = moved.pop(0)
        if at + 2 < PLANES:
            queries[order[at + 1]] = moved.pop(0)
        if at >= 1:
            partial[before], stats_out[before] = moved
    lses = jnp.stack([stats_out[r] for r in range(PLANES)])
    top = jnp.max(lses, axis=0)
    scale = jnp.exp(lses - top)
    total = jnp.sum(scale, axis=0)
    lse_two = top + jnp.log(total)
    share = scale / total
    attn_raw_two = sum(per_row(share[r]) * partial[r].astype(F32) for r in range(PLANES))
    attn_two = attn_raw_two.astype(BF)
    hidden_two = hidden_one + matmul(attn_two, cross_out)

    normed_three = norm_apply(hidden_two, norm_ffn).astype(BF)
    gate_vals = matmul(normed_three, ffn_gate)
    up_vals = matmul(normed_three, ffn_up)
    inner = glu_apply(gate_vals, up_vals).astype(BF)
    output = hidden_two + matmul(inner, ffn_down)
    decoder_out = output.astype(BF)[None]

    branch_three = cotangent[0]
    grad_out = branch_three.astype(F32)
    grad_inner = matmul_t(branch_three, ffn_down)
    _, glu_pull = jax.vjp(glu_apply, gate_vals, up_vals)
    grad_gate_raw, grad_up_raw = glu_pull(grad_inner)
    grad_gate_low = grad_gate_raw.astype(BF)
    grad_up_low = grad_up_raw.astype(BF)
    grad_normed_three = matmul_t(grad_gate_low, ffn_gate) + matmul_t(grad_up_low, ffn_up)
    back_two, grad_norm_ffn = norm_back(hidden_two, norm_ffn, grad_normed_three)
    grad_two = grad_out + back_two
    branch_two = grad_two.astype(BF)
    grad_attn_two = matmul_t(branch_two, cross_out).astype(BF)
    products = grad_attn_two.astype(F32) * attn_raw_two
    delta_two = jnp.sum(products.reshape(-1, H, HD), axis=-1).T.reshape(PAIRS, 2, -1)

    grad_down = tmatmul(inner, branch_three)
    grad_gate = tmatmul(normed_three, grad_gate_low)
    grad_up = tmatmul(normed_three, grad_up_low)
    grad_cross_out = tmatmul(attn_two, branch_two)
    ffn_sums = scatter_sum((grad_gate, grad_up, grad_down, grad_cross_out), devices)

    stats = jnp.stack([lse_two, delta_two])
    grads = {0: grad_attn_two}
    both = {0: stats}
    grad_kv, grad_q, grad_rows, returned = {}, {}, {}, {}
    for r in range(PLANES):
        jobs = []
        if r + 1 < PLANES:
            jobs.append(("line", -(r + 1), grad_attn_two))
            jobs.append(("line", -(r + 1), stats))
        if r >= 1:
            jobs.append(("return", 0, cut(grad_rows[r - 1])))
        if r >= 2:
            jobs.append(("line", r - 1, grad_q[r - 1]))
        (grad_kv[r], grad_q[r], grad_rows[r]), moved = cross_backward(
            Courier(sizes, jobs),
            5 + r,
            queries[r],
            grads[r],
            keyvals[r],
            biases[r],
            both[r][0],
            both[r][1],
            cross_key,
            cross_value,
        )
        moved = list(moved)
        if r + 1 < PLANES:
            grads[r + 1], both[r + 1] = moved.pop(0), moved.pop(0)
        if r >= 1:
            returned[r - 1] = moved.pop(0)
        if r >= 2:
            grad_q[r - 1] = moved.pop(0)
    last = PLANES - 1
    (grad_weights,), (grad_q[last], returned[last]) = weight_terms(
        Courier(sizes, [("line", last, grad_q[last]), ("return", 0, cut(grad_rows[last]))]),
        9,
        [rows[r] for r in range(PLANES)],
        [grad_kv[r] for r in range(PLANES)],
    )
    memory_grad = place([returned[r] for r in range(PLANES)])

    grad_q_two = sum(grad_q[r].astype(F32) for r in range(PLANES)).astype(BF)
    grad_cross_query = tmatmul(normed_two, grad_q_two)
    grad_normed_two = matmul_t(grad_q_two, cross_query)
    back_one, grad_norm_cross = norm_back(hidden_one, norm_cross, grad_normed_two)
    grad_one = grad_two + back_one
    branch_one = grad_one.astype(BF)
    cross_sums = scatter_sum((grad_weights, grad_cross_query), devices)
    grad_self_out = tmatmul(attn_one, branch_one)
    grad_attn_one = matmul_t(branch_one, self_out).astype(BF)
    grad_kv_one, grad_q_one = self_backward(query_one, grad_attn_one, keyval_one, lse_one)
    grad_qkv = jnp.concatenate([grad_q_one, grad_kv_one], axis=1)
    grad_self = tmatmul(normed_one, grad_qkv)
    grad_normed_one = matmul_t(grad_qkv, self_weights)
    back_in, grad_norm_self = norm_back(inputs, norm_self, grad_normed_one)
    decoder_in_grad = (grad_one + back_in)[None]
    self_sums = scatter_sum(
        (grad_self, grad_self_out, grad_norm_self, grad_norm_cross, grad_norm_ffn), devices
    )

    sum_cross_key, sum_cross_value = separate(cross_sums[0])
    sum_self_query = self_sums[0][:, :width]
    sum_self_key, sum_self_value = separate(self_sums[0][:, width:])
    return (
        decoder_out,
        decoder_in_grad,
        memory_grad,
        self_sums[2],
        sum_self_query,
        sum_self_key,
        sum_self_value,
        self_sums[1],
        self_sums[3],
        cross_sums[1],
        sum_cross_key,
        sum_cross_value,
        ffn_sums[3],
        self_sums[4],
        ffn_sums[0],
        ffn_sums[1],
        ffn_sums[2],
    )


def solution(mesh):
    dp, seq = mesh.devices.shape
    cores = 2
    lines = dp // PLANES
    split = Mesh(mesh.devices.reshape(PLANES, lines, seq // cores, cores), ALL)
    sizes = split.devices.shape
    first = P(ALL)
    middle = P(None, ALL)
    whole = P()
    return jax.shard_map(
        functools.partial(on_device, sizes),
        mesh=split,
        in_specs=(first, middle, first, first) + (whole,) * 14,
        out_specs=(first, first, middle) + (first,) * 14,
        check_vma=False,
    )
```

time: 1370 us -> 998 us (0.73)
  Pallas kernels: 625 us -> 440 us
  starting transfers between devices: 115 us -> 6.03 us
  matrix products: 151 us -> 65.2 us
  waiting for transfers between devices: 261 us -> 303 us
  local copies, waits for them, and re-layouts: 145 us -> 124 us
    ppermute x77 -> x4, waiting for transfers between devices: 261 us -> 15.9 us  [along_z(): lax.ppermute(value, 'z', [(i, (i + r) % PLANES) for i in range(PLANES)])]
    pallas_call x11 -> x12, Pallas kernels: 625 us -> 440 us  [the longest x10 417 us: call(): pl.pallas_call(lambda *refs: kernel(*counts, refs), grid=(PAIRS,), out_sh...]
    unnamed x4, waiting for transfers between devices: 0.05 us -> 147 us
    reduce_scatter x2, waiting for transfers between devices: 0.01 us -> 140 us  [scatter_sum(): lax.psum_scatter(joined.reshape(devices, -1, 128), ALL, scatter_dimension...]
    ppermute x77 -> x4, starting transfers between devices: 115 us -> 5.91 us  [along_z(): lax.ppermute(value, 'z', [(i, (i + r) % PLANES) for i in range(PLANES)])]
    dot_general x33 -> x21, matrix products: 151 us -> 65.2 us  [dot(): lax.dot_general(left, right, (((left_dim,), (right_dim,)), ((), ())), pre...]
    unnamed x284 -> x113, local copies, waits for them, and re-layouts: 45.4 us -> 37.5 us
  transfers between devices with their start and end apart: 80 -> 7, of which waited for: 31 -> 4; matrix products, arithmetic and copies ran while one was open for 19% -> 10% of each run, Pallas kernels for 45% -> 1%
where the time goes in v2:
time: 998 us; the launch traced here: 991 us
  Pallas kernels  440 us (44%)
  waiting for transfers between devices  303 us (30%)
  local copies, waits for them, and re-layouts  124 us (12%)
  matrix products  65.2 us (7%)
  other arithmetic  36.9 us (4%)
  between operations  15.4 us (2%)
    pallas_call x10, Pallas kernels, call(): pl.pallas_call(lambda *refs: kernel(*counts, refs), grid=(PAIRS,), out_sh...  417 us
    unnamed x4, waiting for transfers between devices  147 us
    reduce_scatter x2, waiting for transfers between devices, scatter_sum(): lax.psum_scatter(joined.reshape(devices, -1, 128), ALL, scatter_dimension...  140 us
    dot_general x21, matrix products, dot(): lax.dot_general(left, right, (((left_dim,), (right_dim,)), ((), ())), pre...  65.2 us
    unnamed x113, local copies, waits for them, and re-layouts  37.5 us
    reshape x8, local copies, waits for them, and re-layouts, scatter_sum(): flat = [a.astype(BF).reshape(devices, -1) for a in arrays]  31.6 us
  transfers between devices with their start and end apart: 7, of which 4 were waited for; matrix products, arithmetic and copies ran while one was open for 10% of the time, Pallas kernels for 1%

profile of v2, /device:TPU:0, one launch (start us, length us, event | category | flops | bytes accessed | tf_op | source)
XLA Modules:
  0.0 990.9 jit_solution(2987260463366283476)
XLA Ops:
  25.0 40.4 %shard_map.305 = (bf16[512,768]{1,0:T(8,128)(2,1)}, f32[6,2,512]{2,1,0:T(2,128)}, bf16[8,256,768]{2,1,0:T(8,128)(2,1)}) custom-call(bf16[512,768]{1,0:T(8,128)(2,1)} %slice.148.refs_0_.q_ref, bf16[512,1536]{1,0:T(8,128)(2,1)} %slice.149.refs_1_.kv_ref, bf16[32,256,768]{2,1,0:T(8,128)(2,1)} %refs_5_.5), custom_call_target="tpu_custom_call" | custom-call | flops 4294967296 | bytes 16777216 | tf_op jit(solution)/shard_map/pallas_call | solution.py:249
  76.6 15.9 %collective-permute-done.3 = s32[1]{0:T(128)} collective-permute-done((s32[1]{0:T(128)}, s32[1]{0:T(128)}, u32[]{:S(2)}, u32[]{:S(2)}) %collective-permute-start.3) | collective-permute-done | bytes 36 | tf_op jit(solution)/shard_map/ppermute | solution.py:557
  95.6 41.0 %shard_map.306 = (bf16[512,768]{1,0:T(8,128)(2,1)}, f32[6,2,512]{2,1,0:T(2,128)}, bf16[2048,1536]{1,0:T(8,128)(2,1)}, bf16[8,256,768]{2,1,0:T(8,128)(2,1)}, bf16[512,768]{1,0:T(8,128)(2,1)}) custom-call(bf16[512,768]{1,0:T(8,128)(2,1)} %collective-permute-done.refs_0_, bf16[2048,768]{1,0:T(8,128)(2,1)} %bitcast.150, ...), custom_call_target="tpu_custom_call" | custom-call | flops 17179869184 | bytes 16777216 | tf_op jit(solution)/shard_map/pallas_call | solution.py:249
  137.7 43.6 %shard_map.307 = (bf16[512,768]{1,0:T(8,128)(2,1)}, f32[6,2,512]{2,1,0:T(2,128)}, bf16[2048,1536]{1,0:T(8,128)(2,1)}, bf16[8,256,768]{2,1,0:T(8,128)(2,1)}, bf16...) custom-call(bf16[512,768]{1,0:T(8,128)(2,1)} %get-tuple-element.73.refs_0_, ...), custom_call_target="tpu_custom_call" | custom-call | flops 17179869184 | bytes 16777216 | tf_op jit(solution)/shard_map/pallas_call | solution.py:249
  182.5 42.1 %shard_map.308 = (bf16[512,768]{1,0:T(8,128)(2,1)}, f32[6,2,512]{2,1,0:T(2,128)}, bf16[2048,1536]{1,0:T(8,128)(2,1)}, bf16[8,256,768]{2,1,0:T(8,128)(2,1)}, bf16...) custom-call(bf16[512,768]{1,0:T(8,128)(2,1)} %get-tuple-element.77.refs_0_, bf16[2048,768]{1,0:T(8,128)(2,1)} %bitcast.154, ...), custom_call_target="tpu_custom_call" | custom-call | flops 17179869184 | bytes 16777216 | tf_op jit(solution)/shard_map/pallas_call | solution.py:249
  225.7 32.9 %shard_map.309 = (bf16[512,768]{1,0:T(8,128)(2,1)}, f32[6,2,512]{2,1,0:T(2,128)}, bf16[2048,1536]{1,0:T(8,128)(2,1)}, bf16[512,768]{1,0:T(8,128)(2,1)}, f32[6,2,512]{2,1,0:T(2,128)}) custom-call(bf16[512,768]{1,0:T(8,128)(2,1)} %convolution_convert_fusion.10.refs_6_.refs_0_, bf16[2048,768]{1,0:T(8,128)(2,1)} %bitcast.156, ...), custom_call_target="tpu_custom_call" | custom-call | flops 17179869184 | bytes 16777216 | tf_op jit(solution)/shard_map/pallas_call | solution.py:249
  278.3 4.4 multiply_add_fusion
  289.9 6.1 multiply_convert_fusion
  309.3 41.0 %shard_map.310 = (bf16[2048,1536]{1,0:T(8,128)(2,1)}, bf16[512,768]{1,0:T(8,128)(2,1)}, bf16[2048,768]{1,0:T(8,128)(2,1)}, bf16[512,768]{1,0:T(8,128)(2,1)}, f32[2,6,2,512]{3,2,1,0:T(2,128)}) custom-call(bf16[512,768]{1,0:T(8,128)(2,1)} %convolution_convert_fusion.10.refs_6_.refs_0_, bf16[512,768]{1,0:T(8,128)(2,1)} %get-tuple-element.168.refs_1_.refs_8_, ...), custom_call_target="tpu_custom_call" | custom-call | flops 34359738368 | bytes 16777216 | tf_op jit(solution)/shard_map/pallas_call | solution.py:249
  351.7 45.1 %shard_map.311 = (bf16[2048,1536]{1,0:T(8,128)(2,1)}, bf16[512,768]{1,0:T(8,128)(2,1)}, bf16[2048,768]{1,0:T(8,128)(2,1)}, bf16[512,768]{1,0:T(8,128)(2,1)}, f32...) custom-call(bf16[512,768]{1,0:T(8,128)(2,1)} %collective-permute-done.refs_0_, ...), custom_call_target="tpu_custom_call" | custom-call | flops 34359738368 | bytes 16777216 | tf_op jit(solution)/shard_map/pallas_call | solution.py:249
  398.2 44.2 %shard_map.312 = (bf16[2048,1536]{1,0:T(8,128)(2,1)}, bf16[512,768]{1,0:T(8,128)(2,1)}, bf16[2048,768]{1,0:T(8,128)(2,1)}, bf16[512,768]{1,0:T(8,128)(2,1)}, f32...) custom-call(bf16[512,768]{1,0:T(8,128)(2,1)} %get-tuple-element.73.refs_0_, ...), custom_call_target="tpu_custom_call" | custom-call | flops 34359738368 | bytes 16777216 | tf_op jit(solution)/shard_map/pallas_call | solution.py:249
  443.8 43.8 %shard_map.313 = (bf16[2048,1536]{1,0:T(8,128)(2,1)}, bf16[512,768]{1,0:T(8,128)(2,1)}, bf16[2048,768]{1,0:T(8,128)(2,1)}, bf16[8,256,768]{2,1,0:T(8,128)(2,1)}, bf16[512,768]{1,0:T(8,128)(2,1)}) custom-call(bf16[512,768]{1,0:T(8,128)(2,1)} %get-tuple-element.77.refs_0_, bf16[512,768]{1,0:T(8,128)(2,1)} %get-tuple-element.104.refs_1_, ...), custom_call_target="tpu_custom_call" | custom-call | flops 34359738368 | bytes 16777216 | tf_op jit(solution)/shard_map/pallas_call | solution.py:249
  487.6 43.0 %shard_map.314 = (bf16[768,1536]{1,0:T(8,128)(2,1)}, bf16[512,768]{1,0:T(8,128)(2,1)}, bf16[8,256,768]{2,1,0:T(8,128)(2,1)}) custom-call(bf16[2048,768]{1,0:T(8,128)(2,1)} %bitcast.157, bf16[2048,768]{1,0:T(8,128)(2,1)} %bitcast.151, bf16[2048,768]{1,0:T(8,128)(2,1)} %bitcast.153, bf16[2048,768]{1,0:T(8,128)(2,1)} %bitcast.155, ...), custom_call_target="tpu_custom_call" | custom-call | flops 17179869184 | bytes 16777216 | tf_op jit(solution)/shard_map/pallas_call | solution.py:249
  543.4 14.0 %shard_map.315 = (bf16[512,1536]{1,0:T(8,128)(2,1)}, bf16[512,768]{1,0:T(8,128)(2,1)}) custom-call(bf16[512,768]{1,0:T(8,128)(2,1)} %slice.148.refs_0_.q_ref, bf16[512,768]{1,0:T(8,128)(2,1)} %convolution_convert_fusion.8.da_ref, bf16[512,1536]{1,0:T(8,128)(2,1)} %slice.149.refs_1_.kv_ref, f32[6,2,512]{2,1,0:T(2,128)} %get-tuple-element.117.lse_ref), custom_call_target="tpu_custom_call" | custom-call | flops 8589934592 | bytes 8388608 | tf_op jit(solution)/shard_map/pallas_call | solution.py:416
  560.7 4.0 convolution_convert_fusion
  564.6 5.1 reshape.274
  569.8 4.3 reshape.280
  578.7 4.0 constant_dynamic-update-slice_fusion.3
  588.9 6.3 fusion.17
  603.2 6.1 reshape.276
  609.4 5.3 convolution_convert_fusion.2
  614.7 5.0 reshape.285
  619.7 5.3 convolution_convert_fusion.3
  625.1 4.9 reshape.284
  630.0 5.3 convolution_convert_fusion.4
  635.3 4.8 reshape.283
  640.1 3.7 convolution_convert_fusion.5
  646.3 11.3 %maximum_bitcast_fusion = bf16[4,8,1296,128]{3,1,2,0:T(8,128)(2,1)S(1)} fusion(bf16[32,18432]{1,0:T(8,128)(2,1)} %reshape.286, bf16[32,49152]{1,0:T(8,128)(2,1)} %reshape.285, bf16[32,49152]{1,0:T(8,128)(2,1)} %reshape.284, bf16[32,49152]{1,0:T(8,128)(2,1)} %reshape.283), kind=kLoop, calls=%fused_computation | loop fusion | flops 42467328 | bytes 21233664
  657.6 5.0 copy.70
  662.8 9.3 shard_map.316
  686.2 146.8 %reduce-scatter.11.cloned.1.call-done = bf16[1,577,128]{2,1,0:T(8,128)(2,1)} async-done(((bf16[32,577,128]{2,1,0:T(8,128)(2,1)}), bf16[1,577,128]{2,1,0:T(8,128)(2,1)}) %reduce-scatter.11.cloned.1.call-update) | async-done | bytes 147728
  841.7 136.2 %reduce-scatter.9.cloned.1.call-done = bf16[1,1296,128]{2,1,0:T(8,128)(2,1)} async-done(((bf16[32,1296,128]{2,1,0:T(8,128)(2,1)}), bf16[1,1296,128]{2,1,0:T(8,128)(2,1)}) %reduce-scatter.9.cloned.1.call-update) | async-done | bytes 331792 | tf_op jit(solution)/shard_map/reduce_scatter | solution.py:520
  (217 shorter events, 144.8 us)
Async XLA Ops:
  7.2 282.7 %copy-start = (bf16[2048,768]{1,0:T(8,128)(2,1)S(1)}, bf16[2048,768]{1,0:T(8,128)(2,1)}, u32[]{:S(2)}) copy-start(bf16[2048,768]{1,0:T(8,128)(2,1)} %param.35) | copy-start | bytes 9437188
  7.2 674.9 %reduce-scatter.7.cloned.1.call-start = ((), (), s32[]{:S(2)}) async-start(), calls=%async_computation.3 | async-start | bytes 3649536 | tf_op jit(solution)/shard_map/reduce_scatter | solution.py:520
  9.4 9.2 copy-start.30
  18.5 4.3 copy-start.14
  25.0 40.4 %copy-start.44 = (bf16[768,768]{1,0:T(8,128)(2,1)S(1)}, bf16[768,768]{1,0:T(8,128)(2,1)}, u32[]{:S(2)}) copy-start(bf16[768,768]{1,0:T(8,128)(2,1)} %param.26) | copy-start | bytes 3538948
  65.4 2.8 copy-start.37
  65.5 2.8 copy-start.42
  70.0 24.4 %collective-permute-start = (bf16[512,768]{1,0:T(8,128)(2,1)}, bf16[512,768]{1,0:T(8,128)(2,1)}, u32[]{:S(2)}, u32[]{:S(2)}) collective-permute-start(bf16[512,768]{1,0:T(8,128)(2,1)} %convolution_convert_fusion.10.refs_6_.refs_0_), channel_id=1, source_target_pairs={{0,24},{8,0},{16,8},{24,16},{1,25},{9,1},{17,9},{25,17},{2,26},{10... | collective-permute-start | bytes 2359304 | tf_op jit(solution)/shard_map/ppermute | solution.py:557
  73.6 19.5 %collective-permute-start.2 = (s32[1]{0:T(128)}, s32[1]{0:T(128)}, u32[]{:S(2)}, u32[]{:S(2)}) collective-permute-start(s32[1]{0:T(128)} %param.20), channel_id=1, source_target_pairs={{0,16},{8,24},{16,0},{24,8},{1,17},{9,25},{17,1},{25,9},{2,18},{10... | collective-permute-start | bytes 20 | tf_op jit(solution)/shard_map/ppermute | solution.py:557
  73.6 19.6 %collective-permute-start.1 = (s32[1]{0:T(128)}, s32[1]{0:T(128)}, u32[]{:S(2)}, u32[]{:S(2)}) collective-permute-start(s32[1]{0:T(128)} %param.20), channel_id=1, source_target_pairs={{0,24},{8,0},{16,8},{24,16},{1,25},{9,1},{17,9},{25,17},{2,26},{10... | collective-permute-start | bytes 20 | tf_op jit(solution)/shard_map/ppermute | solution.py:557
  74.4 18.1 %collective-permute-start.3 = (s32[1]{0:T(128)}, s32[1]{0:T(128)}, u32[]{:S(2)}, u32[]{:S(2)}) collective-permute-start(s32[1]{0:T(128)} %param.20), channel_id=1, source_target_pairs={{0,8},{8,16},{16,24},{24,0},{1,9},{9,17},{17,25},{25,1},{2,10},{10... | collective-permute-start | bytes 20 | tf_op jit(solution)/shard_map/ppermute | solution.py:557
  225.7 33.0 %copy-start.26 = (f32[6,2,512]{2,1,0:T(2,128)S(1)}, f32[6,2,512]{2,1,0:T(2,128)}, u32[]{:S(2)}) copy-start(f32[6,2,512]{2,1,0:T(2,128)} %get-tuple-element.85) | copy-start | bytes 73732
  225.7 33.0 %copy-start.27 = (f32[6,2,512]{2,1,0:T(2,128)S(1)}, f32[6,2,512]{2,1,0:T(2,128)}, u32[]{:S(2)}) copy-start(f32[6,2,512]{2,1,0:T(2,128)} %get-tuple-element.86) | copy-start | bytes 73732
  260.3 48.4 %copy-start.25 = (f32[6,2,512]{2,1,0:T(2,128)}, f32[6,2,512]{2,1,0:T(2,128)S(1)}, u32[]{:S(2)}) copy-start(f32[6,2,512]{2,1,0:T(2,128)S(1)} %log_add_fusion.refs_4_) | copy-start | bytes 73732
  278.3 4.4 copy-start.8
  278.3 4.5 copy-start.10
  282.8 18.3 %copy-start.1 = (f32[512,768]{1,0:T(8,128)}, f32[512,768]{1,0:T(8,128)S(1)}, u32[]{:S(2)}) copy-start(f32[512,768]{1,0:T(8,128)S(1)} %multiply_add_fusion) | copy-start | bytes 4718596
  282.8 3.0 copy-start.41
  283.7 17.0 %copy-start.5 = (f32[512,768]{1,0:T(8,128)}, f32[512,768]{1,0:T(8,128)S(1)}, u32[]{:S(2)}) copy-start(f32[512,768]{1,0:T(8,128)S(1)} %get-tuple-element.165) | copy-start | bytes 4718596
  487.6 43.1 %copy-start.21 = (bf16[512,768]{1,0:T(8,128)(2,1)S(1)}, bf16[512,768]{1,0:T(8,128)(2,1)}, u32[]{:S(2)}) copy-start(bf16[512,768]{1,0:T(8,128)(2,1)} %get-tuple-element.93) | copy-start | bytes 2359300
  487.6 43.1 %copy-start.22 = (bf16[512,768]{1,0:T(8,128)(2,1)S(1)}, bf16[512,768]{1,0:T(8,128)(2,1)}, u32[]{:S(2)}) copy-start(bf16[512,768]{1,0:T(8,128)(2,1)} %get-tuple-element.103) | copy-start | bytes 2359300
  487.6 43.1 %copy-start.23 = (bf16[512,768]{1,0:T(8,128)(2,1)S(1)}, bf16[512,768]{1,0:T(8,128)(2,1)}, u32[]{:S(2)}) copy-start(bf16[512,768]{1,0:T(8,128)(2,1)} %get-tuple-element.109) | copy-start | bytes 2359300
  538.8 2.9 copy-start.45
  578.6 4.1 copy-start.39
  578.6 254.4 %reduce-scatter.11.cloned.1.call-start = ((), (), s32[]{:S(2)}) async-start(), calls=%async_computation.5 | async-start | bytes 4933632
  609.3 368.6 %reduce-scatter.9.cloned.1.call-start = ((), (), s32[]{:S(2)}) async-start(), calls=%async_computation.4 | async-start | bytes 10948608 | tf_op jit(solution)/shard_map/reduce_scatter | solution.py:520
  662.7 9.4 copy-start.4
  662.7 9.4 copy-start.13
  662.7 10.4 %copy-start.16 = (f32[512,768]{1,0:T(8,128)S(1)}, f32[512,768]{1,0:T(8,128)}, u32[]{:S(2)}) copy-start(f32[512,768]{1,0:T(8,128)} %get-tuple-element.170) | copy-start | bytes 4718596
  662.7 10.4 %copy-start.29 = (f32[512]{0:T(512)S(1)}, f32[512]{0:T(512)}, u32[]{:S(2)}) copy-start(f32[512]{0:T(512)} %get-tuple-element.156) | copy-start | bytes 6148
  673.1 2.7 copy-start.48
  833.0 8.1 copy-start.17
  (24 other events, 43.5 us)
Sparse Core Ops, SparseCore 0:
  578.7 103.3 reduce-scatter.6
  684.5 148.5 reduce-scatter.10
  840.2 137.7 reduce-scatter.8

commit v3 on v2

--- a/solution.py
+++ b/solution.py
@@ -53,8 +53,11 @@
         self.sizes = sizes
         self.jobs = jobs
         self.plane = sizes[1] * sizes[2] * sizes[3]
-        self.in_plane = any(job[0] != "line" for job in jobs)
+        self.in_plane = any(job[0] in ("fetch", "return") for job in jobs)
         self.lines = [job[1] for job in jobs if job[0] == "line"]
+        for job in jobs:
+            if job[0] == "scatter":
+                self.lines += list(range(1, PLANES))
 
     def out_shape(self):
         shapes = []
@@ -62,6 +65,8 @@
             shape = value.shape
             if kind == "fetch":
                 shape = (self.plane,) + shape[1:]
+            elif kind == "scatter":
+                shape = (PLANES - 1,) + shape[1:]
             shapes.append(jax.ShapeDtypeStruct(shape, value.dtype))
         return shapes
 
@@ -72,8 +77,9 @@
         return [job[2] for job in self.jobs]
 
     def scratch(self):
-        count = sum(1 if job[0] == "line" else self.plane - 1 for job in self.jobs)
-        own = max(1, sum(job[0] != "line" for job in self.jobs))
+        each = {"line": 1, "scatter": PLANES - 1}
+        count = max(1, sum(each.get(job[0], self.plane - 1) for job in self.jobs))
+        own = max(1, sum(job[0] in ("fetch", "return") for job in self.jobs))
         return [pltpu.SemaphoreType.DMA((n,)) for n in (count, count, own)]
 
     def params(self, ident):
@@ -138,6 +144,11 @@
             if kind == "line":
                 add(source, target, self.along(offset))
                 continue
+            if kind == "scatter":
+                for k in range(1, PLANES):
+                    there = rem(lax.axis_index("z") + k, PLANES)
+                    add(source.at[there], target.at[k - 1], self.along(k))
+                continue
             base = 0
             if kind == "fetch":
                 base = rem(lax.axis_index("z") + offset, PLANES) * self.plane
@@ -157,6 +168,136 @@
     def wait(self, sources, targets, sems):
         for copy in self.copies(sources, targets, sems):
             copy.wait()
+
+
+class Reducer:
+    def __init__(self, sizes, shape):
+        self.sizes = sizes
+        self.rows, self.lanes = shape[-2:]
+        self.half = self.lanes // 2
+
+    def scratch(self):
+        z, y, x, _ = self.sizes
+        r, w, h = self.rows, self.lanes, self.half
+        crossing = x + y - 2
+        return [
+            pltpu.VMEM((z, y, x, r, w), BF),
+            pltpu.VMEM((z, y, x, r, w), BF),
+            pltpu.VMEM((x - 1, z, y, r, h), BF),
+            pltpu.VMEM((y - 1, z, x, r, h), BF),
+            pltpu.VMEM((y - 1, z, r, h), BF),
+            pltpu.VMEM((x - 1, z, r, h), BF),
+            pltpu.SemaphoreType.DMA((1,)),
+            pltpu.SemaphoreType.DMA((1 + 2 * crossing,)),
+            pltpu.SemaphoreType.DMA((1 + 2 * crossing,)),
+        ]
+
+    def bind(self, source, refs):
+        self.source = source
+        self.own, self.got0, self.got1x, self.got1y, self.got2y, self.got2x = refs[:6]
+        self.local, self.send, self.receive = refs[6:]
+        self.z, self.y, self.x, self.c = (lax.axis_index(name) for name in ALL)
+        return self
+
+    def remote(self, n, source, target, device):
+        return pltpu.make_async_remote_copy(
+            src_ref=source,
+            dst_ref=target,
+            send_sem=self.send.at[n],
+            recv_sem=self.receive.at[n],
+            device_id=device,
+            device_id_type=pl.DeviceIdType.MESH,
+        )
+
+    def first(self):
+        other = 1 - self.c
+        return [
+            pltpu.make_async_copy(self.source.at[:, :, :, self.c], self.own, self.local.at[0]),
+            self.remote(0, self.source.at[:, :, :, other], self.got0, {"c": other}),
+        ]
+
+    def second(self):
+        _, y_size, x_size, _ = self.sizes
+        left, right = pl.ds(0, self.half), pl.ds(self.half, self.half)
+        copies = []
+        for k in range(1, x_size):
+            there = rem(self.x + k, x_size)
+            copies.append((self.own.at[:, :, there, :, left], self.got1x.at[k - 1], {"x": there}))
+        for k in range(1, y_size):
+            there = rem(self.y + k, y_size)
+            copies.append((self.own.at[:, there, :, :, right], self.got1y.at[k - 1], {"y": there}))
+        return [self.remote(1 + n, *copy) for n, copy in enumerate(copies)]
+
+    def third(self):
+        _, y_size, x_size, _ = self.sizes
+        left, right = pl.ds(0, self.half), pl.ds(self.half, self.half)
+        at = 1 + x_size + y_size - 2
+        copies = []
+        for k in range(1, y_size):
+            there = rem(self.y + k, y_size)
+            copies.append(
+                (self.own.at[:, there, self.x, :, left], self.got2y.at[k - 1], {"y": there})
+            )
+        for k in range(1, x_size):
+            there = rem(self.x + k, x_size)
+            copies.append(
+                (self.own.at[:, self.y, there, :, right], self.got2x.at[k - 1], {"x": there})
+            )
+        return [self.remote(at + n, *copy) for n, copy in enumerate(copies)]
+
+    def begin(self):
+        for copy in self.first():
+            copy.start()
+
+    def after_first(self):
+        for copy in self.first():
+            copy.wait()
+
+        @pl.loop(0, self.sizes[0])
+        def _(z):
+            self.own[z] = (self.own[z].astype(F32) + self.got0[z].astype(F32)).astype(BF)
+
+        for copy in self.second():
+            copy.start()
+
+    def after_second(self):
+        _, y_size, x_size, _ = self.sizes
+        for copy in self.second():
+            copy.wait()
+        h = self.half
+
+        @pl.loop(0, self.sizes[0])
+        def _(z):
+            for y in range(y_size):
+                total = self.own[z, y, self.x, :, :h].astype(F32)
+                for k in range(x_size - 1):
+                    total += self.got1x[k, z, y].astype(F32)
+                self.own[z, y, self.x, :, :h] = total.astype(BF)
+            for x in range(x_size):
+                total = self.own[z, self.y, x, :, h:].astype(F32)
+                for k in range(y_size - 1):
+                    total += self.got1y[k, z, x].astype(F32)
+                self.own[z, self.y, x, :, h:] = total.astype(BF)
+
+        for copy in self.third():
+            copy.start()
+
+    def after_third(self, out_ref):
+        _, y_size, x_size, _ = self.sizes
+        for copy in self.third():
+            copy.wait()
+        h = self.half
+
+        @pl.loop(0, self.sizes[0])
+        def _(z):
+            total = self.own[z, self.y, self.x, :, :h].astype(F32)
+            for k in range(y_size - 1):
+                total += self.got2y[k, z].astype(F32)
+            out_ref[z, :, :h] = total.astype(BF)
+            total = self.own[z, self.y, self.x, :, h:].astype(F32)
+            for k in range(x_size - 1):
+                total += self.got2x[k, z].astype(F32)
+            out_ref[z, :, h:] = total.astype(BF)
 
 
 def forward_pair(queries, keys, values, bias):
@@ -222,41 +363,155 @@
     return groups
 
 
-def carried(courier, body):
+def carried(courier, reducer, body):
     jobs = len(courier.jobs)
+    sums = 0 if reducer is None else 1
 
     def kernel(ins, outs, scratch, refs):
-        own_in, sources, own_out, targets, own_scratch, sems = split_refs(
-            refs, ins, jobs, outs, jobs, scratch, 3
+        own_in, sources, summands, own_out, targets, results, own_scratch, sems, rest = split_refs(
+            refs, ins, jobs, sums, outs, jobs, sums, scratch, 3, 9 * sums
         )
-
-        @pl.when(pl.program_id(0) == 0)
+        step = pl.program_id(0)
+
+        @pl.when(step == 0)
         def _():
             courier.start(sources, targets, sems)
+            if sums:
+                reducer.bind(summands[0], rest).begin()
 
         body(own_in, own_out, own_scratch)
 
-        @pl.when(pl.program_id(0) == PAIRS - 1)
+        if sums:
+
+            @pl.when(step == 1)
+            def _():
+                reducer.bind(summands[0], rest).after_first()
+
+            @pl.when(step == 3)
+            def _():
+                reducer.bind(summands[0], rest).after_second()
+
+        @pl.when(step == PAIRS - 1)
         def _():
+            if sums:
+                reducer.bind(summands[0], rest).after_third(results[0])
             courier.wait(sources, targets, sems)
 
     return kernel
 
 
-def call(courier, ident, body, args, in_specs, out_shape, out_specs, scratch, flops):
-    kernel = carried(courier, body)
+def call(courier, ident, body, args, in_specs, out_shape, out_specs, scratch, flops, summand=None):
+    reducer = None
+    extra_in, extra_out, extra_out_specs, extra_scratch = [], [], [], []
+    if summand is not None:
+        courier.in_plane = True
+        reducer = Reducer(courier.sizes, summand.shape)
+        shape = (PLANES,) + summand.shape[-2:]
+        extra_in = [summand]
+        extra_out = [jax.ShapeDtypeStruct(shape, BF)]
+        extra_out_specs = [pl.BlockSpec(shape, lambda p: (0, 0, 0))]
+        extra_scratch = reducer.scratch()
+    kernel = carried(courier, reducer, body)
     counts = (len(args), len(out_shape), len(scratch))
     outs = pl.pallas_call(
         lambda *refs: kernel(*counts, refs),
         grid=(PAIRS,),
-        out_shape=out_shape + courier.out_shape(),
-        in_specs=in_specs + courier.specs(),
-        out_specs=out_specs + courier.specs(),
-        scratch_shapes=scratch + courier.scratch(),
+        out_shape=out_shape + courier.out_shape() + extra_out,
+        in_specs=in_specs + courier.specs() + [pl.BlockSpec(memory_space=pl.ANY)] * len(extra_in),
+        out_specs=out_specs + courier.specs() + extra_out_specs,
+        scratch_shapes=scratch + courier.scratch() + extra_scratch,
         compiler_params=courier.params(ident),
         cost_estimate=pl.CostEstimate(flops=flops, bytes_accessed=2**24, transcendentals=2**20),
-    )(*args, *courier.values())
+    )(*args, *courier.values(), *extra_in)
     return outs[: len(out_shape)], outs[len(out_shape) :]
+
+
+def reduce_all(sizes, ident, summands, scattered):
+    courier = Courier(sizes, [("scatter", 0, value) for value in scattered])
+    courier.in_plane = True
+    courier.lines += list(range(1, PLANES))
+    jobs = len(scattered)
+    count = len(summands)
+    reducers = [Reducer(sizes, value.shape) for value in summands]
+    shapes = [value.shape[-2:] for value in summands]
+
+    def kernel(*refs):
+        sources, arrays, targets, results, sems, rest = split_refs(
+            refs, jobs, count, jobs, count, 3, len(refs) - 2 * jobs - 2 * count - 3
+        )
+        courier.start(sources, targets, sems)
+        bound = []
+        last = []
+        for n in range(count):
+            refs_n = rest[13 * n : 13 * n + 13]
+            bound.append(reducers[n].bind(arrays[n], refs_n[:9]))
+            last.append(refs_n[9:])
+
+        def leave(n):
+            left, got, send, receive = last[n]
+            copies = []
+            for k in range(1, PLANES):
+                copies.append(
+                    pltpu.make_async_remote_copy(
+                        src_ref=left.at[rem(lax.axis_index("z") + k, PLANES)],
+                        dst_ref=got.at[k - 1],
+                        send_sem=send.at[k - 1],
+                        recv_sem=receive.at[k - 1],
+                        device_id=courier.along(k),
+                        device_id_type=pl.DeviceIdType.MESH,
+                    )
+                )
+            return copies
+
+        for one in bound:
+            one.begin()
+        for one in bound:
+            one.after_first()
+        for one in bound:
+            one.after_second()
+        for n, one in enumerate(bound):
+            one.after_third(last[n][0])
+            for copy in leave(n):
+                copy.start()
+        for n in range(count):
+            for copy in leave(n):
+                copy.wait()
+            left, got = last[n][:2]
+            total = left[lax.axis_index("z")].astype(F32)
+            for k in range(PLANES - 1):
+                total += got[k].astype(F32)
+            results[n][...] = total
+        courier.wait(sources, targets, sems)
+
+    scratch = []
+    for n in range(count):
+        scratch += reducers[n].scratch() + [
+            pltpu.VMEM((PLANES,) + shapes[n], BF),
+            pltpu.VMEM((PLANES - 1,) + shapes[n], BF),
+            pltpu.SemaphoreType.DMA((PLANES - 1,)),
+            pltpu.SemaphoreType.DMA((PLANES - 1,)),
+        ]
+    outs = pl.pallas_call(
+        kernel,
+        out_shape=courier.out_shape() + [jax.ShapeDtypeStruct(shape, F32) for shape in shapes],
+        in_specs=courier.specs() + [pl.BlockSpec(memory_space=pl.ANY)] * count,
+        out_specs=courier.specs() + [pl.BlockSpec(memory_space=pltpu.VMEM)] * count,
+        scratch_shapes=courier.scratch() + scratch,
+        compiler_params=courier.params(ident),
+    )(*courier.values(), *summands)
+    return outs[:jobs], outs[jobs:]
+
+
+def summand_of(sizes, arrays):
+    devices = sizes[0] * sizes[1] * sizes[2] * sizes[3]
+    parts = [a.reshape(devices, a.shape[0] // devices, a.shape[1]) for a in arrays]
+    joined = parts[0] if len(parts) == 1 else jnp.concatenate(parts, axis=1)
+    return joined.astype(BF).reshape(tuple(sizes) + joined.shape[1:])
+
+
+def over_z(left, got):
+    own = lax.dynamic_index_in_dim(left, lax.axis_index("z"), 0, keepdims=False)
+    return own.astype(F32) + jnp.sum(got.astype(F32), axis=0)
 
 
 def block_specs(tokens, keys):
@@ -329,7 +584,9 @@
     )
 
 
-def cross_backward(courier, ident, queries, grad, keyvals, bias, lse, delta, key_weight, value_weight):
+def cross_backward(
+    courier, ident, queries, grad, keyvals, bias, lse, delta, key_weight, value_weight, summand=None
+):
     tokens, keys = queries.shape[0], keyvals.shape[0]
     width = H * HD
     spec = block_specs(tokens, keys)
@@ -376,6 +633,7 @@
         [spec["pair"], spec["col"], spec["rows"]],
         [pltpu.VMEM((keys, width), F32)],
         2**35,
+        summand,
     )
 
 
@@ -389,7 +647,8 @@
         for rows_ref, grad_ref in zip(ins[:count], ins[count:]):
             term = dot(rows_ref[...], grad_ref[...], 0, 0)
             total = term if total is None else total + term
-        outs[0][...] = total.astype(BF)
+        outs[0][...] = total[:, :128]
+        outs[1][...] = total[:, 128:]
 
     return call(
         courier,
@@ -397,34 +656,38 @@
         body,
         list(rows) + list(grads),
         [spec["rows"]] * count + [spec["pair"]] * count,
-        [jax.ShapeDtypeStruct((width, 2 * width), BF)],
-        [pl.BlockSpec((width, 256), lambda p: (0, p))],
+        [jax.ShapeDtypeStruct((width, width), F32)] * 2,
+        [spec["weight"]] * 2,
         [],
         2**34,
     )
 
 
-def self_backward_kernel(q_ref, da_ref, kv_ref, lse_ref, dkv_ref, dq_ref):
-    dkv_ref[...], dq_ref[...] = backward_pair(
-        q_ref[...], da_ref[...], kv_ref[:, :128], kv_ref[:, 128:], None, two_rows(lse_ref), None
-    )
-
-
-def self_backward(queries, grad, keyvals, lse):
-    tokens = queries.shape[0]
+def self_backward(courier, ident, queries, grad, keyvals, lse, summand):
+    tokens, width = queries.shape
     spec = block_specs(tokens, tokens)
-    return pl.pallas_call(
-        self_backward_kernel,
-        grid=(PAIRS,),
-        out_shape=[
-            jax.ShapeDtypeStruct((tokens, 2 * H * HD), BF),
-            jax.ShapeDtypeStruct((tokens, H * HD), BF),
-        ],
-        in_specs=[spec["col"], spec["col"], spec["pair"], spec["stat"]],
-        out_specs=[spec["pair"], spec["col"]],
-        compiler_params=pltpu.CompilerParams(vmem_limit_bytes=VMEM),
-        cost_estimate=pl.CostEstimate(flops=2**33, bytes_accessed=2**23, transcendentals=2**20),
-    )(queries, grad, keyvals, lse)
+
+    def body(ins, outs, _):
+        q_ref, da_ref, kv_ref, lse_ref = ins
+        dq_ref, dk_ref, dv_ref = outs
+        grad_kv, dq_ref[...] = backward_pair(
+            q_ref[...], da_ref[...], kv_ref[:, :128], kv_ref[:, 128:], None, two_rows(lse_ref), None
+        )
+        dk_ref[...] = grad_kv[:, :128]
+        dv_ref[...] = grad_kv[:, 128:]
+
+    return call(
+        courier,
+        ident,
+        body,
+        [queries, grad, keyvals, lse],
+        [spec["col"], spec["col"], spec["pair"], spec["stat"]],
+        [jax.ShapeDtypeStruct((tokens, width), BF)] * 3,
+        [spec["col"]] * 3,
+        [],
+        2**33,
+        summand,
+    )
 
 
 def place_kernel(*refs):
@@ -508,24 +771,6 @@
 
 def tmatmul(left, right):
     return dot(left, right, 0, 0)
-
-
-def scatter_sum(arrays, devices):
-    flat = [a.astype(BF).reshape(devices, -1) for a in arrays]
-    sizes = [f.shape[1] for f in flat]
-    extra = -sum(sizes) % 128
-    if extra:
-        flat.append(jnp.zeros((devices, extra), BF))
-    joined = jnp.concatenate(flat, axis=1)
-    mine = lax.psum_scatter(
-        joined.reshape(devices, -1, 128), ALL, scatter_dimension=0, tiled=True
-    ).reshape(-1).astype(F32)
-    out = []
-    at = 0
-    for size, a in zip(sizes, arrays):
-        out.append(mine[at : at + size].reshape((a.shape[0] // devices,) + a.shape[1:]))
-        at += size
-    return out
 
 
 def on_device(
@@ -642,7 +887,8 @@
     grad_gate = tmatmul(normed_three, grad_gate_low)
     grad_up = tmatmul(normed_three, grad_up_low)
     grad_cross_out = tmatmul(attn_two, branch_two)
-    ffn_sums = scatter_sum((grad_gate, grad_up, grad_down, grad_cross_out), devices)
+    summands = {0: summand_of(sizes, (grad_gate, grad_up)), 1: summand_of(sizes, (grad_down,))}
+    left, got = {}, {}
 
     stats = jnp.stack([lse_two, delta_two])
     grads = {0: grad_attn_two}
@@ -657,6 +903,8 @@
             jobs.append(("return", 0, cut(grad_rows[r - 1])))
         if r >= 2:
             jobs.append(("line", r - 1, grad_q[r - 1]))
+        if r - 1 in left:
+            jobs.append(("scatter", 0, left[r - 1]))
         (grad_kv[r], grad_q[r], grad_rows[r]), moved = cross_backward(
             Courier(sizes, jobs),
             5 + r,
@@ -668,16 +916,21 @@
             both[r][1],
             cross_key,
             cross_value,
+            summands.get(r),
         )
         moved = list(moved)
+        if r in summands:
+            left[r] = moved.pop()
         if r + 1 < PLANES:
             grads[r + 1], both[r + 1] = moved.pop(0), moved.pop(0)
         if r >= 1:
             returned[r - 1] = moved.pop(0)
         if r >= 2:
             grad_q[r - 1] = moved.pop(0)
+        if r - 1 in left:
+            got[r - 1] = moved.pop(0)
     last = PLANES - 1
-    (grad_weights,), (grad_q[last], returned[last]) = weight_terms(
+    (grad_cross_key, grad_cross_value), (grad_q[last], returned[last]) = weight_terms(
         Courier(sizes, [("line", last, grad_q[last]), ("return", 0, cut(grad_rows[last]))]),
         9,
         [rows[r] for r in range(PLANES)],
@@ -691,40 +944,63 @@
     back_one, grad_norm_cross = norm_back(hidden_one, norm_cross, grad_normed_two)
     grad_one = grad_two + back_one
     branch_one = grad_one.astype(BF)
-    cross_sums = scatter_sum((grad_weights, grad_cross_query), devices)
     grad_self_out = tmatmul(attn_one, branch_one)
     grad_attn_one = matmul_t(branch_one, self_out).astype(BF)
-    grad_kv_one, grad_q_one = self_backward(query_one, grad_attn_one, keyval_one, lse_one)
-    grad_qkv = jnp.concatenate([grad_q_one, grad_kv_one], axis=1)
-    grad_self = tmatmul(normed_one, grad_qkv)
-    grad_normed_one = matmul_t(grad_qkv, self_weights)
+    (grad_q_one, grad_k_one, grad_v_one), (cross_left,) = self_backward(
+        Courier(sizes, []),
+        10,
+        query_one,
+        grad_attn_one,
+        keyval_one,
+        lse_one,
+        summand_of(sizes, (grad_cross_key, grad_cross_value)),
+    )
+    grad_normed_one = (
+        matmul_t(grad_q_one, self_query)
+        + matmul_t(grad_k_one, self_key)
+        + matmul_t(grad_v_one, self_value)
+    )
     back_in, grad_norm_self = norm_back(inputs, norm_self, grad_normed_one)
     decoder_in_grad = (grad_one + back_in)[None]
-    self_sums = scatter_sum(
-        (grad_self, grad_self_out, grad_norm_self, grad_norm_cross, grad_norm_ffn), devices
-    )
-
-    sum_cross_key, sum_cross_value = separate(cross_sums[0])
-    sum_self_query = self_sums[0][:, :width]
-    sum_self_key, sum_self_value = separate(self_sums[0][:, width:])
+    share_of_norms = width // devices
+    norms = jnp.stack(
+        [g.reshape(devices, share_of_norms) for g in (grad_norm_self, grad_norm_cross, grad_norm_ffn)],
+        axis=1,
+    ).reshape(devices, 1, 3 * share_of_norms)
+    norms = jnp.pad(norms, ((0, 0), (0, 15), (0, 256 - 3 * share_of_norms)))
+    (cross_got,), sums = reduce_all(
+        sizes,
+        11,
+        [
+            norms.astype(BF).reshape(tuple(sizes) + norms.shape[1:]),
+            summand_of(sizes, (grad_cross_query, grad_cross_out)),
+            summand_of(sizes, (tmatmul(normed_one, grad_q_one), tmatmul(normed_one, grad_k_one))),
+            summand_of(sizes, (tmatmul(normed_one, grad_v_one), grad_self_out)),
+        ],
+        [cross_left],
+    )
+    norm_sums = sums[0][0, : 3 * share_of_norms].reshape(3, share_of_norms)
+    gate_up = over_z(left[0], got[0])
+    cross_kv = over_z(cross_left, cross_got)
+    part = share_of_norms
     return (
         decoder_out,
         decoder_in_grad,
         memory_grad,
-        self_sums[2],
-        sum_self_query,
-        sum_self_key,
-        sum_self_value,
-        self_sums[1],
-        self_sums[3],
-        cross_sums[1],
-        sum_cross_key,
-        sum_cross_value,
-        ffn_sums[3],
-        self_sums[4],
-        ffn_sums[0],
-        ffn_sums[1],
-        ffn_sums[2],
+        norm_sums[0],
+        sums[2][:part],
+        sums[2][part:],
+        sums[3][:part],
+        sums[3][part:],
+        norm_sums[1],
+        sums[1][:part],
+        cross_kv[:part],
+        cross_kv[part:],
+        sums[1][part:],
+        norm_sums[2],
+        gate_up[:part],
+        gate_up[part:],
+        over_z(left[1], got[1]),
     )
 
 

time: 998 us -> 717 us (0.72)
  waiting for transfers between devices: 303 us -> 16 us
  Pallas kernels: 440 us -> 537 us
  local copies, waits for them, and re-layouts: 124 us -> 57.1 us
  between operations: 15.4 us -> 2.42 us
    unnamed x4 -> x0, waiting for transfers between devices: 147 us -> none
    reduce_scatter x2 -> x0, waiting for transfers between devices: 140 us -> none  [scatter_sum(): lax.psum_scatter(joined.reshape(devices, -1, 128), ALL, scatter_dimension...]
    pallas_call x10 -> x11, Pallas kernels: 417 us -> 477 us  [call(): pl.pallas_call(lambda *refs: kernel(*counts, refs), grid=(PAIRS,), out_sh...]
    reshape x12 -> x0, local copies, waits for them, and re-layouts: 40.3 us -> none  [the longest x8 31.6 us: scatter_sum(): flat = [a.astype(BF).reshape(devices, -1) for a in arrays]]
    pallas_call x1, Pallas kernels: 14 us -> 51.1 us  [reduce_all(): pl.pallas_call(kernel, out_shape=courier.out_shape() + [jax.ShapeDtypeStr...]
    unnamed x113 -> x118, local copies, waits for them, and re-layouts: 37.5 us -> 15.4 us
    unnamed x2 -> x0, other arithmetic: 13.6 us -> none
    concatenate x0 -> x5, other arithmetic: none -> 12 us  [summand_of(): joined = parts[0] if len(parts) == 1 else jnp.concatenate(parts, axis=1)]
  transfers between devices with their start and end apart: 7 -> 4, of which waited for: 4 -> 1; matrix products, arithmetic and copies ran while one was open for 10% -> 0% of each run, Pallas kernels for 1% -> 0%
where the time goes in v3:
time: 717 us; the launch traced here: 711 us
  Pallas kernels  537 us (75%)
  matrix products  57.6 us (8%)
  local copies, waits for them, and re-layouts  57.1 us (8%)
  other arithmetic  34.8 us (5%)
  waiting for transfers between devices  16 us (2%)
    pallas_call x11, Pallas kernels, call(): pl.pallas_call(lambda *refs: kernel(*counts, refs), grid=(PAIRS,), out_sh...  477 us
    dot_general x25, matrix products, dot(): lax.dot_general(left, right, (((left_dim,), (right_dim,)), ((), ())), pre...  57.6 us
    pallas_call x1, Pallas kernels, reduce_all(): pl.pallas_call(kernel, out_shape=courier.out_shape() + [jax.ShapeDtypeStr...  51.1 us
    ppermute x4, waiting for transfers between devices, along_z(): lax.ppermute(value, 'z', [(i, (i + r) % PLANES) for i in range(PLANES)])  16 us
    unnamed x118, local copies, waits for them, and re-layouts  15.4 us
  transfers between devices with their start and end apart: 4, of which 1 were waited for; matrix products, arithmetic and copies ran while one was open for 0% of the time, Pallas kernels for 0%

profile of v3, /device:TPU:0, one launch (start us, length us, event | category | flops | bytes accessed | tf_op | source)
XLA Modules:
  0.0 710.6 jit_solution(14679124586152902378)
XLA Ops:
  2.8 2.4 copy.46
  7.5 2.4 copy.44
  17.6 40.4 %shard_map.305 = (bf16[512,768]{1,0:T(8,128)(2,1)}, f32[6,2,512]{2,1,0:T(2,128)}, bf16[8,256,768]{2,1,0:T(8,128)(2,1)}) custom-call(bf16[512,768]{1,0:T(8,128)(2,1)} %slice.107.refs_0_, bf16[512,1536]{1,0:T(8,128)(2,1)} %slice.108.refs_1_.refs_2_, bf16[32,256,768]{2,1,0:T(8,128)(2,1)} %refs_5_.5), custom_call_target="tpu_custom_call" | custom-call | flops 4294967296 | bytes 16777216 | tf_op jit(solution)/shard_map/pallas_call | solution.py:416
  62.5 3.6 collective-permute-start
  69.0 16.0 %collective-permute-done.3 = s32[1]{0:T(128)} collective-permute-done((s32[1]{0:T(128)}, s32[1]{0:T(128)}, u32[]{:S(2)}, u32[]{:S(2)}) %collective-permute-start.3) | collective-permute-done | bytes 36 | tf_op jit(solution)/shard_map/ppermute | solution.py:802
  88.1 41.0 %shard_map.306 = (bf16[512,768]{1,0:T(8,128)(2,1)}, f32[6,2,512]{2,1,0:T(2,128)}, bf16[2048,1536]{1,0:T(8,128)(2,1)}, bf16[8,256,768]{2,1,0:T(8,128)(2,1)}, bf16[512,768]{1,0:T(8,128)(2,1)}) custom-call(bf16[512,768]{1,0:T(8,128)(2,1)} %collective-permute-done.refs_0_, bf16[2048,768]{1,0:T(8,128)(2,1)} %bitcast.181, ...), custom_call_target="tpu_custom_call" | custom-call | flops 17179869184 | bytes 16777216 | tf_op jit(solution)/shard_map/pallas_call | solution.py:416
  130.3 43.6 %shard_map.307 = (bf16[512,768]{1,0:T(8,128)(2,1)}, f32[6,2,512]{2,1,0:T(2,128)}, bf16[2048,1536]{1,0:T(8,128)(2,1)}, bf16[8,256,768]{2,1,0:T(8,128)(2,1)}, bf16...) custom-call(bf16[512,768]{1,0:T(8,128)(2,1)} %get-tuple-element.85.refs_0_, ...), custom_call_target="tpu_custom_call" | custom-call | flops 17179869184 | bytes 16777216 | tf_op jit(solution)/shard_map/pallas_call | solution.py:416
  175.0 41.7 %shard_map.308 = (bf16[512,768]{1,0:T(8,128)(2,1)}, f32[6,2,512]{2,1,0:T(2,128)}, bf16[2048,1536]{1,0:T(8,128)(2,1)}, bf16[8,256,768]{2,1,0:T(8,128)(2,1)}, bf16...) custom-call(bf16[512,768]{1,0:T(8,128)(2,1)} %get-tuple-element.89.refs_0_, bf16[2048,768]{1,0:T(8,128)(2,1)} %bitcast.185, ...), custom_call_target="tpu_custom_call" | custom-call | flops 17179869184 | bytes 16777216 | tf_op jit(solution)/shard_map/pallas_call | solution.py:416
  217.9 33.0 %shard_map.309 = (bf16[512,768]{1,0:T(8,128)(2,1)}, f32[6,2,512]{2,1,0:T(2,128)}, bf16[2048,1536]{1,0:T(8,128)(2,1)}, bf16[512,768]{1,0:T(8,128)(2,1)}, f32[6,2,512]{2,1,0:T(2,128)}) custom-call(bf16[512,768]{1,0:T(8,128)(2,1)} %convolution_convert_fusion.12.refs_6_.refs_0_, bf16[2048,768]{1,0:T(8,128)(2,1)} %bitcast.187, ...), custom_call_target="tpu_custom_call" | custom-call | flops 17179869184 | bytes 16777216 | tf_op jit(solution)/shard_map/pallas_call | solution.py:416
  254.2 3.0 copy.48
  258.6 3.0 copy.49
  262.9 3.0 copy.50
  267.3 3.1 copy.47
  270.4 4.4 multiply_add_fusion
  278.6 3.9 fusion.15
  282.5 3.6 fusion.30
  286.1 4.8 multiply_convert_fusion
  292.8 3.5 convolution_convert_fusion.2
  296.3 3.5 convolution_convert_fusion.1
  299.8 2.6 multiply_reduce_fusion
  308.0 3.9 copy.52
  311.9 5.4 convolution_convert_fusion.3
  317.3 3.8 pad_maximum_fusion.refs_10_
  321.7 52.1 %shard_map.310 = (bf16[2048,1536]{1,0:T(8,128)(2,1)}, bf16[512,768]{1,0:T(8,128)(2,1)}, bf16[2048,768]{1,0:T(8,128)(2,1)}, bf16[512,768]{1,0:T(8,128)(2,1)}, f32...) custom-call(bf16[512,768]{1,0:T(8,128)(2,1)} %convolution_convert_fusion.12.refs_6_.refs_0_, ...), custom_call_target="tpu_custom_call" | custom-call | flops 34359738368 | bytes 16777216 | tf_op jit(solution)/shard_map/pallas_call | solution.py:416
  375.2 64.0 %shard_map.311 = (bf16[2048,1536]{1,0:T(8,128)(2,1)}, bf16[512,768]{1,0:T(8,128)(2,1)}, bf16[2048,768]{1,0:T(8,128)(2,1)}, bf16[512,768]{1,0:T(8,128)(2,1)}, f32...) custom-call(bf16[512,768]{1,0:T(8,128)(2,1)} %collective-permute-don, ...), custom_call_target="tpu_custom_call" | custom-call | flops 34359738368 | bytes 16777216 | tf_op jit(solution)/shard_map/pallas_call | solution.py:416
  440.6 50.5 %shard_map.312 = (bf16[2048,1536]{1,0:T(8,128)(2,1)}, bf16[512,768]{1,0:T(8,128)(2,1)}, bf16[2048,768]{1,0:T(8,128)(2,1)}, bf16[512,768]{1,0:T(8,128)(2,1)}, f32...) custom-call(bf16[512,768]{1,0:T(8,128)(2,1)} %get-tuple-element.85.r, ...), custom_call_target="tpu_custom_call" | custom-call | flops 34359738368 | bytes 16777216 | tf_op jit(solution)/shard_map/pallas_call | solution.py:416
  492.5 42.7 %shard_map.313 = (bf16[2048,1536]{1,0:T(8,128)(2,1)}, bf16[512,768]{1,0:T(8,128)(2,1)}, bf16[2048,768]{1,0:T(8,128)(2,1)}, bf16[8,256,768]{2,1,0:T(8,128)(2,1)}, bf16[512,768]{1,0:T(8,128)(2,1)}) custom-call(bf16[512,768]{1,0:T(8,128)(2,1)} %get-tuple-element.89.refs_0_, bf16[512,768]{1,0:T(8,128)(2,1)} %get-tuple-element.118.refs_1_, ...), custom_call_target="tpu_custom_call" | custom-call | flops 34359738368 | bytes 16777216 | tf_op jit(solution)/shard_map/pallas_call | solution.py:416
  535.2 44.7 %shard_map.314 = (f32[768,768]{1,0:T(8,128)}, f32[768,768]{1,0:T(8,128)}, bf16[512,768]{1,0:T(8,128)(2,1)}, bf16[8,256,768]{2,1,0:T(8,128)(2,1)}) custom-call(bf16[2048,768]{1,0:T(8,128)(2,1)} %bitcast.188, bf16[2048,768]{1,0:T(8,128)(2,1)} %bitcast.182, bf16[2048,768]{1,0:T(8,128)(2,1)} %bitcast.184, bf16[2048,768]{1,0:T(8,128)(2,1)} %bitcast.186, ...), custom_call_target="tpu_custom_call" | custom-call | flops 17179869184 | bytes 16777216 | tf_op jit(solution)/shard_map/pallas_call | solution.py:416
  593.1 22.9 %shard_map.315 = (bf16[512,768]{1,0:T(8,128)(2,1)}, bf16[512,768]{1,0:T(8,128)(2,1)}, bf16[512,768]{1,0:T(8,128)(2,1)}, bf16[4,48,768]{2,1,0:T(8,128)(2,1)}) custom-call(bf16[512,768]{1,0:T(8,128)(2,1)} %slice.107.refs_0_, bf16[512,768]{1,0:T(8,128)(2,1)} %convolution_convert_fusion.10.refs_1_, bf16[512,1536]{1,0:T(8,128)(2,1)} %slice.108.refs_1_.refs_2_, ...), custom_call_target="tpu_custom_call" | custom-call | flops 8589934592 | bytes 16777216 | tf_op jit(solution)/shard_map/pallas_call | solution.py:416
  633.6 3.1 pad_maximum_fusion.3.refs_2_
  641.5 51.1 %shard_map.317 = (bf16[3,48,768]{2,1,0:T(8,128)(2,1)}, f32[16,256]{1,0:T(8,128)}, f32[48,768]{1,0:T(8,128)}, f32[48,768]{1,0:T(8,128)}, f32[48,768]{1,0:T(8,128)}) custom-call(bf16[4,48,768]{2,1,0:T(8,128)(2,1)} %get-tuple-element.141.refs_0_, bf16[4,2,2,2,16,256]{5,4,3,2,1,0:T(8,128)(2,1)} %bitcast.165, ...), custom_call_target="tpu_custom_call" | custom-call | tf_op jit(solution)/shard_map/pallas_call | solution.py:494
  700.4 9.2 %shard_map.316 = bf16[32,256,768]{2,1,0:T(8,128)(2,1)} custom-call(bf16[8,256,768]{2,1,0:T(8,128)(2,1)} %get-tuple-element.137.refs_0_, bf16[8,256,768]{2,1,0:T(8,128)(2,1)} %get-tuple-element.138.refs_1_, bf16[8,256,768]{2,1,0:T(8,128)(2,1)} %get-tuple-element.139.refs_2_, bf16[8,256,768]{2,1,0:T(8,128)(2,1)} %get-tuple-element.140.refs_3_), custom_call_target="tpu_custom_call" | custom-call | tf_op jit(solution)/shard_map/pallas_call | solution.py:717
  (208 shorter events, 92.1 us)
Async XLA Ops:
  0.7 278.0 %copy-start = (bf16[768,2048]{1,0:T(8,128)(2,1)S(1)}, bf16[768,2048]{1,0:T(8,128)(2,1)}, u32[]{:S(2)}) copy-start(bf16[768,2048]{1,0:T(8,128)(2,1)} %param.34) | copy-start | bytes 9437188
  2.8 9.2 %copy-start.36 = (f32[512]{0:T(512)}, f32[512]{0:T(512)S(1)}, u32[]{:S(2)}) copy-start(f32[512]{0:T(512)S(1)} %get-tuple-element.185) | copy-start | bytes 6148
  17.6 40.4 %copy-start.52 = (bf16[768,768]{1,0:T(8,128)(2,1)S(1)}, bf16[768,768]{1,0:T(8,128)(2,1)}, u32[]{:S(2)}) copy-start(bf16[768,768]{1,0:T(8,128)(2,1)} %param.26) | copy-start | bytes 3538948
  58.0 2.8 copy-start.45
  58.0 2.8 copy-start.50
  60.1 2.4 copy-start.6
  62.5 24.5 %collective-permute-start = (bf16[512,768]{1,0:T(8,128)(2,1)}, bf16[512,768]{1,0:T(8,128)(2,1)}, u32[]{:S(2)}, u32[]{:S(2)}) collective-permute-start(bf16[512,768]{1,0:T(8,128)(2,1)} %convolution_convert_fusion.12.refs_6_.refs_0_), channel_id=1, source_target_pairs={{0,24},{8,0},{16,8},{24,16},{1,25},{9,1},{17,9},{25,17},{2,26},{10... | collective-permute-start | bytes 2359304 | tf_op jit(solution)/shard_map/ppermute | solution.py:802
  66.1 19.6 %collective-permute-start.2 = (s32[1]{0:T(128)}, s32[1]{0:T(128)}, u32[]{:S(2)}, u32[]{:S(2)}) collective-permute-start(s32[1]{0:T(128)} %param.20), channel_id=1, source_target_pairs={{0,16},{8,24},{16,0},{24,8},{1,17},{9,25},{17,1},{25,9},{2,18},{10... | collective-permute-start | bytes 20 | tf_op jit(solution)/shard_map/ppermute | solution.py:802
  66.1 19.6 %collective-permute-start.1 = (s32[1]{0:T(128)}, s32[1]{0:T(128)}, u32[]{:S(2)}, u32[]{:S(2)}) collective-permute-start(s32[1]{0:T(128)} %param.20), channel_id=1, source_target_pairs={{0,24},{8,0},{16,8},{24,16},{1,25},{9,1},{17,9},{25,17},{2,26},{10... | collective-permute-start | bytes 20 | tf_op jit(solution)/shard_map/ppermute | solution.py:802
  66.9 18.1 %collective-permute-start.3 = (s32[1]{0:T(128)}, s32[1]{0:T(128)}, u32[]{:S(2)}, u32[]{:S(2)}) collective-permute-start(s32[1]{0:T(128)} %param.20), channel_id=1, source_target_pairs={{0,8},{8,16},{16,24},{24,0},{1,9},{9,17},{17,25},{25,1},{2,10},{10... | collective-permute-start | bytes 20 | tf_op jit(solution)/shard_map/ppermute | solution.py:802
  217.9 33.1 %copy-start.34 = (f32[6,2,512]{2,1,0:T(2,128)S(1)}, f32[6,2,512]{2,1,0:T(2,128)}, u32[]{:S(2)}) copy-start(f32[6,2,512]{2,1,0:T(2,128)} %get-tuple-element.97) | copy-start | bytes 73732
  217.9 33.1 %copy-start.35 = (f32[6,2,512]{2,1,0:T(2,128)S(1)}, f32[6,2,512]{2,1,0:T(2,128)}, u32[]{:S(2)}) copy-start(f32[6,2,512]{2,1,0:T(2,128)} %get-tuple-element.98) | copy-start | bytes 73732
  252.7 68.4 %copy-start.33 = (f32[6,2,512]{2,1,0:T(2,128)}, f32[6,2,512]{2,1,0:T(2,128)S(1)}, u32[]{:S(2)}) copy-start(f32[6,2,512]{2,1,0:T(2,128)S(1)} %log_add_fusion.refs_4_) | copy-start | bytes 73732
  270.4 4.4 copy-start.7
  270.4 4.5 copy-start.10
  278.6 3.9 copy-start.48
  282.5 3.6 copy-start.23
  311.9 5.4 copy-start.13
  311.9 5.4 copy-start.14
  535.2 44.7 %copy-start.27 = (bf16[512,768]{1,0:T(8,128)(2,1)S(1)}, bf16[512,768]{1,0:T(8,128)(2,1)}, u32[]{:S(2)}) copy-start(bf16[512,768]{1,0:T(8,128)(2,1)} %get-tuple-element.105) | copy-start | bytes 2359300
  535.2 44.7 %copy-start.28 = (bf16[512,768]{1,0:T(8,128)(2,1)S(1)}, bf16[512,768]{1,0:T(8,128)(2,1)}, u32[]{:S(2)}) copy-start(bf16[512,768]{1,0:T(8,128)(2,1)} %get-tuple-element.117) | copy-start | bytes 2359300
  535.2 44.7 %copy-start.29 = (bf16[512,768]{1,0:T(8,128)(2,1)S(1)}, bf16[512,768]{1,0:T(8,128)(2,1)}, u32[]{:S(2)}) copy-start(bf16[512,768]{1,0:T(8,128)(2,1)} %get-tuple-element.123) | copy-start | bytes 2359300
  593.1 22.9 %copy-start.17 = (bf16[768,768]{1,0:T(8,128)(2,1)S(1)}, bf16[768,768]{1,0:T(8,128)(2,1)}, u32[]{:S(2)}) copy-start(bf16[768,768]{1,0:T(8,128)(2,1)} %param.23) | copy-start | bytes 3538948
  616.0 2.1 copy-start.18
  616.0 2.1 copy-start.55
  629.5 2.0 copy-start.31
  629.7 3.9 copy-start.12
  633.6 3.8 copy-start.11
  633.6 3.8 copy-start.20
  637.4 2.5 copy-start.22
  692.7 7.1 %copy-start.32 = (f32[48,768]{1,0:T(8,128)S(1)}, f32[48,768]{1,0:T(8,128)}, u32[]{:S(2)}) copy-start(f32[48,768]{1,0:T(8,128)} %get-tuple-element.145) | copy-start | bytes 442372
  700.4 9.9 %copy-start.1 = (bf16[768,2048]{1,0:T(8,128)(2,1)S(1)}, bf16[768,2048]{1,0:T(8,128)(2,1)}, u32[]{:S(2)}) copy-start(bf16[768,2048]{1,0:T(8,128)(2,1)} %param.34) | copy-start | bytes 9437188
  (29 other events, 46.0 us)

commit v4 on v3

--- a/solution.py
+++ b/solution.py
@@ -350,6 +350,11 @@
     return grad_kv, jnp.concatenate(grad_q, axis=0).T.astype(BF)
 
 
+def key_bias(keys, lens_ref):
+    row = lax.broadcasted_iota(jnp.int32, (keys, 128), 0) + lax.axis_index("z") * keys
+    return jnp.where(row < lens_ref[0:1, :], 0.0, MASKED).astype(BF)
+
+
 def two_rows(ref):
     return [ref[0, h : h + 1, :] for h in range(2)]
 
@@ -518,21 +523,244 @@
     return dict(
         col=pl.BlockSpec((tokens, 128), lambda p: (0, p)),
         pair=pl.BlockSpec((keys, 256), lambda p: (0, p)),
-        bias=pl.BlockSpec((keys, 128), lambda p: (0, 0)),
+        lens=pl.BlockSpec((8, 128), lambda p: (0, 0)),
         rows=pl.BlockSpec((keys, H * HD), lambda p: (0, 0)),
         weight=pl.BlockSpec((H * HD, 128), lambda p: (0, p)),
         stat=pl.BlockSpec((1, 2, tokens), lambda p: (p, 0, 0)),
     )
 
 
-def self_forward(courier, ident, queries, keyvals):
-    tokens = queries.shape[0]
-    spec = block_specs(tokens, tokens)
+def rms(values, gain):
+    r = lax.rsqrt(jnp.mean(values * values, axis=-1, keepdims=True) + EPSILON)
+    return values * r * gain
+
+
+def self_part(courier, ident, inputs, gains, weights):
+    tokens, width = inputs.shape
+    jobs = len(courier.jobs)
+
+    def kernel(*refs):
+        ins, sources, outs, targets, sems = split_refs(refs, 8, jobs - 1, 7, jobs, 3)
+        x_ref, self_gain, cross_gain, wq_ref, wk_ref, wv_ref, wo_ref, wc_ref = ins
+        q_ref, k_ref, v_ref, lse_ref, attn_ref, hidden_ref, query_ref = outs
+        copies = courier.copies(list(sources) + [query_ref], targets, sems)
+        courier.greet()
+        for copy in copies[:-1]:
+            copy.start()
+        values = x_ref[...].astype(F32)
+        normed = rms(values, self_gain[...]).astype(BF)
+        q_ref[...] = dot(normed, wq_ref[...], 1, 0).astype(BF)
+        k_ref[...] = dot(normed, wk_ref[...], 1, 0).astype(BF)
+        v_ref[...] = dot(normed, wv_ref[...], 1, 0).astype(BF)
+
+        for p in range(PAIRS):
+            cols = pl.ds(p * 128, 128)
+            out, lse = forward_pair(q_ref[:, cols], k_ref[:, cols], v_ref[:, cols], None)
+            attn_ref[:, cols] = out
+            for h in range(2):
+                lse_ref[p, h : h + 1, :] = lse[h]
+
+        hidden = values + dot(attn_ref[...], wo_ref[...], 1, 0)
+        hidden_ref[...] = hidden
+        query_ref[...] = dot(rms(hidden, cross_gain[...]).astype(BF), wc_ref[...], 1, 0).astype(BF)
+        copies[-1].start()
+        for copy in copies:
+            copy.wait()
+
+    rows = jax.ShapeDtypeStruct((tokens, width), BF)
+    vmem = pl.BlockSpec(memory_space=pltpu.VMEM)
+    stat = jax.ShapeDtypeStruct((PAIRS, 2, tokens), F32)
+    wide = jax.ShapeDtypeStruct((tokens, width), F32)
+    outs = pl.pallas_call(
+        kernel,
+        out_shape=[rows, rows, rows, stat, rows, wide, rows] + courier.out_shape(),
+        in_specs=[vmem] * 8 + courier.specs()[1:],
+        out_specs=[vmem] * 7 + courier.specs(),
+        scratch_shapes=courier.scratch(),
+        compiler_params=courier.params(ident),
+    )(inputs, *gains, *weights, *courier.values()[:-1])
+    return outs[:7], outs[7:]
+
+
+def glu_parts(gate_vals):
+    inner = 0.7978845608028654 * (gate_vals + 0.044715 * gate_vals * gate_vals * gate_vals)
+    t = jnp.tanh(inner)
+    gelu = 0.5 * gate_vals * (1.0 + t)
+    slope = 0.5 * (1.0 + t) + 0.5 * gate_vals * (1.0 - t * t) * 0.7978845608028654 * (
+        1.0 + 0.134145 * gate_vals * gate_vals
+    )
+    return gelu, slope
+
+
+def spread(rows):
+    both = [jnp.broadcast_to(rows[h : h + 1], (HD, rows.shape[1])) for h in range(2)]
+    return jnp.concatenate(both, axis=0).T
+
+
+def middle_kernel(*refs, devices, packed):
+    (
+        part0,
+        part1,
+        part2,
+        part3,
+        lse0,
+        lse1,
+        lse2,
+        lse3,
+        h1_ref,
+        wo_ref,
+        gain_ref,
+        cot_ref,
+        gate_ref,
+        up_ref,
+        down_ref,
+        out_ref,
+        attn_ref,
+        two_ref,
+        da_ref,
+        stats_ref,
+        gnorm_ref,
+        gwo_ref,
+        *grad_refs,
+        gdown_ref,
+        raw_ref,
+        h2_ref,
+        n3_ref,
+        total_ref,
+        dn3_ref,
+    ) = refs
+    step = pl.program_id(0)
+    parts = (part0, part1, part2, part3)
+    lses = (lse0, lse1, lse2, lse3)
+
+    @pl.when(step == 0)
+    def _():
+        for p in range(PAIRS):
+            cols = pl.ds(p * 128, 128)
+            values = [ref[p] for ref in lses]
+            top = functools.reduce(jnp.maximum, values)
+            scales = [jnp.exp(v - top) for v in values]
+            total = functools.reduce(jnp.add, scales)
+            stats_ref[0, p] = top + jnp.log(total)
+            raw = None
+            for ref, scale in zip(parts, scales):
+                term = spread(scale / total) * ref[:, cols].astype(F32)
+                raw = term if raw is None else raw + term
+            raw_ref[:, cols] = raw
+            attn_ref[:, cols] = raw.astype(BF)
+        hidden = h1_ref[...] + dot(attn_ref[...], wo_ref[...], 1, 0)
+        h2_ref[...] = hidden
+        n3_ref[...] = rms(hidden, gain_ref[...]).astype(BF)
+        total_ref[...] = hidden
+        dn3_ref[...] = jnp.zeros_like(dn3_ref)
+
+    normed = n3_ref[...]
+    branch = cot_ref[...]
+    gate_vals = dot(normed, gate_ref[...], 1, 0)
+    up_vals = dot(normed, up_ref[...], 1, 0)
+    grad_inner = dot(branch, down_ref[...], 1, 1)
+    gelu, slope = glu_parts(gate_vals)
+    inner = (gelu * up_vals).astype(BF)
+    grad_gate = (grad_inner * up_vals * slope).astype(BF)
+    grad_up = (grad_inner * gelu).astype(BF)
+    total_ref[...] += dot(inner, down_ref[...], 1, 0)
+    dn3_ref[...] += dot(grad_gate, gate_ref[...], 1, 1) + dot(grad_up, up_ref[...], 1, 1)
+    terms = [dot(normed, grad_gate, 0, 0), dot(normed, grad_up, 0, 0)]
+    if packed:
+        shape = (devices, terms[0].shape[0] // devices, terms[0].shape[1])
+        grad_refs[0][...] = jnp.concatenate([t.reshape(shape) for t in terms], axis=1).astype(BF)
+    else:
+        for ref, term in zip(grad_refs, terms):
+            ref[...] = term
+    gdown_ref[...] = dot(inner, branch, 0, 0).astype(BF).reshape(gdown_ref.shape)
+
+    @pl.when(step == pl.num_programs(0) - 1)
+    def _():
+        out_ref[...] = total_ref[...].astype(BF)
+        hidden = h2_ref[...]
+        grad = dn3_ref[...]
+        r = lax.rsqrt(jnp.mean(hidden * hidden, axis=-1, keepdims=True) + EPSILON)
+        u = gain_ref[...] * grad
+        back = r * u - hidden * (r * r * r) * jnp.mean(u * hidden, axis=-1, keepdims=True)
+        gnorm_ref[...] = jnp.sum(grad * hidden * r, axis=0, keepdims=True)
+        two = cot_ref[...].astype(F32) + back
+        two_ref[...] = two
+        low = two.astype(BF)
+        da_ref[...] = dot(low, wo_ref[...], 1, 1).astype(BF)
+        gwo_ref[...] = dot(attn_ref[...], low, 0, 0)
+        for p in range(PAIRS):
+            cols = pl.ds(p * 128, 128)
+            product = (da_ref[:, cols].astype(F32) * raw_ref[:, cols]).T
+            for h in range(2):
+                stats_ref[1, p, h : h + 1] = jnp.sum(
+                    product[h * HD : (h + 1) * HD], axis=0, keepdims=True
+                )
+
+
+def middle(devices, parts, lses, hidden, out_weight, gain, cotangent, gate, up, down):
+    tokens, width = hidden.shape
+    inner = gate.shape[1]
+    chunk = 512
+    share = width // devices
+    packed = share % 8 == 0
+    down_share = inner // devices
+    fixed = lambda *shape: pl.BlockSpec(shape, lambda p: (0,) * len(shape))
+    whole = fixed(tokens, width)
+    square = fixed(width, width)
+    stat = fixed(PAIRS, 2, tokens)
+    column = pl.BlockSpec((width, chunk), lambda p: (0, p))
+    if packed:
+        grad_shapes = [jax.ShapeDtypeStruct((devices, 2 * share, inner), BF)]
+        grad_specs = [pl.BlockSpec((devices, 2 * share, chunk), lambda p: (0, 0, p))]
+    else:
+        grad_shapes = [jax.ShapeDtypeStruct((width, inner), F32)] * 2
+        grad_specs = [column] * 2
+    rows = jax.ShapeDtypeStruct((tokens, width), BF)
+    wide = jax.ShapeDtypeStruct((tokens, width), F32)
+    return pl.pallas_call(
+        functools.partial(middle_kernel, devices=devices, packed=packed),
+        grid=(inner // chunk,),
+        out_shape=[
+            rows,
+            rows,
+            wide,
+            rows,
+            jax.ShapeDtypeStruct((2, PAIRS, 2, tokens), F32),
+            jax.ShapeDtypeStruct((1, width), F32),
+            jax.ShapeDtypeStruct((width, width), F32),
+        ]
+        + grad_shapes
+        + [jax.ShapeDtypeStruct((devices, down_share, width), BF)],
+        in_specs=[whole] * 4
+        + [stat] * 4
+        + [whole, square, fixed(1, width), whole]
+        + [column, column, pl.BlockSpec((chunk, width), lambda p: (p, 0))],
+        out_specs=[whole] * 4
+        + [fixed(2, PAIRS, 2, tokens), fixed(1, width), square]
+        + grad_specs
+        + [pl.BlockSpec((chunk // down_share, down_share, width), lambda p: (p, 0, 0))],
+        scratch_shapes=[
+            pltpu.VMEM((tokens, width), F32),
+            pltpu.VMEM((tokens, width), F32),
+            pltpu.VMEM((tokens, width), BF),
+            pltpu.VMEM((tokens, width), F32),
+            pltpu.VMEM((tokens, width), F32),
+        ],
+        compiler_params=pltpu.CompilerParams(vmem_limit_bytes=VMEM),
+    )(*parts, *lses, hidden, out_weight, gain, cotangent, gate, up, down)
+
+
+def cross_forward(courier, ident, queries, rows, lens, key_weight, value_weight):
+    tokens, keys = queries.shape[0], rows.shape[0]
+    spec = block_specs(tokens, keys)
 
     def body(ins, outs, _):
-        q_ref, kv_ref = ins
-        o_ref, lse_ref = outs
-        out, lse = forward_pair(q_ref[...], kv_ref[:, :128], kv_ref[:, 128:], None)
+        q_ref, rows_ref, lens_ref, wk_ref, wv_ref = ins
+        o_ref, lse_ref, kv_ref = outs
+        weights = jnp.concatenate([wk_ref[...], wv_ref[...]], axis=1)
+        kv_ref[...] = dot(rows_ref[...], weights, 1, 0).astype(BF)
+        bias = key_bias(keys, lens_ref)
+        out, lse = forward_pair(q_ref[...], kv_ref[:, :128], kv_ref[:, 128:], bias)
         o_ref[...] = out
         for h in range(2):
             lse_ref[0, h : h + 1, :] = lse[h]
@@ -541,38 +769,8 @@
         courier,
         ident,
         body,
-        [queries, keyvals],
-        [spec["col"], spec["pair"]],
-        [
-            jax.ShapeDtypeStruct((tokens, H * HD), BF),
-            jax.ShapeDtypeStruct((PAIRS, 2, tokens), F32),
-        ],
-        [spec["col"], spec["stat"]],
-        [],
-        2**32,
-    )
-
-
-def cross_forward(courier, ident, queries, rows, bias, key_weight, value_weight):
-    tokens, keys = queries.shape[0], rows.shape[0]
-    spec = block_specs(tokens, keys)
-
-    def body(ins, outs, _):
-        q_ref, rows_ref, bias_ref, wk_ref, wv_ref = ins
-        o_ref, lse_ref, kv_ref = outs
-        weights = jnp.concatenate([wk_ref[...], wv_ref[...]], axis=1)
-        kv_ref[...] = dot(rows_ref[...], weights, 1, 0).astype(BF)
-        out, lse = forward_pair(q_ref[...], kv_ref[:, :128], kv_ref[:, 128:], bias_ref[...])
-        o_ref[...] = out
-        for h in range(2):
-            lse_ref[0, h : h + 1, :] = lse[h]
-
-    return call(
-        courier,
-        ident,
-        body,
-        [queries, rows, bias, key_weight, value_weight],
-        [spec["col"], spec["rows"], spec["bias"], spec["weight"], spec["weight"]],
+        [queries, rows, lens, key_weight, value_weight],
+        [spec["col"], spec["rows"], spec["lens"], spec["weight"], spec["weight"]],
         [
             jax.ShapeDtypeStruct((tokens, H * HD), BF),
             jax.ShapeDtypeStruct((PAIRS, 2, tokens), F32),
@@ -585,14 +783,14 @@
 
 
 def cross_backward(
-    courier, ident, queries, grad, keyvals, bias, lse, delta, key_weight, value_weight, summand=None
+    courier, ident, queries, grad, keyvals, lens, lse, delta, key_weight, value_weight, summand=None
 ):
     tokens, keys = queries.shape[0], keyvals.shape[0]
     width = H * HD
     spec = block_specs(tokens, keys)
 
     def body(ins, outs, scratch):
-        q_ref, da_ref, kv_ref, bias_ref, lse_ref, delta_ref, wk_ref, wv_ref = ins
+        q_ref, da_ref, kv_ref, lens_ref, lse_ref, delta_ref, wk_ref, wv_ref = ins
         dkv_ref, dq_ref, dm_ref = outs
         (total_ref,) = scratch
         step = pl.program_id(0)
@@ -607,7 +805,7 @@
             da_ref[...],
             kv_ref[:, :128],
             kv_ref[:, 128:],
-            bias_ref[...],
+            key_bias(keys, lens_ref),
             two_rows(lse_ref),
             two_rows(delta_ref),
         )
@@ -623,8 +821,8 @@
         courier,
         ident,
         body,
-        [queries, grad, keyvals, bias, lse, delta, key_weight, value_weight],
-        [spec[n] for n in ("col", "col", "pair", "bias", "stat", "stat", "weight", "weight")],
+        [queries, grad, keyvals, lens, lse, delta, key_weight, value_weight],
+        [spec[n] for n in ("col", "col", "pair", "lens", "stat", "stat", "weight", "weight")],
         [
             jax.ShapeDtypeStruct((keys, 2 * width), BF),
             jax.ShapeDtypeStruct((tokens, width), BF),
@@ -663,15 +861,15 @@
     )
 
 
-def self_backward(courier, ident, queries, grad, keyvals, lse, summand):
+def self_backward(courier, ident, queries, grad, keys, values, lse, summand):
     tokens, width = queries.shape
     spec = block_specs(tokens, tokens)
 
     def body(ins, outs, _):
-        q_ref, da_ref, kv_ref, lse_ref = ins
+        q_ref, da_ref, k_ref, v_ref, lse_ref = ins
         dq_ref, dk_ref, dv_ref = outs
         grad_kv, dq_ref[...] = backward_pair(
-            q_ref[...], da_ref[...], kv_ref[:, :128], kv_ref[:, 128:], None, two_rows(lse_ref), None
+            q_ref[...], da_ref[...], k_ref[...], v_ref[...], None, two_rows(lse_ref), None
         )
         dk_ref[...] = grad_kv[:, :128]
         dv_ref[...] = grad_kv[:, 128:]
@@ -680,8 +878,8 @@
         courier,
         ident,
         body,
-        [queries, grad, keyvals, lse],
-        [spec["col"], spec["col"], spec["pair"], spec["stat"]],
+        [queries, grad, keys, values, lse],
+        [spec["col"]] * 4 + [spec["stat"]],
         [jax.ShapeDtypeStruct((tokens, width), BF)] * 3,
         [spec["col"]] * 3,
         [],
@@ -728,24 +926,6 @@
     )(*blocks)
 
 
-def interleave(keys, values):
-    width = keys.shape[0]
-    return jnp.stack(
-        [keys.reshape(width, PAIRS, 128), values.reshape(width, PAIRS, 128)], axis=2
-    ).reshape(width, 2 * H * HD)
-
-
-def separate(both):
-    rows = both.shape[0]
-    parts = both.reshape(rows, PAIRS, 2, 128)
-    return parts[:, :, 0].reshape(rows, H * HD), parts[:, :, 1].reshape(rows, H * HD)
-
-
-def per_row(stat):
-    tokens = stat.shape[-1]
-    return jnp.repeat(stat.reshape(H, tokens).T, HD, axis=1)
-
-
 def norm_apply(values, gain):
     return values * lax.rsqrt(jnp.mean(values * values, axis=-1, keepdims=True) + EPSILON) * gain
 
@@ -755,10 +935,6 @@
     u = gain * grad
     dv = r * u - values * (r * r * r) * jnp.mean(u * values, axis=-1, keepdims=True)
     return dv, jnp.sum(grad * values * r, axis=0)
-
-
-def glu_apply(gate_vals, up_vals):
-    return jax.nn.gelu(gate_vals, approximate=True) * up_vals
 
 
 def matmul(left, right):
@@ -798,37 +974,28 @@
     plane_size = sizes[1] * sizes[2] * sizes[3]
     z = lax.axis_index("z")
 
-    def along_z(value, r):
-        return lax.ppermute(value, "z", [(i, (i + r) % PLANES) for i in range(PLANES)])
-
     def flat(blocks):
         return blocks.reshape(plane_size * positions, width)
 
     def cut(rows):
         return rows.reshape(plane_size, positions, width)
 
-    span = plane_size * positions
-    places = z * span + jnp.arange(span, dtype=jnp.int32)
-
     inputs = decoder_in[0].astype(F32)
+    lens = {0: jnp.broadcast_to(memory_lengths[None, :], (8, 128))}
+    jobs = [("fetch", 1, memory)]
+    jobs += [("line", -r, lens[0]) for r in range(1, PLANES)]
+    jobs += [("line", -1, jax.ShapeDtypeStruct(decoder_in.shape[1:], BF))]
+    (query_one, key_one, value_one, lse_one, attn_one, hidden_one, query_two), moved = self_part(
+        Courier(sizes, jobs),
+        0,
+        decoder_in[0],
+        (norm_self[None], norm_cross[None]),
+        (self_query, self_key, self_value, self_out, cross_query),
+    )
+    fetched, lens[1], lens[2], lens[3], query_near = moved
     normed_one = norm_apply(inputs, norm_self).astype(BF)
-    self_weights = jnp.concatenate([self_query, interleave(self_key, self_value)], axis=1)
-    qkv_one = matmul(normed_one, self_weights).astype(BF)
-    query_one, keyval_one = qkv_one[:, :width], qkv_one[:, width:]
-    (attn_one, lse_one), (fetched,) = self_forward(
-        Courier(sizes, [("fetch", 1, memory)]), 0, query_one, keyval_one
-    )
-    hidden_one = inputs + matmul(attn_one, self_out)
     normed_two = norm_apply(hidden_one, norm_cross).astype(BF)
-    query_two = matmul(normed_two, cross_query).astype(BF)
-
-    queries, rows, keyvals, biases, partial, stats_out = {}, {}, {}, {}, {}, {}
-    for r in range(PLANES):
-        limit = memory_lengths if r == 0 else along_z(memory_lengths, -r)
-        bias = jnp.where(places < limit, 0.0, MASKED).astype(BF)
-        biases[r] = jnp.broadcast_to(bias[:, None], (bias.shape[0], 128))
-    queries[0] = query_two
-    queries[1] = along_z(query_two, -1)
+    queries, rows, keyvals, partial, stats_out = {0: query_two, 1: query_near}, {}, {}, {}, {}
     order = (1, 2, 3, 0)
     for at, r in enumerate(order):
         rows[r] = flat(fetched)
@@ -842,7 +1009,7 @@
             jobs.append(("line", before, partial[before]))
             jobs.append(("line", before, stats_out[before]))
         (partial[r], stats_out[r], keyvals[r]), moved = cross_forward(
-            Courier(sizes, jobs), 1 + at, queries[r], rows[r], biases[r], cross_key, cross_value
+            Courier(sizes, jobs), 1 + at, queries[r], rows[r], lens[r], cross_key, cross_value
         )
         moved = list(moved)
         if at + 1 < PLANES:
@@ -851,46 +1018,36 @@
             queries[order[at + 1]] = moved.pop(0)
         if at >= 1:
             partial[before], stats_out[before] = moved
-    lses = jnp.stack([stats_out[r] for r in range(PLANES)])
-    top = jnp.max(lses, axis=0)
-    scale = jnp.exp(lses - top)
-    total = jnp.sum(scale, axis=0)
-    lse_two = top + jnp.log(total)
-    share = scale / total
-    attn_raw_two = sum(per_row(share[r]) * partial[r].astype(F32) for r in range(PLANES))
-    attn_two = attn_raw_two.astype(BF)
-    hidden_two = hidden_one + matmul(attn_two, cross_out)
-
-    normed_three = norm_apply(hidden_two, norm_ffn).astype(BF)
-    gate_vals = matmul(normed_three, ffn_gate)
-    up_vals = matmul(normed_three, ffn_up)
-    inner = glu_apply(gate_vals, up_vals).astype(BF)
-    output = hidden_two + matmul(inner, ffn_down)
-    decoder_out = output.astype(BF)[None]
-
-    branch_three = cotangent[0]
-    grad_out = branch_three.astype(F32)
-    grad_inner = matmul_t(branch_three, ffn_down)
-    _, glu_pull = jax.vjp(glu_apply, gate_vals, up_vals)
-    grad_gate_raw, grad_up_raw = glu_pull(grad_inner)
-    grad_gate_low = grad_gate_raw.astype(BF)
-    grad_up_low = grad_up_raw.astype(BF)
-    grad_normed_three = matmul_t(grad_gate_low, ffn_gate) + matmul_t(grad_up_low, ffn_up)
-    back_two, grad_norm_ffn = norm_back(hidden_two, norm_ffn, grad_normed_three)
-    grad_two = grad_out + back_two
-    branch_two = grad_two.astype(BF)
-    grad_attn_two = matmul_t(branch_two, cross_out).astype(BF)
-    products = grad_attn_two.astype(F32) * attn_raw_two
-    delta_two = jnp.sum(products.reshape(-1, H, HD), axis=-1).T.reshape(PAIRS, 2, -1)
-
-    grad_down = tmatmul(inner, branch_three)
-    grad_gate = tmatmul(normed_three, grad_gate_low)
-    grad_up = tmatmul(normed_three, grad_up_low)
-    grad_cross_out = tmatmul(attn_two, branch_two)
-    summands = {0: summand_of(sizes, (grad_gate, grad_up)), 1: summand_of(sizes, (grad_down,))}
+    (
+        output,
+        attn_two,
+        grad_two,
+        grad_attn_two,
+        stats,
+        grad_norm_ffn,
+        grad_cross_out,
+        *grads_in,
+        grad_down,
+    ) = middle(
+        devices,
+        [partial[r] for r in range(PLANES)],
+        [stats_out[r] for r in range(PLANES)],
+        hidden_one,
+        cross_out,
+        norm_ffn[None],
+        cotangent[0],
+        ffn_gate,
+        ffn_up,
+        ffn_down,
+    )
+    decoder_out = output[None]
+    if len(grads_in) == 2:
+        summand = summand_of(sizes, grads_in)
+    else:
+        summand = grads_in[0].reshape(tuple(sizes) + grads_in[0].shape[1:])
+    summands = {0: summand, 1: grad_down.reshape(tuple(sizes) + grad_down.shape[1:])}
     left, got = {}, {}
 
-    stats = jnp.stack([lse_two, delta_two])
     grads = {0: grad_attn_two}
     both = {0: stats}
     grad_kv, grad_q, grad_rows, returned = {}, {}, {}, {}
@@ -903,15 +1060,13 @@
             jobs.append(("return", 0, cut(grad_rows[r - 1])))
         if r >= 2:
             jobs.append(("line", r - 1, grad_q[r - 1]))
-        if r - 1 in left:
-            jobs.append(("scatter", 0, left[r - 1]))
         (grad_kv[r], grad_q[r], grad_rows[r]), moved = cross_backward(
             Courier(sizes, jobs),
             5 + r,
             queries[r],
             grads[r],
             keyvals[r],
-            biases[r],
+            lens[r],
             both[r][0],
             both[r][1],
             cross_key,
@@ -927,11 +1082,15 @@
             returned[r - 1] = moved.pop(0)
         if r >= 2:
             grad_q[r - 1] = moved.pop(0)
-        if r - 1 in left:
-            got[r - 1] = moved.pop(0)
     last = PLANES - 1
-    (grad_cross_key, grad_cross_value), (grad_q[last], returned[last]) = weight_terms(
-        Courier(sizes, [("line", last, grad_q[last]), ("return", 0, cut(grad_rows[last]))]),
+    jobs = [
+        ("line", last, grad_q[last]),
+        ("return", 0, cut(grad_rows[last])),
+        ("scatter", 0, left[0]),
+        ("scatter", 0, left[1]),
+    ]
+    (grad_cross_key, grad_cross_value), (grad_q[last], returned[last], got[0], got[1]) = weight_terms(
+        Courier(sizes, jobs),
         9,
         [rows[r] for r in range(PLANES)],
         [grad_kv[r] for r in range(PLANES)],
@@ -951,7 +1110,8 @@
         10,
         query_one,
         grad_attn_one,
-        keyval_one,
+        key_one,
+        value_one,
         lse_one,
         summand_of(sizes, (grad_cross_key, grad_cross_value)),
     )
@@ -964,7 +1124,7 @@
     decoder_in_grad = (grad_one + back_in)[None]
     share_of_norms = width // devices
     norms = jnp.stack(
-        [g.reshape(devices, share_of_norms) for g in (grad_norm_self, grad_norm_cross, grad_norm_ffn)],
+        [g.reshape(devices, share_of_norms) for g in (grad_norm_self, grad_norm_cross, grad_norm_ffn[0])],
         axis=1,
     ).reshape(devices, 1, 3 * share_of_norms)
     norms = jnp.pad(norms, ((0, 0), (0, 15), (0, 256 - 3 * share_of_norms)))

time: 717 us -> 637 us (0.89)
  matrix products: 57.6 us -> 10.5 us
  Pallas kernels: 537 us -> 574 us
  local copies, waits for them, and re-layouts: 57.1 us -> 22.6 us
  waiting for transfers between devices: 16 us -> 0 us
  other arithmetic: 34.8 us -> 21.3 us
    pallas_call x0 -> x2, Pallas kernels: none -> 73.4 us  [the longest x1 44.7 us: self_part(): pl.pallas_call(kernel, out_shape=[rows, rows, rows, stat, rows, wide, row...]
    dot_general x25 -> x10, matrix products: 57.6 us -> 10.5 us  [dot(): lax.dot_general(left, right, (((left_dim,), (right_dim,)), ((), ())), pre...]
    pallas_call x11 -> x10, Pallas kernels: 477 us -> 439 us  [call(): pl.pallas_call(lambda *refs: kernel(*counts, refs), grid=(PAIRS,), out_sh...]
    ppermute x4 -> x0, waiting for transfers between devices: 16 us -> none  [along_z(): lax.ppermute(value, 'z', [(i, (i + r) % PLANES) for i in range(PLANES)])]
    reshape x4 -> x0, local copies, waits for them, and re-layouts: 12.2 us -> none  [per_row(): return jnp.repeat(stat.reshape(H, tokens).T, HD, axis=1)]
    unnamed x118 -> x59, local copies, waits for them, and re-layouts: 15.4 us -> 4.48 us
  transfers between devices with their start and end apart: 4 -> 0, of which waited for: 1 -> 0; matrix products, arithmetic and copies ran while one was open for 0% -> 0% of each run, Pallas kernels for 0% -> 0%
where the time goes in v4:
time: 637 us; the launch traced here: 630 us
  Pallas kernels  574 us (90%)
  local copies, waits for them, and re-layouts  22.6 us (4%)
  other arithmetic  21.3 us (3%)
  matrix products  10.5 us (2%)
    pallas_call x10, Pallas kernels, call(): pl.pallas_call(lambda *refs: kernel(*counts, refs), grid=(PAIRS,), out_sh...  439 us
    pallas_call x1, Pallas kernels, reduce_all(): pl.pallas_call(kernel, out_shape=courier.out_shape() + [jax.ShapeDtypeStr...  52.8 us
    pallas_call x1, Pallas kernels, self_part(): pl.pallas_call(kernel, out_shape=[rows, rows, rows, stat, rows, wide, row...  44.7 us
    pallas_call x1, Pallas kernels, middle(): pl.pallas_call(functools.partial(middle_kernel, devices=devices, packed=p...  28.7 us

profile of v4, /device:TPU:0, one launch (start us, length us, event | category | flops | bytes accessed | tf_op | source)
XLA Modules:
  0.0 630.3 jit_solution(7584705269972426535)
XLA Ops:
  7.7 44.7 %shard_map.305 = (bf16[512,768]{1,0:T(8,128)(2,1)}, bf16[512,768]{1,0:T(8,128)(2,1)}, bf16[512,768]{1,0:T(8,128)(2,1)}, f32[6,2,512]{2,1,0:T(2,128)}, bf16[512,7...) custom-call(bf16[512,768]{1,0:T(8,128)(2,1)} %bitcast.92, ...), custom_call_target="tpu_custom_call" | custom-call | tf_op jit(solution)/shard_map/pallas_call | solution.py:574
  52.3 1.6 multiply_reduce_fusion.2
  54.5 43.6 %shard_map.306 = (bf16[512,768]{1,0:T(8,128)(2,1)}, f32[6,2,512]{2,1,0:T(2,128)}, bf16[2048,1536]{1,0:T(8,128)(2,1)}, bf16[8,256,768]{2,1,0:T(8,128)(2,1)}, bf16[512,768]{1,0:T(8,128)(2,1)}) custom-call(bf16[512,768]{1,0:T(8,128)(2,1)} %get-tuple-element.101.refs_0_, bf16[2048,768]{1,0:T(8,128)(2,1)} %bitcast.105, ...), custom_call_target="tpu_custom_call" | custom-call | flops 17179869184 | bytes 16777216 | tf_op jit(solution)/shard_map/pallas_call | solution.py:421
  98.1 42.5 %shard_map.307 = (bf16[512,768]{1,0:T(8,128)(2,1)}, f32[6,2,512]{2,1,0:T(2,128)}, bf16[2048,1536]{1,0:T(8,128)(2,1)}, bf16[8,256,768]{2,1,0:T(8,128)(2,1)}, bf16...) custom-call(bf16[512,768]{1,0:T(8,128)(2,1)} %get-tuple-element.104.refs_0_, ...), custom_call_target="tpu_custom_call" | custom-call | flops 17179869184 | bytes 16777216 | tf_op jit(solution)/shard_map/pallas_call | solution.py:421
  140.6 41.5 %shard_map.308 = (bf16[512,768]{1,0:T(8,128)(2,1)}, f32[6,2,512]{2,1,0:T(2,128)}, bf16[2048,1536]{1,0:T(8,128)(2,1)}, bf16[8,256,768]{2,1,0:T(8,128)(2,1)}, bf16...) custom-call(bf16[512,768]{1,0:T(8,128)(2,1)} %get-tuple-element.109.refs_0_, bf16[2048,768]{1,0:T(8,128)(2,1)} %bitcast.111, ...), custom_call_target="tpu_custom_call" | custom-call | flops 17179869184 | bytes 16777216 | tf_op jit(solution)/shard_map/pallas_call | solution.py:421
  182.1 34.8 %shard_map.309 = (bf16[512,768]{1,0:T(8,128)(2,1)}, f32[6,2,512]{2,1,0:T(2,128)}, bf16[2048,1536]{1,0:T(8,128)(2,1)}, bf16[512,768]{1,0:T(8,128)(2,1)}, f32[6,2,512]{2,1,0:T(2,128)}) custom-call(bf16[512,768]{1,0:T(8,128)(2,1)} %get-tuple-element.100.refs_6_.refs_0_, bf16[2048,768]{1,0:T(8,128)(2,1)} %bitcast.113, ...), custom_call_target="tpu_custom_call" | custom-call | flops 17179869184 | bytes 16777216 | tf_op jit(solution)/shard_map/pallas_call | solution.py:421
  216.9 28.7 %shard_map.310 = (bf16[512,768]{1,0:T(8,128)(2,1)}, bf16[512,768]{1,0:T(8,128)(2,1)}, f32[512,768]{1,0:T(8,128)}, bf16[512,768]{1,0:T(8,128)(2,1)}, f32[2,6,2,51...) custom-call(bf16[512,768]{1,0:T(8,128)(2,1)} %get-tuple-element.117., ...), custom_call_target="tpu_custom_call" | custom-call | tf_op jit(solution)/shard_map/pallas_call | solution.py:720
  247.1 1.4 slice_bitcast_fusion.6
  248.5 51.7 %shard_map.311 = (bf16[2048,1536]{1,0:T(8,128)(2,1)}, bf16[512,768]{1,0:T(8,128)(2,1)}, bf16[2048,768]{1,0:T(8,128)(2,1)}, bf16[512,768]{1,0:T(8,128)(2,1)}, f32...) custom-call(bf16[512,768]{1,0:T(8,128)(2,1)} %get-tuple-element.100.refs_6_.refs_0_, ...), custom_call_target="tpu_custom_call" | custom-call | flops 34359738368 | bytes 16777216 | tf_op jit(solution)/shard_map/pallas_call | solution.py:421
  300.1 1.4 slice_bitcast_fusion.4
  301.5 63.5 %shard_map.312 = (bf16[2048,1536]{1,0:T(8,128)(2,1)}, bf16[512,768]{1,0:T(8,128)(2,1)}, bf16[2048,768]{1,0:T(8,128)(2,1)}, bf16[512,768]{1,0:T(8,128)(2,1)}, f32...) custom-call(bf16[512,768]{1,0:T(8,128)(2,1)} %get-tuple-element.101.refs_0_, ...), custom_call_target="tpu_custom_call" | custom-call | flops 34359738368 | bytes 16777216 | tf_op jit(solution)/shard_map/pallas_call | solution.py:421
  365.1 1.4 slice_bitcast_fusion.2
  366.6 43.6 %shard_map.313 = (bf16[2048,1536]{1,0:T(8,128)(2,1)}, bf16[512,768]{1,0:T(8,128)(2,1)}, bf16[2048,768]{1,0:T(8,128)(2,1)}, bf16[512,768]{1,0:T(8,128)(2,1)}, f32...) custom-call(bf16[512,768]{1,0:T(8,128)(2,1)} %get-tuple-element.104.refs_0_, ...), custom_call_target="tpu_custom_call" | custom-call | flops 34359738368 | bytes 16777216 | tf_op jit(solution)/shard_map/pallas_call | solution.py:421
  410.2 1.4 slice_bitcast_fusion
  411.6 43.4 %shard_map.314 = (bf16[2048,1536]{1,0:T(8,128)(2,1)}, bf16[512,768]{1,0:T(8,128)(2,1)}, bf16[2048,768]{1,0:T(8,128)(2,1)}, bf16[8,256,768]{2,1,0:T(8,128)(2,1)}, bf16[512,768]{1,0:T(8,128)(2,1)}) custom-call(bf16[512,768]{1,0:T(8,128)(2,1)} %get-tuple-element.109.refs_0_, bf16[512,768]{1,0:T(8,128)(2,1)} %get-tuple-element.144.refs_1_, ...), custom_call_target="tpu_custom_call" | custom-call | flops 34359738368 | bytes 16777216 | tf_op jit(solution)/shard_map/pallas_call | solution.py:421
  455.1 52.7 %shard_map.315 = (f32[768,768]{1,0:T(8,128)}, f32[768,768]{1,0:T(8,128)}, bf16[512,768]{1,0:T(8,128)(2,1)}, bf16[8,256,768]{2,1,0:T(8,128)(2,1)}, bf16[3,48,2048...) custom-call(bf16[2048,768]{1,0:T(8,128)(2,1)} %bitcast.114, bf16[2048,768]{1,0:T(8,128)(2,1)} %bitcast.106, ...), custom_call_target="tpu_custom_call" | custom-call | flops 17179869184 | bytes 16777216 | tf_op jit(solution)/shard_map/pallas_call | solution.py:421
  507.9 1.6 add_convert_fusion
  509.5 1.7 convert_add_fusion.1
  514.0 1.6 pad_maximum_fusion.1.refs_2_
  519.5 1.7 convolution_convert_fusion.5.refs_1_
  521.3 1.5 copy-done.4
  523.0 1.7 pad_maximum_fusion.refs_5_
  524.6 21.6 %shard_map.316 = (bf16[512,768]{1,0:T(8,128)(2,1)}, bf16[512,768]{1,0:T(8,128)(2,1)}, bf16[512,768]{1,0:T(8,128)(2,1)}, bf16[4,48,768]{2,1,0:T(8,128)(2,1)}) custom-call(bf16[512,768]{1,0:T(8,128)(2,1)} %get-tuple-element.159.refs_0_, bf16[512,768]{1,0:T(8,128)(2,1)} %convolution_convert_fusion.5.refs_1_, bf16[512,768]{1,0:T(8,128)(2,1)} %get-tuple-element.160.refs_2_, ...), custom_call_target="tpu_custom_call" | custom-call | flops 8589934592 | bytes 16777216 | tf_op jit(solution)/shard_map/pallas_call | solution.py:421
  546.2 2.1 fusion.23
  552.1 1.6 fusion.4
  556.6 1.7 pad_maximum_fusion.3.refs_4_
  560.2 1.7 pad_maximum_fusion.2.refs_3_
  561.9 52.8 %shard_map.318 = (bf16[3,48,768]{2,1,0:T(8,128)(2,1)}, f32[16,256]{1,0:T(8,128)}, f32[48,768]{1,0:T(8,128)}, f32[48,768]{1,0:T(8,128)}, f32[48,768]{1,0:T(8,128)}) custom-call(bf16[4,48,768]{2,1,0:T(8,128)(2,1)} %get-tuple-element.172.refs_0_, bf16[4,2,2,2,16,256]{5,4,3,2,1,0:T(8,128)(2,1)} %bitcast.98, ...), custom_call_target="tpu_custom_call" | custom-call | tf_op jit(solution)/shard_map/pallas_call | solution.py:499
  614.7 1.4 slice_bitcast_fusion.8
  618.0 1.6 fusion.20
  619.6 1.7 fusion.19
  621.3 8.7 %shard_map.317 = bf16[32,256,768]{2,1,0:T(8,128)(2,1)} custom-call(bf16[8,256,768]{2,1,0:T(8,128)(2,1)} %get-tuple-element.168.refs_0_, bf16[8,256,768]{2,1,0:T(8,128)(2,1)} %get-tuple-element.169.refs_1_, bf16[8,256,768]{2,1,0:T(8,128)(2,1)} %get-tuple-element.170.refs_2_, bf16[8,256,768]{2,1,0:T(8,128)(2,1)} %get-tuple-element.171.refs_3_), custom_call_target="tpu_custom_call" | custom-call | tf_op jit(solution)/shard_map/pallas_call | solution.py:915
  (94 shorter events, 25.7 us)
Async XLA Ops:
  301.5 64.9 %copy-start.3 = (f32[768,768]{1,0:T(8,128)S(1)}, f32[768,768]{1,0:T(8,128)}, u32[]{:S(2)}) copy-start(f32[768,768]{1,0:T(8,128)} %get-tuple-element.174) | copy-start | bytes 7077892
  455.0 52.8 %copy-start.14 = (bf16[512,768]{1,0:T(8,128)(2,1)S(1)}, bf16[512,768]{1,0:T(8,128)(2,1)}, u32[]{:S(2)}) copy-start(bf16[512,768]{1,0:T(8,128)(2,1)} %get-tuple-element.132) | copy-start | bytes 2359300
  455.0 52.8 %copy-start.15 = (bf16[512,768]{1,0:T(8,128)(2,1)S(1)}, bf16[512,768]{1,0:T(8,128)(2,1)}, u32[]{:S(2)}) copy-start(bf16[512,768]{1,0:T(8,128)(2,1)} %get-tuple-element.143) | copy-start | bytes 2359300
  455.0 52.8 %copy-start.16 = (bf16[512,768]{1,0:T(8,128)(2,1)S(1)}, bf16[512,768]{1,0:T(8,128)(2,1)}, u32[]{:S(2)}) copy-start(bf16[512,768]{1,0:T(8,128)(2,1)} %get-tuple-element.149) | copy-start | bytes 2359300
  507.8 1.6 copy-start.18
  507.8 3.4 copy-start.17
  509.5 3.6 copy-start
  509.5 3.6 copy-start.22
  509.5 3.6 copy-start.25
  514.0 1.6 copy-start.7
  515.7 1.4 copy-start.6
  515.7 1.4 copy-start.24
  517.1 1.1 copy-start.11
  518.2 1.3 copy-start.8
  519.5 1.7 copy-start.5
  521.2 1.7 copy-start.4
  524.6 21.6 %copy-start.9 = (bf16[768,768]{1,0:T(8,128)(2,1)S(1)}, bf16[768,768]{1,0:T(8,128)(2,1)}, u32[]{:S(2)}) copy-start(bf16[768,768]{1,0:T(8,128)(2,1)} %refs_3_.5) | copy-start | bytes 3538948
  546.2 2.1 copy-start.10
  546.2 2.1 copy-start.27
  548.3 1.3 copy-start.2
  548.4 1.5 copy-start.12
  549.8 1.1 copy-start.1
  549.8 1.1 copy-start.19
  549.8 1.1 copy-start.21
  551.0 1.1 copy-start.23
  552.1 2.4 copy-start.20
  553.7 2.1 copy-start.13
  556.6 1.7 copy-start.28
  558.3 1.1 copy-start.26

commit v5 on v4

--- a/solution.py
+++ b/solution.py
@@ -19,6 +19,7 @@
 F32 = jnp.float32
 ALL = ("z", "y", "x", "c")
 PLANE = ("y", "x", "c")
+EVERY = slice(None)
 
 
 def dot(left, right, left_dim, right_dim):
@@ -194,10 +195,16 @@
 
     def bind(self, source, refs):
         self.source = source
-        self.own, self.got0, self.got1x, self.got1y, self.got2y, self.got2x = refs[:6]
+        self.held, self.got0, self.got1x, self.got1y, self.got2y, self.got2x = refs[:6]
         self.local, self.send, self.receive = refs[6:]
         self.z, self.y, self.x, self.c = (lax.axis_index(name) for name in ALL)
         return self
+
+    def index(self, z, y, x, lanes):
+        return (z, y, x, EVERY, lanes)
+
+    def slab(self, z, y, x, lanes):
+        return self.held.at[self.index(z, y, x, lanes)]
 
     def remote(self, n, source, target, device):
         return pltpu.make_async_remote_copy(
@@ -212,7 +219,7 @@
     def first(self):
         other = 1 - self.c
         return [
-            pltpu.make_async_copy(self.source.at[:, :, :, self.c], self.own, self.local.at[0]),
+            pltpu.make_async_copy(self.source.at[:, :, :, self.c], self.held, self.local.at[0]),
             self.remote(0, self.source.at[:, :, :, other], self.got0, {"c": other}),
         ]
 
@@ -222,10 +229,10 @@
         copies = []
         for k in range(1, x_size):
             there = rem(self.x + k, x_size)
-            copies.append((self.own.at[:, :, there, :, left], self.got1x.at[k - 1], {"x": there}))
+            copies.append((self.slab(EVERY, EVERY, there, left), self.got1x.at[k - 1], {"x": there}))
         for k in range(1, y_size):
             there = rem(self.y + k, y_size)
-            copies.append((self.own.at[:, there, :, :, right], self.got1y.at[k - 1], {"y": there}))
+            copies.append((self.slab(EVERY, there, EVERY, right), self.got1y.at[k - 1], {"y": there}))
         return [self.remote(1 + n, *copy) for n, copy in enumerate(copies)]
 
     def third(self):
@@ -236,12 +243,12 @@
         for k in range(1, y_size):
             there = rem(self.y + k, y_size)
             copies.append(
-                (self.own.at[:, there, self.x, :, left], self.got2y.at[k - 1], {"y": there})
+                (self.slab(EVERY, there, self.x, left), self.got2y.at[k - 1], {"y": there})
             )
         for k in range(1, x_size):
             there = rem(self.x + k, x_size)
             copies.append(
-                (self.own.at[:, self.y, there, :, right], self.got2x.at[k - 1], {"x": there})
+                (self.slab(EVERY, self.y, there, right), self.got2x.at[k - 1], {"x": there})
             )
         return [self.remote(at + n, *copy) for n, copy in enumerate(copies)]
 
@@ -255,7 +262,8 @@
 
         @pl.loop(0, self.sizes[0])
         def _(z):
-            self.own[z] = (self.own[z].astype(F32) + self.got0[z].astype(F32)).astype(BF)
+            at = self.index(z, EVERY, EVERY, EVERY)
+            self.held[at] = (self.held[at].astype(F32) + self.got0[z].astype(F32)).astype(BF)
 
         for copy in self.second():
             copy.start()
@@ -269,15 +277,17 @@
         @pl.loop(0, self.sizes[0])
         def _(z):
             for y in range(y_size):
-                total = self.own[z, y, self.x, :, :h].astype(F32)
+                at = self.index(z, y, self.x, pl.ds(0, h))
+                total = self.held[at].astype(F32)
                 for k in range(x_size - 1):
                     total += self.got1x[k, z, y].astype(F32)
-                self.own[z, y, self.x, :, :h] = total.astype(BF)
+                self.held[at] = total.astype(BF)
             for x in range(x_size):
-                total = self.own[z, self.y, x, :, h:].astype(F32)
+                at = self.index(z, self.y, x, pl.ds(h, h))
+                total = self.held[at].astype(F32)
                 for k in range(y_size - 1):
                     total += self.got1y[k, z, x].astype(F32)
-                self.own[z, self.y, x, :, h:] = total.astype(BF)
+                self.held[at] = total.astype(BF)
 
         for copy in self.third():
             copy.start()
@@ -290,14 +300,121 @@
 
         @pl.loop(0, self.sizes[0])
         def _(z):
-            total = self.own[z, self.y, self.x, :, :h].astype(F32)
+            total = self.held[self.index(z, self.y, self.x, pl.ds(0, h))].astype(F32)
             for k in range(y_size - 1):
                 total += self.got2y[k, z].astype(F32)
             out_ref[z, :, :h] = total.astype(BF)
-            total = self.own[z, self.y, self.x, :, h:].astype(F32)
+            total = self.held[self.index(z, self.y, self.x, pl.ds(h, h))].astype(F32)
             for k in range(x_size - 1):
                 total += self.got2x[k, z].astype(F32)
             out_ref[z, :, h:] = total.astype(BF)
+
+
+class Resident(Reducer):
+    def scratch(self):
+        z, y, x, c = self.sizes
+        r, w, h = self.rows, self.lanes, self.half
+        count = 1 + 2 * (x + y - 2) + z - 1
+        return [
+            pltpu.VMEM((z, y, x, c, r, w), BF),
+            pltpu.VMEM((z, y, x, r, w), BF),
+            pltpu.VMEM((x - 1, z, y, r, h), BF),
+            pltpu.VMEM((y - 1, z, x, r, h), BF),
+            pltpu.VMEM((y - 1, z, r, h), BF),
+            pltpu.VMEM((x - 1, z, r, h), BF),
+            pltpu.VMEM((z, r, w), BF),
+            pltpu.VMEM((z - 1, r, w), BF),
+            pltpu.SemaphoreType.DMA((count,)),
+            pltpu.SemaphoreType.DMA((count,)),
+        ]
+
+    def bind(self, refs):
+        self.held, self.got0, self.got1x, self.got1y, self.got2y, self.got2x = refs[:6]
+        self.left, self.got3, self.send, self.receive = refs[6:]
+        self.z, self.y, self.x, self.c = (lax.axis_index(name) for name in ALL)
+        return self
+
+    def index(self, z, y, x, lanes):
+        return (z, y, x, self.c, EVERY, lanes)
+
+    def first(self):
+        other = 1 - self.c
+        return [self.remote(0, self.held.at[:, :, :, other], self.got0, {"c": other})]
+
+    def fourth(self):
+        _, y_size, x_size, _ = self.sizes
+        at = 1 + 2 * (x_size + y_size - 2)
+        copies = []
+        for k in range(1, PLANES):
+            there = rem(self.z + k, PLANES)
+            copies.append(
+                self.remote(at + k - 1, self.left.at[there], self.got3.at[k - 1], {"z": there})
+            )
+        return copies
+
+    def after_third_start(self):
+        self.after_third(self.left)
+        for copy in self.fourth():
+            copy.start()
+
+    def finish(self, out_ref):
+        for copy in self.fourth():
+            copy.wait()
+        total = self.left[self.z].astype(F32)
+        for k in range(PLANES - 1):
+            total += self.got3[k].astype(F32)
+        out_ref[...] = total
+
+
+class SmallSum:
+    def __init__(self, sizes, shape):
+        self.shape = shape
+        self.steps = list(zip(("c", "x", "y", "z"), (sizes[3], sizes[2], sizes[1], sizes[0])))
+
+    def scratch(self):
+        count = sum(n - 1 for _, n in self.steps)
+        return (
+            [pltpu.VMEM(self.shape, F32) for _ in range(4)]
+            + [pltpu.VMEM((n - 1,) + self.shape, F32) for _, n in self.steps]
+            + [pltpu.SemaphoreType.DMA((count,))] * 2
+        )
+
+    def bind(self, refs):
+        self.held, self.got = refs[:4], refs[4:8]
+        self.send, self.receive = refs[8:]
+        return self
+
+    def copies(self, step):
+        axis, n = self.steps[step]
+        at = sum(m - 1 for _, m in self.steps[:step])
+        me = lax.axis_index(axis)
+        return [
+            pltpu.make_async_remote_copy(
+                src_ref=self.held[step],
+                dst_ref=self.got[step].at[k - 1],
+                send_sem=self.send.at[at + k - 1],
+                recv_sem=self.receive.at[at + k - 1],
+                device_id={axis: rem(me + k, n)},
+                device_id_type=pl.DeviceIdType.MESH,
+            )
+            for k in range(1, n)
+        ]
+
+    def start(self, step):
+        for copy in self.copies(step):
+            copy.start()
+
+    def advance(self, step, out_ref=None):
+        for copy in self.copies(step):
+            copy.wait()
+        total = self.held[step][...]
+        for k in range(self.steps[step][1] - 1):
+            total += self.got[step][k]
+        if step < 3:
+            self.held[step + 1][...] = total
+            self.start(step + 1)
+        else:
+            out_ref[...] = total
 
 
 def forward_pair(queries, keys, values, bias):
@@ -687,7 +804,7 @@
         two_ref[...] = two
         low = two.astype(BF)
         da_ref[...] = dot(low, wo_ref[...], 1, 1).astype(BF)
-        gwo_ref[...] = dot(attn_ref[...], low, 0, 0)
+        gwo_ref[...] = dot(attn_ref[...], low, 0, 0).astype(BF)
         for p in range(PAIRS):
             cols = pl.ds(p * 128, 128)
             product = (da_ref[:, cols].astype(F32) * raw_ref[:, cols]).T
@@ -727,7 +844,7 @@
             rows,
             jax.ShapeDtypeStruct((2, PAIRS, 2, tokens), F32),
             jax.ShapeDtypeStruct((1, width), F32),
-            jax.ShapeDtypeStruct((width, width), F32),
+            jax.ShapeDtypeStruct((width, width), BF),
         ]
         + grad_shapes
         + [jax.ShapeDtypeStruct((devices, down_share, width), BF)],
@@ -886,6 +1003,250 @@
         2**33,
         summand,
     )
+
+
+def rms_back(values, gain, grad):
+    r = lax.rsqrt(jnp.mean(values * values, axis=-1, keepdims=True) + EPSILON)
+    u = gain * grad
+    back = r * u - values * (r * r * r) * jnp.mean(u * values, axis=-1, keepdims=True)
+    return back, jnp.sum(grad * values * r, axis=0, keepdims=True)
+
+
+def ending(sizes, ident, rows, grads, grad_q, grad_rows, left, two, held, lse, small_in):
+    courier = Courier(
+        sizes,
+        [("line", PLANES - 1, grad_q[-1]), ("return", 0, grad_rows)]
+        + [("scatter", 0, value) for value in left],
+    )
+    courier.lines = list(range(1, PLANES))
+    jobs = len(courier.jobs)
+    devices = sizes[0] * sizes[1] * sizes[2] * sizes[3]
+    keys, width = rows[0].shape
+    tokens = two.shape[0]
+    share = width // devices
+    chunk = 512
+    cuts = keys // chunk
+    groups = [Resident(sizes, (2 * share, width)) for _ in range(4)]
+    small = SmallSum(sizes, (8, width))
+    early = [two] + list(held) + list(grad_q[:-1])
+    far = list(rows) + list(grads) + early
+    counts = (len(far), len(small_in) + 1, jobs, 6, jobs - 1, 4, len(early) - 1, 8, 3, 40, 10)
+
+    def pack(ref, first, second, cols=EVERY):
+        lanes = first.shape[1]
+        parts = [v.astype(F32).reshape(devices, share, lanes) for v in (first, second)]
+        both = jnp.concatenate(parts, axis=1).astype(BF)
+        ref[:, :, :, :, :, cols] = both.reshape(tuple(sizes) + both.shape[1:])
+
+    def kernel(*refs):
+        far_refs, near, sources, outs, targets, stage, loaded, work, sems, group_refs, rest = (
+            split_refs(refs, *counts)
+        )
+        self_gain, cross_gain, ffn_term, lse_ref = near
+        grad_in, *sums, norm_sums = outs
+        row_buf, grad_buf, total, load_sems = stage
+        dq_got, da_ref, dq1, dk1, dv1, *_ = work
+        chunk_sems, early_sems = load_sems, work[5]
+        copies = courier.copies(sources, [dq_got] + list(targets), sems)
+        courier.greet()
+        for copy in copies:
+            copy.start()
+
+        def chunk_loads(r, i):
+            slot = rem(i, 2)
+            where = pl.ds(pl.multiple_of(rem(i, cuts) * chunk, chunk), chunk)
+            return [
+                pltpu.make_async_copy(
+                    far_refs[r].at[where], row_buf.at[slot], chunk_sems.at[slot, 0]
+                ),
+                pltpu.make_async_copy(
+                    far_refs[PLANES + r].at[where], grad_buf.at[slot], chunk_sems.at[slot, 1]
+                ),
+            ]
+
+        def start_chunk(i):
+            for r in range(PLANES):
+
+                @pl.when(lax.div(jnp.int32(i), cuts) == r)
+                def _(r=r):
+                    for copy in chunk_loads(r, i):
+                        copy.start()
+
+        total[...] = jnp.zeros_like(total)
+        early_refs = far_refs[2 * PLANES :]
+        early_loads = [
+            pltpu.make_async_copy(source, target, early_sems.at[n])
+            for n, (source, target) in enumerate(zip(early_refs, [grad_in] + list(loaded)))
+        ]
+        start_chunk(0)
+        for copy in early_loads:
+            copy.start()
+
+        @pl.loop(0, PLANES * cuts)
+        def _(i):
+            @pl.when(i + 1 < PLANES * cuts)
+            def _():
+                start_chunk(i + 1)
+
+            for copy in chunk_loads(0, i):
+                copy.wait()
+            slot = rem(i, 2)
+            total[...] += dot(row_buf[slot], grad_buf[slot], 0, 0)
+
+        bound = [
+            one.bind(group_refs[10 * n : 10 * n + 10]) for n, one in enumerate(groups)
+        ]
+        bits = small.bind(rest)
+
+        @pl.loop(0, PAIRS)
+        def _(p):
+            at = pl.multiple_of(p * 256, 256)
+            pack(
+                bound[0].held,
+                total[:, pl.ds(at, 128)],
+                total[:, pl.ds(at + 128, 128)],
+                pl.ds(pl.multiple_of(p * 128, 128), 128),
+            )
+
+        bound[0].begin()
+        for copy in early_loads:
+            copy.wait()
+        copies[1].wait()
+        x_ref, h1_ref, gco_ref, q_ref, k_ref, v_ref, attn_ref = loaded[:7]
+        wq_ref, wk_ref, wv_ref, wo_ref, wc_ref, *dq_refs = loaded[7:]
+        grad = dq_got[...].astype(F32)
+        for ref in dq_refs:
+            grad += ref[...].astype(F32)
+        dq_got[...] = grad.astype(BF)
+        hidden = h1_ref[...]
+        back, cross_norm = rms_back(hidden, cross_gain[...], dot(dq_got[...], wc_ref[...], 1, 1))
+        grad_in[...] += back
+        dv1[...] = rms(hidden, cross_gain[...]).astype(BF)
+        bound[0].after_first()
+
+        @pl.loop(0, 3)
+        def _(i):
+            cols = pl.ds(pl.multiple_of(i * 256, 256), 256)
+            pack(bound[1].held, dot(dv1[...], dq_got[:, cols], 0, 0), gco_ref[:, cols], cols)
+
+        bound[1].begin()
+        low_ref = dq_got
+        low_ref[...] = grad_in[...].astype(BF)
+        da_ref[...] = dot(low_ref[...], wo_ref[...], 1, 1).astype(BF)
+
+        @pl.loop(0, PAIRS)
+        def _(p):
+            cols = pl.ds(pl.multiple_of(p * 128, 128), 128)
+            grad_kv, grad_q_p = backward_pair(
+                q_ref[:, cols],
+                da_ref[:, cols],
+                k_ref[:, cols],
+                v_ref[:, cols],
+                None,
+                [lse_ref[p, h : h + 1, :] for h in range(2)],
+                None,
+            )
+            dq1[:, cols] = grad_q_p
+            dk1[:, cols] = grad_kv[:, :128]
+            dv1[:, cols] = grad_kv[:, 128:]
+
+            @pl.when(p == 1)
+            def _():
+                bound[0].after_second()
+                bound[1].after_first()
+
+            @pl.when(p == 3)
+            def _():
+                bound[0].after_third_start()
+                bound[1].after_second()
+
+            @pl.when(p == 5)
+            def _():
+                bound[1].after_third_start()
+
+        values = x_ref[...].astype(F32)
+        normed_ref = da_ref
+        normed_ref[...] = rms(values, self_gain[...]).astype(BF)
+
+        @pl.loop(0, 3)
+        def _(i):
+            cols = pl.ds(pl.multiple_of(i * 256, 256), 256)
+            pack(
+                bound[2].held,
+                dot(normed_ref[...], dv1[:, cols], 0, 0),
+                dot(attn_ref[...], low_ref[:, cols], 0, 0),
+                cols,
+            )
+
+        bound[2].begin()
+
+        @pl.loop(0, 3)
+        def _(i):
+            cols = pl.ds(pl.multiple_of(i * 256, 256), 256)
+            pack(
+                bound[3].held,
+                dot(normed_ref[...], dq1[:, cols], 0, 0),
+                dot(normed_ref[...], dk1[:, cols], 0, 0),
+                cols,
+            )
+
+        bound[3].begin()
+        grad_normed = (
+            dot(dq1[...], wq_ref[...], 1, 1)
+            + dot(dk1[...], wk_ref[...], 1, 1)
+            + dot(dv1[...], wv_ref[...], 1, 1)
+        )
+        back, self_norm = rms_back(values, self_gain[...], grad_normed)
+        grad_in[...] += back
+        bits.held[0][...] = jnp.concatenate(
+            [self_norm, cross_norm, ffn_term[...], jnp.zeros((5, width), F32)], axis=0
+        )
+        bits.start(0)
+        bound[2].after_first()
+        bound[3].after_first()
+        bits.advance(0)
+        bound[2].after_second()
+        bound[3].after_second()
+        bits.advance(1)
+        bound[2].after_third_start()
+        bound[3].after_third_start()
+        bits.advance(2)
+        for n in range(4):
+            bound[n].finish(sums[n])
+        bits.advance(3, norm_sums)
+        for n, copy in enumerate(copies):
+            if n != 1:
+                copy.wait()
+
+    any_spec = pl.BlockSpec(memory_space=pl.ANY)
+    vmem = pl.BlockSpec(memory_space=pltpu.VMEM)
+    row = pltpu.VMEM((tokens, width), BF)
+    scratch = [
+        pltpu.VMEM((2, chunk, width), BF),
+        pltpu.VMEM((2, chunk, 2 * width), BF),
+        pltpu.VMEM((width, 2 * width), F32),
+        pltpu.SemaphoreType.DMA((2, 2)),
+    ]
+    scratch += [pltpu.VMEM(v.shape, v.dtype) for v in early[1:]]
+    scratch += [row] * 5 + [pltpu.SemaphoreType.DMA((len(early),))]
+    scratch += [pltpu.SemaphoreType.DMA((1,))] * 2 + courier.scratch()
+    for one in groups:
+        scratch += one.scratch()
+    scratch += small.scratch()
+    outs = pl.pallas_call(
+        kernel,
+        out_shape=[jax.ShapeDtypeStruct((tokens, width), F32)]
+        + [jax.ShapeDtypeStruct((2 * share, width), F32)] * 4
+        + [jax.ShapeDtypeStruct((8, width), F32)]
+        + courier.out_shape()[1:],
+        in_specs=[any_spec] * len(far) + [vmem] * (len(small_in) + 1) + courier.specs(),
+        out_specs=[vmem] * 6 + courier.specs()[1:],
+        scratch_shapes=scratch,
+        compiler_params=pltpu.CompilerParams(
+            vmem_limit_bytes=62 * 2**20, collective_id=ident, has_side_effects=True
+        ),
+    )(*far, *small_in, lse, *courier.values())
+    return outs[0], outs[1:5], outs[5], outs[6:]
 
 
 def place_kernel(*refs):
@@ -980,7 +1341,6 @@
     def cut(rows):
         return rows.reshape(plane_size, positions, width)
 
-    inputs = decoder_in[0].astype(F32)
     lens = {0: jnp.broadcast_to(memory_lengths[None, :], (8, 128))}
     jobs = [("fetch", 1, memory)]
     jobs += [("line", -r, lens[0]) for r in range(1, PLANES)]
@@ -993,8 +1353,6 @@
         (self_query, self_key, self_value, self_out, cross_query),
     )
     fetched, lens[1], lens[2], lens[3], query_near = moved
-    normed_one = norm_apply(inputs, norm_self).astype(BF)
-    normed_two = norm_apply(hidden_one, norm_cross).astype(BF)
     queries, rows, keyvals, partial, stats_out = {0: query_two, 1: query_near}, {}, {}, {}, {}
     order = (1, 2, 3, 0)
     for at, r in enumerate(order):
@@ -1083,6 +1441,49 @@
         if r >= 2:
             grad_q[r - 1] = moved.pop(0)
     last = PLANES - 1
+    part = width // devices
+    if part % 8 == 0:
+        decoder_in_grad, sums, norm_sums, moved = ending(
+            sizes,
+            9,
+            [rows[r] for r in range(PLANES)],
+            [grad_kv[r] for r in range(PLANES)],
+            [grad_q[r] for r in range(PLANES)],
+            cut(grad_rows[last]),
+            [left[0], left[1]],
+            grad_two,
+            (decoder_in[0], hidden_one, grad_cross_out, query_one, key_one, value_one, attn_one)
+            + (self_query, self_key, self_value, self_out, cross_query),
+            lse_one,
+            (norm_self[None], norm_cross[None], grad_norm_ffn),
+        )
+        returned[last], got[0], got[1] = moved
+        memory_grad = place([returned[r] for r in range(PLANES)])
+        gate_up = over_z(left[0], got[0])
+        here = lax.axis_index(ALL) * part
+        norm_self_sum, norm_cross_sum, norm_ffn_sum = (
+            lax.dynamic_slice_in_dim(norm_sums[n], here, part) for n in range(3)
+        )
+        return (
+            decoder_out,
+            decoder_in_grad[None],
+            memory_grad,
+            norm_self_sum,
+            sums[3][:part],
+            sums[3][part:],
+            sums[2][:part],
+            sums[2][part:],
+            norm_cross_sum,
+            sums[1][:part],
+            sums[0][:part],
+            sums[0][part:],
+            sums[1][part:],
+            norm_ffn_sum,
+            gate_up[:part],
+            gate_up[part:],
+            over_z(left[1], got[1]),
+        )
+
     jobs = [
         ("line", last, grad_q[last]),
         ("return", 0, cut(grad_rows[last])),
@@ -1097,6 +1498,9 @@
     )
     memory_grad = place([returned[r] for r in range(PLANES)])
 
+    inputs = decoder_in[0].astype(F32)
+    normed_one = norm_apply(inputs, norm_self).astype(BF)
+    normed_two = norm_apply(hidden_one, norm_cross).astype(BF)
     grad_q_two = sum(grad_q[r].astype(F32) for r in range(PLANES)).astype(BF)
     grad_cross_query = tmatmul(normed_two, grad_q_two)
     grad_normed_two = matmul_t(grad_q_two, cross_query)
@@ -1133,7 +1537,7 @@
         11,
         [
             norms.astype(BF).reshape(tuple(sizes) + norms.shape[1:]),
-            summand_of(sizes, (grad_cross_query, grad_cross_out)),
+            summand_of(sizes, (grad_cross_query, grad_cross_out.astype(F32))),
             summand_of(sizes, (tmatmul(normed_one, grad_q_one), tmatmul(normed_one, grad_k_one))),
             summand_of(sizes, (tmatmul(normed_one, grad_v_one), grad_self_out)),
         ],

time: 637 us -> 577 us (0.906)
  Pallas kernels: 574 us -> 550 us
  other arithmetic: 21.3 us -> 4.86 us
  matrix products: 10.5 us -> 0 us
  local copies, waits for them, and re-layouts: 22.6 us -> 14.6 us
    pallas_call x10 -> x8, Pallas kernels: 439 us -> 365 us  [call(): pl.pallas_call(lambda *refs: kernel(*counts, refs), grid=(PAIRS,), out_sh...]
    pallas_call x1, Pallas kernels: 52.8 us -> 103 us  [ending(): pl.pallas_call(kernel, out_shape=[jax.ShapeDtypeStruct((tokens, width), F...]
    dot_general x10 -> x0, matrix products: 10.5 us -> none  [dot(): lax.dot_general(left, right, (((left_dim,), (right_dim,)), ((), ())), pre...]
    concatenate x4 -> x0, other arithmetic: 6.63 us -> none  [summand_of(): joined = parts[0] if len(parts) == 1 else jnp.concatenate(parts, axis=1)]
where the time goes in v5:
time: 577 us; the launch traced here: 571 us
  Pallas kernels  550 us (95%)
  local copies, waits for them, and re-layouts  14.6 us (3%)
    pallas_call x8, Pallas kernels, call(): pl.pallas_call(lambda *refs: kernel(*counts, refs), grid=(PAIRS,), out_sh...  365 us
    pallas_call x1, Pallas kernels, ending(): pl.pallas_call(kernel, out_shape=[jax.ShapeDtypeStruct((tokens, width), F...  103 us
    pallas_call x1, Pallas kernels, self_part(): pl.pallas_call(kernel, out_shape=[rows, rows, rows, stat, rows, wide, row...  44.6 us
    pallas_call x1, Pallas kernels, middle(): pl.pallas_call(functools.partial(middle_kernel, devices=devices, packed=p...  28.1 us

profile of v5, /device:TPU:0, one launch (start us, length us, event | category | flops | bytes accessed | tf_op | source)
XLA Modules:
  0.0 570.9 jit_solution(15996397600522256810)
XLA Ops:
  1.3 0.6 broadcast_in_dim.28.refs_9_.refs_10_.refs_11_.refs_2_.refs_3_
  1.9 1.3 broadcast_in_dim.25.refs_1_.refs_24_
  3.2 1.3 broadcast_in_dim.26.refs_2_.refs_25_
  4.4 44.6 %shard_map.305 = (bf16[512,768]{1,0:T(8,128)(2,1)}, bf16[512,768]{1,0:T(8,128)(2,1)}, bf16[512,768]{1,0:T(8,128)(2,1)}, f32[6,2,512]{2,1,0:T(2,128)}, bf16[512,7...) custom-call(bf16[512,768]{1,0:T(8,128)(2,1)} %bitcast.44, ...), custom_call_target="tpu_custom_call" | custom-call | tf_op jit(solution)/shard_map/pallas_call | solution.py:691
  49.1 43.9 %shard_map.306 = (bf16[512,768]{1,0:T(8,128)(2,1)}, f32[6,2,512]{2,1,0:T(2,128)}, bf16[2048,1536]{1,0:T(8,128)(2,1)}, bf16[8,256,768]{2,1,0:T(8,128)(2,1)}, bf16[512,768]{1,0:T(8,128)(2,1)}) custom-call(bf16[512,768]{1,0:T(8,128)(2,1)} %get-tuple-element.95.refs_0_, bf16[2048,768]{1,0:T(8,128)(2,1)} %bitcast.46, s32[8,128]{1,0:T(8,128)} %get-tuple-element.97.refs_2_.refs_3_, ...), custom_call_target="tpu_custom_call" | custom-call | flops 17179869184 | bytes 16777216 | tf_op jit(solution)/shard_map/pallas_call | solution.py:538
  93.0 42.5 %shard_map.307 = (bf16[512,768]{1,0:T(8,128)(2,1)}, f32[6,2,512]{2,1,0:T(2,128)}, bf16[2048,1536]{1,0:T(8,128)(2,1)}, bf16[8,256,768]{2,1,0:T(8,128)(2,1)}, bf16...) custom-call(bf16[512,768]{1,0:T(8,128)(2,1)} %get-tuple-element.98.refs_0_, ...), custom_call_target="tpu_custom_call" | custom-call | flops 17179869184 | bytes 16777216 | tf_op jit(solution)/shard_map/pallas_call | solution.py:538
  135.5 41.4 %shard_map.308 = (bf16[512,768]{1,0:T(8,128)(2,1)}, f32[6,2,512]{2,1,0:T(2,128)}, bf16[2048,1536]{1,0:T(8,128)(2,1)}, bf16[8,256,768]{2,1,0:T(8,128)(2,1)}, bf16...) custom-call(bf16[512,768]{1,0:T(8,128)(2,1)} %get-tuple-element.103.refs_0_, bf16[2048,768]{1,0:T(8,128)(2,1)} %bitcast.50, ...), custom_call_target="tpu_custom_call" | custom-call | flops 17179869184 | bytes 16777216 | tf_op jit(solution)/shard_map/pallas_call | solution.py:538
  176.9 0.0 copy-start.5
  176.9 34.8 %shard_map.309 = (bf16[512,768]{1,0:T(8,128)(2,1)}, f32[6,2,512]{2,1,0:T(2,128)}, bf16[2048,1536]{1,0:T(8,128)(2,1)}, bf16[512,768]{1,0:T(8,128)(2,1)}, f32[6,2,512]{2,1,0:T(2,128)}) custom-call(bf16[512,768]{1,0:T(8,128)(2,1)} %get-tuple-element.94.refs_6_.refs_0_, bf16[2048,768]{1,0:T(8,128)(2,1)} %bitcast.52, ...), custom_call_target="tpu_custom_call" | custom-call | flops 17179869184 | bytes 16777216 | tf_op jit(solution)/shard_map/pallas_call | solution.py:538
  211.7 0.6 broadcast_in_dim.29.refs_10_
  212.3 28.1 %shard_map.310 = (bf16[512,768]{1,0:T(8,128)(2,1)}, bf16[512,768]{1,0:T(8,128)(2,1)}, f32[512,768]{1,0:T(8,128)}, bf16[512,768]{1,0:T(8,128)(2,1)}, f32[2,6,2,51...) custom-call(bf16[512,768]{1,0:T(8,128)(2,1)} %get-tuple-element.111., ...), custom_call_target="tpu_custom_call" | custom-call | tf_op jit(solution)/shard_map/pallas_call | solution.py:837
  240.4 1.4 slice_bitcast_fusion.6
  241.8 51.8 %shard_map.311 = (bf16[2048,1536]{1,0:T(8,128)(2,1)}, bf16[512,768]{1,0:T(8,128)(2,1)}, bf16[2048,768]{1,0:T(8,128)(2,1)}, bf16[512,768]{1,0:T(8,128)(2,1)}, f32...) custom-call(bf16[512,768]{1,0:T(8,128)(2,1)} %get-tuple-element.94.refs_6_.refs_0_, ...), custom_call_target="tpu_custom_call" | custom-call | flops 34359738368 | bytes 16777216 | tf_op jit(solution)/shard_map/pallas_call | solution.py:538
  293.5 1.4 slice_bitcast_fusion.4
  294.9 63.6 %shard_map.312 = (bf16[2048,1536]{1,0:T(8,128)(2,1)}, bf16[512,768]{1,0:T(8,128)(2,1)}, bf16[2048,768]{1,0:T(8,128)(2,1)}, bf16[512,768]{1,0:T(8,128)(2,1)}, f32...) custom-call(bf16[512,768]{1,0:T(8,128)(2,1)} %get-tuple-element.95.refs_0_, ...), custom_call_target="tpu_custom_call" | custom-call | flops 34359738368 | bytes 16777216 | tf_op jit(solution)/shard_map/pallas_call | solution.py:538
  358.6 1.4 slice_bitcast_fusion.2
  359.9 43.4 %shard_map.313 = (bf16[2048,1536]{1,0:T(8,128)(2,1)}, bf16[512,768]{1,0:T(8,128)(2,1)}, bf16[2048,768]{1,0:T(8,128)(2,1)}, bf16[512,768]{1,0:T(8,128)(2,1)}, f32...) custom-call(bf16[512,768]{1,0:T(8,128)(2,1)} %get-tuple-element.98.refs_0_, ...), custom_call_target="tpu_custom_call" | custom-call | flops 34359738368 | bytes 16777216 | tf_op jit(solution)/shard_map/pallas_call | solution.py:538
  403.4 1.4 slice_bitcast_fusion
  404.7 43.2 %shard_map.314 = (bf16[2048,1536]{1,0:T(8,128)(2,1)}, bf16[512,768]{1,0:T(8,128)(2,1)}, bf16[2048,768]{1,0:T(8,128)(2,1)}, bf16[8,256,768]{2,1,0:T(8,128)(2,1)}, bf16[512,768]{1,0:T(8,128)(2,1)}) custom-call(bf16[512,768]{1,0:T(8,128)(2,1)} %get-tuple-element.103.refs_0_, bf16[512,768]{1,0:T(8,128)(2,1)} %get-tuple-element.138.refs_1_, ...), custom_call_target="tpu_custom_call" | custom-call | flops 34359738368 | bytes 16777216 | tf_op jit(solution)/shard_map/pallas_call | solution.py:538
  447.9 103.5 %shard_map.315 = (f32[512,768]{1,0:T(8,128)}, f32[48,768]{1,0:T(8,128)}, f32[48,768]{1,0:T(8,128)}, f32[48,768]{1,0:T(8,128)}, f32[48,768]{1,0:T(8,128)}, /*inde...) custom-call(bf16[2048,768]{1,0:T(8,128)(2,1)} %bitcast.53, ...), custom_call_target="tpu_custom_call" | custom-call | tf_op jit(solution)/shard_map/pallas_call | solution.py:1236
  551.5 1.1 convert_reduce_fusion.1
  552.6 1.6 convert_add_fusion.1
  554.2 1.2 convert_reduce_fusion
  555.4 1.0 convert_add_fusion
  556.3 0.8 fusion.3
  557.1 0.7 fusion.4
  557.8 0.7 fusion.6
  558.6 0.9 fusion.8
  559.4 0.6 fusion
  560.0 8.9 %shard_map.316 = bf16[32,256,768]{2,1,0:T(8,128)(2,1)} custom-call(bf16[8,256,768]{2,1,0:T(8,128)(2,1)} %get-tuple-element.160.refs_0_, bf16[8,256,768]{2,1,0:T(8,128)(2,1)} %get-tuple-element.161.refs_1_, bf16[8,256,768]{2,1,0:T(8,128)(2,1)} %get-tuple-element.162.refs_2_, bf16[8,256,768]{2,1,0:T(8,128)(2,1)} %get-tuple-element.163.refs_3_), custom_call_target="tpu_custom_call" | custom-call | tf_op jit(solution)/shard_map/pallas_call | solution.py:1276
  568.9 0.6 fusion.2
  569.5 1.1 copy.37
  (11 shorter events, 0.0 us)
Async XLA Ops:
  176.9 34.8 %copy-start.5 = (f32[768]{0:T(1024)S(1)}, f32[768]{0:T(1024)}, u32[]{:S(2)}) copy-start(f32[768]{0:T(1024)} %param.32) | copy-start | bytes 9220
  551.4 5.7 copy-start.3
  551.4 5.7 copy-start.4
  551.5 6.4 %copy-start.1 = (f32[48,768]{1,0:T(8,128)S(1)}, f32[48,768]{1,0:T(8,128)}, u32[]{:S(2)}) copy-start(f32[48,768]{1,0:T(8,128)} %get-tuple-element.166) | copy-start | bytes 442372
  551.5 6.4 %copy-start.2 = (f32[48,768]{1,0:T(8,128)S(1)}, f32[48,768]{1,0:T(8,128)}, u32[]{:S(2)}) copy-start(f32[48,768]{1,0:T(8,128)} %get-tuple-element.165) | copy-start | bytes 442372
  560.0 9.5 %copy-start = (f32[512,768]{1,0:T(8,128)S(1)}, f32[512,768]{1,0:T(8,128)}, u32[]{:S(2)}) copy-start(f32[512,768]{1,0:T(8,128)} %get-tuple-element.159) | copy-start | bytes 4718596

commit v6 on v5

--- a/solution.py
+++ b/solution.py
@@ -206,6 +206,8 @@
     def slab(self, z, y, x, lanes):
         return self.held.at[self.index(z, y, x, lanes)]
 
+    given = slab
+
     def remote(self, n, source, target, device):
         return pltpu.make_async_remote_copy(
             src_ref=source,
@@ -229,10 +231,10 @@
         copies = []
         for k in range(1, x_size):
             there = rem(self.x + k, x_size)
-            copies.append((self.slab(EVERY, EVERY, there, left), self.got1x.at[k - 1], {"x": there}))
+            copies.append((self.given(EVERY, EVERY, there, left), self.got1x.at[k - 1], {"x": there}))
         for k in range(1, y_size):
             there = rem(self.y + k, y_size)
-            copies.append((self.slab(EVERY, there, EVERY, right), self.got1y.at[k - 1], {"y": there}))
+            copies.append((self.given(EVERY, there, EVERY, right), self.got1y.at[k - 1], {"y": there}))
         return [self.remote(1 + n, *copy) for n, copy in enumerate(copies)]
 
     def third(self):
@@ -308,6 +310,48 @@
             for k in range(x_size - 1):
                 total += self.got2x[k, z].astype(F32)
             out_ref[z, :, h:] = total.astype(BF)
+
+
+class Halved(Reducer):
+    def scratch(self):
+        z, y, x, _ = self.sizes
+        r, w, h = self.rows, self.lanes, self.half
+        crossing = x + y - 2
+        return [
+            pltpu.VMEM((z, y, x, r, w), BF),
+            pltpu.VMEM((x - 1, z, y, r, h), BF),
+            pltpu.VMEM((y - 1, z, x, r, h), BF),
+            pltpu.VMEM((y - 1, z, r, h), BF),
+            pltpu.VMEM((x - 1, z, r, h), BF),
+            pltpu.SemaphoreType.DMA((1,)),
+            pltpu.SemaphoreType.DMA((1 + 2 * crossing,)),
+            pltpu.SemaphoreType.DMA((1 + 2 * crossing,)),
+        ]
+
+    def bind(self, source, refs):
+        self.source = source
+        self.held, self.got1x, self.got1y, self.got2y, self.got2x = refs[:5]
+        self.local, self.send, self.receive = refs[5:]
+        self.z, self.y, self.x, self.c = (lax.axis_index(name) for name in ALL)
+        return self
+
+    def given(self, z, y, x, lanes):
+        return self.source.at[self.index(z, y, x, lanes)]
+
+    def first(self):
+        return [pltpu.make_async_copy(self.source, self.held, self.local.at[0])]
+
+    def begin(self):
+        for copy in self.first() + self.second():
+            copy.start()
+
+    def after_first(self):
+        pass
+
+    def after_second(self):
+        for copy in self.first():
+            copy.wait()
+        super().after_second()
 
 
 class Resident(Reducer):
@@ -485,21 +529,26 @@
     return groups
 
 
-def carried(courier, reducer, body):
+def carried(courier, reducers, body):
     jobs = len(courier.jobs)
-    sums = 0 if reducer is None else 1
+    sums = len(reducers)
+    parts = [len(one.scratch()) for one in reducers]
 
     def kernel(ins, outs, scratch, refs):
         own_in, sources, summands, own_out, targets, results, own_scratch, sems, rest = split_refs(
-            refs, ins, jobs, sums, outs, jobs, sums, scratch, 3, 9 * sums
+            refs, ins, jobs, sums, outs, jobs, sums, scratch, 3, sum(parts)
         )
         step = pl.program_id(0)
+        work = split_refs(rest, *parts)
+
+        def bound():
+            return [one.bind(value, refs) for one, value, refs in zip(reducers, summands, work)]
 
         @pl.when(step == 0)
         def _():
             courier.start(sources, targets, sems)
-            if sums:
-                reducer.bind(summands[0], rest).begin()
+            for one in bound():
+                one.begin()
 
         body(own_in, own_out, own_scratch)
 
@@ -507,44 +556,48 @@
 
             @pl.when(step == 1)
             def _():
-                reducer.bind(summands[0], rest).after_first()
+                for one in bound():
+                    one.after_first()
 
             @pl.when(step == 3)
             def _():
-                reducer.bind(summands[0], rest).after_second()
+                for one in bound():
+                    one.after_second()
 
         @pl.when(step == PAIRS - 1)
         def _():
-            if sums:
-                reducer.bind(summands[0], rest).after_third(results[0])
+            for one, result in zip(bound(), results):
+                one.after_third(result)
             courier.wait(sources, targets, sems)
 
     return kernel
 
 
-def call(courier, ident, body, args, in_specs, out_shape, out_specs, scratch, flops, summand=None):
-    reducer = None
-    extra_in, extra_out, extra_out_specs, extra_scratch = [], [], [], []
-    if summand is not None:
+def call(courier, ident, body, args, in_specs, out_shape, out_specs, scratch, flops, summands=()):
+    if summands:
         courier.in_plane = True
-        reducer = Reducer(courier.sizes, summand.shape)
-        shape = (PLANES,) + summand.shape[-2:]
-        extra_in = [summand]
-        extra_out = [jax.ShapeDtypeStruct(shape, BF)]
-        extra_out_specs = [pl.BlockSpec(shape, lambda p: (0, 0, 0))]
-        extra_scratch = reducer.scratch()
-    kernel = carried(courier, reducer, body)
+    reducers = [
+        (Halved if value.ndim == 5 else Reducer)(courier.sizes, value.shape) for value in summands
+    ]
+    shapes = [(PLANES,) + value.shape[-2:] for value in summands]
+    kernel = carried(courier, reducers, body)
     counts = (len(args), len(out_shape), len(scratch))
     outs = pl.pallas_call(
         lambda *refs: kernel(*counts, refs),
         grid=(PAIRS,),
-        out_shape=out_shape + courier.out_shape() + extra_out,
-        in_specs=in_specs + courier.specs() + [pl.BlockSpec(memory_space=pl.ANY)] * len(extra_in),
-        out_specs=out_specs + courier.specs() + extra_out_specs,
-        scratch_shapes=scratch + courier.scratch() + extra_scratch,
+        out_shape=out_shape
+        + courier.out_shape()
+        + [jax.ShapeDtypeStruct(shape, BF) for shape in shapes],
+        in_specs=in_specs + courier.specs() + [pl.BlockSpec(memory_space=pl.ANY)] * len(shapes),
+        out_specs=out_specs
+        + courier.specs()
+        + [pl.BlockSpec(shape, lambda p: (0, 0, 0)) for shape in shapes],
+        scratch_shapes=scratch
+        + courier.scratch()
+        + [ref for one in reducers for ref in one.scratch()],
         compiler_params=courier.params(ident),
         cost_estimate=pl.CostEstimate(flops=flops, bytes_accessed=2**24, transcendentals=2**20),
-    )(*args, *courier.values(), *extra_in)
+    )(*args, *courier.values(), *summands)
     return outs[: len(out_shape)], outs[len(out_shape) :]
 
 
@@ -714,7 +767,7 @@
     return jnp.concatenate(both, axis=0).T
 
 
-def middle_kernel(*refs, devices, packed):
+def middle_kernel(*refs, sizes, packed):
     (
         part0,
         part1,
@@ -745,8 +798,32 @@
         n3_ref,
         total_ref,
         dn3_ref,
-    ) = refs
+    ) = refs[: 29 + (not packed)]
     step = pl.program_id(0)
+    last = pl.num_programs(0) - 1
+    devices = sizes[0] * sizes[1] * sizes[2] * sizes[3]
+    if packed:
+        wide_ref, wide_got, tall_ref, tall_got, send, receive = refs[29:]
+        core = lax.axis_index("c")
+
+    def exchange(n):
+        slot = rem(n, 2)
+        return [
+            pltpu.make_async_remote_copy(
+                src_ref=source,
+                dst_ref=target,
+                send_sem=send.at[n, at],
+                recv_sem=receive.at[n, at],
+                device_id={"c": 1 - core},
+                device_id_type=pl.DeviceIdType.MESH,
+            )
+            for at, (source, target) in enumerate(
+                (
+                    (wide_ref.at[slot, :, :, :, 1 - core], wide_got.at[n]),
+                    (tall_ref.at[slot, :, :, 1 - core], tall_got.at[n]),
+                )
+            )
+        ]
     parts = (part0, part1, part2, part3)
     lses = (lse0, lse1, lse2, lse3)
 
@@ -770,28 +847,52 @@
         n3_ref[...] = rms(hidden, gain_ref[...]).astype(BF)
         total_ref[...] = hidden
         dn3_ref[...] = jnp.zeros_like(dn3_ref)
-
-    normed = n3_ref[...]
-    branch = cot_ref[...]
-    gate_vals = dot(normed, gate_ref[...], 1, 0)
-    up_vals = dot(normed, up_ref[...], 1, 0)
-    grad_inner = dot(branch, down_ref[...], 1, 1)
-    gelu, slope = glu_parts(gate_vals)
-    inner = (gelu * up_vals).astype(BF)
-    grad_gate = (grad_inner * up_vals * slope).astype(BF)
-    grad_up = (grad_inner * gelu).astype(BF)
-    total_ref[...] += dot(inner, down_ref[...], 1, 0)
-    dn3_ref[...] += dot(grad_gate, gate_ref[...], 1, 1) + dot(grad_up, up_ref[...], 1, 1)
-    terms = [dot(normed, grad_gate, 0, 0), dot(normed, grad_up, 0, 0)]
+        if packed:
+            barrier = pltpu.get_barrier_semaphore()
+            pl.semaphore_signal(
+                barrier,
+                inc=1,
+                device_id={"c": 1 - core},
+                device_id_type=pl.DeviceIdType.MESH,
+            )
+            pl.semaphore_wait(barrier, 1)
+
+    def one_chunk():
+        normed = n3_ref[...]
+        branch = cot_ref[...]
+        gate_vals = dot(normed, gate_ref[...], 1, 0)
+        up_vals = dot(normed, up_ref[...], 1, 0)
+        grad_inner = dot(branch, down_ref[...], 1, 1)
+        gelu, slope = glu_parts(gate_vals)
+        inner = (gelu * up_vals).astype(BF)
+        grad_gate = (grad_inner * up_vals * slope).astype(BF)
+        grad_up = (grad_inner * gelu).astype(BF)
+        total_ref[...] += dot(inner, down_ref[...], 1, 0)
+        dn3_ref[...] += dot(grad_gate, gate_ref[...], 1, 1) + dot(grad_up, up_ref[...], 1, 1)
+        terms = [dot(normed, grad_gate, 0, 0), dot(normed, grad_up, 0, 0)]
+        if packed:
+            shape = (devices, terms[0].shape[0] // devices, terms[0].shape[1])
+            both = jnp.concatenate([t.reshape(shape) for t in terms], axis=1).astype(BF)
+            slot = rem(step, 2)
+            wide_ref[slot] = both.reshape(wide_ref.shape[1:])
+            tall_ref[slot] = dot(inner, branch, 0, 0).astype(BF).reshape(tall_ref.shape[1:])
+            for copy in exchange(step):
+                copy.start()
+        else:
+            for ref, term in zip(grad_refs, terms):
+                ref[...] = term
+            gdown_ref[...] = dot(inner, branch, 0, 0).astype(BF).reshape(gdown_ref.shape)
+
     if packed:
-        shape = (devices, terms[0].shape[0] // devices, terms[0].shape[1])
-        grad_refs[0][...] = jnp.concatenate([t.reshape(shape) for t in terms], axis=1).astype(BF)
+
+        @pl.when(step < last)
+        def _():
+            one_chunk()
+
     else:
-        for ref, term in zip(grad_refs, terms):
-            ref[...] = term
-    gdown_ref[...] = dot(inner, branch, 0, 0).astype(BF).reshape(gdown_ref.shape)
-
-    @pl.when(step == pl.num_programs(0) - 1)
+        one_chunk()
+
+    @pl.when(step == last)
     def _():
         out_ref[...] = total_ref[...].astype(BF)
         hidden = h2_ref[...]
@@ -813,30 +914,77 @@
                     product[h * HD : (h + 1) * HD], axis=0, keepdims=True
                 )
 
-
-def middle(devices, parts, lses, hidden, out_weight, gain, cotangent, gate, up, down):
+    if packed:
+
+        @pl.when(step > 0)
+        def _():
+            before = step - 1
+            slot = rem(before, 2)
+            for copy in exchange(before):
+                copy.wait()
+            mine = wide_ref[slot, :, :, :, core].astype(F32)
+            grad_refs[0][...] = (mine + wide_got[before].astype(F32)).astype(BF)
+            mine = tall_ref[slot, :, :, core].astype(F32)
+            gdown_ref[0] = (mine + tall_got[before].astype(F32)).astype(BF)
+
+
+def middle(sizes, parts, lses, hidden, out_weight, gain, cotangent, gate, up, down):
     tokens, width = hidden.shape
     inner = gate.shape[1]
     chunk = 512
+    count = inner // chunk
+    devices = sizes[0] * sizes[1] * sizes[2] * sizes[3]
     share = width // devices
-    packed = share % 8 == 0
     down_share = inner // devices
+    packed = share % 8 == 0 and chunk * PLANES == inner
+    first = lambda p: jnp.minimum(p, count - 1)
     fixed = lambda *shape: pl.BlockSpec(shape, lambda p: (0,) * len(shape))
     whole = fixed(tokens, width)
     square = fixed(width, width)
     stat = fixed(PAIRS, 2, tokens)
-    column = pl.BlockSpec((width, chunk), lambda p: (0, p))
+    column = pl.BlockSpec((width, chunk), lambda p: (0, first(p)))
+    scratch = [
+        pltpu.VMEM((tokens, width), F32),
+        pltpu.VMEM((tokens, width), F32),
+        pltpu.VMEM((tokens, width), BF),
+        pltpu.VMEM((tokens, width), F32),
+        pltpu.VMEM((tokens, width), F32),
+    ]
+    params = dict(vmem_limit_bytes=VMEM)
     if packed:
-        grad_shapes = [jax.ShapeDtypeStruct((devices, 2 * share, inner), BF)]
-        grad_specs = [pl.BlockSpec((devices, 2 * share, chunk), lambda p: (0, 0, p))]
+        z, y, x, c = sizes
+        wide_shape = (z, y, x, 2 * share)
+        tall_shape = (y, x, down_share, width)
+        grad_shapes = [
+            jax.ShapeDtypeStruct(wide_shape + (inner,), BF),
+            jax.ShapeDtypeStruct((z,) + tall_shape, BF),
+        ]
+        before = lambda p: jnp.maximum(p - 1, 0)
+        grad_specs = [
+            pl.BlockSpec(wide_shape + (chunk,), lambda p: (0, 0, 0, 0, before(p))),
+            pl.BlockSpec((1,) + tall_shape, lambda p: (before(p), 0, 0, 0, 0)),
+        ]
+        scratch += [
+            pltpu.VMEM((2, z, y, x, c, 2 * share, chunk), BF),
+            pltpu.VMEM((count,) + wide_shape + (chunk,), BF),
+            pltpu.VMEM((2, y, x, c, down_share, width), BF),
+            pltpu.VMEM((count,) + tall_shape, BF),
+            pltpu.SemaphoreType.DMA((count, 2)),
+            pltpu.SemaphoreType.DMA((count, 2)),
+        ]
+        params.update(collective_id=12, has_side_effects=True)
     else:
         grad_shapes = [jax.ShapeDtypeStruct((width, inner), F32)] * 2
+        grad_shapes.append(jax.ShapeDtypeStruct((devices, down_share, width), BF))
         grad_specs = [column] * 2
+        grad_specs.append(
+            pl.BlockSpec((chunk // down_share, down_share, width), lambda p: (p, 0, 0))
+        )
     rows = jax.ShapeDtypeStruct((tokens, width), BF)
     wide = jax.ShapeDtypeStruct((tokens, width), F32)
     return pl.pallas_call(
-        functools.partial(middle_kernel, devices=devices, packed=packed),
-        grid=(inner // chunk,),
+        functools.partial(middle_kernel, sizes=sizes, packed=packed),
+        grid=(count + packed,),
         out_shape=[
             rows,
             rows,
@@ -846,24 +994,16 @@
             jax.ShapeDtypeStruct((1, width), F32),
             jax.ShapeDtypeStruct((width, width), BF),
         ]
-        + grad_shapes
-        + [jax.ShapeDtypeStruct((devices, down_share, width), BF)],
+        + grad_shapes,
         in_specs=[whole] * 4
         + [stat] * 4
         + [whole, square, fixed(1, width), whole]
-        + [column, column, pl.BlockSpec((chunk, width), lambda p: (p, 0))],
+        + [column, column, pl.BlockSpec((chunk, width), lambda p: (first(p), 0))],
         out_specs=[whole] * 4
         + [fixed(2, PAIRS, 2, tokens), fixed(1, width), square]
-        + grad_specs
-        + [pl.BlockSpec((chunk // down_share, down_share, width), lambda p: (p, 0, 0))],
-        scratch_shapes=[
-            pltpu.VMEM((tokens, width), F32),
-            pltpu.VMEM((tokens, width), F32),
-            pltpu.VMEM((tokens, width), BF),
-            pltpu.VMEM((tokens, width), F32),
-            pltpu.VMEM((tokens, width), F32),
-        ],
-        compiler_params=pltpu.CompilerParams(vmem_limit_bytes=VMEM),
+        + grad_specs,
+        scratch_shapes=scratch,
+        compiler_params=pltpu.CompilerParams(**params),
     )(*parts, *lses, hidden, out_weight, gain, cotangent, gate, up, down)
 
 
@@ -900,7 +1040,7 @@
 
 
 def cross_backward(
-    courier, ident, queries, grad, keyvals, lens, lse, delta, key_weight, value_weight, summand=None
+    courier, ident, queries, grad, keyvals, lens, lse, delta, key_weight, value_weight, summands=()
 ):
     tokens, keys = queries.shape[0], keyvals.shape[0]
     width = H * HD
@@ -948,7 +1088,7 @@
         [spec["pair"], spec["col"], spec["rows"]],
         [pltpu.VMEM((keys, width), F32)],
         2**35,
-        summand,
+        summands,
     )
 
 
@@ -1001,7 +1141,7 @@
         [spec["col"]] * 3,
         [],
         2**33,
-        summand,
+        [summand],
     )
 
 
@@ -1026,11 +1166,12 @@
     share = width // devices
     chunk = 512
     cuts = keys // chunk
-    groups = [Resident(sizes, (2 * share, width)) for _ in range(4)]
+    groups = [Resident(sizes, (2 * share, width)) for _ in range(2)]
+    groups += [Resident(sizes, (2 * share, 256)) for _ in range(6)]
     small = SmallSum(sizes, (8, width))
     early = [two] + list(held) + list(grad_q[:-1])
     far = list(rows) + list(grads) + early
-    counts = (len(far), len(small_in) + 1, jobs, 6, jobs - 1, 4, len(early) - 1, 8, 3, 40, 10)
+    counts = (len(far), len(small_in) + 1, jobs, 6, jobs - 1, 4, len(early) - 1, 8, 3, 80, 10)
 
     def pack(ref, first, second, cols=EVERY):
         lanes = first.shape[1]
@@ -1045,8 +1186,8 @@
         self_gain, cross_gain, ffn_term, lse_ref = near
         grad_in, *sums, norm_sums = outs
         row_buf, grad_buf, total, load_sems = stage
-        dq_got, da_ref, dq1, dk1, dv1, *_ = work
-        chunk_sems, early_sems = load_sems, work[5]
+        dq_got, da_ref, dq1, dk1, dv1, normed_ref, *_ = work
+        chunk_sems, early_sems = load_sems, work[6]
         copies = courier.copies(sources, [dq_got] + list(targets), sems)
         courier.greet()
         for copy in copies:
@@ -1133,64 +1274,52 @@
         low_ref = dq_got
         low_ref[...] = grad_in[...].astype(BF)
         da_ref[...] = dot(low_ref[...], wo_ref[...], 1, 1).astype(BF)
-
-        @pl.loop(0, PAIRS)
-        def _(p):
-            cols = pl.ds(pl.multiple_of(p * 128, 128), 128)
-            grad_kv, grad_q_p = backward_pair(
-                q_ref[:, cols],
-                da_ref[:, cols],
-                k_ref[:, cols],
-                v_ref[:, cols],
-                None,
-                [lse_ref[p, h : h + 1, :] for h in range(2)],
-                None,
+        values = x_ref[...].astype(F32)
+        normed_ref[...] = rms(values, self_gain[...]).astype(BF)
+
+        for third in range(3):
+
+            @pl.loop(2 * third, 2 * third + 2)
+            def _(p):
+                cols = pl.ds(pl.multiple_of(p * 128, 128), 128)
+                grad_kv, grad_q_p = backward_pair(
+                    q_ref[:, cols],
+                    da_ref[:, cols],
+                    k_ref[:, cols],
+                    v_ref[:, cols],
+                    None,
+                    [lse_ref[p, h : h + 1, :] for h in range(2)],
+                    None,
+                )
+                dq1[:, cols] = grad_q_p
+                dk1[:, cols] = grad_kv[:, :128]
+                dv1[:, cols] = grad_kv[:, 128:]
+
+            cols = pl.ds(third * 256, 256)
+            near_sum, far_sum = bound[2 + 2 * third], bound[3 + 2 * third]
+            normed = normed_ref[...]
+            pack(near_sum.held, dot(normed, dq1[:, cols], 0, 0), dot(normed, dk1[:, cols], 0, 0))
+            near_sum.begin()
+            pack(
+                far_sum.held,
+                dot(normed, dv1[:, cols], 0, 0),
+                dot(attn_ref[...], low_ref[:, cols], 0, 0),
             )
-            dq1[:, cols] = grad_q_p
-            dk1[:, cols] = grad_kv[:, :128]
-            dv1[:, cols] = grad_kv[:, 128:]
-
-            @pl.when(p == 1)
-            def _():
+            far_sum.begin()
+            if third == 0:
                 bound[0].after_second()
                 bound[1].after_first()
-
-            @pl.when(p == 3)
-            def _():
+            if third == 1:
                 bound[0].after_third_start()
                 bound[1].after_second()
-
-            @pl.when(p == 5)
-            def _():
+                bound[2].after_first()
+                bound[3].after_first()
+            if third == 2:
                 bound[1].after_third_start()
-
-        values = x_ref[...].astype(F32)
-        normed_ref = da_ref
-        normed_ref[...] = rms(values, self_gain[...]).astype(BF)
-
-        @pl.loop(0, 3)
-        def _(i):
-            cols = pl.ds(pl.multiple_of(i * 256, 256), 256)
-            pack(
-                bound[2].held,
-                dot(normed_ref[...], dv1[:, cols], 0, 0),
-                dot(attn_ref[...], low_ref[:, cols], 0, 0),
-                cols,
-            )
-
-        bound[2].begin()
-
-        @pl.loop(0, 3)
-        def _(i):
-            cols = pl.ds(pl.multiple_of(i * 256, 256), 256)
-            pack(
-                bound[3].held,
-                dot(normed_ref[...], dq1[:, cols], 0, 0),
-                dot(normed_ref[...], dk1[:, cols], 0, 0),
-                cols,
-            )
-
-        bound[3].begin()
+                bound[2].after_second()
+                bound[3].after_second()
+                bound[4].after_first()
+                bound[5].after_first()
         grad_normed = (
             dot(dq1[...], wq_ref[...], 1, 1)
             + dot(dk1[...], wk_ref[...], 1, 1)
@@ -1202,17 +1331,26 @@
             [self_norm, cross_norm, ffn_term[...], jnp.zeros((5, width), F32)], axis=0
         )
         bits.start(0)
-        bound[2].after_first()
-        bound[3].after_first()
-        bits.advance(0)
-        bound[2].after_second()
-        bound[3].after_second()
-        bits.advance(1)
         bound[2].after_third_start()
         bound[3].after_third_start()
+        bound[4].after_second()
+        bound[5].after_second()
+        bound[6].after_first()
+        bound[7].after_first()
+        bits.advance(0)
+        bound[4].after_third_start()
+        bound[5].after_third_start()
+        bound[6].after_second()
+        bound[7].after_second()
+        bits.advance(1)
+        bound[6].after_third_start()
+        bound[7].after_third_start()
         bits.advance(2)
-        for n in range(4):
-            bound[n].finish(sums[n])
+        bound[0].finish(sums[0])
+        bound[1].finish(sums[1])
+        for n in range(2, 8):
+            third, kind = divmod(n - 2, 2)
+            bound[n].finish(sums[2 + kind].at[:, pl.ds(third * 256, 256)])
         bits.advance(3, norm_sums)
         for n, copy in enumerate(copies):
             if n != 1:
@@ -1228,8 +1366,8 @@
         pltpu.SemaphoreType.DMA((2, 2)),
     ]
     scratch += [pltpu.VMEM(v.shape, v.dtype) for v in early[1:]]
-    scratch += [row] * 5 + [pltpu.SemaphoreType.DMA((len(early),))]
-    scratch += [pltpu.SemaphoreType.DMA((1,))] * 2 + courier.scratch()
+    scratch += [row] * 6 + [pltpu.SemaphoreType.DMA((len(early),))]
+    scratch += [pltpu.SemaphoreType.DMA((1,))] + courier.scratch()
     for one in groups:
         scratch += one.scratch()
     scratch += small.scratch()
@@ -1387,7 +1525,7 @@
         *grads_in,
         grad_down,
     ) = middle(
-        devices,
+        sizes,
         [partial[r] for r in range(PLANES)],
         [stats_out[r] for r in range(PLANES)],
         hidden_one,
@@ -1400,10 +1538,12 @@
     )
     decoder_out = output[None]
     if len(grads_in) == 2:
-        summand = summand_of(sizes, grads_in)
+        summands = {
+            0: [summand_of(sizes, grads_in)],
+            1: [grad_down.reshape(tuple(sizes) + grad_down.shape[1:])],
+        }
     else:
-        summand = grads_in[0].reshape(tuple(sizes) + grads_in[0].shape[1:])
-    summands = {0: summand, 1: grad_down.reshape(tuple(sizes) + grad_down.shape[1:])}
+        summands = {0: [grads_in[0], grad_down]}
     left, got = {}, {}
 
     grads = {0: grad_attn_two}
@@ -1429,11 +1569,12 @@
             both[r][1],
             cross_key,
             cross_value,
-            summands.get(r),
+            summands.get(r, []),
         )
         moved = list(moved)
         if r in summands:
-            left[r] = moved.pop()
+            for value in moved[len(moved) - len(summands[r]) :]:
+                left[len(left)] = value
         if r + 1 < PLANES:
             grads[r + 1], both[r + 1] = moved.pop(0), moved.pop(0)
         if r >= 1:
@@ -1469,10 +1610,10 @@
             decoder_in_grad[None],
             memory_grad,
             norm_self_sum,
+            sums[2][:part],
+            sums[2][part:],
             sums[3][:part],
             sums[3][part:],
-            sums[2][:part],
-            sums[2][part:],
             norm_cross_sum,
             sums[1][:part],
             sums[0][:part],

time: 577 us -> 542 us (0.939)
  Pallas kernels: 550 us -> 514 us
    pallas_call x8, Pallas kernels: 365 us -> 340 us  [call(): pl.pallas_call(lambda *refs: kernel(*counts, refs), grid=(PAIRS,), out_sh...]
    pallas_call x1, Pallas kernels: 103 us -> 90.4 us  [ending(): pl.pallas_call(kernel, out_shape=[jax.ShapeDtypeStruct((tokens, width), F...]
where the time goes in v6:
time: 542 us; the launch traced here: 536 us
  Pallas kernels  514 us (95%)
  local copies, waits for them, and re-layouts  15.5 us (3%)
    pallas_call x8, Pallas kernels, call(): pl.pallas_call(lambda *refs: kernel(*counts, refs), grid=(PAIRS,), out_sh...  340 us
    pallas_call x1, Pallas kernels, ending(): pl.pallas_call(kernel, out_shape=[jax.ShapeDtypeStruct((tokens, width), F...  90.4 us
    pallas_call x1, Pallas kernels, self_part(): pl.pallas_call(kernel, out_shape=[rows, rows, rows, stat, rows, wide, row...  44.6 us
    pallas_call x1, Pallas kernels, middle(): pl.pallas_call(functools.partial(middle_kernel, sizes=sizes, packed=packe...  29.6 us

profile of v6, /device:TPU:0, one launch (start us, length us, event | category | flops | bytes accessed | tf_op | source)
XLA Modules:
  0.0 535.9 jit_solution(11552862790069262111)
XLA Ops:
  1.3 0.6 broadcast_in_dim.28.refs_9_.refs_10_.refs_11_.refs_2_.refs_3_
  1.9 1.3 broadcast_in_dim.25.refs_1_.refs_24_
  3.2 1.3 broadcast_in_dim.26.refs_2_.refs_25_
  4.4 44.6 %shard_map.305 = (bf16[512,768]{1,0:T(8,128)(2,1)}, bf16[512,768]{1,0:T(8,128)(2,1)}, bf16[512,768]{1,0:T(8,128)(2,1)}, f32[6,2,512]{2,1,0:T(2,128)}, bf16[512,7...) custom-call(bf16[512,768]{1,0:T(8,128)(2,1)} %bitcast.42, ...), custom_call_target="tpu_custom_call" | custom-call | tf_op jit(solution)/shard_map/pallas_call | solution.py:744
  49.1 43.6 %shard_map.306 = (bf16[512,768]{1,0:T(8,128)(2,1)}, f32[6,2,512]{2,1,0:T(2,128)}, bf16[2048,1536]{1,0:T(8,128)(2,1)}, bf16[8,256,768]{2,1,0:T(8,128)(2,1)}, bf16[512,768]{1,0:T(8,128)(2,1)}) custom-call(bf16[512,768]{1,0:T(8,128)(2,1)} %get-tuple-element.95.refs_0_, bf16[2048,768]{1,0:T(8,128)(2,1)} %bitcast.44, s32[8,128]{1,0:T(8,128)} %get-tuple-element.97.refs_2_.refs_3_, ...), custom_call_target="tpu_custom_call" | custom-call | flops 17179869184 | bytes 16777216 | tf_op jit(solution)/shard_map/pallas_call | solution.py:585
  92.7 42.5 %shard_map.307 = (bf16[512,768]{1,0:T(8,128)(2,1)}, f32[6,2,512]{2,1,0:T(2,128)}, bf16[2048,1536]{1,0:T(8,128)(2,1)}, bf16[8,256,768]{2,1,0:T(8,128)(2,1)}, bf16...) custom-call(bf16[512,768]{1,0:T(8,128)(2,1)} %get-tuple-element.98.refs_0_, ...), custom_call_target="tpu_custom_call" | custom-call | flops 17179869184 | bytes 16777216 | tf_op jit(solution)/shard_map/pallas_call | solution.py:585
  135.2 41.5 %shard_map.308 = (bf16[512,768]{1,0:T(8,128)(2,1)}, f32[6,2,512]{2,1,0:T(2,128)}, bf16[2048,1536]{1,0:T(8,128)(2,1)}, bf16[8,256,768]{2,1,0:T(8,128)(2,1)}, bf16...) custom-call(bf16[512,768]{1,0:T(8,128)(2,1)} %get-tuple-element.103.refs_0_, bf16[2048,768]{1,0:T(8,128)(2,1)} %bitcast.48, ...), custom_call_target="tpu_custom_call" | custom-call | flops 17179869184 | bytes 16777216 | tf_op jit(solution)/shard_map/pallas_call | solution.py:585
  176.6 34.8 %shard_map.309 = (bf16[512,768]{1,0:T(8,128)(2,1)}, f32[6,2,512]{2,1,0:T(2,128)}, bf16[2048,1536]{1,0:T(8,128)(2,1)}, bf16[512,768]{1,0:T(8,128)(2,1)}, f32[6,2,512]{2,1,0:T(2,128)}) custom-call(bf16[512,768]{1,0:T(8,128)(2,1)} %get-tuple-element.94.refs_6_.refs_0_, bf16[2048,768]{1,0:T(8,128)(2,1)} %bitcast.50, ...), custom_call_target="tpu_custom_call" | custom-call | flops 17179869184 | bytes 16777216 | tf_op jit(solution)/shard_map/pallas_call | solution.py:585
  211.5 0.6 broadcast_in_dim.29.refs_10_
  212.1 29.6 %shard_map.310 = (bf16[512,768]{1,0:T(8,128)(2,1)}, bf16[512,768]{1,0:T(8,128)(2,1)}, f32[512,768]{1,0:T(8,128)}, bf16[512,768]{1,0:T(8,128)(2,1)}, f32[2,6,2,51...) custom-call(bf16[512,768]{1,0:T(8,128)(2,1)} %get-tuple-element.111., ...), custom_call_target="tpu_custom_call" | custom-call | tf_op jit(solution)/shard_map/pallas_call | solution.py:985
  241.7 1.4 slice_bitcast_fusion.6
  243.1 47.3 %shard_map.311 = (bf16[2048,1536]{1,0:T(8,128)(2,1)}, bf16[512,768]{1,0:T(8,128)(2,1)}, bf16[2048,768]{1,0:T(8,128)(2,1)}, bf16[512,768]{1,0:T(8,128)(2,1)}, f32...) custom-call(bf16[512,768]{1,0:T(8,128)(2,1)} %get-tuple-element.94.refs_6_.refs_0_, ...), custom_call_target="tpu_custom_call" | custom-call | flops 34359738368 | bytes 16777216 | tf_op jit(solution)/shard_map/pallas_call | solution.py:585
  290.4 1.4 slice_bitcast_fusion.4
  291.8 43.4 %shard_map.312 = (bf16[2048,1536]{1,0:T(8,128)(2,1)}, bf16[512,768]{1,0:T(8,128)(2,1)}, bf16[2048,768]{1,0:T(8,128)(2,1)}, bf16[512,768]{1,0:T(8,128)(2,1)}, f32...) custom-call(bf16[512,768]{1,0:T(8,128)(2,1)} %get-tuple-element.95.refs_0_, ...), custom_call_target="tpu_custom_call" | custom-call | flops 34359738368 | bytes 16777216 | tf_op jit(solution)/shard_map/pallas_call | solution.py:585
  335.2 1.4 slice_bitcast_fusion.2
  336.6 44.0 %shard_map.313 = (bf16[2048,1536]{1,0:T(8,128)(2,1)}, bf16[512,768]{1,0:T(8,128)(2,1)}, bf16[2048,768]{1,0:T(8,128)(2,1)}, bf16[512,768]{1,0:T(8,128)(2,1)}, f32...) custom-call(bf16[512,768]{1,0:T(8,128)(2,1)} %get-tuple-element.98.refs_0_, ...), custom_call_target="tpu_custom_call" | custom-call | flops 34359738368 | bytes 16777216 | tf_op jit(solution)/shard_map/pallas_call | solution.py:585
  380.5 1.4 slice_bitcast_fusion
  381.9 43.3 %shard_map.314 = (bf16[2048,1536]{1,0:T(8,128)(2,1)}, bf16[512,768]{1,0:T(8,128)(2,1)}, bf16[2048,768]{1,0:T(8,128)(2,1)}, bf16[8,256,768]{2,1,0:T(8,128)(2,1)}, bf16[512,768]{1,0:T(8,128)(2,1)}) custom-call(bf16[512,768]{1,0:T(8,128)(2,1)} %get-tuple-element.103.refs_0_, bf16[512,768]{1,0:T(8,128)(2,1)} %get-tuple-element.138.refs_1_, ...), custom_call_target="tpu_custom_call" | custom-call | flops 34359738368 | bytes 16777216 | tf_op jit(solution)/shard_map/pallas_call | solution.py:585
  425.2 90.4 %shard_map.315 = (f32[512,768]{1,0:T(8,128)}, f32[48,768]{1,0:T(8,128)}, f32[48,768]{1,0:T(8,128)}, f32[48,768]{1,0:T(8,128)}, f32[48,768]{1,0:T(8,128)}, /*inde...) custom-call(bf16[2048,768]{1,0:T(8,128)(2,1)} %bitcast.51, ...), custom_call_target="tpu_custom_call" | custom-call | tf_op jit(solution)/shard_map/pallas_call | solution.py:1374
  515.7 1.1 convert_reduce_fusion.1
  516.8 1.6 convert_add_fusion.1
  518.4 1.2 convert_reduce_fusion
  519.6 1.0 convert_add_fusion
  520.5 0.8 fusion.3
  521.3 0.7 fusion.4
  522.0 0.7 fusion.6
  522.7 0.9 fusion.8
  523.6 0.6 fusion
  524.2 8.9 %shard_map.316 = bf16[32,256,768]{2,1,0:T(8,128)(2,1)} custom-call(bf16[8,256,768]{2,1,0:T(8,128)(2,1)} %get-tuple-element.160.refs_0_, bf16[8,256,768]{2,1,0:T(8,128)(2,1)} %get-tuple-element.161.refs_1_, bf16[8,256,768]{2,1,0:T(8,128)(2,1)} %get-tuple-element.162.refs_2_, bf16[8,256,768]{2,1,0:T(8,128)(2,1)} %get-tuple-element.163.refs_3_), custom_call_target="tpu_custom_call" | custom-call | tf_op jit(solution)/shard_map/pallas_call | solution.py:1414
  533.1 0.6 fusion.2
  533.7 0.9 copy.38
  534.6 1.1 copy.39
  (14 shorter events, 0.0 us)
Async XLA Ops:
  176.6 34.8 %copy-start.6 = (f32[768]{0:T(1024)S(1)}, f32[768]{0:T(1024)}, u32[]{:S(2)}) copy-start(f32[768]{0:T(1024)} %param.32) | copy-start | bytes 9220
  515.6 5.7 %copy-start.4 = (f32[48,768]{1,0:T(8,128)S(1)}, f32[48,768]{1,0:T(8,128)}, u32[]{:S(2)}) copy-start(f32[48,768]{1,0:T(8,128)} %get-tuple-element.168) | copy-start | bytes 442372
  515.6 5.7 %copy-start.5 = (f32[48,768]{1,0:T(8,128)S(1)}, f32[48,768]{1,0:T(8,128)}, u32[]{:S(2)}) copy-start(f32[48,768]{1,0:T(8,128)} %get-tuple-element.167) | copy-start | bytes 442372
  515.6 6.4 %copy-start.2 = (f32[48,768]{1,0:T(8,128)S(1)}, f32[48,768]{1,0:T(8,128)}, u32[]{:S(2)}) copy-start(f32[48,768]{1,0:T(8,128)} %get-tuple-element.165) | copy-start | bytes 442372
  515.7 6.4 %copy-start.3 = (f32[48,768]{1,0:T(8,128)S(1)}, f32[48,768]{1,0:T(8,128)}, u32[]{:S(2)}) copy-start(f32[48,768]{1,0:T(8,128)} %get-tuple-element.166) | copy-start | bytes 442372
  524.2 9.5 %copy-start.1 = (bf16[512,768]{1,0:T(8,128)(2,1)S(1)}, bf16[512,768]{1,0:T(8,128)(2,1)}, u32[]{:S(2)}) copy-start(bf16[512,768]{1,0:T(8,128)(2,1)} %get-tuple-element.120) | copy-start | bytes 2359300
  524.2 10.4 %copy-start = (f32[512,768]{1,0:T(8,128)S(1)}, f32[512,768]{1,0:T(8,128)}, u32[]{:S(2)}) copy-start(f32[512,768]{1,0:T(8,128)} %get-tuple-element.159) | copy-start | bytes 4718596

commit v7 on v6

--- a/solution.py
+++ b/solution.py
@@ -470,7 +470,8 @@
         else:
             all_scores.append(dot(keys * mine + bias * one, queries * mine + one, 1, 1))
     parts = []
-    lse = []
+    stats = []
+    held = []
     for h in range(2):
         mine, other, _ = masks[h]
         scores = all_scores[h]
@@ -480,22 +481,19 @@
         halves = (both[:HD], both[HD:])
         total = halves[1 - h]
         parts.append(halves[h] / total)
-        lse.append(row_max + jnp.log(total[0:1]))
-    return jnp.concatenate(parts, axis=0).T.astype(BF), lse
-
-
-def backward_pair(queries, grad, keys, values, bias, lse, delta):
+        stats.append((row_max + jnp.log(total[0:1]), row_max))
+        held.append(probs)
+    return jnp.concatenate(parts, axis=0).T.astype(BF), stats, held
+
+
+def backward_pair(queries, grad, keys, values, probs_of, delta):
     grad_k = None
     grad_v = None
     grad_q = []
     for h, (mine, other, one) in enumerate(lane_masks()):
         query_h = queries * mine
         grad_h = grad * mine
-        if bias is None:
-            scores = causal_mask(dot(keys, query_h, 1, 1))
-        else:
-            scores = dot(keys * mine + bias * one, query_h + one, 1, 1)
-        probs = jnp.exp(scores - lse[h])
+        probs = probs_of(h, keys, query_h)
         grad_p = dot(values, grad_h, 1, 1)
         if delta is None:
             delta_h = jnp.sum(probs * grad_p, axis=0, keepdims=True)
@@ -511,13 +509,13 @@
     return grad_kv, jnp.concatenate(grad_q, axis=0).T.astype(BF)
 
 
-def key_bias(keys, lens_ref):
+def causal_probs(lse):
+    return lambda h, keys, query: jnp.exp(causal_mask(dot(keys, query, 1, 1)) - lse[h])
+
+
+def key_bias(keys, lens):
     row = lax.broadcasted_iota(jnp.int32, (keys, 128), 0) + lax.axis_index("z") * keys
-    return jnp.where(row < lens_ref[0:1, :], 0.0, MASKED).astype(BF)
-
-
-def two_rows(ref):
-    return [ref[0, h : h + 1, :] for h in range(2)]
+    return jnp.where(row < lens[0:1, :], 0.0, MASKED).astype(BF)
 
 
 def split_refs(refs, *counts):
@@ -693,7 +691,6 @@
     return dict(
         col=pl.BlockSpec((tokens, 128), lambda p: (0, p)),
         pair=pl.BlockSpec((keys, 256), lambda p: (0, p)),
-        lens=pl.BlockSpec((8, 128), lambda p: (0, 0)),
         rows=pl.BlockSpec((keys, H * HD), lambda p: (0, 0)),
         weight=pl.BlockSpec((H * HD, 128), lambda p: (0, p)),
         stat=pl.BlockSpec((1, 2, tokens), lambda p: (p, 0, 0)),
@@ -705,51 +702,211 @@
     return values * r * gain
 
 
-def self_part(courier, ident, inputs, gains, weights):
+ORDER = (1, 2, 3, 0)
+
+
+def forward_part(sizes, ident, memory, lens, inputs, gains, weights, key_weight, value_weight):
     tokens, width = inputs.shape
-    jobs = len(courier.jobs)
+    positions = memory.shape[1]
+    plane = sizes[1] * sizes[2] * sizes[3]
+    keys = plane * positions
+    rows = jax.ShapeDtypeStruct((tokens, width), BF)
+    wide = jax.ShapeDtypeStruct((tokens, width), F32)
+    stat = jax.ShapeDtypeStruct((PAIRS, 2, tokens), F32)
+    near = range(1, PLANES)
+    jobs = [("fetch", r, memory) for r in ORDER]
+    jobs += [("line", -r, lens) for r in near] + [("line", -r, rows) for r in near]
+    jobs += [("line", r, rows) for r in near] + [("line", r, stat) for r in near]
+    courier = Courier(sizes, jobs)
+    courier.lines = list(near)
+    count = PLANES * PAIRS
 
     def kernel(*refs):
-        ins, sources, outs, targets, sems = split_refs(refs, 8, jobs - 1, 7, jobs, 3)
-        x_ref, self_gain, cross_gain, wq_ref, wk_ref, wv_ref, wo_ref, wc_ref = ins
-        q_ref, k_ref, v_ref, lse_ref, attn_ref, hidden_ref, query_ref = outs
-        copies = courier.copies(list(sources) + [query_ref], targets, sems)
-        courier.greet()
-        for copy in copies[:-1]:
-            copy.start()
-        values = x_ref[...].astype(F32)
-        normed = rms(values, self_gain[...]).astype(BF)
-        q_ref[...] = dot(normed, wq_ref[...], 1, 0).astype(BF)
-        k_ref[...] = dot(normed, wk_ref[...], 1, 0).astype(BF)
-        v_ref[...] = dot(normed, wv_ref[...], 1, 0).astype(BF)
-
-        for p in range(PAIRS):
-            cols = pl.ds(p * 128, 128)
-            out, lse = forward_pair(q_ref[:, cols], k_ref[:, cols], v_ref[:, cols], None)
-            attn_ref[:, cols] = out
-            for h in range(2):
-                lse_ref[p, h : h + 1, :] = lse[h]
-
-        hidden = values + dot(attn_ref[...], wo_ref[...], 1, 0)
-        hidden_ref[...] = hidden
-        query_ref[...] = dot(rms(hidden, cross_gain[...]).astype(BF), wc_ref[...], 1, 0).astype(BF)
-        copies[-1].start()
-        for copy in copies:
-            copy.wait()
-
-    rows = jax.ShapeDtypeStruct((tokens, width), BF)
-    vmem = pl.BlockSpec(memory_space=pltpu.VMEM)
-    stat = jax.ShapeDtypeStruct((PAIRS, 2, tokens), F32)
-    wide = jax.ShapeDtypeStruct((tokens, width), F32)
+        ins, sources, outs, parts, targets, work, sems = split_refs(refs, 11, 1, 8, 4, 13, 7, 3)
+        x_ref, self_gain, cross_gain, wq_ref, wk_ref, wv_ref, wo_ref, wc_ref = ins[:8]
+        lens_ref, key_ref, value_ref = ins[8:]
+        (memory_ref,) = sources
+        q_ref, k_ref, v_ref, lse_ref, attn_ref, hidden_ref, query_ref, top_ref = outs
+        part_ref, part_lse_ref, kv_ref, probs_ref = parts
+        row_buf, query_buf, out_buf, lse_buf, lens_buf, near_lens, load_sems = work
+        copies = courier.copies(
+            [memory_ref] * PLANES
+            + [lens_ref] * 3
+            + [query_ref] * 3
+            + [out_buf.at[n] for n in range(3)]
+            + [lse_buf.at[n] for n in range(3)],
+            list(targets[:4])
+            + [near_lens.at[n] for n in range(3)]
+            + list(targets[4:]),
+            sems,
+        )
+        own, remote = copies[:PLANES], copies[PLANES:]
+        far = plane - 1
+        lines = remote[PLANES * far :]
+        lens_lines, query_lines, out_lines, lse_lines = split_refs(lines, 3, 3, 3, 3)
+        step = pl.program_id(0)
+        me = courier.me()
+
+        def start_fetch(n):
+            for copy in [own[n]] + remote[n * far : n * far + far]:
+                copy.start()
+
+        @pl.when(step == 0)
+        def _():
+            courier.greet()
+            start_fetch(0)
+            for copy in lens_lines:
+                copy.start()
+            values = x_ref[...].astype(F32)
+            normed = rms(values, self_gain[...]).astype(BF)
+            q_ref[...] = dot(normed, wq_ref[...], 1, 0).astype(BF)
+            k_ref[...] = dot(normed, wk_ref[...], 1, 0).astype(BF)
+            v_ref[...] = dot(normed, wv_ref[...], 1, 0).astype(BF)
+
+            @pl.loop(0, PAIRS)
+            def _(p):
+                cols = pl.ds(pl.multiple_of(p * 128, 128), 128)
+                out, stats, _ = forward_pair(q_ref[:, cols], k_ref[:, cols], v_ref[:, cols], None)
+                attn_ref[:, cols] = out
+                for h in range(2):
+                    lse_ref[p, h : h + 1, :] = stats[h][0]
+
+            hidden = values + dot(attn_ref[...], wo_ref[...], 1, 0)
+            hidden_ref[...] = hidden
+            normed = rms(hidden, cross_gain[...]).astype(BF)
+            query_ref[...] = dot(normed, wc_ref[...], 1, 0).astype(BF)
+            query_lines[0].start()
+
+        for n, r in enumerate(ORDER):
+
+            @pl.when(step == n * PAIRS)
+            def _(n=n, r=r):
+                loads = []
+
+                def load(block):
+                    at = pl.ds(pl.multiple_of(block * positions, positions), positions)
+                    copy = pltpu.make_async_copy(
+                        targets[n].at[block], row_buf.at[at], load_sems.at[len(loads)]
+                    )
+                    copy.start()
+                    loads.append(copy)
+
+                own[n].wait()
+                load(me)
+                for k in range(1, plane):
+                    remote[n * far + k - 1].wait()
+                    load(rem(me + (plane - k), plane))
+                if n + 1 < PLANES:
+                    start_fetch(n + 1)
+                if r > 0:
+                    query_lines[r - 1].wait()
+                    copy = pltpu.make_async_copy(
+                        targets[3 + r], query_buf, load_sems.at[plane]
+                    )
+                    copy.start()
+                    if r + 1 < PLANES:
+                        query_lines[r].start()
+                    lens_lines[r - 1].wait()
+                    lens_buf[...] = near_lens[r - 1]
+                    copy.wait()
+                else:
+                    query_buf[...] = query_ref[...]
+                    lens_buf[...] = lens_ref[...]
+                for copy in loads:
+                    copy.wait()
+
+        phase = lax.div(step, PAIRS)
+        p = rem(step, PAIRS)
+        cols = pl.ds(pl.multiple_of(p * 128, 128), 128)
+        both = jnp.concatenate([key_ref[...], value_ref[...]], axis=1)
+        kv_ref[...] = dot(row_buf[...], both, 1, 0).astype(BF)
+        bias = key_bias(keys, lens_buf[...])
+        out, stats, held = forward_pair(query_buf[:, cols], kv_ref[:, :128], kv_ref[:, 128:], bias)
+        out_buf[phase, :, cols] = out
+        for h in range(2):
+            probs_ref[h] = held[h]
+            lse_buf[phase, p, h : h + 1, :] = stats[h][0]
+            top_ref[phase, p, h : h + 1, :] = stats[h][1]
+
+        for n, r in enumerate(ORDER[:-1]):
+
+            @pl.when(step == n * PAIRS + PAIRS - 1)
+            def _(r=r):
+                out_lines[r - 1].start()
+                lse_lines[r - 1].start()
+
+        @pl.when(step == count - 1)
+        def _():
+            part_ref[...] = out_buf[PLANES - 1]
+            part_lse_ref[...] = lse_buf[PLANES - 1]
+            for copy in out_lines + lse_lines:
+                copy.wait()
+
+    once = pl.Buffered(1)
+
+    def fixed(*shape):
+        return pl.BlockSpec(shape, lambda t: (0,) * len(shape), pipeline_mode=once)
+
+    def out_fixed(*shape):
+        return pl.BlockSpec(shape, lambda t: (0,) * len(shape))
+
+    def where(t):
+        return rem(lax.div(t, PAIRS) + 1, PLANES), rem(t, PAIRS)
+
+    square = fixed(width, width)
+    weight = pl.BlockSpec((width, 128), lambda t: (0, rem(t, PAIRS)))
+    hbm = pl.BlockSpec(memory_space=pl.ANY)
+    flat = out_fixed(tokens, width)
+    flat_stat = out_fixed(PAIRS, 2, tokens)
+    shapes = courier.out_shape()
     outs = pl.pallas_call(
         kernel,
-        out_shape=[rows, rows, rows, stat, rows, wide, rows] + courier.out_shape(),
-        in_specs=[vmem] * 8 + courier.specs()[1:],
-        out_specs=[vmem] * 7 + courier.specs(),
-        scratch_shapes=courier.scratch(),
-        compiler_params=courier.params(ident),
-    )(inputs, *gains, *weights, *courier.values()[:-1])
-    return outs[:7], outs[7:]
+        grid=(count,),
+        out_shape=[rows, rows, rows, stat, rows, wide, rows]
+        + [jax.ShapeDtypeStruct((PLANES, PAIRS, 2, tokens), F32), rows, stat]
+        + [
+            jax.ShapeDtypeStruct((PLANES, keys, 2 * width), BF),
+            jax.ShapeDtypeStruct((PLANES, H, keys, tokens), BF),
+        ]
+        + shapes[:4]
+        + shapes[7:],
+        in_specs=[fixed(tokens, width), fixed(1, width), fixed(1, width)]
+        + [square] * 5
+        + [fixed(8, 128), weight, weight, hbm],
+        out_specs=[flat] * 3
+        + [flat_stat]
+        + [flat] * 3
+        + [out_fixed(PLANES, PAIRS, 2, tokens), flat, flat_stat]
+        + [
+            pl.BlockSpec((None, keys, 256), lambda t: (where(t)[0], 0, where(t)[1])),
+            pl.BlockSpec((None, 2, keys, tokens), lambda t: where(t) + (0, 0)),
+        ]
+        + [hbm] * 13,
+        scratch_shapes=[
+            pltpu.VMEM((keys, width), BF),
+            pltpu.VMEM((tokens, width), BF),
+            pltpu.VMEM((PLANES, tokens, width), BF),
+            pltpu.VMEM((PLANES, PAIRS, 2, tokens), F32),
+            pltpu.VMEM((8, 128), jnp.int32),
+            pltpu.VMEM((3, 8, 128), jnp.int32),
+            pltpu.SemaphoreType.DMA((plane + 1,)),
+        ]
+        + courier.scratch(),
+        compiler_params=pltpu.CompilerParams(
+            vmem_limit_bytes=62 * 2**20, collective_id=ident, has_side_effects=True
+        ),
+    )(inputs, *gains, *weights, lens, key_weight, value_weight, memory)
+    saved, (tops, part0, lse0, kv, probs), moved = outs[:7], outs[7:12], outs[12:]
+    return dict(
+        saved=saved,
+        tops=tops,
+        keyvals=kv,
+        probs=probs,
+        rows={r: moved[n] for n, r in enumerate(ORDER)},
+        queries={0: saved[6], **{r: moved[3 + r] for r in near}},
+        parts=[part0] + [moved[6 + r] for r in near],
+        lses=[lse0] + [moved[9 + r] for r in near],
+    )
 
 
 def glu_parts(gate_vals):
@@ -1007,47 +1164,15 @@
     )(*parts, *lses, hidden, out_weight, gain, cotangent, gate, up, down)
 
 
-def cross_forward(courier, ident, queries, rows, lens, key_weight, value_weight):
-    tokens, keys = queries.shape[0], rows.shape[0]
-    spec = block_specs(tokens, keys)
-
-    def body(ins, outs, _):
-        q_ref, rows_ref, lens_ref, wk_ref, wv_ref = ins
-        o_ref, lse_ref, kv_ref = outs
-        weights = jnp.concatenate([wk_ref[...], wv_ref[...]], axis=1)
-        kv_ref[...] = dot(rows_ref[...], weights, 1, 0).astype(BF)
-        bias = key_bias(keys, lens_ref)
-        out, lse = forward_pair(q_ref[...], kv_ref[:, :128], kv_ref[:, 128:], bias)
-        o_ref[...] = out
-        for h in range(2):
-            lse_ref[0, h : h + 1, :] = lse[h]
-
-    return call(
-        courier,
-        ident,
-        body,
-        [queries, rows, lens, key_weight, value_weight],
-        [spec["col"], spec["rows"], spec["lens"], spec["weight"], spec["weight"]],
-        [
-            jax.ShapeDtypeStruct((tokens, H * HD), BF),
-            jax.ShapeDtypeStruct((PAIRS, 2, tokens), F32),
-            jax.ShapeDtypeStruct((keys, 2 * H * HD), BF),
-        ],
-        [spec["col"], spec["stat"], spec["pair"]],
-        [],
-        2**34,
-    )
-
-
 def cross_backward(
-    courier, ident, queries, grad, keyvals, lens, lse, delta, key_weight, value_weight, summands=()
+    courier, ident, r, queries, grad, keyvals, probs, tops, stats, key_weight, value_weight, summands=()
 ):
-    tokens, keys = queries.shape[0], keyvals.shape[0]
+    tokens, keys = queries.shape[0], keyvals.shape[1]
     width = H * HD
     spec = block_specs(tokens, keys)
 
     def body(ins, outs, scratch):
-        q_ref, da_ref, kv_ref, lens_ref, lse_ref, delta_ref, wk_ref, wv_ref = ins
+        q_ref, da_ref, kv_ref, probs_ref, top_ref, stats_ref, wk_ref, wv_ref = ins
         dkv_ref, dq_ref, dm_ref = outs
         (total_ref,) = scratch
         step = pl.program_id(0)
@@ -1055,6 +1180,10 @@
         @pl.when(step == 0)
         def _():
             total_ref[...] = jnp.zeros_like(total_ref)
+
+        def stored(h, keys_h, query_h):
+            scale = jnp.exp(top_ref[0, h : h + 1, :] - stats_ref[0, 0, h : h + 1, :])
+            return probs_ref[h].astype(F32) * scale
 
         weights = jnp.concatenate([wk_ref[...], wv_ref[...]], axis=1)
         grad_kv, grad_q = backward_pair(
@@ -1062,9 +1191,8 @@
             da_ref[...],
             kv_ref[:, :128],
             kv_ref[:, 128:],
-            key_bias(keys, lens_ref),
-            two_rows(lse_ref),
-            two_rows(delta_ref),
+            stored,
+            [stats_ref[1, 0, h : h + 1, :] for h in range(2)],
         )
         dkv_ref[...] = grad_kv
         dq_ref[...] = grad_q
@@ -1078,8 +1206,17 @@
         courier,
         ident,
         body,
-        [queries, grad, keyvals, lens, lse, delta, key_weight, value_weight],
-        [spec[n] for n in ("col", "col", "pair", "lens", "stat", "stat", "weight", "weight")],
+        [queries, grad, keyvals, probs, tops, stats, key_weight, value_weight],
+        [
+            spec["col"],
+            spec["col"],
+            pl.BlockSpec((None, keys, 256), lambda p: (r, 0, p)),
+            pl.BlockSpec((None, 2, keys, tokens), lambda p: (r, p, 0, 0)),
+            pl.BlockSpec((None, 1, 2, tokens), lambda p: (rem(r + 3, PLANES), p, 0, 0)),
+            pl.BlockSpec((2, 1, 2, tokens), lambda p: (0, p, 0, 0)),
+            spec["weight"],
+            spec["weight"],
+        ],
         [
             jax.ShapeDtypeStruct((keys, 2 * width), BF),
             jax.ShapeDtypeStruct((tokens, width), BF),
@@ -1126,7 +1263,12 @@
         q_ref, da_ref, k_ref, v_ref, lse_ref = ins
         dq_ref, dk_ref, dv_ref = outs
         grad_kv, dq_ref[...] = backward_pair(
-            q_ref[...], da_ref[...], k_ref[...], v_ref[...], None, two_rows(lse_ref), None
+            q_ref[...],
+            da_ref[...],
+            k_ref[...],
+            v_ref[...],
+            causal_probs([lse_ref[0, h : h + 1, :] for h in range(2)]),
+            None,
         )
         dk_ref[...] = grad_kv[:, :128]
         dv_ref[...] = grad_kv[:, 128:]
@@ -1287,8 +1429,7 @@
                     da_ref[:, cols],
                     k_ref[:, cols],
                     v_ref[:, cols],
-                    None,
-                    [lse_ref[p, h : h + 1, :] for h in range(2)],
+                    causal_probs([lse_ref[p, h : h + 1, :] for h in range(2)]),
                     None,
                 )
                 dq1[:, cols] = grad_q_p
@@ -1407,6 +1548,58 @@
         copy.wait()
 
 
+def finish_kernel(*refs):
+    blocks = refs[:PLANES]
+    left0, got0, left1, got1, out_ref, gate_ref, up_ref, down_ref = refs[PLANES : PLANES + 8]
+    held, arrive, leave = refs[PLANES + 8 :]
+    z = lax.axis_index("z")
+    size = held.shape[1]
+    inward = []
+    outward = []
+    for r, block in enumerate(blocks):
+        at = rem(z + r, PLANES) * size
+        inward.append(pltpu.make_async_copy(block, held.at[r], arrive.at[r]))
+        outward.append(
+            pltpu.make_async_copy(held.at[r], out_ref.at[pl.ds(at, size)], leave.at[r])
+        )
+        inward[r].start()
+    for r in range(PLANES):
+        inward[r].wait()
+        outward[r].start()
+    share = gate_ref.shape[0]
+    wide = left0[z].astype(F32)
+    tall = left1[z].astype(F32)
+    for k in range(PLANES - 1):
+        wide += got0[k].astype(F32)
+        tall += got1[k].astype(F32)
+    gate_ref[...] = wide[:share]
+    up_ref[...] = wide[share:]
+    down_ref[...] = tall
+    for copy in outward:
+        copy.wait()
+
+
+def finish(blocks, left0, got0, left1, got1):
+    shape = blocks[0].shape
+    share, inner = left0.shape[1] // 2, left0.shape[2]
+    hbm = pl.BlockSpec(memory_space=pl.ANY)
+    vmem = pl.BlockSpec(memory_space=pltpu.VMEM)
+    return pl.pallas_call(
+        finish_kernel,
+        out_shape=[jax.ShapeDtypeStruct((PLANES * shape[0],) + shape[1:], BF)]
+        + [jax.ShapeDtypeStruct((share, inner), F32)] * 2
+        + [jax.ShapeDtypeStruct(left1.shape[1:], F32)],
+        in_specs=[hbm] * PLANES + [vmem] * 4,
+        out_specs=[hbm] + [vmem] * 3,
+        scratch_shapes=[
+            pltpu.VMEM((PLANES,) + shape, BF),
+            pltpu.SemaphoreType.DMA((PLANES,)),
+            pltpu.SemaphoreType.DMA((PLANES,)),
+        ],
+        compiler_params=pltpu.CompilerParams(vmem_limit_bytes=VMEM),
+    )(*blocks, left0, got0, left1, got1)
+
+
 def place(blocks):
     shape = blocks[0].shape
     count = len(blocks)
@@ -1479,41 +1672,21 @@
     def cut(rows):
         return rows.reshape(plane_size, positions, width)
 
-    lens = {0: jnp.broadcast_to(memory_lengths[None, :], (8, 128))}
-    jobs = [("fetch", 1, memory)]
-    jobs += [("line", -r, lens[0]) for r in range(1, PLANES)]
-    jobs += [("line", -1, jax.ShapeDtypeStruct(decoder_in.shape[1:], BF))]
-    (query_one, key_one, value_one, lse_one, attn_one, hidden_one, query_two), moved = self_part(
-        Courier(sizes, jobs),
+    forward = forward_part(
+        sizes,
         0,
+        memory,
+        jnp.broadcast_to(memory_lengths[None, :], (8, 128)),
         decoder_in[0],
         (norm_self[None], norm_cross[None]),
         (self_query, self_key, self_value, self_out, cross_query),
+        cross_key,
+        cross_value,
     )
-    fetched, lens[1], lens[2], lens[3], query_near = moved
-    queries, rows, keyvals, partial, stats_out = {0: query_two, 1: query_near}, {}, {}, {}, {}
-    order = (1, 2, 3, 0)
-    for at, r in enumerate(order):
-        rows[r] = flat(fetched)
-        jobs = []
-        if at + 1 < PLANES:
-            jobs.append(("fetch", order[at + 1], memory))
-        if at + 2 < PLANES:
-            jobs.append(("line", -order[at + 1], query_two))
-        if at >= 1:
-            before = order[at - 1]
-            jobs.append(("line", before, partial[before]))
-            jobs.append(("line", before, stats_out[before]))
-        (partial[r], stats_out[r], keyvals[r]), moved = cross_forward(
-            Courier(sizes, jobs), 1 + at, queries[r], rows[r], lens[r], cross_key, cross_value
-        )
-        moved = list(moved)
-        if at + 1 < PLANES:
-            fetched = moved.pop(0)
-        if at + 2 < PLANES:
-            queries[order[at + 1]] = moved.pop(0)
-        if at >= 1:
-            partial[before], stats_out[before] = moved
+    query_one, key_one, value_one, lse_one, attn_one, hidden_one, _ = forward["saved"]
+    queries = forward["queries"]
+    rows = {r: flat(forward["rows"][r]) for r in range(PLANES)}
+
     (
         output,
         attn_two,
@@ -1526,8 +1699,8 @@
         grad_down,
     ) = middle(
         sizes,
-        [partial[r] for r in range(PLANES)],
-        [stats_out[r] for r in range(PLANES)],
+        forward["parts"],
+        forward["lses"],
         hidden_one,
         cross_out,
         norm_ffn[None],
@@ -1561,12 +1734,13 @@
         (grad_kv[r], grad_q[r], grad_rows[r]), moved = cross_backward(
             Courier(sizes, jobs),
             5 + r,
+            r,
             queries[r],
             grads[r],
-            keyvals[r],
-            lens[r],
-            both[r][0],
-            both[r][1],
+            forward["keyvals"],
+            forward["probs"],
+            forward["tops"],
+            both[r],
             cross_key,
             cross_value,
             summands.get(r, []),
@@ -1599,8 +1773,9 @@
             (norm_self[None], norm_cross[None], grad_norm_ffn),
         )
         returned[last], got[0], got[1] = moved
-        memory_grad = place([returned[r] for r in range(PLANES)])
-        gate_up = over_z(left[0], got[0])
+        memory_grad, sum_gate, sum_up, sum_down = finish(
+            [returned[r] for r in range(PLANES)], left[0], got[0], left[1], got[1]
+        )
         here = lax.axis_index(ALL) * part
         norm_self_sum, norm_cross_sum, norm_ffn_sum = (
             lax.dynamic_slice_in_dim(norm_sums[n], here, part) for n in range(3)
@@ -1620,9 +1795,9 @@
             sums[0][part:],
             sums[1][part:],
             norm_ffn_sum,
-            gate_up[:part],
-            gate_up[part:],
-            over_z(left[1], got[1]),
+            sum_gate,
+            sum_up,
+            sum_down,
         )
 
     jobs = [

time: 542 us -> 525 us (0.969)
  Pallas kernels: 514 us -> 504 us
    pallas_call x8 -> x4, Pallas kernels: 340 us -> 179 us  [call(): pl.pallas_call(lambda *refs: kernel(*counts, refs), grid=(PAIRS,), out_sh...]
    pallas_call x2, Pallas kernels: 53.5 us -> 203 us  [the longest x1 192 us: forward_part(): pl.pallas_call(kernel, grid=(count,), out_shape=[rows, rows, rows, stat,...]
    squeeze x4 -> x0, local copies, waits for them, and re-layouts: 5.51 us -> none  [on_device(): both[r][1]]
where the time goes in v7:
time: 525 us; the launch traced here: 517 us
  Pallas kernels  504 us (96%)
  local copies, waits for them, and re-layouts  11.2 us (2%)
    pallas_call x1, Pallas kernels, forward_part(): pl.pallas_call(kernel, grid=(count,), out_shape=[rows, rows, rows, stat,...  192 us
    pallas_call x4, Pallas kernels, call(): pl.pallas_call(lambda *refs: kernel(*counts, refs), grid=(PAIRS,), out_sh...  179 us
    pallas_call x1, Pallas kernels, ending(): pl.pallas_call(kernel, out_shape=[jax.ShapeDtypeStruct((tokens, width), F...  91.6 us
    pallas_call x1, Pallas kernels, middle(): pl.pallas_call(functools.partial(middle_kernel, sizes=sizes, packed=packe...  30.7 us
    pallas_call x1, Pallas kernels, finish(): pl.pallas_call(finish_kernel, out_shape=[jax.ShapeDtypeStruct((PLANES * s...  11.2 us

profile of v7, /device:TPU:0, one launch (start us, length us, event | category | flops | bytes accessed | tf_op | source)
XLA Modules:
  0.0 517.4 jit_solution(8804871295657330903)
XLA Ops:
  0.7 1.3 broadcast_in_dim.25.refs_1_.refs_24_
  1.9 1.3 broadcast_in_dim.26.refs_2_.refs_25_
  3.8 0.6 broadcast_in_dim.28.refs_8_
  4.4 0.0 copy-start.2
  4.4 191.9 %shard_map.305 = (bf16[512,768]{1,0:T(8,128)(2,1)}, bf16[512,768]{1,0:T(8,128)(2,1)}, bf16[512,768]{1,0:T(8,128)(2,1)}, f32[6,2,512]{2,1,0:T(2,128)}, bf16[512,7...) custom-call(bf16[512,768]{1,0:T(8,128)(2,1)} %bitcast.25, ...), custom_call_target="tpu_custom_call" | custom-call | tf_op jit(solution)/shard_map/pallas_call | solution.py:862
  196.3 0.0 copy-done.2
  196.3 0.6 broadcast_in_dim.29.refs_10_
  196.9 30.7 %shard_map.306 = (bf16[512,768]{1,0:T(8,128)(2,1)}, bf16[512,768]{1,0:T(8,128)(2,1)}, f32[512,768]{1,0:T(8,128)}, bf16[512,768]{1,0:T(8,128)(2,1)}, f32[2,6,2,51...) custom-call(bf16[512,768]{1,0:T(8,128)(2,1)} %get-tuple-element.88.r, ...), custom_call_target="tpu_custom_call" | custom-call | tf_op jit(solution)/shard_map/pallas_call | solution.py:1142
  227.6 48.6 %shard_map.307 = (bf16[2048,1536]{1,0:T(8,128)(2,1)}, bf16[512,768]{1,0:T(8,128)(2,1)}, bf16[2048,768]{1,0:T(8,128)(2,1)}, bf16[512,768]{1,0:T(8,128)(2,1)}, f32...) custom-call(bf16[512,768]{1,0:T(8,128)(2,1)} %get-tuple-element.102.refs_0_, ...), custom_call_target="tpu_custom_call" | custom-call | flops 34359738368 | bytes 16777216 | tf_op jit(solution)/shard_map/pallas_call | solution.py:583
  276.2 44.8 %shard_map.308 = (bf16[2048,1536]{1,0:T(8,128)(2,1)}, bf16[512,768]{1,0:T(8,128)(2,1)}, bf16[2048,768]{1,0:T(8,128)(2,1)}, bf16[512,768]{1,0:T(8,128)(2,1)}, f32...) custom-call(bf16[512,768]{1,0:T(8,128)(2,1)} %get-tuple-element.111.refs_0_, ...), custom_call_target="tpu_custom_call" | custom-call | flops 34359738368 | bytes 16777216 | tf_op jit(solution)/shard_map/pallas_call | solution.py:583
  320.9 44.2 %shard_map.309 = (bf16[2048,1536]{1,0:T(8,128)(2,1)}, bf16[512,768]{1,0:T(8,128)(2,1)}, bf16[2048,768]{1,0:T(8,128)(2,1)}, bf16[512,768]{1,0:T(8,128)(2,1)}, f32...) custom-call(bf16[512,768]{1,0:T(8,128)(2,1)} %get-tuple-element.116.refs_0_, ...), custom_call_target="tpu_custom_call" | custom-call | flops 34359738368 | bytes 16777216 | tf_op jit(solution)/shard_map/pallas_call | solution.py:583
  365.2 41.5 %shard_map.310 = (bf16[2048,1536]{1,0:T(8,128)(2,1)}, bf16[512,768]{1,0:T(8,128)(2,1)}, bf16[2048,768]{1,0:T(8,128)(2,1)}, bf16[8,256,768]{2,1,0:T(8,128)(2,1)}, bf16[512,768]{1,0:T(8,128)(2,1)}) custom-call(bf16[512,768]{1,0:T(8,128)(2,1)} %get-tuple-element.122.refs_0_, bf16[512,768]{1,0:T(8,128)(2,1)} %get-tuple-element.123.refs_1_, ...), custom_call_target="tpu_custom_call" | custom-call | flops 34359738368 | bytes 16777216 | tf_op jit(solution)/shard_map/pallas_call | solution.py:583
  406.6 91.6 %shard_map.311 = (f32[512,768]{1,0:T(8,128)}, f32[48,768]{1,0:T(8,128)}, f32[48,768]{1,0:T(8,128)}, f32[48,768]{1,0:T(8,128)}, f32[48,768]{1,0:T(8,128)}, /*inde...) custom-call(bf16[2048,768]{1,0:T(8,128)(2,1)} %bitcast.23, ...), custom_call_target="tpu_custom_call" | custom-call | tf_op jit(solution)/shard_map/pallas_call | solution.py:1515
  498.3 1.7 fusion.3
  500.0 1.7 fusion.5
  501.7 0.9 fusion.7
  502.6 0.6 fusion
  503.1 0.0 copy-start.1
  503.1 0.0 copy-start
  503.1 11.2 %shard_map.312 = (bf16[32,256,768]{2,1,0:T(8,128)(2,1)}, f32[24,2048]{1,0:T(8,128)}, f32[24,2048]{1,0:T(8,128)}, f32[64,768]{1,0:T(8,128)}) custom-call(bf16[8,256,768]{2,1,0:T(8,128)(2,1)} %get-tuple-element.144.refs_0_, bf16[8,256,768]{2,1,0:T(8,128)(2,1)} %get-tuple-element.145.refs_1_, bf16[8,256,768]{2,1,0:T(8,128)(2,1)} %get-tuple-element.146.refs_2_, ...), custom_call_target="tpu_custom_call" | custom-call | tf_op jit(solution)/shard_map/pallas_call | solution.py:1587
  514.4 0.6 fusion.2
  514.9 0.0 copy-done.1
  514.9 0.9 copy.38
  515.8 0.0 copy-done
  515.8 1.1 copy.39
Async XLA Ops:
  4.4 191.9 %copy-start.2 = (f32[768]{0:T(1024)S(1)}, f32[768]{0:T(1024)}, u32[]{:S(2)}) copy-start(f32[768]{0:T(1024)} %param.32) | copy-start | bytes 9220
  503.1 11.8 %copy-start.1 = (bf16[512,768]{1,0:T(8,128)(2,1)S(1)}, bf16[512,768]{1,0:T(8,128)(2,1)}, u32[]{:S(2)}) copy-start(bf16[512,768]{1,0:T(8,128)(2,1)} %get-tuple-element.97) | copy-start | bytes 2359300
  503.1 12.7 %copy-start = (f32[512,768]{1,0:T(8,128)S(1)}, f32[512,768]{1,0:T(8,128)}, u32[]{:S(2)}) copy-start(f32[512,768]{1,0:T(8,128)} %get-tuple-element.143) | copy-start | bytes 4718596

commit v8 on v7

--- a/solution.py
+++ b/solution.py
@@ -1229,6 +1229,199 @@
     )
 
 
+def backward_part(
+    sizes, ident, queries, grad, stats, keyvals, probs, tops, key_weight, value_weight, summands
+):
+    tokens, width = grad.shape
+    plane = sizes[1] * sizes[2] * sizes[3]
+    keys = keyvals.shape[1]
+    positions = keys // plane
+    rows = jax.ShapeDtypeStruct((tokens, width), BF)
+    blocks = jax.ShapeDtypeStruct((plane, positions, width), BF)
+    near = range(1, PLANES)
+    jobs = [("return", 0, blocks)] * 3
+    jobs += [("line", -r, rows) for r in near] + [("line", -r, stats) for r in near]
+    jobs += [("line", 1, rows), ("line", 2, rows)]
+    courier = Courier(sizes, jobs)
+    courier.lines = list(near)
+    count = PLANES * PAIRS
+    reducers = [Halved(sizes, value.shape) for value in summands]
+    parts = [len(one.scratch()) for one in reducers]
+    sums = len(reducers)
+
+    def kernel(*refs):
+        ins, far, arrays, outs, results, targets, work, sems, rest = split_refs(
+            refs, 5, 6, sums, 1, sums, 8, 7, 3, sum(parts)
+        )
+        kv_ref, probs_ref, top_ref, wk_ref, wv_ref = ins
+        (dkv_ref,) = outs
+        query_all, grad_all, stats_all, dq_all, total_ref, dm_buf, load_sems = work
+        dq0, dq_near, dq_next, dq3, back0, back1, back2, rows3 = targets
+        copies = courier.copies(
+            [dm_buf.at[0], dm_buf.at[1], dm_buf.at[0]]
+            + [far[4]] * 3
+            + [far[5]] * 3
+            + [dq_all.at[1], dq_all.at[2]],
+            [back0, back1, back2]
+            + [grad_all.at[r] for r in near]
+            + [stats_all.at[r] for r in near]
+            + [dq_near, dq_next],
+            sems,
+        )
+        own, remote = copies[:3], copies[3:]
+        others = plane - 1
+        grad_lines, stats_lines, dq_lines = split_refs(remote[3 * others :], 3, 3, 2)
+        returns = [[own[n]] + remote[n * others : n * others + others] for n in range(3)]
+        work_of = split_refs(rest, *parts)
+        step = pl.program_id(0)
+        r_now = lax.div(step, PAIRS)
+        p = rem(step, PAIRS)
+
+        def bound():
+            return [one.bind(v, held) for one, v, held in zip(reducers, arrays, work_of)]
+
+        loads = [
+            pltpu.make_async_copy(far[n], query_all.at[n], load_sems.at[n]) for n in range(PLANES)
+        ]
+        loads.append(pltpu.make_async_copy(far[4], grad_all.at[0], load_sems.at[4]))
+        loads.append(pltpu.make_async_copy(far[5], stats_all.at[0], load_sems.at[5]))
+        leave = [
+            pltpu.make_async_copy(dq_all.at[0], dq0, load_sems.at[6]),
+            pltpu.make_async_copy(dq_all.at[3], dq3, load_sems.at[7]),
+            pltpu.make_async_copy(dm_buf.at[1], rows3, load_sems.at[8]),
+        ]
+
+        @pl.when(step == 0)
+        def _():
+            for copy in loads:
+                copy.start()
+            courier.greet()
+            grad_lines[0].start()
+            stats_lines[0].start()
+            for one in bound():
+                one.begin()
+            for copy in loads:
+                copy.wait()
+
+        for r in near:
+
+            @pl.when(step == r * PAIRS)
+            def _(r=r):
+                grad_lines[r - 1].wait()
+                stats_lines[r - 1].wait()
+                if r + 1 < PLANES:
+                    grad_lines[r].start()
+                    stats_lines[r].start()
+
+        @pl.when(p == 0)
+        def _():
+            total_ref[...] = jnp.zeros_like(total_ref)
+
+        cols = pl.ds(pl.multiple_of(p * 128, 128), 128)
+        top_at = rem(r_now + 3, PLANES)
+
+        def stored(h, keys_h, query_h):
+            lse = stats_all[r_now, 0, p, h : h + 1, :]
+            return probs_ref[h].astype(F32) * jnp.exp(top_ref[top_at, p, h : h + 1, :] - lse)
+
+        weights = jnp.concatenate([wk_ref[...], wv_ref[...]], axis=1)
+        grad_kv, grad_q = backward_pair(
+            query_all[r_now, :, cols],
+            grad_all[r_now, :, cols],
+            kv_ref[:, :128],
+            kv_ref[:, 128:],
+            stored,
+            [stats_all[r_now, 1, p, h : h + 1, :] for h in range(2)],
+        )
+        dkv_ref[...] = grad_kv
+        dq_all[r_now, :, cols] = grad_q
+        total_ref[...] += dot(grad_kv, weights, 1, 1)
+
+        @pl.when(step == 3)
+        def _():
+            for one in bound():
+                one.after_second()
+
+        @pl.when(step == PAIRS - 1)
+        def _():
+            for one, result in zip(bound(), results):
+                one.after_third(result)
+
+        for r in range(PLANES):
+
+            @pl.when(step == r * PAIRS + PAIRS - 1)
+            def _(r=r):
+                if r >= 2:
+                    for copy in returns[r - 2]:
+                        copy.wait()
+                dm_buf[r % 2] = total_ref[...].astype(BF).reshape(dm_buf.shape[1:])
+                if r < 3:
+                    for copy in returns[r]:
+                        copy.start()
+                if r == 0:
+                    leave[0].start()
+                elif r < 3:
+                    dq_lines[r - 1].start()
+                else:
+                    leave[1].start()
+                    leave[2].start()
+                    for copy in returns[2] + list(dq_lines) + leave:
+                        copy.wait()
+
+    once = pl.Buffered(1)
+
+    def where(t):
+        return lax.div(t, PAIRS), rem(t, PAIRS)
+
+    hbm = pl.BlockSpec(memory_space=pl.ANY)
+    weight = pl.BlockSpec((width, 128), lambda t: (0, rem(t, PAIRS)))
+    pair = pl.BlockSpec((None, keys, 256), lambda t: (where(t)[0], 0, where(t)[1]))
+    shapes = [(PLANES,) + value.shape[-2:] for value in summands]
+    scratch = [
+        pltpu.VMEM((PLANES, tokens, width), BF),
+        pltpu.VMEM((PLANES, tokens, width), BF),
+        pltpu.VMEM((PLANES,) + stats.shape, F32),
+        pltpu.VMEM((PLANES, tokens, width), BF),
+        pltpu.VMEM((keys, width), F32),
+        pltpu.VMEM((2, plane, positions, width), BF),
+        pltpu.SemaphoreType.DMA((9,)),
+    ]
+    outs = pl.pallas_call(
+        kernel,
+        grid=(count,),
+        out_shape=[jax.ShapeDtypeStruct((PLANES, keys, 2 * width), BF)]
+        + [jax.ShapeDtypeStruct(shape, BF) for shape in shapes]
+        + [rows] * 4
+        + [blocks] * 4,
+        in_specs=[
+            pair,
+            pl.BlockSpec((None, 2, keys, tokens), lambda t: where(t) + (0, 0)),
+            pl.BlockSpec(tops.shape, lambda t: (0, 0, 0, 0), pipeline_mode=once),
+            weight,
+            weight,
+        ]
+        + [hbm] * (6 + sums),
+        out_specs=[pair] + [pl.BlockSpec(shape, lambda t: (0, 0, 0)) for shape in shapes] + [hbm] * 8,
+        scratch_shapes=scratch
+        + courier.scratch()
+        + [ref for one in reducers for ref in one.scratch()],
+        compiler_params=pltpu.CompilerParams(
+            vmem_limit_bytes=62 * 2**20, collective_id=ident, has_side_effects=True
+        ),
+    )(
+        keyvals,
+        probs,
+        tops,
+        key_weight,
+        value_weight,
+        *[queries[r] for r in range(PLANES)],
+        grad,
+        stats,
+        *summands,
+    )
+    return outs[0], outs[1 : 1 + sums], outs[1 + sums : 5 + sums], outs[5 + sums :]
+
+
 def weight_terms(courier, ident, rows, grads):
     keys, width = rows[0].shape
     spec = block_specs(keys, keys)
@@ -1312,7 +1505,7 @@
     groups += [Resident(sizes, (2 * share, 256)) for _ in range(6)]
     small = SmallSum(sizes, (8, width))
     early = [two] + list(held) + list(grad_q[:-1])
-    far = list(rows) + list(grads) + early
+    far = list(rows) + [grads] + early
     counts = (len(far), len(small_in) + 1, jobs, 6, jobs - 1, 4, len(early) - 1, 8, 3, 80, 10)
 
     def pack(ref, first, second, cols=EVERY):
@@ -1343,7 +1536,7 @@
                     far_refs[r].at[where], row_buf.at[slot], chunk_sems.at[slot, 0]
                 ),
                 pltpu.make_async_copy(
-                    far_refs[PLANES + r].at[where], grad_buf.at[slot], chunk_sems.at[slot, 1]
+                    far_refs[PLANES].at[r, where], grad_buf.at[slot], chunk_sems.at[slot, 1]
                 ),
             ]
 
@@ -1356,7 +1549,7 @@
                         copy.start()
 
         total[...] = jnp.zeros_like(total)
-        early_refs = far_refs[2 * PLANES :]
+        early_refs = far_refs[PLANES + 1 :]
         early_loads = [
             pltpu.make_async_copy(source, target, early_sems.at[n])
             for n, (source, target) in enumerate(zip(early_refs, [grad_in] + list(loaded)))
@@ -1719,6 +1912,65 @@
         summands = {0: [grads_in[0], grad_down]}
     left, got = {}, {}
 
+    last = PLANES - 1
+    part = width // devices
+    if len(grads_in) == 1:
+        grad_kv, left, grad_q, returned = backward_part(
+            sizes,
+            5,
+            queries,
+            grad_attn_two,
+            stats,
+            forward["keyvals"],
+            forward["probs"],
+            forward["tops"],
+            cross_key,
+            cross_value,
+            summands[0],
+        )
+        returned = list(returned)
+        decoder_in_grad, sums, norm_sums, moved = ending(
+            sizes,
+            9,
+            [rows[r] for r in range(PLANES)],
+            grad_kv,
+            grad_q,
+            returned[last],
+            left,
+            grad_two,
+            (decoder_in[0], hidden_one, grad_cross_out, query_one, key_one, value_one, attn_one)
+            + (self_query, self_key, self_value, self_out, cross_query),
+            lse_one,
+            (norm_self[None], norm_cross[None], grad_norm_ffn),
+        )
+        returned[last], got_wide, got_tall = moved
+        memory_grad, sum_gate, sum_up, sum_down = finish(
+            returned, left[0], got_wide, left[1], got_tall
+        )
+        here = lax.axis_index(ALL) * part
+        norm_self_sum, norm_cross_sum, norm_ffn_sum = (
+            lax.dynamic_slice_in_dim(norm_sums[n], here, part) for n in range(3)
+        )
+        return (
+            decoder_out,
+            decoder_in_grad[None],
+            memory_grad,
+            norm_self_sum,
+            sums[2][:part],
+            sums[2][part:],
+            sums[3][:part],
+            sums[3][part:],
+            norm_cross_sum,
+            sums[1][:part],
+            sums[0][:part],
+            sums[0][part:],
+            sums[1][part:],
+            norm_ffn_sum,
+            sum_gate,
+            sum_up,
+            sum_down,
+        )
+
     grads = {0: grad_attn_two}
     both = {0: stats}
     grad_kv, grad_q, grad_rows, returned = {}, {}, {}, {}
@@ -1755,51 +2007,6 @@
             returned[r - 1] = moved.pop(0)
         if r >= 2:
             grad_q[r - 1] = moved.pop(0)
-    last = PLANES - 1
-    part = width // devices
-    if part % 8 == 0:
-        decoder_in_grad, sums, norm_sums, moved = ending(
-            sizes,
-            9,
-            [rows[r] for r in range(PLANES)],
-            [grad_kv[r] for r in range(PLANES)],
-            [grad_q[r] for r in range(PLANES)],
-            cut(grad_rows[last]),
-            [left[0], left[1]],
-            grad_two,
-            (decoder_in[0], hidden_one, grad_cross_out, query_one, key_one, value_one, attn_one)
-            + (self_query, self_key, self_value, self_out, cross_query),
-            lse_one,
-            (norm_self[None], norm_cross[None], grad_norm_ffn),
-        )
-        returned[last], got[0], got[1] = moved
-        memory_grad, sum_gate, sum_up, sum_down = finish(
-            [returned[r] for r in range(PLANES)], left[0], got[0], left[1], got[1]
-        )
-        here = lax.axis_index(ALL) * part
-        norm_self_sum, norm_cross_sum, norm_ffn_sum = (
-            lax.dynamic_slice_in_dim(norm_sums[n], here, part) for n in range(3)
-        )
-        return (
-            decoder_out,
-            decoder_in_grad[None],
-            memory_grad,
-            norm_self_sum,
-            sums[2][:part],
-            sums[2][part:],
-            sums[3][:part],
-            sums[3][part:],
-            norm_cross_sum,
-            sums[1][:part],
-            sums[0][:part],
-            sums[0][part:],
-            sums[1][part:],
-            norm_ffn_sum,
-            sum_gate,
-            sum_up,
-            sum_down,
-        )
-
     jobs = [
         ("line", last, grad_q[last]),
         ("return", 0, cut(grad_rows[last])),

time: 525 us -> 550 us (1.048)
  Pallas kernels: 504 us -> 529 us
    pallas_call x1, Pallas kernels: 91.6 us -> 107 us  [ending(): pl.pallas_call(kernel, out_shape=[jax.ShapeDtypeStruct((tokens, width), F...]
    pallas_call x4 -> x1, Pallas kernels: 179 us -> 188 us  [backward_part(): pl.pallas_call(kernel, grid=(count,), out_shape=[jax.ShapeDtypeStruct((PL...]
where the time goes in v8:
time: 550 us; the launch traced here: 542 us
  Pallas kernels  529 us (96%)
  local copies, waits for them, and re-layouts  11.2 us (2%)
    pallas_call x1, Pallas kernels, forward_part(): pl.pallas_call(kernel, grid=(count,), out_shape=[rows, rows, rows, stat,...  192 us
    pallas_call x1, Pallas kernels, backward_part(): pl.pallas_call(kernel, grid=(count,), out_shape=[jax.ShapeDtypeStruct((PL...  188 us
    pallas_call x1, Pallas kernels, ending(): pl.pallas_call(kernel, out_shape=[jax.ShapeDtypeStruct((tokens, width), F...  107 us
    pallas_call x1, Pallas kernels, middle(): pl.pallas_call(functools.partial(middle_kernel, sizes=sizes, packed=packe...  30.7 us
    pallas_call x1, Pallas kernels, finish(): pl.pallas_call(finish_kernel, out_shape=[jax.ShapeDtypeStruct((PLANES * s...  11.2 us

profile of v8, /device:TPU:0, one launch (start us, length us, event | category | flops | bytes accessed | tf_op | source)
XLA Modules:
  0.0 542.0 jit_solution(6155479535057583226)
XLA Ops:
  0.7 1.3 broadcast_in_dim.25.refs_1_.refs_21_
  1.9 1.3 broadcast_in_dim.26.refs_2_.refs_22_
  3.8 0.6 broadcast_in_dim.28.refs_8_
  4.4 0.0 copy-start.2
  4.4 191.8 %shard_map.305 = (bf16[512,768]{1,0:T(8,128)(2,1)}, bf16[512,768]{1,0:T(8,128)(2,1)}, bf16[512,768]{1,0:T(8,128)(2,1)}, f32[6,2,512]{2,1,0:T(2,128)}, bf16[512,7...) custom-call(bf16[512,768]{1,0:T(8,128)(2,1)} %bitcast.20, ...), custom_call_target="tpu_custom_call" | custom-call | tf_op jit(solution)/shard_map/pallas_call | solution.py:862
  196.3 0.0 copy-done.2
  196.3 0.6 broadcast_in_dim.29.refs_10_
  196.9 30.7 %shard_map.306 = (bf16[512,768]{1,0:T(8,128)(2,1)}, bf16[512,768]{1,0:T(8,128)(2,1)}, f32[512,768]{1,0:T(8,128)}, bf16[512,768]{1,0:T(8,128)(2,1)}, f32[2,6,2,51...) custom-call(bf16[512,768]{1,0:T(8,128)(2,1)} %get-tuple-element.74.r, ...), custom_call_target="tpu_custom_call" | custom-call | tf_op jit(solution)/shard_map/pallas_call | solution.py:1142
  227.6 188.0 %shard_map.307 = (bf16[4,2048,1536]{2,1,0:T(8,128)(2,1)}, bf16[4,48,2048]{2,1,0:T(8,128)(2,1)}, bf16[4,64,768]{2,1,0:T(8,128)(2,1)}, bf16[512,768]{1,0:T(8,128)(...) custom-call(bf16[4,2048,1536]{2,1,0:T(8,128)(2,1)} %get-tuple-elemen, ...), custom_call_target="tpu_custom_call" | custom-call | tf_op jit(solution)/shard_map/pallas_call | solution.py:1389
  415.5 107.3 %shard_map.308 = (f32[512,768]{1,0:T(8,128)}, f32[48,768]{1,0:T(8,128)}, f32[48,768]{1,0:T(8,128)}, f32[48,768]{1,0:T(8,128)}, f32[48,768]{1,0:T(8,128)}, /*inde...) custom-call(bf16[2048,768]{1,0:T(8,128)(2,1)} %bitcast.19, ...), custom_call_target="tpu_custom_call" | custom-call | tf_op jit(solution)/shard_map/pallas_call | solution.py:1708
  522.8 1.7 fusion.3
  524.5 1.7 fusion.5
  526.2 0.9 fusion.7
  527.1 0.6 fusion
  527.7 0.0 copy-start.1
  527.7 0.0 copy-start
  527.7 11.2 %shard_map.309 = (bf16[32,256,768]{2,1,0:T(8,128)(2,1)}, f32[24,2048]{1,0:T(8,128)}, f32[24,2048]{1,0:T(8,128)}, f32[64,768]{1,0:T(8,128)}) custom-call(bf16[8,256,768]{2,1,0:T(8,128)(2,1)} %get-tuple-element.116.refs_0_, bf16[8,256,768]{2,1,0:T(8,128)(2,1)} %get-tuple-element.117.refs_1_, bf16[8,256,768]{2,1,0:T(8,128)(2,1)} %get-tuple-element.118.refs_2_, ...), custom_call_target="tpu_custom_call" | custom-call | tf_op jit(solution)/shard_map/pallas_call | solution.py:1780
  538.9 0.6 fusion.2
  539.5 0.0 copy-done.1
  539.5 0.9 copy.38
  540.4 0.0 copy-done
  540.4 1.1 copy.39
Async XLA Ops:
  4.4 191.8 %copy-start.2 = (f32[768]{0:T(1024)S(1)}, f32[768]{0:T(1024)}, u32[]{:S(2)}) copy-start(f32[768]{0:T(1024)} %param.32) | copy-start | bytes 9220
  527.7 11.8 %copy-start.1 = (bf16[512,768]{1,0:T(8,128)(2,1)S(1)}, bf16[512,768]{1,0:T(8,128)(2,1)}, u32[]{:S(2)}) copy-start(bf16[512,768]{1,0:T(8,128)(2,1)} %get-tuple-element.83) | copy-start | bytes 2359300
  527.7 12.7 %copy-start = (f32[512,768]{1,0:T(8,128)S(1)}, f32[512,768]{1,0:T(8,128)}, u32[]{:S(2)}) copy-start(f32[512,768]{1,0:T(8,128)} %get-tuple-element.115) | copy-start | bytes 4718596

commit v9 on v7

--- a/solution.py
+++ b/solution.py
@@ -550,22 +550,22 @@
 
         body(own_in, own_out, own_scratch)
 
-        if sums:
+        for n in range(sums):
 
             @pl.when(step == 1)
-            def _():
-                for one in bound():
-                    one.after_first()
-
-            @pl.when(step == 3)
-            def _():
-                for one in bound():
-                    one.after_second()
+            def _(n=n):
+                bound()[n].after_first()
+
+            @pl.when(step == (2 + n if sums > 1 else 3))
+            def _(n=n):
+                bound()[n].after_second()
+
+            @pl.when(step == PAIRS - sums + n)
+            def _(n=n):
+                bound()[n].after_third(results[n])
 
         @pl.when(step == PAIRS - 1)
         def _():
-            for one, result in zip(bound(), results):
-                one.after_third(result)
             courier.wait(sources, targets, sems)
 
     return kernel
@@ -1165,15 +1165,21 @@
 
 
 def cross_backward(
-    courier, ident, r, queries, grad, keyvals, probs, tops, stats, key_weight, value_weight, summands=()
+    courier, ident, r, queries, grad, keyvals, probs, tops, stats, key_weight, value_weight,
+    summands=(), before=()
 ):
     tokens, keys = queries.shape[0], keyvals.shape[1]
     width = H * HD
     spec = block_specs(tokens, keys)
+    earlier = [
+        pl.BlockSpec((keys, width), lambda p: (0, 0), pipeline_mode=pl.Buffered(1)),
+        spec["pair"],
+        pl.BlockSpec((width, 256), lambda p: (0, p)),
+    ]
 
     def body(ins, outs, scratch):
-        q_ref, da_ref, kv_ref, probs_ref, top_ref, stats_ref, wk_ref, wv_ref = ins
-        dkv_ref, dq_ref, dm_ref = outs
+        q_ref, da_ref, kv_ref, probs_ref, top_ref, stats_ref, wk_ref, wv_ref = ins[:8]
+        dkv_ref, dq_ref, dm_ref = outs[:3]
         (total_ref,) = scratch
         step = pl.program_id(0)
 
@@ -1197,6 +1203,9 @@
         dkv_ref[...] = grad_kv
         dq_ref[...] = grad_q
         total_ref[...] += dot(grad_kv, weights, 1, 1)
+        if before:
+            term = dot(ins[8][...], ins[9][...], 0, 0)
+            outs[3][...] = term if len(before) == 2 else term + ins[10][...]
 
         @pl.when(step == PAIRS - 1)
         def _():
@@ -1206,7 +1215,7 @@
         courier,
         ident,
         body,
-        [queries, grad, keyvals, probs, tops, stats, key_weight, value_weight],
+        [queries, grad, keyvals, probs, tops, stats, key_weight, value_weight] + list(before),
         [
             spec["col"],
             spec["col"],
@@ -1216,13 +1225,15 @@
             pl.BlockSpec((2, 1, 2, tokens), lambda p: (0, p, 0, 0)),
             spec["weight"],
             spec["weight"],
-        ],
+        ]
+        + earlier[: len(before)],
         [
             jax.ShapeDtypeStruct((keys, 2 * width), BF),
             jax.ShapeDtypeStruct((tokens, width), BF),
             jax.ShapeDtypeStruct((keys, width), BF),
-        ],
-        [spec["pair"], spec["col"], spec["rows"]],
+        ]
+        + [jax.ShapeDtypeStruct((width, 2 * width), F32)] * bool(before),
+        [spec["pair"], spec["col"], spec["rows"]] + [earlier[2]] * bool(before),
         [pltpu.VMEM((keys, width), F32)],
         2**35,
         summands,
@@ -1294,7 +1305,7 @@
     return back, jnp.sum(grad * values * r, axis=0, keepdims=True)
 
 
-def ending(sizes, ident, rows, grads, grad_q, grad_rows, left, two, held, lse, small_in):
+def ending(sizes, ident, rows, grads, summed, grad_q, grad_rows, left, two, held, lse, small_in):
     courier = Courier(
         sizes,
         [("line", PLANES - 1, grad_q[-1]), ("return", 0, grad_rows)]
@@ -1312,7 +1323,8 @@
     groups += [Resident(sizes, (2 * share, 256)) for _ in range(6)]
     small = SmallSum(sizes, (8, width))
     early = [two] + list(held) + list(grad_q[:-1])
-    far = list(rows) + list(grads) + early
+    count = len(rows)
+    far = list(rows) + list(grads) + [summed] + early
     counts = (len(far), len(small_in) + 1, jobs, 6, jobs - 1, 4, len(early) - 1, 8, 3, 80, 10)
 
     def pack(ref, first, second, cols=EVERY):
@@ -1328,7 +1340,7 @@
         self_gain, cross_gain, ffn_term, lse_ref = near
         grad_in, *sums, norm_sums = outs
         row_buf, grad_buf, total, load_sems = stage
-        dq_got, da_ref, dq1, dk1, dv1, normed_ref, *_ = work
+        dq_got, da_ref, dq1, dk1, dv1, normed_ref, _, norm_all = work
         chunk_sems, early_sems = load_sems, work[6]
         copies = courier.copies(sources, [dq_got] + list(targets), sems)
         courier.greet()
@@ -1343,20 +1355,21 @@
                     far_refs[r].at[where], row_buf.at[slot], chunk_sems.at[slot, 0]
                 ),
                 pltpu.make_async_copy(
-                    far_refs[PLANES + r].at[where], grad_buf.at[slot], chunk_sems.at[slot, 1]
+                    far_refs[count + r].at[where], grad_buf.at[slot], chunk_sems.at[slot, 1]
                 ),
             ]
 
         def start_chunk(i):
-            for r in range(PLANES):
+            for r in range(count):
 
                 @pl.when(lax.div(jnp.int32(i), cuts) == r)
                 def _(r=r):
                     for copy in chunk_loads(r, i):
                         copy.start()
 
-        total[...] = jnp.zeros_like(total)
-        early_refs = far_refs[2 * PLANES :]
+        begin = pltpu.make_async_copy(far_refs[2 * count], total, early_sems.at[len(early)])
+        begin.start()
+        early_refs = far_refs[2 * count + 1 :]
         early_loads = [
             pltpu.make_async_copy(source, target, early_sems.at[n])
             for n, (source, target) in enumerate(zip(early_refs, [grad_in] + list(loaded)))
@@ -1365,9 +1378,11 @@
         for copy in early_loads:
             copy.start()
 
-        @pl.loop(0, PLANES * cuts)
+        begin.wait()
+
+        @pl.loop(0, count * cuts)
         def _(i):
-            @pl.when(i + 1 < PLANES * cuts)
+            @pl.when(i + 1 < count * cuts)
             def _():
                 start_chunk(i + 1)
 
@@ -1492,7 +1507,18 @@
         for n in range(2, 8):
             third, kind = divmod(n - 2, 2)
             bound[n].finish(sums[2 + kind].at[:, pl.ds(third * 256, 256)])
-        bits.advance(3, norm_sums)
+        bits.advance(3, norm_all)
+        device = lax.axis_index("z") * courier.plane + courier.me()
+        lane = lax.broadcasted_iota(jnp.int32, (width, 128), 0)
+        place_of = lax.broadcasted_iota(jnp.int32, (width, 128), 1) + device * share
+        pick = jnp.where(lane == place_of, 1.0, 0.0)
+        norm_sums[...] = lax.dot_general(
+            norm_all[...],
+            pick,
+            (((1,), (0,)), ((), ())),
+            precision=lax.Precision.HIGHEST,
+            preferred_element_type=F32,
+        )
         for n, copy in enumerate(copies):
             if n != 1:
                 copy.wait()
@@ -1507,8 +1533,8 @@
         pltpu.SemaphoreType.DMA((2, 2)),
     ]
     scratch += [pltpu.VMEM(v.shape, v.dtype) for v in early[1:]]
-    scratch += [row] * 6 + [pltpu.SemaphoreType.DMA((len(early),))]
-    scratch += [pltpu.SemaphoreType.DMA((1,))] + courier.scratch()
+    scratch += [row] * 6 + [pltpu.SemaphoreType.DMA((len(early) + 1,))]
+    scratch += [pltpu.VMEM((8, width), F32)] + courier.scratch()
     for one in groups:
         scratch += one.scratch()
     scratch += small.scratch()
@@ -1516,7 +1542,7 @@
         kernel,
         out_shape=[jax.ShapeDtypeStruct((tokens, width), F32)]
         + [jax.ShapeDtypeStruct((2 * share, width), F32)] * 4
-        + [jax.ShapeDtypeStruct((8, width), F32)]
+        + [jax.ShapeDtypeStruct((8, 128), F32)]
         + courier.out_shape()[1:],
         in_specs=[any_spec] * len(far) + [vmem] * (len(small_in) + 1) + courier.specs(),
         out_specs=[vmem] * 6 + courier.specs()[1:],
@@ -1717,6 +1743,8 @@
         }
     else:
         summands = {0: [grads_in[0], grad_down]}
+    part = width // devices
+    terms = ()
     left, got = {}, {}
 
     grads = {0: grad_attn_two}
@@ -1731,7 +1759,10 @@
             jobs.append(("return", 0, cut(grad_rows[r - 1])))
         if r >= 2:
             jobs.append(("line", r - 1, grad_q[r - 1]))
-        (grad_kv[r], grad_q[r], grad_rows[r]), moved = cross_backward(
+        before = ()
+        if part % 8 == 0 and r in (1, 2):
+            before = (rows[r - 1], grad_kv[r - 1]) + terms
+        (grad_kv[r], grad_q[r], grad_rows[r], *terms), moved = cross_backward(
             Courier(sizes, jobs),
             5 + r,
             r,
@@ -1744,7 +1775,11 @@
             cross_key,
             cross_value,
             summands.get(r, []),
+            before,
         )
+        terms = tuple(terms)
+        if terms:
+            summed = terms[0]
         moved = list(moved)
         if r in summands:
             for value in moved[len(moved) - len(summands[r]) :]:
@@ -1756,13 +1791,13 @@
         if r >= 2:
             grad_q[r - 1] = moved.pop(0)
     last = PLANES - 1
-    part = width // devices
     if part % 8 == 0:
         decoder_in_grad, sums, norm_sums, moved = ending(
             sizes,
             9,
-            [rows[r] for r in range(PLANES)],
-            [grad_kv[r] for r in range(PLANES)],
+            [rows[r] for r in (2, 3)],
+            [grad_kv[r] for r in (2, 3)],
+            summed,
             [grad_q[r] for r in range(PLANES)],
             cut(grad_rows[last]),
             [left[0], left[1]],
@@ -1776,10 +1811,7 @@
         memory_grad, sum_gate, sum_up, sum_down = finish(
             [returned[r] for r in range(PLANES)], left[0], got[0], left[1], got[1]
         )
-        here = lax.axis_index(ALL) * part
-        norm_self_sum, norm_cross_sum, norm_ffn_sum = (
-            lax.dynamic_slice_in_dim(norm_sums[n], here, part) for n in range(3)
-        )
+        norm_self_sum, norm_cross_sum, norm_ffn_sum = (norm_sums[n, :part] for n in range(3))
         return (
             decoder_out,
             decoder_in_grad[None],

time: 525 us -> 542 us (1.032)
  Pallas kernels: 504 us -> 521 us
    pallas_call x4, Pallas kernels: 179 us -> 196 us  [call(): pl.pallas_call(lambda *refs: kernel(*counts, refs), grid=(PAIRS,), out_sh...]
where the time goes in v9:
time: 542 us; the launch traced here: 534 us
  Pallas kernels  521 us (96%)
  local copies, waits for them, and re-layouts  11.1 us (2%)
    pallas_call x4, Pallas kernels, call(): pl.pallas_call(lambda *refs: kernel(*counts, refs), grid=(PAIRS,), out_sh...  196 us
    pallas_call x1, Pallas kernels, forward_part(): pl.pallas_call(kernel, grid=(count,), out_shape=[rows, rows, rows, stat,...  192 us
    pallas_call x1, Pallas kernels, ending(): pl.pallas_call(kernel, out_shape=[jax.ShapeDtypeStruct((tokens, width), F...  91.2 us
    pallas_call x1, Pallas kernels, middle(): pl.pallas_call(functools.partial(middle_kernel, sizes=sizes, packed=packe...  30.7 us
    pallas_call x1, Pallas kernels, finish(): pl.pallas_call(finish_kernel, out_shape=[jax.ShapeDtypeStruct((PLANES * s...  11.2 us

profile of v9, /device:TPU:0, one launch (start us, length us, event | category | flops | bytes accessed | tf_op | source)
XLA Modules:
  0.0 534.2 jit_solution(2059361440752323920)
XLA Ops:
  1.3 1.3 broadcast_in_dim.25.refs_1_.refs_21_
  2.6 1.3 broadcast_in_dim.26.refs_2_.refs_22_
  3.8 1.3 broadcast_in_dim.29.refs_10_
  5.1 0.6 broadcast_in_dim.28.refs_8_
  5.7 192.0 %shard_map.305 = (bf16[512,768]{1,0:T(8,128)(2,1)}, bf16[512,768]{1,0:T(8,128)(2,1)}, bf16[512,768]{1,0:T(8,128)(2,1)}, f32[6,2,512]{2,1,0:T(2,128)}, bf16[512,7...) custom-call(bf16[512,768]{1,0:T(8,128)(2,1)} %bitcast.28, ...), custom_call_target="tpu_custom_call" | custom-call | tf_op jit(solution)/shard_map/pallas_call | solution.py:862
  197.7 30.7 %shard_map.306 = (bf16[512,768]{1,0:T(8,128)(2,1)}, bf16[512,768]{1,0:T(8,128)(2,1)}, f32[512,768]{1,0:T(8,128)}, bf16[512,768]{1,0:T(8,128)(2,1)}, f32[2,6,2,51...) custom-call(bf16[512,768]{1,0:T(8,128)(2,1)} %get-tuple-element.90.r, ...), custom_call_target="tpu_custom_call" | custom-call | tf_op jit(solution)/shard_map/pallas_call | solution.py:1142
  228.4 50.5 %shard_map.307 = (bf16[2048,1536]{1,0:T(8,128)(2,1)}, bf16[512,768]{1,0:T(8,128)(2,1)}, bf16[2048,768]{1,0:T(8,128)(2,1)}, bf16[512,768]{1,0:T(8,128)(2,1)}, f32...) custom-call(bf16[512,768]{1,0:T(8,128)(2,1)} %get-tuple-element.104.refs_0_, ...), custom_call_target="tpu_custom_call" | custom-call | flops 34359738368 | bytes 16777216 | tf_op jit(solution)/shard_map/pallas_call | solution.py:583
  278.9 51.2 %shard_map.308 = (bf16[2048,1536]{1,0:T(8,128)(2,1)}, bf16[512,768]{1,0:T(8,128)(2,1)}, bf16[2048,768]{1,0:T(8,128)(2,1)}, f32[768,1536]{1,0:T(8,128)}, bf16[512...) custom-call(bf16[512,768]{1,0:T(8,128)(2,1)} %get-tuple-element.103.refs_0_, ...), custom_call_target="tpu_custom_call" | custom-call | flops 34359738368 | bytes 16777216 | tf_op jit(solution)/shard_map/pallas_call | solution.py:583
  330.1 51.3 %shard_map.309 = (bf16[2048,1536]{1,0:T(8,128)(2,1)}, bf16[512,768]{1,0:T(8,128)(2,1)}, bf16[2048,768]{1,0:T(8,128)(2,1)}, f32[768,1536]{1,0:T(8,128)}, bf16[512...) custom-call(bf16[512,768]{1,0:T(8,128)(2,1)} %get-tuple-element.102.refs_0, ...), custom_call_target="tpu_custom_call" | custom-call | flops 34359738368 | bytes 16777216 | tf_op jit(solution)/shard_map/pallas_call | solution.py:583
  381.4 43.2 %shard_map.310 = (bf16[2048,1536]{1,0:T(8,128)(2,1)}, bf16[512,768]{1,0:T(8,128)(2,1)}, bf16[2048,768]{1,0:T(8,128)(2,1)}, bf16[8,256,768]{2,1,0:T(8,128)(2,1)}, bf16[512,768]{1,0:T(8,128)(2,1)}) custom-call(bf16[512,768]{1,0:T(8,128)(2,1)} %get-tuple-element.125.refs_0_, bf16[512,768]{1,0:T(8,128)(2,1)} %get-tuple-element.126.refs_1_, ...), custom_call_target="tpu_custom_call" | custom-call | flops 34359738368 | bytes 16777216 | tf_op jit(solution)/shard_map/pallas_call | solution.py:583
  424.6 91.2 %shard_map.311 = (f32[512,768]{1,0:T(8,128)}, f32[48,768]{1,0:T(8,128)}, f32[48,768]{1,0:T(8,128)}, f32[48,768]{1,0:T(8,128)}, f32[48,768]{1,0:T(8,128)}, /*inde...) custom-call(bf16[2048,768]{1,0:T(8,128)(2,1)} %bitcast.20, ...), custom_call_target="tpu_custom_call" | custom-call | tf_op jit(solution)/shard_map/pallas_call | solution.py:1541
  515.8 1.3 slice_bitcast_fusion
  517.1 1.7 fusion.2
  518.8 1.7 fusion
  520.5 0.0 copy-start.1
  520.5 0.0 copy-start
  520.5 11.2 %shard_map.312 = (bf16[32,256,768]{2,1,0:T(8,128)(2,1)}, f32[24,2048]{1,0:T(8,128)}, f32[24,2048]{1,0:T(8,128)}, f32[64,768]{1,0:T(8,128)}) custom-call(bf16[8,256,768]{2,1,0:T(8,128)(2,1)} %get-tuple-element.148.refs_0_, bf16[8,256,768]{2,1,0:T(8,128)(2,1)} %get-tuple-element.149.refs_1_, bf16[8,256,768]{2,1,0:T(8,128)(2,1)} %get-tuple-element.150.refs_2_, ...), custom_call_target="tpu_custom_call" | custom-call | tf_op jit(solution)/shard_map/pallas_call | solution.py:1613
  531.7 0.0 copy-done.1
  531.8 0.9 copy.38
  532.6 0.0 copy-done
  532.6 1.1 copy.39
Async XLA Ops:
  520.5 11.2 %copy-start.1 = (bf16[512,768]{1,0:T(8,128)(2,1)S(1)}, bf16[512,768]{1,0:T(8,128)(2,1)}, u32[]{:S(2)}) copy-start(bf16[512,768]{1,0:T(8,128)(2,1)} %get-tuple-element.99) | copy-start | bytes 2359300
  520.5 12.1 %copy-start = (f32[512,768]{1,0:T(8,128)S(1)}, f32[512,768]{1,0:T(8,128)}, u32[]{:S(2)}) copy-start(f32[512,768]{1,0:T(8,128)} %get-tuple-element.147) | copy-start | bytes 4718596

commit v10 on v7

--- a/solution.py
+++ b/solution.py
@@ -470,8 +470,7 @@
         else:
             all_scores.append(dot(keys * mine + bias * one, queries * mine + one, 1, 1))
     parts = []
-    stats = []
-    held = []
+    lse = []
     for h in range(2):
         mine, other, _ = masks[h]
         scores = all_scores[h]
@@ -481,9 +480,8 @@
         halves = (both[:HD], both[HD:])
         total = halves[1 - h]
         parts.append(halves[h] / total)
-        stats.append((row_max + jnp.log(total[0:1]), row_max))
-        held.append(probs)
-    return jnp.concatenate(parts, axis=0).T.astype(BF), stats, held
+        lse.append(row_max + jnp.log(total[0:1]))
+    return jnp.concatenate(parts, axis=0).T.astype(BF), lse
 
 
 def backward_pair(queries, grad, keys, values, probs_of, delta):
@@ -722,12 +720,12 @@
     count = PLANES * PAIRS
 
     def kernel(*refs):
-        ins, sources, outs, parts, targets, work, sems = split_refs(refs, 11, 1, 8, 4, 13, 7, 3)
+        ins, sources, outs, parts, targets, work, sems = split_refs(refs, 11, 1, 8, 3, 13, 7, 3)
         x_ref, self_gain, cross_gain, wq_ref, wk_ref, wv_ref, wo_ref, wc_ref = ins[:8]
         lens_ref, key_ref, value_ref = ins[8:]
         (memory_ref,) = sources
-        q_ref, k_ref, v_ref, lse_ref, attn_ref, hidden_ref, query_ref, top_ref = outs
-        part_ref, part_lse_ref, kv_ref, probs_ref = parts
+        q_ref, k_ref, v_ref, lse_ref, attn_ref, hidden_ref, query_ref, lens_out = outs
+        part_ref, part_lse_ref, kv_ref = parts
         row_buf, query_buf, out_buf, lse_buf, lens_buf, near_lens, load_sems = work
         copies = courier.copies(
             [memory_ref] * PLANES
@@ -766,10 +764,10 @@
             @pl.loop(0, PAIRS)
             def _(p):
                 cols = pl.ds(pl.multiple_of(p * 128, 128), 128)
-                out, stats, _ = forward_pair(q_ref[:, cols], k_ref[:, cols], v_ref[:, cols], None)
+                out, lse = forward_pair(q_ref[:, cols], k_ref[:, cols], v_ref[:, cols], None)
                 attn_ref[:, cols] = out
                 for h in range(2):
-                    lse_ref[p, h : h + 1, :] = stats[h][0]
+                    lse_ref[p, h : h + 1, :] = lse[h]
 
             hidden = values + dot(attn_ref[...], wo_ref[...], 1, 0)
             hidden_ref[...] = hidden
@@ -821,12 +819,10 @@
         both = jnp.concatenate([key_ref[...], value_ref[...]], axis=1)
         kv_ref[...] = dot(row_buf[...], both, 1, 0).astype(BF)
         bias = key_bias(keys, lens_buf[...])
-        out, stats, held = forward_pair(query_buf[:, cols], kv_ref[:, :128], kv_ref[:, 128:], bias)
+        out, lse = forward_pair(query_buf[:, cols], kv_ref[:, :128], kv_ref[:, 128:], bias)
         out_buf[phase, :, cols] = out
         for h in range(2):
-            probs_ref[h] = held[h]
-            lse_buf[phase, p, h : h + 1, :] = stats[h][0]
-            top_ref[phase, p, h : h + 1, :] = stats[h][1]
+            lse_buf[phase, p, h : h + 1, :] = lse[h]
 
         for n, r in enumerate(ORDER[:-1]):
 
@@ -837,6 +833,9 @@
 
         @pl.when(step == count - 1)
         def _():
+            lens_out[0] = lens_ref[...]
+            for r in near:
+                lens_out[r] = near_lens[r - 1]
             part_ref[...] = out_buf[PLANES - 1]
             part_lse_ref[...] = lse_buf[PLANES - 1]
             for copy in out_lines + lse_lines:
@@ -863,11 +862,8 @@
         kernel,
         grid=(count,),
         out_shape=[rows, rows, rows, stat, rows, wide, rows]
-        + [jax.ShapeDtypeStruct((PLANES, PAIRS, 2, tokens), F32), rows, stat]
-        + [
-            jax.ShapeDtypeStruct((PLANES, keys, 2 * width), BF),
-            jax.ShapeDtypeStruct((PLANES, H, keys, tokens), BF),
-        ]
+        + [jax.ShapeDtypeStruct((PLANES, 8, 128), jnp.int32), rows, stat]
+        + [jax.ShapeDtypeStruct((PLANES, keys, 2 * width), BF)]
         + shapes[:4]
         + shapes[7:],
         in_specs=[fixed(tokens, width), fixed(1, width), fixed(1, width)]
@@ -876,11 +872,8 @@
         out_specs=[flat] * 3
         + [flat_stat]
         + [flat] * 3
-        + [out_fixed(PLANES, PAIRS, 2, tokens), flat, flat_stat]
-        + [
-            pl.BlockSpec((None, keys, 256), lambda t: (where(t)[0], 0, where(t)[1])),
-            pl.BlockSpec((None, 2, keys, tokens), lambda t: where(t) + (0, 0)),
-        ]
+        + [out_fixed(PLANES, 8, 128), flat, flat_stat]
+        + [pl.BlockSpec((None, keys, 256), lambda t: (where(t)[0], 0, where(t)[1]))]
         + [hbm] * 13,
         scratch_shapes=[
             pltpu.VMEM((keys, width), BF),
@@ -896,12 +889,11 @@
             vmem_limit_bytes=62 * 2**20, collective_id=ident, has_side_effects=True
         ),
     )(inputs, *gains, *weights, lens, key_weight, value_weight, memory)
-    saved, (tops, part0, lse0, kv, probs), moved = outs[:7], outs[7:12], outs[12:]
+    saved, (all_lens, part0, lse0, kv), moved = outs[:7], outs[7:11], outs[11:]
     return dict(
         saved=saved,
-        tops=tops,
+        lens=all_lens,
         keyvals=kv,
-        probs=probs,
         rows={r: moved[n] for n, r in enumerate(ORDER)},
         queries={0: saved[6], **{r: moved[3 + r] for r in near}},
         parts=[part0] + [moved[6 + r] for r in near],
@@ -1165,14 +1157,14 @@
 
 
 def cross_backward(
-    courier, ident, r, queries, grad, keyvals, probs, tops, stats, key_weight, value_weight, summands=()
+    courier, ident, r, queries, grad, keyvals, lens, stats, key_weight, value_weight, summands=()
 ):
     tokens, keys = queries.shape[0], keyvals.shape[1]
     width = H * HD
     spec = block_specs(tokens, keys)
 
     def body(ins, outs, scratch):
-        q_ref, da_ref, kv_ref, probs_ref, top_ref, stats_ref, wk_ref, wv_ref = ins
+        q_ref, da_ref, kv_ref, lens_ref, stats_ref, wk_ref, wv_ref = ins
         dkv_ref, dq_ref, dm_ref = outs
         (total_ref,) = scratch
         step = pl.program_id(0)
@@ -1181,9 +1173,12 @@
         def _():
             total_ref[...] = jnp.zeros_like(total_ref)
 
-        def stored(h, keys_h, query_h):
-            scale = jnp.exp(top_ref[0, h : h + 1, :] - stats_ref[0, 0, h : h + 1, :])
-            return probs_ref[h].astype(F32) * scale
+        bias = key_bias(keys, lens_ref[...])
+
+        def again(h, keys_h, query_h):
+            mine, _, one = lane_masks()[h]
+            scores = dot(keys_h * mine + bias * one, query_h + one, 1, 1)
+            return jnp.exp(scores - stats_ref[0, 0, h : h + 1, :])
 
         weights = jnp.concatenate([wk_ref[...], wv_ref[...]], axis=1)
         grad_kv, grad_q = backward_pair(
@@ -1191,7 +1186,7 @@
             da_ref[...],
             kv_ref[:, :128],
             kv_ref[:, 128:],
-            stored,
+            again,
             [stats_ref[1, 0, h : h + 1, :] for h in range(2)],
         )
         dkv_ref[...] = grad_kv
@@ -1206,13 +1201,12 @@
         courier,
         ident,
         body,
-        [queries, grad, keyvals, probs, tops, stats, key_weight, value_weight],
+        [queries, grad, keyvals, lens, stats, key_weight, value_weight],
         [
             spec["col"],
             spec["col"],
             pl.BlockSpec((None, keys, 256), lambda p: (r, 0, p)),
-            pl.BlockSpec((None, 2, keys, tokens), lambda p: (r, p, 0, 0)),
-            pl.BlockSpec((None, 1, 2, tokens), lambda p: (rem(r + 3, PLANES), p, 0, 0)),
+            pl.BlockSpec((None, 8, 128), lambda p: (r, 0, 0)),
             pl.BlockSpec((2, 1, 2, tokens), lambda p: (0, p, 0, 0)),
             spec["weight"],
             spec["weight"],
@@ -1328,7 +1322,7 @@
         self_gain, cross_gain, ffn_term, lse_ref = near
         grad_in, *sums, norm_sums = outs
         row_buf, grad_buf, total, load_sems = stage
-        dq_got, da_ref, dq1, dk1, dv1, normed_ref, *_ = work
+        dq_got, da_ref, dq1, dk1, dv1, normed_ref, _, norm_all = work
         chunk_sems, early_sems = load_sems, work[6]
         copies = courier.copies(sources, [dq_got] + list(targets), sems)
         courier.greet()
@@ -1461,38 +1455,46 @@
                 bound[3].after_second()
                 bound[4].after_first()
                 bound[5].after_first()
-        grad_normed = (
-            dot(dq1[...], wq_ref[...], 1, 1)
-            + dot(dk1[...], wk_ref[...], 1, 1)
-            + dot(dv1[...], wv_ref[...], 1, 1)
-        )
+        grad_normed = dot(dq1[...], wq_ref[...], 1, 1) + dot(dk1[...], wk_ref[...], 1, 1)
+        bound[6].after_first()
+        bound[7].after_first()
+        bound[2].after_third_start()
+        bound[3].after_third_start()
+        grad_normed += dot(dv1[...], wv_ref[...], 1, 1)
         back, self_norm = rms_back(values, self_gain[...], grad_normed)
+        bound[4].after_second()
+        bound[5].after_second()
+        bound[6].after_second()
+        bound[7].after_second()
         grad_in[...] += back
         bits.held[0][...] = jnp.concatenate(
             [self_norm, cross_norm, ffn_term[...], jnp.zeros((5, width), F32)], axis=0
         )
         bits.start(0)
-        bound[2].after_third_start()
-        bound[3].after_third_start()
-        bound[4].after_second()
-        bound[5].after_second()
-        bound[6].after_first()
-        bound[7].after_first()
-        bits.advance(0)
         bound[4].after_third_start()
         bound[5].after_third_start()
-        bound[6].after_second()
-        bound[7].after_second()
-        bits.advance(1)
+        bits.advance(0)
         bound[6].after_third_start()
         bound[7].after_third_start()
+        bits.advance(1)
         bits.advance(2)
         bound[0].finish(sums[0])
         bound[1].finish(sums[1])
         for n in range(2, 8):
             third, kind = divmod(n - 2, 2)
             bound[n].finish(sums[2 + kind].at[:, pl.ds(third * 256, 256)])
-        bits.advance(3, norm_sums)
+        bits.advance(3, norm_all)
+        device = lax.axis_index("z") * courier.plane + courier.me()
+        lane = lax.broadcasted_iota(jnp.int32, (width, 128), 0)
+        place_of = lax.broadcasted_iota(jnp.int32, (width, 128), 1) + device * share
+        pick = jnp.where(lane == place_of, 1.0, 0.0)
+        norm_sums[...] = lax.dot_general(
+            norm_all[...],
+            pick,
+            (((1,), (0,)), ((), ())),
+            precision=lax.Precision.HIGHEST,
+            preferred_element_type=F32,
+        )
         for n, copy in enumerate(copies):
             if n != 1:
                 copy.wait()
@@ -1508,7 +1510,7 @@
     ]
     scratch += [pltpu.VMEM(v.shape, v.dtype) for v in early[1:]]
     scratch += [row] * 6 + [pltpu.SemaphoreType.DMA((len(early),))]
-    scratch += [pltpu.SemaphoreType.DMA((1,))] + courier.scratch()
+    scratch += [pltpu.VMEM((8, width), F32)] + courier.scratch()
     for one in groups:
         scratch += one.scratch()
     scratch += small.scratch()
@@ -1516,7 +1518,7 @@
         kernel,
         out_shape=[jax.ShapeDtypeStruct((tokens, width), F32)]
         + [jax.ShapeDtypeStruct((2 * share, width), F32)] * 4
-        + [jax.ShapeDtypeStruct((8, width), F32)]
+        + [jax.ShapeDtypeStruct((8, 128), F32)]
         + courier.out_shape()[1:],
         in_specs=[any_spec] * len(far) + [vmem] * (len(small_in) + 1) + courier.specs(),
         out_specs=[vmem] * 6 + courier.specs()[1:],
@@ -1548,24 +1550,34 @@
         copy.wait()
 
 
-def finish_kernel(*refs):
-    blocks = refs[:PLANES]
-    left0, got0, left1, got1, out_ref, gate_ref, up_ref, down_ref = refs[PLANES : PLANES + 8]
-    held, arrive, leave = refs[PLANES + 8 :]
+def finish_kernel(*refs, pieces):
+    ins, far, outs, far_outs, work = split_refs(refs, 9, PLANES + 2, 14, 3, 5)
+    left0, got0, left1, got1, *sums, norms = ins
+    gate_ref, up_ref, down_ref, *halves = outs
+    halves, norm_outs = halves[:8], halves[8:]
+    blocks, others = far[:PLANES], far[PLANES:]
+    out_ref, *other_outs = far_outs
+    held, held_in, held_out, arrive, leave = work
     z = lax.axis_index("z")
     size = held.shape[1]
+    part = size // pieces
+    moves = []
+    for r, block in enumerate(blocks):
+        at = rem(z + r, PLANES) * size
+        for n in range(pieces):
+            rows = pl.ds(n * part, part)
+            moves.append((block.at[rows], held.at[r, rows], out_ref.at[pl.ds(at + n * part, part)]))
+    moves.append((others[0], held_in, other_outs[0]))
+    moves.append((others[1], held_out, other_outs[1]))
     inward = []
     outward = []
-    for r, block in enumerate(blocks):
-        at = rem(z + r, PLANES) * size
-        inward.append(pltpu.make_async_copy(block, held.at[r], arrive.at[r]))
-        outward.append(
-            pltpu.make_async_copy(held.at[r], out_ref.at[pl.ds(at, size)], leave.at[r])
-        )
-        inward[r].start()
-    for r in range(PLANES):
-        inward[r].wait()
-        outward[r].start()
+    for n, (source, middle_ref, target) in enumerate(moves):
+        inward.append(pltpu.make_async_copy(source, middle_ref, arrive.at[n]))
+        outward.append(pltpu.make_async_copy(middle_ref, target, leave.at[n]))
+        inward[n].start()
+    for n in range(len(moves)):
+        inward[n].wait()
+        outward[n].start()
     share = gate_ref.shape[0]
     wide = left0[z].astype(F32)
     tall = left1[z].astype(F32)
@@ -1575,29 +1587,43 @@
     gate_ref[...] = wide[:share]
     up_ref[...] = wide[share:]
     down_ref[...] = tall
+    for n, ref in enumerate(sums):
+        halves[2 * n][...] = ref[:share]
+        halves[2 * n + 1][...] = ref[share:]
+    for n, ref in enumerate(norm_outs):
+        ref[...] = norms[n : n + 1]
     for copy in outward:
         copy.wait()
 
 
-def finish(blocks, left0, got0, left1, got1):
+def finish(blocks, left0, got0, left1, got1, sums, norms, grad_in, output):
     shape = blocks[0].shape
+    pieces = 4 if shape[0] % 4 == 0 else 1
     share, inner = left0.shape[1] // 2, left0.shape[2]
+    width = sums[0].shape[1]
     hbm = pl.BlockSpec(memory_space=pl.ANY)
     vmem = pl.BlockSpec(memory_space=pltpu.VMEM)
-    return pl.pallas_call(
-        finish_kernel,
-        out_shape=[jax.ShapeDtypeStruct((PLANES * shape[0],) + shape[1:], BF)]
-        + [jax.ShapeDtypeStruct((share, inner), F32)] * 2
-        + [jax.ShapeDtypeStruct(left1.shape[1:], F32)],
-        in_specs=[hbm] * PLANES + [vmem] * 4,
-        out_specs=[hbm] + [vmem] * 3,
+    moves = PLANES * pieces + 2
+    outs = pl.pallas_call(
+        functools.partial(finish_kernel, pieces=pieces),
+        out_shape=[jax.ShapeDtypeStruct((share, inner), F32)] * 2
+        + [jax.ShapeDtypeStruct(left1.shape[1:], F32)]
+        + [jax.ShapeDtypeStruct((share, width), F32)] * 8
+        + [jax.ShapeDtypeStruct((1, norms.shape[1]), F32)] * 3
+        + [jax.ShapeDtypeStruct((PLANES * shape[0],) + shape[1:], BF)]
+        + [jax.ShapeDtypeStruct(v.shape, v.dtype) for v in (grad_in, output)],
+        in_specs=[vmem] * 9 + [hbm] * (PLANES + 2),
+        out_specs=[vmem] * 14 + [hbm] * 3,
         scratch_shapes=[
             pltpu.VMEM((PLANES,) + shape, BF),
-            pltpu.SemaphoreType.DMA((PLANES,)),
-            pltpu.SemaphoreType.DMA((PLANES,)),
+            pltpu.VMEM(grad_in.shape, grad_in.dtype),
+            pltpu.VMEM(output.shape, output.dtype),
+            pltpu.SemaphoreType.DMA((moves,)),
+            pltpu.SemaphoreType.DMA((moves,)),
         ],
         compiler_params=pltpu.CompilerParams(vmem_limit_bytes=VMEM),
-    )(*blocks, left0, got0, left1, got1)
+    )(left0, got0, left1, got1, *sums, norms, *blocks, grad_in, output)
+    return outs[:3], outs[3:11], outs[11:14], outs[14:]
 
 
 def place(blocks):
@@ -1738,8 +1764,7 @@
             queries[r],
             grads[r],
             forward["keyvals"],
-            forward["probs"],
-            forward["tops"],
+            forward["lens"],
             both[r],
             cross_key,
             cross_value,
@@ -1773,31 +1798,33 @@
             (norm_self[None], norm_cross[None], grad_norm_ffn),
         )
         returned[last], got[0], got[1] = moved
-        memory_grad, sum_gate, sum_up, sum_down = finish(
-            [returned[r] for r in range(PLANES)], left[0], got[0], left[1], got[1]
+        ffn, halves, norm_rows, whole = finish(
+            [returned[r] for r in range(PLANES)],
+            left[0],
+            got[0],
+            left[1],
+            got[1],
+            sums,
+            norm_sums,
+            decoder_in_grad,
+            output,
         )
-        here = lax.axis_index(ALL) * part
-        norm_self_sum, norm_cross_sum, norm_ffn_sum = (
-            lax.dynamic_slice_in_dim(norm_sums[n], here, part) for n in range(3)
-        )
+        memory_grad, decoder_in_grad, output = whole
+        norm_self_sum, norm_cross_sum, norm_ffn_sum = (v[0, :part] for v in norm_rows)
+        sum_cross_key, sum_cross_value, sum_cross_query, sum_cross_out = halves[:4]
         return (
-            decoder_out,
+            output[None],
             decoder_in_grad[None],
             memory_grad,
             norm_self_sum,
-            sums[2][:part],
-            sums[2][part:],
-            sums[3][:part],
-            sums[3][part:],
+            *halves[4:],
             norm_cross_sum,
-            sums[1][:part],
-            sums[0][:part],
-            sums[0][part:],
-            sums[1][part:],
+            sum_cross_query,
+            sum_cross_key,
+            sum_cross_value,
+            sum_cross_out,
             norm_ffn_sum,
-            sum_gate,
-            sum_up,
-            sum_down,
+            *ffn,
         )
 
     jobs = [

time: 525 us -> 562 us (1.070)
  Pallas kernels: 504 us -> 546 us
    pallas_call x1, Pallas kernels: 192 us -> 215 us  [forward_part(): pl.pallas_call(kernel, grid=(count,), out_shape=[rows, rows, rows, stat,...]
    pallas_call x1, Pallas kernels: 30.7 us -> 46.5 us  [middle(): pl.pallas_call(functools.partial(middle_kernel, sizes=sizes, packed=packe...]
where the time goes in v10:
time: 562 us; the launch traced here: 555 us
  Pallas kernels  546 us (97%)
  local copies, waits for them, and re-layouts  6.75 us (1%)
    pallas_call x1, Pallas kernels, forward_part(): pl.pallas_call(kernel, grid=(count,), out_shape=[rows, rows, rows, stat,...  215 us
    pallas_call x4, Pallas kernels, call(): pl.pallas_call(lambda *refs: kernel(*counts, refs), grid=(PAIRS,), out_sh...  178 us
    pallas_call x1, Pallas kernels, ending(): pl.pallas_call(kernel, out_shape=[jax.ShapeDtypeStruct((tokens, width), F...  93.4 us
    pallas_call x1, Pallas kernels, middle(): pl.pallas_call(functools.partial(middle_kernel, sizes=sizes, packed=packe...  46.5 us
    pallas_call x1, Pallas kernels, finish(): pl.pallas_call(functools.partial(finish_kernel, pieces=pieces), out_shape...  13.9 us

profile of v10, /device:TPU:0, one launch (start us, length us, event | category | flops | bytes accessed | tf_op | source)
XLA Modules:
  0.0 554.9 jit_solution(9446751458777880477)
XLA Ops:
  1.3 1.3 broadcast_in_dim.25.refs_1_.refs_24_
  2.6 1.3 broadcast_in_dim.26.refs_2_.refs_25_
  3.8 1.3 broadcast_in_dim.29.refs_10_
  5.1 0.6 broadcast_in_dim.28.refs_8_
  5.7 214.5 %shard_map.305 = (bf16[512,768]{1,0:T(8,128)(2,1)}, bf16[512,768]{1,0:T(8,128)(2,1)}, bf16[512,768]{1,0:T(8,128)(2,1)}, f32[6,2,512]{2,1,0:T(2,128)}, bf16[512,7...) custom-call(bf16[512,768]{1,0:T(8,128)(2,1)} %bitcast.25, ...), custom_call_target="tpu_custom_call" | custom-call | tf_op jit(solution)/shard_map/pallas_call | solution.py:861
  220.2 46.5 %shard_map.306 = (bf16[512,768]{1,0:T(8,128)(2,1)}, bf16[512,768]{1,0:T(8,128)(2,1)}, f32[512,768]{1,0:T(8,128)}, bf16[512,768]{1,0:T(8,128)(2,1)}, f32[2,6,2,51...) custom-call(bf16[512,768]{1,0:T(8,128)(2,1)} %get-tuple-element.101., ...), custom_call_target="tpu_custom_call" | custom-call | tf_op jit(solution)/shard_map/pallas_call | solution.py:1134
  266.7 47.5 %shard_map.307 = (bf16[2048,1536]{1,0:T(8,128)(2,1)}, bf16[512,768]{1,0:T(8,128)(2,1)}, bf16[2048,768]{1,0:T(8,128)(2,1)}, bf16[512,768]{1,0:T(8,128)(2,1)}, f32...) custom-call(bf16[512,768]{1,0:T(8,128)(2,1)} %get-tuple-element.100.refs_0_, ...), custom_call_target="tpu_custom_call" | custom-call | flops 34359738368 | bytes 16777216 | tf_op jit(solution)/shard_map/pallas_call | solution.py:581
  314.2 43.5 %shard_map.308 = (bf16[2048,1536]{1,0:T(8,128)(2,1)}, bf16[512,768]{1,0:T(8,128)(2,1)}, bf16[2048,768]{1,0:T(8,128)(2,1)}, bf16[512,768]{1,0:T(8,128)(2,1)}, f32...) custom-call(bf16[512,768]{1,0:T(8,128)(2,1)} %get-tuple-element.122.refs_0_, ...), custom_call_target="tpu_custom_call" | custom-call | flops 34359738368 | bytes 16777216 | tf_op jit(solution)/shard_map/pallas_call | solution.py:581
  357.8 43.8 %shard_map.309 = (bf16[2048,1536]{1,0:T(8,128)(2,1)}, bf16[512,768]{1,0:T(8,128)(2,1)}, bf16[2048,768]{1,0:T(8,128)(2,1)}, bf16[512,768]{1,0:T(8,128)(2,1)}, f32...) custom-call(bf16[512,768]{1,0:T(8,128)(2,1)} %get-tuple-element.127.refs_0_, ...), custom_call_target="tpu_custom_call" | custom-call | flops 34359738368 | bytes 16777216 | tf_op jit(solution)/shard_map/pallas_call | solution.py:581
  401.6 43.2 %shard_map.310 = (bf16[2048,1536]{1,0:T(8,128)(2,1)}, bf16[512,768]{1,0:T(8,128)(2,1)}, bf16[2048,768]{1,0:T(8,128)(2,1)}, bf16[8,256,768]{2,1,0:T(8,128)(2,1)}, bf16[512,768]{1,0:T(8,128)(2,1)}) custom-call(bf16[512,768]{1,0:T(8,128)(2,1)} %get-tuple-element.133.refs_0_, bf16[512,768]{1,0:T(8,128)(2,1)} %get-tuple-element.134.refs_1_, ...), custom_call_target="tpu_custom_call" | custom-call | flops 34359738368 | bytes 16777216 | tf_op jit(solution)/shard_map/pallas_call | solution.py:581
  444.8 93.4 %shard_map.311 = (f32[512,768]{1,0:T(8,128)}, f32[48,768]{1,0:T(8,128)}, f32[48,768]{1,0:T(8,128)}, f32[48,768]{1,0:T(8,128)}, f32[48,768]{1,0:T(8,128)}, /*inde...) custom-call(bf16[2048,768]{1,0:T(8,128)(2,1)} %bitcast.23, ...), custom_call_target="tpu_custom_call" | custom-call | tf_op jit(solution)/shard_map/pallas_call | solution.py:1517
  538.2 13.9 %shard_map.312 = (f32[24,2048]{1,0:T(8,128)}, f32[24,2048]{1,0:T(8,128)}, f32[64,768]{1,0:T(8,128)}, f32[24,768]{1,0:T(8,128)}, f32[24,768]{1,0:T(8,128)}, /*ind...) custom-call(bf16[4,48,2048]{2,1,0:T(8,128)(2,1)} %get-tuple-element., ...), custom_call_target="tpu_custom_call" | custom-call | tf_op jit(solution)/shard_map/pallas_call | solution.py:1607
  552.1 1.2 slice_bitcast_fusion.2
  553.3 1.2 slice_bitcast_fusion

commit v11 on v10

--- a/solution.py
+++ b/solution.py
@@ -470,7 +470,8 @@
         else:
             all_scores.append(dot(keys * mine + bias * one, queries * mine + one, 1, 1))
     parts = []
-    lse = []
+    stats = []
+    held = []
     for h in range(2):
         mine, other, _ = masks[h]
         scores = all_scores[h]
@@ -480,8 +481,9 @@
         halves = (both[:HD], both[HD:])
         total = halves[1 - h]
         parts.append(halves[h] / total)
-        lse.append(row_max + jnp.log(total[0:1]))
-    return jnp.concatenate(parts, axis=0).T.astype(BF), lse
+        stats.append((row_max + jnp.log(total[0:1]), row_max))
+        held.append(probs)
+    return jnp.concatenate(parts, axis=0).T.astype(BF), stats, held
 
 
 def backward_pair(queries, grad, keys, values, probs_of, delta):
@@ -703,7 +705,7 @@
 ORDER = (1, 2, 3, 0)
 
 
-def forward_part(sizes, ident, memory, lens, inputs, gains, weights, key_weight, value_weight):
+def forward_part(sizes, ident, memory, length, inputs, gains, weights, key_weight, value_weight):
     tokens, width = inputs.shape
     positions = memory.shape[1]
     plane = sizes[1] * sizes[2] * sizes[3]
@@ -712,6 +714,7 @@
     wide = jax.ShapeDtypeStruct((tokens, width), F32)
     stat = jax.ShapeDtypeStruct((PAIRS, 2, tokens), F32)
     near = range(1, PLANES)
+    lens = jax.ShapeDtypeStruct((8, 128), jnp.int32)
     jobs = [("fetch", r, memory) for r in ORDER]
     jobs += [("line", -r, lens) for r in near] + [("line", -r, rows) for r in near]
     jobs += [("line", r, rows) for r in near] + [("line", r, stat) for r in near]
@@ -720,13 +723,13 @@
     count = PLANES * PAIRS
 
     def kernel(*refs):
-        ins, sources, outs, parts, targets, work, sems = split_refs(refs, 11, 1, 8, 3, 13, 7, 3)
+        ins, sources, outs, parts, targets, work, sems = split_refs(refs, 11, 1, 8, 4, 13, 8, 3)
         x_ref, self_gain, cross_gain, wq_ref, wk_ref, wv_ref, wo_ref, wc_ref = ins[:8]
-        lens_ref, key_ref, value_ref = ins[8:]
+        length_ref, key_ref, value_ref = ins[8:]
         (memory_ref,) = sources
-        q_ref, k_ref, v_ref, lse_ref, attn_ref, hidden_ref, query_ref, lens_out = outs
-        part_ref, part_lse_ref, kv_ref = parts
-        row_buf, query_buf, out_buf, lse_buf, lens_buf, near_lens, load_sems = work
+        q_ref, k_ref, v_ref, lse_ref, attn_ref, hidden_ref, query_ref, top_ref = outs
+        part_ref, part_lse_ref, kv_ref, probs_ref = parts
+        row_buf, query_buf, out_buf, lse_buf, lens_buf, near_lens, lens_ref, load_sems = work
         copies = courier.copies(
             [memory_ref] * PLANES
             + [lens_ref] * 3
@@ -753,6 +756,7 @@
         def _():
             courier.greet()
             start_fetch(0)
+            lens_ref[...] = jnp.full((8, 128), length_ref[0], jnp.int32)
             for copy in lens_lines:
                 copy.start()
             values = x_ref[...].astype(F32)
@@ -764,10 +768,10 @@
             @pl.loop(0, PAIRS)
             def _(p):
                 cols = pl.ds(pl.multiple_of(p * 128, 128), 128)
-                out, lse = forward_pair(q_ref[:, cols], k_ref[:, cols], v_ref[:, cols], None)
+                out, stats, _ = forward_pair(q_ref[:, cols], k_ref[:, cols], v_ref[:, cols], None)
                 attn_ref[:, cols] = out
                 for h in range(2):
-                    lse_ref[p, h : h + 1, :] = lse[h]
+                    lse_ref[p, h : h + 1, :] = stats[h][0]
 
             hidden = values + dot(attn_ref[...], wo_ref[...], 1, 0)
             hidden_ref[...] = hidden
@@ -819,10 +823,12 @@
         both = jnp.concatenate([key_ref[...], value_ref[...]], axis=1)
         kv_ref[...] = dot(row_buf[...], both, 1, 0).astype(BF)
         bias = key_bias(keys, lens_buf[...])
-        out, lse = forward_pair(query_buf[:, cols], kv_ref[:, :128], kv_ref[:, 128:], bias)
+        out, stats, held = forward_pair(query_buf[:, cols], kv_ref[:, :128], kv_ref[:, 128:], bias)
         out_buf[phase, :, cols] = out
         for h in range(2):
-            lse_buf[phase, p, h : h + 1, :] = lse[h]
+            probs_ref[h] = held[h]
+            lse_buf[phase, p, h : h + 1, :] = stats[h][0]
+            top_ref[phase, p, h : h + 1, :] = stats[h][1]
 
         for n, r in enumerate(ORDER[:-1]):
 
@@ -833,9 +839,6 @@
 
         @pl.when(step == count - 1)
         def _():
-            lens_out[0] = lens_ref[...]
-            for r in near:
-                lens_out[r] = near_lens[r - 1]
             part_ref[...] = out_buf[PLANES - 1]
             part_lse_ref[...] = lse_buf[PLANES - 1]
             for copy in out_lines + lse_lines:
@@ -862,18 +865,24 @@
         kernel,
         grid=(count,),
         out_shape=[rows, rows, rows, stat, rows, wide, rows]
-        + [jax.ShapeDtypeStruct((PLANES, 8, 128), jnp.int32), rows, stat]
-        + [jax.ShapeDtypeStruct((PLANES, keys, 2 * width), BF)]
+        + [jax.ShapeDtypeStruct((PLANES, PAIRS, 2, tokens), F32), rows, stat]
+        + [
+            jax.ShapeDtypeStruct((PLANES, keys, 2 * width), BF),
+            jax.ShapeDtypeStruct((PLANES, H, keys, tokens), BF),
+        ]
         + shapes[:4]
         + shapes[7:],
-        in_specs=[fixed(tokens, width), fixed(1, width), fixed(1, width)]
+        in_specs=[fixed(tokens, width), fixed(width), fixed(width)]
         + [square] * 5
-        + [fixed(8, 128), weight, weight, hbm],
+        + [pl.BlockSpec(memory_space=pltpu.SMEM), weight, weight, hbm],
         out_specs=[flat] * 3
         + [flat_stat]
         + [flat] * 3
-        + [out_fixed(PLANES, 8, 128), flat, flat_stat]
-        + [pl.BlockSpec((None, keys, 256), lambda t: (where(t)[0], 0, where(t)[1]))]
+        + [out_fixed(PLANES, PAIRS, 2, tokens), flat, flat_stat]
+        + [
+            pl.BlockSpec((None, keys, 256), lambda t: (where(t)[0], 0, where(t)[1])),
+            pl.BlockSpec((None, 2, keys, tokens), lambda t: where(t) + (0, 0)),
+        ]
         + [hbm] * 13,
         scratch_shapes=[
             pltpu.VMEM((keys, width), BF),
@@ -882,18 +891,20 @@
             pltpu.VMEM((PLANES, PAIRS, 2, tokens), F32),
             pltpu.VMEM((8, 128), jnp.int32),
             pltpu.VMEM((3, 8, 128), jnp.int32),
+            pltpu.VMEM((8, 128), jnp.int32),
             pltpu.SemaphoreType.DMA((plane + 1,)),
         ]
         + courier.scratch(),
         compiler_params=pltpu.CompilerParams(
             vmem_limit_bytes=62 * 2**20, collective_id=ident, has_side_effects=True
         ),
-    )(inputs, *gains, *weights, lens, key_weight, value_weight, memory)
-    saved, (all_lens, part0, lse0, kv), moved = outs[:7], outs[7:11], outs[11:]
+    )(inputs, *gains, *weights, length, key_weight, value_weight, memory)
+    saved, (tops, part0, lse0, kv, probs), moved = outs[:7], outs[7:12], outs[12:]
     return dict(
         saved=saved,
-        lens=all_lens,
+        tops=tops,
         keyvals=kv,
+        probs=probs,
         rows={r: moved[n] for n, r in enumerate(ORDER)},
         queries={0: saved[6], **{r: moved[3 + r] for r in near}},
         parts=[part0] + [moved[6 + r] for r in near],
@@ -1146,7 +1157,7 @@
         + grad_shapes,
         in_specs=[whole] * 4
         + [stat] * 4
-        + [whole, square, fixed(1, width), whole]
+        + [whole, square, fixed(width), whole]
         + [column, column, pl.BlockSpec((chunk, width), lambda p: (first(p), 0))],
         out_specs=[whole] * 4
         + [fixed(2, PAIRS, 2, tokens), fixed(1, width), square]
@@ -1157,14 +1168,14 @@
 
 
 def cross_backward(
-    courier, ident, r, queries, grad, keyvals, lens, stats, key_weight, value_weight, summands=()
+    courier, ident, r, queries, grad, keyvals, probs, tops, stats, key_weight, value_weight, summands=()
 ):
     tokens, keys = queries.shape[0], keyvals.shape[1]
     width = H * HD
     spec = block_specs(tokens, keys)
 
     def body(ins, outs, scratch):
-        q_ref, da_ref, kv_ref, lens_ref, stats_ref, wk_ref, wv_ref = ins
+        q_ref, da_ref, kv_ref, probs_ref, top_ref, stats_ref, wk_ref, wv_ref = ins
         dkv_ref, dq_ref, dm_ref = outs
         (total_ref,) = scratch
         step = pl.program_id(0)
@@ -1173,12 +1184,9 @@
         def _():
             total_ref[...] = jnp.zeros_like(total_ref)
 
-        bias = key_bias(keys, lens_ref[...])
-
-        def again(h, keys_h, query_h):
-            mine, _, one = lane_masks()[h]
-            scores = dot(keys_h * mine + bias * one, query_h + one, 1, 1)
-            return jnp.exp(scores - stats_ref[0, 0, h : h + 1, :])
+        def stored(h, keys_h, query_h):
+            scale = jnp.exp(top_ref[0, h : h + 1, :] - stats_ref[0, 0, h : h + 1, :])
+            return probs_ref[h].astype(F32) * scale
 
         weights = jnp.concatenate([wk_ref[...], wv_ref[...]], axis=1)
         grad_kv, grad_q = backward_pair(
@@ -1186,7 +1194,7 @@
             da_ref[...],
             kv_ref[:, :128],
             kv_ref[:, 128:],
-            again,
+            stored,
             [stats_ref[1, 0, h : h + 1, :] for h in range(2)],
         )
         dkv_ref[...] = grad_kv
@@ -1201,12 +1209,13 @@
         courier,
         ident,
         body,
-        [queries, grad, keyvals, lens, stats, key_weight, value_weight],
+        [queries, grad, keyvals, probs, tops, stats, key_weight, value_weight],
         [
             spec["col"],
             spec["col"],
             pl.BlockSpec((None, keys, 256), lambda p: (r, 0, p)),
-            pl.BlockSpec((None, 8, 128), lambda p: (r, 0, 0)),
+            pl.BlockSpec((None, 2, keys, tokens), lambda p: (r, p, 0, 0)),
+            pl.BlockSpec((None, 1, 2, tokens), lambda p: (rem(r + 3, PLANES), p, 0, 0)),
             pl.BlockSpec((2, 1, 2, tokens), lambda p: (0, p, 0, 0)),
             spec["weight"],
             spec["weight"],
@@ -1326,8 +1335,10 @@
         chunk_sems, early_sems = load_sems, work[6]
         copies = courier.copies(sources, [dq_got] + list(targets), sems)
         courier.greet()
-        for copy in copies:
-            copy.start()
+        later = copies[6 : 1 + courier.plane]
+        for n, copy in enumerate(copies):
+            if not 6 <= n < 1 + courier.plane:
+                copy.start()
 
         def chunk_loads(r, i):
             slot = rem(i, 2)
@@ -1385,6 +1396,7 @@
                 pl.ds(pl.multiple_of(p * 128, 128), 128),
             )
 
+        later[0].start()
         bound[0].begin()
         for copy in early_loads:
             copy.wait()
@@ -1442,9 +1454,12 @@
             )
             far_sum.begin()
             if third == 0:
+                later[1].start()
                 bound[0].after_second()
                 bound[1].after_first()
             if third == 1:
+                for copy in later[2:]:
+                    copy.start()
                 bound[0].after_third_start()
                 bound[1].after_second()
                 bound[2].after_first()
@@ -1455,28 +1470,31 @@
                 bound[3].after_second()
                 bound[4].after_first()
                 bound[5].after_first()
-        grad_normed = dot(dq1[...], wq_ref[...], 1, 1) + dot(dk1[...], wk_ref[...], 1, 1)
-        bound[6].after_first()
-        bound[7].after_first()
-        bound[2].after_third_start()
-        bound[3].after_third_start()
-        grad_normed += dot(dv1[...], wv_ref[...], 1, 1)
+        grad_normed = (
+            dot(dq1[...], wq_ref[...], 1, 1)
+            + dot(dk1[...], wk_ref[...], 1, 1)
+            + dot(dv1[...], wv_ref[...], 1, 1)
+        )
         back, self_norm = rms_back(values, self_gain[...], grad_normed)
-        bound[4].after_second()
-        bound[5].after_second()
-        bound[6].after_second()
-        bound[7].after_second()
         grad_in[...] += back
         bits.held[0][...] = jnp.concatenate(
             [self_norm, cross_norm, ffn_term[...], jnp.zeros((5, width), F32)], axis=0
         )
         bits.start(0)
+        bound[2].after_third_start()
+        bound[3].after_third_start()
+        bound[4].after_second()
+        bound[5].after_second()
+        bound[6].after_first()
+        bound[7].after_first()
+        bits.advance(0)
         bound[4].after_third_start()
         bound[5].after_third_start()
-        bits.advance(0)
+        bound[6].after_second()
+        bound[7].after_second()
+        bits.advance(1)
         bound[6].after_third_start()
         bound[7].after_third_start()
-        bits.advance(1)
         bits.advance(2)
         bound[0].finish(sums[0])
         bound[1].finish(sums[1])
@@ -1702,9 +1720,9 @@
         sizes,
         0,
         memory,
-        jnp.broadcast_to(memory_lengths[None, :], (8, 128)),
+        memory_lengths,
         decoder_in[0],
-        (norm_self[None], norm_cross[None]),
+        (norm_self, norm_cross),
         (self_query, self_key, self_value, self_out, cross_query),
         cross_key,
         cross_value,
@@ -1729,7 +1747,7 @@
         forward["lses"],
         hidden_one,
         cross_out,
-        norm_ffn[None],
+        norm_ffn,
         cotangent[0],
         ffn_gate,
         ffn_up,
@@ -1764,7 +1782,8 @@
             queries[r],
             grads[r],
             forward["keyvals"],
-            forward["lens"],
+            forward["probs"],
+            forward["tops"],
             both[r],
             cross_key,
             cross_value,
@@ -1795,7 +1814,7 @@
             (decoder_in[0], hidden_one, grad_cross_out, query_one, key_one, value_one, attn_one)
             + (self_query, self_key, self_value, self_out, cross_query),
             lse_one,
-            (norm_self[None], norm_cross[None], grad_norm_ffn),
+            (norm_self, norm_cross, grad_norm_ffn),
         )
         returned[last], got[0], got[1] = moved
         ffn, halves, norm_rows, whole = finish(

time: 562 us -> 538 us (0.957)
  Pallas kernels: 546 us -> 527 us
    pallas_call x1, Pallas kernels: 215 us -> 192 us  [forward_part(): pl.pallas_call(kernel, grid=(count,), out_shape=[rows, rows, rows, stat,...]
    pallas_call x1, Pallas kernels: 93.4 us -> 111 us  [ending(): pl.pallas_call(kernel, out_shape=[jax.ShapeDtypeStruct((tokens, width), F...]
    pallas_call x1, Pallas kernels: 46.5 us -> 30.7 us  [middle(): pl.pallas_call(functools.partial(middle_kernel, sizes=sizes, packed=packe...]
where the time goes in v11:
time: 538 us; the launch traced here: 531 us
  Pallas kernels  527 us (98%)
    pallas_call x1, Pallas kernels, forward_part(): pl.pallas_call(kernel, grid=(count,), out_shape=[rows, rows, rows, stat,...  192 us
    pallas_call x4, Pallas kernels, call(): pl.pallas_call(lambda *refs: kernel(*counts, refs), grid=(PAIRS,), out_sh...  179 us
    pallas_call x1, Pallas kernels, ending(): pl.pallas_call(kernel, out_shape=[jax.ShapeDtypeStruct((tokens, width), F...  111 us
    pallas_call x1, Pallas kernels, middle(): pl.pallas_call(functools.partial(middle_kernel, sizes=sizes, packed=packe...  30.7 us
    pallas_call x1, Pallas kernels, finish(): pl.pallas_call(functools.partial(finish_kernel, pieces=pieces), out_shape...  13.9 us

profile of v11, /device:TPU:0, one launch (start us, length us, event | category | flops | bytes accessed | tf_op | source)
XLA Modules:
  0.0 530.7 jit_solution(9273879042510354695)
XLA Ops:
  1.3 192.0 %shard_map.305 = (bf16[512,768]{1,0:T(8,128)(2,1)}, bf16[512,768]{1,0:T(8,128)(2,1)}, bf16[512,768]{1,0:T(8,128)(2,1)}, f32[6,2,512]{2,1,0:T(2,128)}, bf16[512,7...) custom-call(bf16[512,768]{1,0:T(8,128)(2,1)} %bitcast.18, ...), custom_call_target="tpu_custom_call" | custom-call | tf_op jit(solution)/shard_map/pallas_call | solution.py:864
  193.3 30.7 %shard_map.306 = (bf16[512,768]{1,0:T(8,128)(2,1)}, bf16[512,768]{1,0:T(8,128)(2,1)}, f32[512,768]{1,0:T(8,128)}, bf16[512,768]{1,0:T(8,128)(2,1)}, f32[2,6,2,51...) custom-call(bf16[512,768]{1,0:T(8,128)(2,1)} %get-tuple-element.102., ...), custom_call_target="tpu_custom_call" | custom-call | tf_op jit(solution)/shard_map/pallas_call | solution.py:1145
  224.0 48.6 %shard_map.307 = (bf16[2048,1536]{1,0:T(8,128)(2,1)}, bf16[512,768]{1,0:T(8,128)(2,1)}, bf16[2048,768]{1,0:T(8,128)(2,1)}, bf16[512,768]{1,0:T(8,128)(2,1)}, f32...) custom-call(bf16[512,768]{1,0:T(8,128)(2,1)} %get-tuple-element.101.refs_0_, ...), custom_call_target="tpu_custom_call" | custom-call | flops 34359738368 | bytes 16777216 | tf_op jit(solution)/shard_map/pallas_call | solution.py:583
  272.5 44.7 %shard_map.308 = (bf16[2048,1536]{1,0:T(8,128)(2,1)}, bf16[512,768]{1,0:T(8,128)(2,1)}, bf16[2048,768]{1,0:T(8,128)(2,1)}, bf16[512,768]{1,0:T(8,128)(2,1)}, f32...) custom-call(bf16[512,768]{1,0:T(8,128)(2,1)} %get-tuple-element.124.refs_0_, ...), custom_call_target="tpu_custom_call" | custom-call | flops 34359738368 | bytes 16777216 | tf_op jit(solution)/shard_map/pallas_call | solution.py:583
  317.3 44.3 %shard_map.309 = (bf16[2048,1536]{1,0:T(8,128)(2,1)}, bf16[512,768]{1,0:T(8,128)(2,1)}, bf16[2048,768]{1,0:T(8,128)(2,1)}, bf16[512,768]{1,0:T(8,128)(2,1)}, f32...) custom-call(bf16[512,768]{1,0:T(8,128)(2,1)} %get-tuple-element.129.refs_0_, ...), custom_call_target="tpu_custom_call" | custom-call | flops 34359738368 | bytes 16777216 | tf_op jit(solution)/shard_map/pallas_call | solution.py:583
  361.6 41.4 %shard_map.310 = (bf16[2048,1536]{1,0:T(8,128)(2,1)}, bf16[512,768]{1,0:T(8,128)(2,1)}, bf16[2048,768]{1,0:T(8,128)(2,1)}, bf16[8,256,768]{2,1,0:T(8,128)(2,1)}, bf16[512,768]{1,0:T(8,128)(2,1)}) custom-call(bf16[512,768]{1,0:T(8,128)(2,1)} %get-tuple-element.135.refs_0_, bf16[512,768]{1,0:T(8,128)(2,1)} %get-tuple-element.136.refs_1_, ...), custom_call_target="tpu_custom_call" | custom-call | flops 34359738368 | bytes 16777216 | tf_op jit(solution)/shard_map/pallas_call | solution.py:583
  403.0 111.0 %shard_map.311 = (f32[512,768]{1,0:T(8,128)}, f32[48,768]{1,0:T(8,128)}, f32[48,768]{1,0:T(8,128)}, f32[48,768]{1,0:T(8,128)}, f32[48,768]{1,0:T(8,128)}, /*inde...) custom-call(bf16[2048,768]{1,0:T(8,128)(2,1)} %bitcast.23, ...), custom_call_target="tpu_custom_call" | custom-call | tf_op jit(solution)/shard_map/pallas_call | solution.py:1535
  514.0 13.9 %shard_map.312 = (f32[24,2048]{1,0:T(8,128)}, f32[24,2048]{1,0:T(8,128)}, f32[64,768]{1,0:T(8,128)}, f32[24,768]{1,0:T(8,128)}, f32[24,768]{1,0:T(8,128)}, /*ind...) custom-call(bf16[4,48,2048]{2,1,0:T(8,128)(2,1)} %get-tuple-element., ...), custom_call_target="tpu_custom_call" | custom-call | tf_op jit(solution)/shard_map/pallas_call | solution.py:1625
  527.9 1.2 slice_bitcast_fusion.2
  529.1 1.2 slice_bitcast_fusion

commit v12 on v11

--- a/solution.py
+++ b/solution.py
@@ -1335,10 +1335,8 @@
         chunk_sems, early_sems = load_sems, work[6]
         copies = courier.copies(sources, [dq_got] + list(targets), sems)
         courier.greet()
-        later = copies[6 : 1 + courier.plane]
-        for n, copy in enumerate(copies):
-            if not 6 <= n < 1 + courier.plane:
-                copy.start()
+        for copy in copies:
+            copy.start()
 
         def chunk_loads(r, i):
             slot = rem(i, 2)
@@ -1396,7 +1394,6 @@
                 pl.ds(pl.multiple_of(p * 128, 128), 128),
             )
 
-        later[0].start()
         bound[0].begin()
         for copy in early_loads:
             copy.wait()
@@ -1454,12 +1451,9 @@
             )
             far_sum.begin()
             if third == 0:
-                later[1].start()
                 bound[0].after_second()
                 bound[1].after_first()
             if third == 1:
-                for copy in later[2:]:
-                    copy.start()
                 bound[0].after_third_start()
                 bound[1].after_second()
                 bound[2].after_first()

time: 538 us -> 519 us (0.965)
  Pallas kernels: 527 us -> 508 us
    pallas_call x1, Pallas kernels: 111 us -> 92 us  [ending(): pl.pallas_call(kernel, out_shape=[jax.ShapeDtypeStruct((tokens, width), F...]
where the time goes in v12:
time: 519 us; the launch traced here: 512 us
  Pallas kernels  508 us (98%)
    pallas_call x1, Pallas kernels, forward_part(): pl.pallas_call(kernel, grid=(count,), out_shape=[rows, rows, rows, stat,...  192 us
    pallas_call x4, Pallas kernels, call(): pl.pallas_call(lambda *refs: kernel(*counts, refs), grid=(PAIRS,), out_sh...  179 us
    pallas_call x1, Pallas kernels, ending(): pl.pallas_call(kernel, out_shape=[jax.ShapeDtypeStruct((tokens, width), F...  92 us
    pallas_call x1, Pallas kernels, middle(): pl.pallas_call(functools.partial(middle_kernel, sizes=sizes, packed=packe...  30.7 us
    pallas_call x1, Pallas kernels, finish(): pl.pallas_call(functools.partial(finish_kernel, pieces=pieces), out_shape...  13.9 us

profile of v12, /device:TPU:0, one launch (start us, length us, event | category | flops | bytes accessed | tf_op | source)
XLA Modules:
  0.0 511.7 jit_solution(10060139748480733472)
XLA Ops:
  1.3 192.0 %shard_map.305 = (bf16[512,768]{1,0:T(8,128)(2,1)}, bf16[512,768]{1,0:T(8,128)(2,1)}, bf16[512,768]{1,0:T(8,128)(2,1)}, f32[6,2,512]{2,1,0:T(2,128)}, bf16[512,7...) custom-call(bf16[512,768]{1,0:T(8,128)(2,1)} %bitcast.18, ...), custom_call_target="tpu_custom_call" | custom-call | tf_op jit(solution)/shard_map/pallas_call | solution.py:864
  193.3 30.7 %shard_map.306 = (bf16[512,768]{1,0:T(8,128)(2,1)}, bf16[512,768]{1,0:T(8,128)(2,1)}, f32[512,768]{1,0:T(8,128)}, bf16[512,768]{1,0:T(8,128)(2,1)}, f32[2,6,2,51...) custom-call(bf16[512,768]{1,0:T(8,128)(2,1)} %get-tuple-element.102., ...), custom_call_target="tpu_custom_call" | custom-call | tf_op jit(solution)/shard_map/pallas_call | solution.py:1145
  224.0 48.6 %shard_map.307 = (bf16[2048,1536]{1,0:T(8,128)(2,1)}, bf16[512,768]{1,0:T(8,128)(2,1)}, bf16[2048,768]{1,0:T(8,128)(2,1)}, bf16[512,768]{1,0:T(8,128)(2,1)}, f32...) custom-call(bf16[512,768]{1,0:T(8,128)(2,1)} %get-tuple-element.101.refs_0_, ...), custom_call_target="tpu_custom_call" | custom-call | flops 34359738368 | bytes 16777216 | tf_op jit(solution)/shard_map/pallas_call | solution.py:583
  272.5 44.7 %shard_map.308 = (bf16[2048,1536]{1,0:T(8,128)(2,1)}, bf16[512,768]{1,0:T(8,128)(2,1)}, bf16[2048,768]{1,0:T(8,128)(2,1)}, bf16[512,768]{1,0:T(8,128)(2,1)}, f32...) custom-call(bf16[512,768]{1,0:T(8,128)(2,1)} %get-tuple-element.124.refs_0_, ...), custom_call_target="tpu_custom_call" | custom-call | flops 34359738368 | bytes 16777216 | tf_op jit(solution)/shard_map/pallas_call | solution.py:583
  317.3 44.3 %shard_map.309 = (bf16[2048,1536]{1,0:T(8,128)(2,1)}, bf16[512,768]{1,0:T(8,128)(2,1)}, bf16[2048,768]{1,0:T(8,128)(2,1)}, bf16[512,768]{1,0:T(8,128)(2,1)}, f32...) custom-call(bf16[512,768]{1,0:T(8,128)(2,1)} %get-tuple-element.129.refs_0_, ...), custom_call_target="tpu_custom_call" | custom-call | flops 34359738368 | bytes 16777216 | tf_op jit(solution)/shard_map/pallas_call | solution.py:583
  361.6 41.4 %shard_map.310 = (bf16[2048,1536]{1,0:T(8,128)(2,1)}, bf16[512,768]{1,0:T(8,128)(2,1)}, bf16[2048,768]{1,0:T(8,128)(2,1)}, bf16[8,256,768]{2,1,0:T(8,128)(2,1)}, bf16[512,768]{1,0:T(8,128)(2,1)}) custom-call(bf16[512,768]{1,0:T(8,128)(2,1)} %get-tuple-element.135.refs_0_, bf16[512,768]{1,0:T(8,128)(2,1)} %get-tuple-element.136.refs_1_, ...), custom_call_target="tpu_custom_call" | custom-call | flops 34359738368 | bytes 16777216 | tf_op jit(solution)/shard_map/pallas_call | solution.py:583
  403.0 92.0 %shard_map.311 = (f32[512,768]{1,0:T(8,128)}, f32[48,768]{1,0:T(8,128)}, f32[48,768]{1,0:T(8,128)}, f32[48,768]{1,0:T(8,128)}, f32[48,768]{1,0:T(8,128)}, /*inde...) custom-call(bf16[2048,768]{1,0:T(8,128)(2,1)} %bitcast.23, ...), custom_call_target="tpu_custom_call" | custom-call | tf_op jit(solution)/shard_map/pallas_call | solution.py:1529
  495.0 13.9 %shard_map.312 = (f32[24,2048]{1,0:T(8,128)}, f32[24,2048]{1,0:T(8,128)}, f32[64,768]{1,0:T(8,128)}, f32[24,768]{1,0:T(8,128)}, f32[24,768]{1,0:T(8,128)}, /*ind...) custom-call(bf16[4,48,2048]{2,1,0:T(8,128)(2,1)} %get-tuple-element., ...), custom_call_target="tpu_custom_call" | custom-call | tf_op jit(solution)/shard_map/pallas_call | solution.py:1619
  508.9 1.2 slice_bitcast_fusion.2
  510.1 1.2 slice_bitcast_fusion
